TPU v7x, 512 devices: a whole 4x4x16 slice. The times are simulated.
512 devices in a mesh: dp: 8 (over y_lo, x), shard: 64 (over y_hi, z, core).
Axes of the slice: x: 4, y: 4 (y_hi: 2, y_lo: 2; y = y_hi * 2 + y_lo), z: 16, core: 2. Of those that a mesh axis runs over, the one named last changes fastest.
Arguments:
- features: bfloat16 [16, 4096, 512], P('dp', 'shard'), may hold values from -6 to 6
- upstream: bfloat16 [16, 4096, 14336], P('dp', 'shard'), may hold values from -6 to 6
- lengths: int32 [16], P('dp'), may hold values from 2048 to 4096, as said below
- weights: bfloat16 [14336, 512], P(('dp', 'shard')), may hold values from -0.25 to 0.25
Outputs:
- inv_diag: float32 [14336, 512], P(('dp', 'shard'))
- saliency: float32 [14336, 512], P(('dp', 'shard'))
- fisher_step: float32 [14336, 512], P(('dp', 'shard'))
Inputs may be any that keep to these rules, and one draw needn't show every extreme that they name: `lengths`: some example has all 4096 positions valid and some exactly half of them.
All inputs are finite; a program needn't handle non-finite values.
Results may differ from a plain program's by a relative error of at most 0.002.
Values may be sent and summed in bfloat16 or wider, within the bound.
No kernel may reach another device: no remote copies, remote signals or barrier semaphores. Data moves between devices by JAX's collectives and lax.ppermute only.
A program may use at most 128 MiB of HBM per device.

v0:
```python
import jax
import jax.numpy as jnp
from jax import lax
from jax.sharding import PartitionSpec as P

BLOCK = 128


def body(features, upstream, lengths, weights):
    n_shard = lax.axis_size("shard")
    n_groups = lax.axis_size("dp")
    ex_local, seg_len, rows = features.shape
    units = upstream.shape[2]
    span_units = units // (n_groups * n_shard)
    total_len = seg_len * n_shard
    block_len = BLOCK
    positions = lax.axis_index("shard") * seg_len + jnp.arange(seg_len, dtype=jnp.int32)
    kept_rows = positions[None, :] < lengths[:, None]
    masked = jnp.where(kept_rows[:, :, None], features, jnp.zeros_like(features))
    by_owner = upstream.reshape(ex_local, seg_len, n_groups, n_shard, span_units)
    columns = lax.all_to_all(by_owner, "shard", split_axis=3, concat_axis=1, tiled=True)
    columns = columns.reshape(ex_local, total_len, n_groups * span_units)
    summed = lax.dot_general(
        columns,
        lax.all_gather(masked, "shard", axis=1, tiled=True),
        (((1,), (1,)), ((0,), (0,))),
        preferred_element_type=jnp.float32,
    )
    summed = summed.reshape(ex_local, n_groups, span_units, rows)
    grads = summed / lengths.astype(jnp.float32)[:, None, None, None]
    owned = lax.all_to_all(grads, "dp", split_axis=1, concat_axis=0, tiled=True)
    rank = ex_local * n_groups
    nblocks = span_units * rows // block_len
    blocks = owned.reshape(rank, nblocks, block_len).transpose(1, 0, 2)
    shift = block_len / total_len
    wblocks = weights.astype(jnp.float32).reshape(nblocks, block_len)
    gram = jnp.einsum("nib,njb->nij", blocks, blocks, precision=lax.Precision.HIGHEST)
    kernel = gram + shift * jnp.eye(rank, dtype=jnp.float32)[None]
    factor = jnp.linalg.cholesky(kernel)
    solved = jax.scipy.linalg.cho_solve((factor, True), blocks)
    diag_part = 1.0 - jnp.sum(blocks * solved, axis=1)
    projected = jnp.einsum("nib,nb->ni", solved, wblocks, precision=lax.Precision.HIGHEST)
    step_part = wblocks - jnp.einsum(
        "nib,ni->nb", blocks, projected, precision=lax.Precision.HIGHEST
    )
    inv_diag = diag_part.reshape(span_units, rows)
    saliency = rows * jnp.square(weights.astype(jnp.float32)) / (2.0 * inv_diag)
    fisher_step = jnp.sqrt(float(rows)) * step_part.reshape(span_units, rows)
    return (inv_diag, saliency, fisher_step)


def solution(mesh):
    in_specs = (P("dp", "shard", None), P("dp", "shard", None), P("dp"), P(("dp", "shard"), None))
    out_specs = (P(("dp", "shard"), None), P(("dp", "shard"), None), P(("dp", "shard"), None))
    return jax.shard_map(body, mesh=mesh, in_specs=in_specs, out_specs=out_specs, check_vma=False)
```

profile of v0, /device:TPU:1, one launch (start us, length us, event | category | flops | bytes accessed | tf_op | source)
XLA Modules:
  0.0 503.6 jit_solution(3415303485355451039)
XLA Ops:
  7.2 0.7 broadcast_compare_fusion
  8.0 1.6 broadcast_select_fusion
  9.6 15.8 %copy.21 = bf16[2,64,14336]{1,0,2:T(2,128)(2,1)} copy(bf16[2,64,14336]{2,1,0:T(8,128)(2,1)} %param.5) | data formatting | bytes 7340032 | tf_op args[1]
  25.4 10.0 %copy.50 = bf16[2,64,8,64,28]{1,0,4,2,3:T(2,128)(2,1)} copy(bf16[2,64,8,64,28]{1,0,4,3,2:T(2,128)(2,1)} %bitcast.58) | data formatting | bytes 7340032 | tf_op jit(solution)/shard_map/reshape | solution.py:20
  35.4 15.8 %reshape.100 = bf16[64,2,14336]{2,1,0:T(2,128)(2,1)} reshape(bf16[64,8,28,2,64]{4,3,2,1,0:T(2,128)(2,1)} %bitcast.57) | data formatting | bytes 7340032
  51.2 20.0 %all-to-all-start = ((bf16[64,2,14336]{2,1,0:T(2,128)(2,1)}), bf16[64,2,14336]{2,1,0:T(2,128)(2,1)}, u32[]{:S(2)}, u32[]{:S(2)}) async-start(bf16[64,2,14336]{2,1,0:T(2,128)(2,1)} %reshape.100), calls=%async_computation | async-start | bytes 7340032 | tf_op jit(solution)/shard_map/all_to_all | solution.py:21
  71.2 182.3 %all-to-all-done = bf16[64,2,14336]{2,1,0:T(2,128)(2,1)} async-done(((bf16[64,2,14336]{2,1,0:T(2,128)(2,1)}), bf16[64,2,14336]{2,1,0:T(2,128)(2,1)}, u32[]{:S(2)}, u32[]{:S(2)}) %all-to-all-start) | async-done | bytes 3670048 | tf_op jit(solution)/shard_map/all_to_all | solution.py:21
  253.5 15.9 %reshape.101 = bf16[64,8,28,2,64]{4,3,2,1,0:T(2,128)(2,1)} reshape(bf16[64,2,14336]{2,1,0:T(2,128)(2,1)} %all-to-all-done) | data formatting | bytes 7340032
  269.4 7.5 %bitcast_bitcast_fusion = bf16[2,64,64,8,1,28]{2,0,5,3,1,4:T(2,128)(2,1)S(1)} fusion(bf16[64,8,28,2,64]{4,3,2,1,0:T(2,128)(2,1)} %reshape.101), kind=kLoop, calls=%fused_computation.31 | loop fusion | bytes 7340032 | tf_op jit(solution)/shard_map/all_to_all | solution.py:21
  276.9 7.7 %copy.23 = bf16[2,64,64,8,1,28]{2,1,5,3,0,4:T(8,128)(2,1)} copy(bf16[2,64,64,8,1,28]{2,0,5,3,1,4:T(2,128)(2,1)S(1)} %bitcast_bitcast_fusion) | data formatting | bytes 7340032 | tf_op jit(solution)/shard_map/all_to_all | solution.py:21
  284.6 10.5 %reshape.89 = bf16[2,4096,224]{1,2,0:T(8,128)(2,1)} reshape(bf16[2,64,64,8,1,28]{2,1,5,3,0,4:T(8,128)(2,1)} %copy.23) | data formatting | bytes 7340032 | tf_op jit(solution)/shard_map/reshape | solution.py:22
  295.2 6.6 %convolution_bitcast_fusion = f32[2,224,512]{2,1,0:T(8,128)S(1)} fusion(bf16[2,4096,224]{1,2,0:T(8,128)(2,1)} %reshape.89, bf16[2,4096,512]{2,1,0:T(8,128)(2,1)} %all-gather.2.cloned.1.call-done), kind=kOutput, calls=%fused_computation | convolution fusion | flops 1879048192 | bytes 12976128 | tf_op jit(solution)/shard_map/dot_general | solution.py:23
  301.7 0.7 copy.24
  302.4 1.3 broadcast_divide_fusion
  303.8 4.6 all-to-all-start.1
  308.5 9.9 %all-to-all-done.1 = f32[2,8,28,512]{3,0,2,1:T(2,128)S(1)} async-done(((f32[2,8,28,512]{3,0,2,1:T(2,128)}), f32[2,8,28,512]{3,0,2,1:T(2,128)S(1)}, u32[]{:S(2)}, u32[]{:S(2)}) %all-to-all-start.1) | async-done | bytes 917536 | tf_op jit(solution)/shard_map/all_to_all | solution.py:31
  318.3 0.2 copy.25
  318.6 1.8 fusion.6
  320.4 0.3 copy.27
  320.7 1.1 fusion.1
  321.7 164.8 %custom-call.11 = f32[112,16,16]{2,1,0:T(8,128)S(1)} custom-call(f32[112,16,16]{2,1,0:T(8,128)} %fusion.1), custom_call_target="Cholesky" | custom-call | tf_op jit(solution)/shard_map/jit(cholesky)/cholesky | solution.py:39
  486.5 0.4 copy.28
  486.9 0.1 select_reduce_fusion
  487.0 0.1 select_bitcast_fusion
  487.1 2.7 custom-call.12
  489.9 0.4 copy.31
  490.3 1.8 fusion.4
  492.1 1.4 fusion.8
  493.4 0.8 convolution_bitcast_fusion.1
  494.3 1.1 fusion.2
  495.5 0.6 mul.48
  496.1 0.7 multiply_divide_fusion
  (21 shorter events, 0.3 us)
Async XLA Ops:
  7.2 288.0 %all-gather.2.cloned.1.call-start = ((), (), s32[]{:S(2)}) async-start(), calls=%async_computation.2 | async-start | bytes 8519680 | tf_op jit(solution)/shard_map/all_gather | solution.py:25
  35.4 35.8 %copy-start.2 = (s32[2]{0:T(128)S(1)}, s32[2]{0:T(128)}, u32[]{:S(2)}) copy-start(s32[2]{0:T(128)} %param.6) | copy-start | bytes 28
  51.2 202.2 %all-to-all-start = ((bf16[64,2,14336]{2,1,0:T(2,128)(2,1)}), bf16[64,2,14336]{2,1,0:T(2,128)(2,1)}, u32[]{:S(2)}, u32[]{:S(2)}) async-start(bf16[64,2,14336]{2,1,0:T(2,128)(2,1)} %reshape.100), calls=%async_computation | async-start | bytes 7340032 | tf_op jit(solution)/shard_map/all_to_all | solution.py:21
  295.2 13.2 %copy-start = (bf16[28,512]{1,0:T(8,128)(2,1)S(1)}, bf16[28,512]{1,0:T(8,128)(2,1)}, u32[]{:S(2)}) copy-start(bf16[28,512]{1,0:T(8,128)(2,1)} %param.7) | copy-start | bytes 86020
  303.8 14.5 %all-to-all-start.1 = ((f32[2,8,28,512]{3,0,2,1:T(2,128)}), f32[2,8,28,512]{3,0,2,1:T(2,128)S(1)}, u32[]{:S(2)}, u32[]{:S(2)}) async-start(f32[2,8,28,512]{3,0,2,1:T(2,128)} %broadcast_divide_fusion), calls=%async_computation.1 | async-start | bytes 1835008 | tf_op jit(solution)/shard_map/all_to_all | solution.py:31
  496.1 0.7 copy-start.1
Sparse Core Ops, SparseCore 0:
  11.3 246.1 all-gather.1
where the time goes:
time: 512 us; the launch traced here: 504 us
  waiting for transfers between devices  192 us (38%)
  other arithmetic  173 us (34%)
  local copies, waits for them, and re-layouts  86.1 us (17%)
  starting transfers between devices  24.6 us (5%)
  between operations  14.2 us (3%)
  matrix products  13.5 us (3%)
    all_to_all x1, waiting for transfers between devices, body(): lax.all_to_all(by_owner, 'shard', split_axis=3, concat_axis=1, tiled=True)  182 us
    another operation x4, other arithmetic, body(): factor = jnp.linalg.cholesky(kernel)  165 us
    unnamed x9, local copies, waits for them, and re-layouts  47.6 us
    all_to_all x1, starting transfers between devices, body(): lax.all_to_all(by_owner, 'shard', split_axis=3, concat_axis=1, tiled=True)  20 us
    all_to_all x2, local copies, waits for them, and re-layouts, body(): lax.all_to_all(by_owner, 'shard', split_axis=3, concat_axis=1, tiled=True)  15.2 us
    reshape x1, local copies, waits for them, and re-layouts, body(): columns = columns.reshape(ex_local, total_len, n_groups * span_units)  10.5 us
  transfers between devices with their start and end apart: 3, of which 2 were waited for; matrix products, arithmetic and copies ran while one was open for 17% of the time, Pallas kernels for 0%

commit v1 on v0

v1 whole, which is shorter than its diff:
```python
import functools

import jax
import jax.numpy as jnp
from jax import lax
from jax.experimental import pallas as pl
from jax.experimental.pallas import tpu as pltpu
from jax.sharding import Mesh, PartitionSpec as P

BLOCK = 128
AXES = ("ylo", "x", "yhi", "z", "core")
NZ = 16
GROUPS = ((8, 7, 9), (6, 10, 5, 11), (4, 12, 3, 13), (2, 14, 1, 15, 0))
SWAP = [(0, 1), (1, 0)]
f32 = jnp.float32
f16 = jnp.float16


def turn_kernel(s_ref, k0, k1, r0, r1, *rest):
    outs, hold = rest[:-1], rest[-1]
    turned = []
    for k, r in ((k0, r0), (k1, r1)):
        both = jnp.concatenate([k[...].astype(f32), r[...].astype(f32)], axis=0)
        turned.append(both.T)
    span = turned[0].shape[0] // NZ
    for dest in range(NZ):
        rows = [t[dest * span:(dest + 1) * span] for t in turned]
        hold[dest] = jnp.concatenate(rows, axis=0).astype(hold.dtype)
    z, sign = s_ref[1], s_ref[2]
    for out, group in zip(outs, GROUPS):
        for i, slot in enumerate(group):
            out[i, 0] = hold[lax.rem(z + sign * slot + NZ, NZ)]


def turn(upstream, other, scalars, n_groups):
    _, seg, units = upstream.shape
    width = units // (2 * n_groups)
    span2 = 2 * width // NZ
    kept = lambda j: pl.BlockSpec((None, seg, width), lambda i, s: (s[0], 0, 2 * (2 * i + j) + s[3]))
    sent = lambda j: pl.BlockSpec((seg, width), lambda i, s: (0, 2 * (2 * i + j) + s[3]))
    grid = (n_groups // 2,)
    return pl.pallas_call(
        turn_kernel,
        grid_spec=pltpu.PrefetchScalarGridSpec(
            num_scalar_prefetch=1,
            grid=grid,
            in_specs=[kept(0), kept(1), sent(0), sent(1)],
            out_specs=[
                pl.BlockSpec((len(g), 1, span2, 2 * seg), lambda i, s: (0, i, 0, 0)) for g in GROUPS
            ],
            scratch_shapes=[pltpu.VMEM((NZ, span2, 2 * seg), upstream.dtype)],
        ),
        out_shape=[
            jax.ShapeDtypeStruct((len(g), grid[0], span2, 2 * seg), upstream.dtype) for g in GROUPS
        ],
        compiler_params=pltpu.CompilerParams(vmem_limit_bytes=40 * 1024 * 1024),
    )(scalars, upstream, upstream, other, other)


def solve_kernel(shift, scale, g_ref, w_ref, inv_ref, sal_ref, step_ref, y_ref):
    n_ex = g_ref.shape[0]
    units = w_ref.shape[0]
    rows = w_ref.shape[1]
    pad = g_ref.shape[1]
    nb = rows // BLOCK

    def blocks(x):
        return jnp.concatenate([x[:, b * BLOCK:(b + 1) * BLOCK] for b in range(nb)], axis=0).T

    for e in range(n_ex):
        y_ref[e] = blocks(g_ref[e])
    weights = w_ref[...].astype(f32)
    w = blocks(jnp.concatenate([weights, jnp.zeros((pad - units, rows), f32)], axis=0))
    lane_rows = lax.broadcasted_iota(jnp.int32, (n_ex, BLOCK), 0)
    kern = []
    for i in range(n_ex):
        gi = y_ref[i]
        row = jnp.zeros((n_ex, BLOCK), f32)
        for j in range(i, n_ex):
            dot = jnp.sum(gi * y_ref[j], axis=0, keepdims=True)
            if j == i:
                dot = dot + shift
            row = jnp.where(lane_rows == j, dot, row)
        kern.append(row)
    diag = jnp.ones((BLOCK, BLOCK), f32)
    step = w
    for k in range(n_ex):
        pivot = kern[k]
        inv = 1.0 / pivot[k:k + 1]
        yk = y_ref[k]
        scaled = yk * inv
        diag = diag - yk * scaled
        step = step - scaled * jnp.sum(yk * w, axis=0, keepdims=True)
        for i in range(k + 1, n_ex):
            m = pivot[i:i + 1] * inv
            kern[i] = kern[i] - m * pivot
            y_ref[i] = y_ref[i] - m * yk
    diag = diag.T
    step = step.T * scale
    for b in range(nb):
        at = pl.ds(b * BLOCK, BLOCK)
        d = diag[b * pad:b * pad + units]
        wb = weights[:, b * BLOCK:(b + 1) * BLOCK]
        inv_ref[:, at] = d
        sal_ref[:, at] = rows * (wb * wb) / (2.0 * d)
        step_ref[:, at] = step[b * pad:b * pad + units]


def solve(grads, weights, shift):
    units, rows = weights.shape
    out = jax.ShapeDtypeStruct((units, rows), f32)
    return pl.pallas_call(
        functools.partial(solve_kernel, shift, float(rows) ** 0.5),
        out_shape=[out, out, out],
        scratch_shapes=[pltpu.VMEM((grads.shape[0], BLOCK, BLOCK), f32)],
        compiler_params=pltpu.CompilerParams(vmem_limit_bytes=40 * 1024 * 1024),
    )(grads, weights)


def ring_pairs(direction):
    pairs = []
    for z in range(NZ):
        for core in range(2):
            step = direction if core == 0 else -direction
            pairs.append((z * 2 + core, ((z + step) % NZ) * 2 + core))
    return pairs


def body(features, upstream, lengths, weights):
    yhi, z, core = lax.axis_index("yhi"), lax.axis_index("z"), lax.axis_index("core")
    _, seg, rows = features.shape
    units = upstream.shape[2]
    n_groups = 8
    total_len = seg * 64
    shard = (yhi * NZ + z) * 2 + core
    positions = shard * seg + jnp.arange(seg, dtype=jnp.int32)
    kept_rows = positions[None, :] < lengths[:, None]
    masked = jnp.where(kept_rows[:, :, None], features, jnp.zeros_like(features)) * jnp.asarray(0.25, features.dtype)

    pick = lambda x, i: lax.dynamic_index_in_dim(x, i, 0, keepdims=False)
    other = lax.ppermute(pick(upstream, 1 - core), "core", SWAP)
    mine = jnp.concatenate([pick(masked, core), lax.ppermute(pick(masked, 1 - core), "core", SWAP)], axis=0)
    theirs = lax.ppermute(mine, "yhi", SWAP)

    sign = 1 - 2 * core
    scalars = lambda half: jnp.stack([core, z, sign, half]).astype(jnp.int32)
    away = turn(upstream, other, scalars(1 - yhi), n_groups)
    arrived = [lax.ppermute(a, "yhi", SWAP) for a in away]
    home = turn(upstream, other, scalars(yhi), n_groups)

    parts = {}
    chunk = units // 2 // NZ
    for group, a, b in zip(GROUPS, home, arrived):
        dims = (((1,), (0,)), ((), ()))
        flat = lambda x: x.reshape(-1, x.shape[-1])
        part = lax.dot_general(flat(a), mine, dims, preferred_element_type=f32)
        part = part + lax.dot_general(flat(b), theirs, dims, preferred_element_type=f32)
        for i, slot in enumerate(group):
            parts[slot] = part[i * chunk:(i + 1) * chunk]

    half = chunk // 2
    pairs = (ring_pairs(1), ring_pairs(-1))
    slot_of = (lambda d: d, lambda d: NZ - d)
    sums = [parts[8][:half].astype(f16), parts[8][half:].astype(f16)]
    for dist in range(7, -1, -1):
        for k in range(2):
            got = lax.ppermute(sums[k], ("z", "core"), pairs[k])
            if dist == 0:
                sums[k] = got
                continue
            if dist == 7:
                empty = jnp.zeros_like(got)
                got = jnp.concatenate([got, empty] if k == 0 else [empty, got], axis=0)
            sums[k] = (got.astype(f32) + parts[slot_of[k](dist)]).astype(f16)
        if dist:
            sums = list(lax.optimization_barrier(tuple(sums)))
    length = pick(lengths, core).astype(f32)
    total = (sums[0].astype(f32) + sums[1].astype(f32) + parts[0]) * (4096.0 / length)
    pieces = total.astype(f16).reshape(2 * n_groups, -1, rows)
    owned = lax.all_to_all(pieces, ("ylo", "x", "core"), 0, 0, tiled=True)
    own_units = owned.shape[1]
    grads = owned.astype(f32) * (1.0 / 1024.0)
    grads = jnp.pad(grads, ((0, 0), (0, -own_units % 8), (0, 0)))
    return tuple(solve(grads, weights, BLOCK / total_len))


def solution(mesh):
    fine = Mesh(mesh.devices.reshape(2, 4, 2, NZ, 2), AXES)
    dp, shard = ("ylo", "x"), ("yhi", "z", "core")
    in_specs = (P(dp, shard, None), P(dp, shard, None), P(dp), P(dp + shard, None))
    out_specs = (P(dp + shard, None),) * 3
    return jax.shard_map(body, mesh=fine, in_specs=in_specs, out_specs=out_specs, check_vma=False)
```

time: 512 us -> 181 us (0.35); the launches traced: 504 us -> 180 us
  other arithmetic: 173 us -> 3.16 us
  waiting for transfers between devices: 192 us -> 65 us
  local copies, waits for them, and re-layouts: 86.1 us -> 5.89 us
  starting transfers between devices: 24.6 us -> 78.4 us
  blocking collectives: 0 us -> 14.1 us
  between operations: 14.2 us -> 1.72 us
  matrix products: 13.5 us -> 4.95 us
  Pallas kernels: 0 us -> 6.58 us
    all_to_all x2 -> x0, waiting for transfers between devices: 192 us -> none  [the longest x1 182 us: body(): lax.all_to_all(by_owner, 'shard', split_axis=3, concat_axis=1, tiled=True)]
    another operation x7 -> x2, other arithmetic: 168 us -> 0.16 us  [body(): scalars = lambda half: jnp.stack([core, z, sign, half]).astype(jnp.int32)]
    ppermute x0 -> x23, starting transfers between devices: none -> 78.4 us  [the longest x16 49.6 us: body(): got = lax.ppermute(sums[k], ('z', 'core'), pairs[k])]
    ppermute x0 -> x23, waiting for transfers between devices: none -> 65 us  [the longest x16 55.3 us: body(): got = lax.ppermute(sums[k], ('z', 'core'), pairs[k])]
    unnamed x9 -> x8, local copies, waits for them, and re-layouts: 47.6 us -> 2.05 us
    all_to_all x2 -> x0, starting transfers between devices: 24.5 us -> none  [the longest x1 20 us: body(): lax.all_to_all(by_owner, 'shard', split_axis=3, concat_axis=1, tiled=True)]
    reshape x5 -> x1, local copies, waits for them, and re-layouts: 20.6 us -> 0.14 us  [body(): pieces = total.astype(f16).reshape(2 * n_groups, -1, rows)]
    all_to_all x3 -> x0, local copies, waits for them, and re-layouts: 15.4 us -> none  [the longest x2 15.2 us: body(): lax.all_to_all(by_owner, 'shard', split_axis=3, concat_axis=1, tiled=True)]
  transfers between devices with their start and end apart: 3 -> 23, of which waited for: 2 -> 19; matrix products, arithmetic and copies ran while one was open for 17% -> 3% of each run, Pallas kernels for 0% -> 1%
where the time goes in v1:
time: 181 us; the launch traced here: 180 us
  starting transfers between devices  78.4 us (43%)
  waiting for transfers between devices  65 us (36%)
  blocking collectives  14.1 us (8%)
  Pallas kernels  6.58 us (4%)
  local copies, waits for them, and re-layouts  5.89 us (3%)
  matrix products  4.95 us (3%)
  other arithmetic  3.16 us (2%)
    ppermute x16, waiting for transfers between devices, body(): got = lax.ppermute(sums[k], ('z', 'core'), pairs[k])  55.3 us
    ppermute x16, starting transfers between devices, body(): got = lax.ppermute(sums[k], ('z', 'core'), pairs[k])  49.6 us
    all_to_all x1, blocking collectives, body(): owned = lax.all_to_all(pieces, ('ylo', 'x', 'core'), 0, 0, tiled=True)  14.1 us
    ppermute x4, starting transfers between devices, body(): arrived = [lax.ppermute(a, 'yhi', SWAP) for a in away]  12.6 us
    ppermute x1, starting transfers between devices, body(): other = lax.ppermute(pick(upstream, 1 - core), 'core', SWAP)  8.77 us
    ppermute x1, starting transfers between devices, body(): theirs = lax.ppermute(mine, 'yhi', SWAP)  5.15 us
    pallas_call x2, Pallas kernels, turn(): pl.pallas_call(turn_kernel, grid_spec=pltpu.PrefetchScalarGridSpec(num_sc...  4.17 us
  transfers between devices with their start and end apart: 23, of which 19 were waited for; matrix products, arithmetic and copies ran while one was open for 3% of the time, Pallas kernels for 1%

profile of v1, /device:TPU:1, one launch (start us, length us, event | category | flops | bytes accessed | tf_op | source)
XLA Modules:
  0.0 179.9 jit_solution(7105557316937767830)
XLA Ops:
  0.7 2.9 %dynamic-slice_bitcast_fusion = bf16[64,14336]{1,0:T(8,128)(2,1)} fusion(bf16[2,64,14336]{2,1,0:T(8,128)(2,1)} %k1.3, s32[]{:T(128)S(6)} %select_n.15), kind=kLoop, calls=%fused_computation.4 | loop fusion | bytes 3670020 | tf_op jit(solution)/shard_map/jit(dynamic_index_in_dim)/squeeze | solution.py:140
  3.6 8.8 %collective-permute-start = (bf16[64,14336]{1,0:T(8,128)(2,1)}, bf16[64,14336]{1,0:T(8,128)(2,1)S(1)}, u32[]{:S(2)}, u32[]{:S(2)}) collective-permute-start(bf16[64,14336]{1,0:T(8,128)(2,1)} %dynamic-slice_bitcast_fusion), channel_id=1, source_target_pairs={{0,1},{1,0},{2,3},{3,2},{4,5},{5,4},{6,7},{7,6},{8,9},{9,8},{10,11... | collective-permute-start | bytes 5505032 | tf_op jit(solution)/shard_map/ppermute | solution.py:141
  12.7 3.2 %collective-permute-done.r0.r1 = bf16[64,14336]{1,0:T(8,128)(2,1)S(1)} collective-permute-done((bf16[64,14336]{1,0:T(8,128)(2,1)}, bf16[64,14336]{1,0:T(8,128)(2,1)S(1)}, u32[]{:S(2)}, u32[]{:S(2)}) %collective-permute-start) | collective-permute-done | bytes 1835040 | tf_op jit(solution)/shard_map/ppermute | solution.py:141
  22.0 2.3 %collective-permute-start.1 = (bf16[64,512]{1,0:T(8,128)(2,1)S(1)}, bf16[64,512]{1,0:T(8,128)(2,1)S(1)}, u32[]{:S(2)}, u32[]{:S(2)}) collective-permute-start(bf16[64,512]{1,0:T(8,128)(2,1)S(1)} %get-tuple-element.66), channel_id=1, source_target_pairs={{0,1},{1,0},{2,3},{3,2},{4,5},{5,4},{6,7},{7,6},{8,9},{9,8},{10,11... | collective-permute-start | bytes 196616 | tf_op jit(solution)/shard_map/ppermute | solution.py:142
  25.2 5.1 %collective-permute-start.3 = (bf16[128,512]{1,0:T(8,128)(2,1)S(1)}, bf16[128,512]{1,0:T(8,128)(2,1)S(1)}, u32[]{:S(2)}, u32[]{:S(2)}) collective-permute-start(bf16[128,512]{1,0:T(8,128)(2,1)S(1)} %pad_maximum_fusion), channel_id=1, source_target_pairs={{0,32},{32,0},{1,33},{33,1},{2,34},{34,2},{3,35},{35,3},{4,36},{36... | collective-permute-start | bytes 393224 | tf_op jit(solution)/shard_map/ppermute | solution.py:143
  32.5 3.1 %collective-permute-done.3 = bf16[128,512]{1,0:T(8,128)(2,1)S(1)} collective-permute-done((bf16[128,512]{1,0:T(8,128)(2,1)S(1)}, bf16[128,512]{1,0:T(8,128)(2,1)S(1)}, u32[]{:S(2)}, u32[]{:S(2)}) %collective-permute-start.3) | collective-permute-done | bytes 131104 | tf_op jit(solution)/shard_map/ppermute | solution.py:143
  36.7 6.7 %collective-permute-start.4 = (f16[224,512]{1,0:T(8,128)(2,1)S(1)}, f16[224,512]{1,0:T(8,128)(2,1)S(1)}, u32[]{:S(2)}, u32[]{:S(2)}) collective-permute-start(f16[224,512]{1,0:T(8,128)(2,1)S(1)} %get-tuple-element.64), channel_id=1, source_target_pairs={{0,2},{1,31},{2,4},{3,1},{4,6},{5,3},{6,8},{7,5},{8,10},{9,7},{10,... | collective-permute-start | bytes 688136 | tf_op jit(solution)/shard_map/ppermute | solution.py:167
  45.3 3.9 %collective-permute-start.7 = (bf16[4,4,112,128]{3,2,1,0:T(8,128)(2,1)S(1)}, bf16[4,4,112,128]{3,2,1,0:T(8,128)(2,1)S(1)}, u32[]{:S(2)}, u32[]{:S(2)}) collective-permute-start(bf16[4,4,112,128]{3,2,1,0:T(8,128)(2,1)S(1)} %get-tuple-element.29), channel_id=1, source_target_pairs={{0,32},{32,0},{1,33},{33,1},{2,34},{34,2},{3,35},{35,3},{4,36},{36... | collective-permute-start | bytes 1376264 | tf_op jit(solution)/shard_map/ppermute | solution.py:148
  49.2 2.2 %collective-permute-done.5 = f16[224,512]{1,0:T(8,128)(2,1)S(1)} collective-permute-done((f16[224,512]{1,0:T(8,128)(2,1)S(1)}, f16[224,512]{1,0:T(8,128)(2,1)S(1)}, u32[]{:S(2)}, u32[]{:S(2)}) %collective-permute-start.5) | collective-permute-done | bytes 229408 | tf_op jit(solution)/shard_map/ppermute | solution.py:167
  51.7 3.2 %collective-permute-start.6 = (f16[448,512]{1,0:T(8,128)(2,1)S(1)}, f16[448,512]{1,0:T(8,128)(2,1)S(1)}, u32[]{:S(2)}, u32[]{:S(2)}) collective-permute-start(f16[448,512]{1,0:T(8,128)(2,1)S(1)} %get-tuple-element.27), channel_id=1, source_target_pairs={{0,2},{1,31},{2,4},{3,1},{4,6},{5,3},{6,8},{7,5},{8,10},{9,7},{10,... | collective-permute-start | bytes 1376264 | tf_op jit(solution)/shard_map/ppermute | solution.py:167
  57.0 2.3 %collective-permute-done.7 = bf16[4,4,112,128]{3,2,1,0:T(8,128)(2,1)S(1)} collective-permute-done((bf16[4,4,112,128]{3,2,1,0:T(8,128)(2,1)S(1)}, bf16[4,4,112,128]{3,2,1,0:T(8,128)(2,1)S(1)}, u32[]{:S(2)}, u32[]{:S(2)}) %collective-permute-start.7) | collective-permute-done | bytes 458784 | tf_op jit(solution)/shard_map/ppermute | solution.py:148
  60.5 3.6 %collective-permute-done.6 = f16[448,512]{1,0:T(8,128)(2,1)S(1)} collective-permute-done((f16[448,512]{1,0:T(8,128)(2,1)S(1)}, f16[448,512]{1,0:T(8,128)(2,1)S(1)}, u32[]{:S(2)}, u32[]{:S(2)}) %collective-permute-start.6) | collective-permute-done | bytes 458784 | tf_op jit(solution)/shard_map/ppermute | solution.py:167
  64.1 3.0 %collective-permute-done.8 = f16[448,512]{1,0:T(8,128)(2,1)S(1)} collective-permute-done((f16[448,512]{1,0:T(8,128)(2,1)S(1)}, f16[448,512]{1,0:T(8,128)(2,1)S(1)}, u32[]{:S(2)}, u32[]{:S(2)}) %collective-permute-start.8) | collective-permute-done | bytes 458784 | tf_op jit(solution)/shard_map/ppermute | solution.py:167
  69.4 4.6 %collective-permute-start.9 = (f16[448,512]{1,0:T(8,128)(2,1)S(1)}, f16[448,512]{1,0:T(8,128)(2,1)S(1)}, u32[]{:S(2)}, u32[]{:S(2)}) collective-permute-start(f16[448,512]{1,0:T(8,128)(2,1)S(1)} %get-tuple-element.31), channel_id=1, source_target_pairs={{0,2},{1,31},{2,4},{3,1},{4,6},{5,3},{6,8},{7,5},{8,10},{9,7},{10,... | collective-permute-start | bytes 1376264 | tf_op jit(solution)/shard_map/ppermute | solution.py:167
  73.9 3.7 %collective-permute-start.12 = (bf16[4,4,112,128]{3,2,1,0:T(8,128)(2,1)S(1)}, bf16[4,4,112,128]{3,2,1,0:T(8,128)(2,1)S(1)}, u32[]{:S(2)}, u32[]{:S(2)}) collective-permute-start(bf16[4,4,112,128]{3,2,1,0:T(8,128)(2,1)S(1)} %get-tuple-element.35), channel_id=1, source_target_pairs={{0,32},{32,0},{1,33},{33,1},{2,34},{34,2},{3,35},{35,3},{4,36},{36... | collective-permute-start | bytes 1376264 | tf_op jit(solution)/shard_map/ppermute | solution.py:148
  77.6 3.1 %collective-permute-start.17 = (bf16[5,4,112,128]{3,2,1,0:T(8,128)(2,1)S(1)}, bf16[5,4,112,128]{3,2,1,0:T(8,128)(2,1)S(1)}, u32[]{:S(2)}, u32[]{:S(2)}) collective-permute-start(bf16[5,4,112,128]{3,2,1,0:T(8,128)(2,1)S(1)} %get-tuple-element.41), channel_id=1, source_target_pairs={{0,32},{32,0},{1,33},{33,1},{2,34},{34,2},{3,35},{35,3},{4,36},{36... | collective-permute-start | bytes 1720328 | tf_op jit(solution)/shard_map/ppermute | solution.py:148
  82.4 5.3 %collective-permute-start.11 = (f16[448,512]{1,0:T(8,128)(2,1)S(1)}, f16[448,512]{1,0:T(8,128)(2,1)S(1)}, u32[]{:S(2)}, u32[]{:S(2)}) collective-permute-start(f16[448,512]{1,0:T(8,128)(2,1)S(1)} %get-tuple-element.33), channel_id=1, source_target_pairs={{0,2},{1,31},{2,4},{3,1},{4,6},{5,3},{6,8},{7,5},{8,10},{9,7},{10,... | collective-permute-start | bytes 1376264 | tf_op jit(solution)/shard_map/ppermute | solution.py:167
  91.1 3.5 %collective-permute-done.11 = f16[448,512]{1,0:T(8,128)(2,1)S(1)} collective-permute-done((f16[448,512]{1,0:T(8,128)(2,1)S(1)}, f16[448,512]{1,0:T(8,128)(2,1)S(1)}, u32[]{:S(2)}, u32[]{:S(2)}) %collective-permute-start.11) | collective-permute-done | bytes 458784 | tf_op jit(solution)/shard_map/ppermute | solution.py:167
  94.6 5.3 %collective-permute-done.13 = f16[448,512]{1,0:T(8,128)(2,1)S(1)} collective-permute-done((f16[448,512]{1,0:T(8,128)(2,1)S(1)}, f16[448,512]{1,0:T(8,128)(2,1)S(1)}, u32[]{:S(2)}, u32[]{:S(2)}) %collective-permute-start.13) | collective-permute-done | bytes 458784 | tf_op jit(solution)/shard_map/ppermute | solution.py:167
  102.2 3.4 %collective-permute-start.15 = (f16[448,512]{1,0:T(8,128)(2,1)S(1)}, f16[448,512]{1,0:T(8,128)(2,1)S(1)}, u32[]{:S(2)}, u32[]{:S(2)}) collective-permute-start(f16[448,512]{1,0:T(8,128)(2,1)S(1)} %get-tuple-element.38), channel_id=1, source_target_pairs={{0,30},{1,3},{2,0},{3,5},{4,2},{5,7},{6,4},{7,9},{8,6},{9,11},{10,... | collective-permute-start | bytes 1376264 | tf_op jit(solution)/shard_map/ppermute | solution.py:167
  106.3 7.5 %collective-permute-done.14 = f16[448,512]{1,0:T(8,128)(2,1)S(1)} collective-permute-done((f16[448,512]{1,0:T(8,128)(2,1)S(1)}, f16[448,512]{1,0:T(8,128)(2,1)S(1)}, u32[]{:S(2)}, u32[]{:S(2)}) %collective-permute-start.14) | collective-permute-done | bytes 458784 | tf_op jit(solution)/shard_map/ppermute | solution.py:167
  115.4 3.6 %collective-permute-start.16 = (f16[448,512]{1,0:T(8,128)(2,1)S(1)}, f16[448,512]{1,0:T(8,128)(2,1)S(1)}, u32[]{:S(2)}, u32[]{:S(2)}) collective-permute-start(f16[448,512]{1,0:T(8,128)(2,1)S(1)} %get-tuple-element.39), channel_id=1, source_target_pairs={{0,2},{1,31},{2,4},{3,1},{4,6},{5,3},{6,8},{7,5},{8,10},{9,7},{10,... | collective-permute-start | bytes 1376264 | tf_op jit(solution)/shard_map/ppermute | solution.py:167
  121.8 5.6 %collective-permute-done.16 = f16[448,512]{1,0:T(8,128)(2,1)S(1)} collective-permute-done((f16[448,512]{1,0:T(8,128)(2,1)S(1)}, f16[448,512]{1,0:T(8,128)(2,1)S(1)}, u32[]{:S(2)}, u32[]{:S(2)}) %collective-permute-start.16) | collective-permute-done | bytes 458784 | tf_op jit(solution)/shard_map/ppermute | solution.py:167
  127.3 4.0 %collective-permute-done.18 = f16[448,512]{1,0:T(8,128)(2,1)S(1)} collective-permute-done((f16[448,512]{1,0:T(8,128)(2,1)S(1)}, f16[448,512]{1,0:T(8,128)(2,1)S(1)}, u32[]{:S(2)}, u32[]{:S(2)}) %collective-permute-start.18) | collective-permute-done | bytes 458784 | tf_op jit(solution)/shard_map/ppermute | solution.py:167
  131.7 3.1 %collective-permute-start.19 = (f16[448,512]{1,0:T(8,128)(2,1)S(1)}, f16[448,512]{1,0:T(8,128)(2,1)S(1)}, u32[]{:S(2)}, u32[]{:S(2)}) collective-permute-start(f16[448,512]{1,0:T(8,128)(2,1)S(1)} %get-tuple-element.43), channel_id=1, source_target_pairs={{0,2},{1,31},{2,4},{3,1},{4,6},{5,3},{6,8},{7,5},{8,10},{9,7},{10,... | collective-permute-start | bytes 1376264 | tf_op jit(solution)/shard_map/ppermute | solution.py:167
  134.7 2.2 %collective-permute-start.20 = (f16[448,512]{1,0:T(8,128)(2,1)S(1)}, f16[448,512]{1,0:T(8,128)(2,1)S(1)}, u32[]{:S(2)}, u32[]{:S(2)}) collective-permute-start(f16[448,512]{1,0:T(8,128)(2,1)S(1)} %get-tuple-element.44), channel_id=1, source_target_pairs={{0,30},{1,3},{2,0},{3,5},{4,2},{5,7},{6,4},{7,9},{8,6},{9,11},{10,... | collective-permute-start | bytes 1376264 | tf_op jit(solution)/shard_map/ppermute | solution.py:167
  137.0 7.7 %collective-permute-done.19 = f16[448,512]{1,0:T(8,128)(2,1)S(1)} collective-permute-done((f16[448,512]{1,0:T(8,128)(2,1)S(1)}, f16[448,512]{1,0:T(8,128)(2,1)S(1)}, u32[]{:S(2)}, u32[]{:S(2)}) %collective-permute-start.19) | collective-permute-done | bytes 458784 | tf_op jit(solution)/shard_map/ppermute | solution.py:167
  146.8 3.9 %collective-permute-start.21 = (f16[448,512]{1,0:T(8,128)(2,1)S(1)}, f16[448,512]{1,0:T(8,128)(2,1)S(1)}, u32[]{:S(2)}, u32[]{:S(2)}) collective-permute-start(f16[448,512]{1,0:T(8,128)(2,1)S(1)} %get-tuple-element.45), channel_id=1, source_target_pairs={{0,2},{1,31},{2,4},{3,1},{4,6},{5,3},{6,8},{7,5},{8,10},{9,7},{10,... | collective-permute-start | bytes 1376264 | tf_op jit(solution)/shard_map/ppermute | solution.py:167
  154.0 4.8 %collective-permute-done.21 = f16[448,512]{1,0:T(8,128)(2,1)S(1)} collective-permute-done((f16[448,512]{1,0:T(8,128)(2,1)S(1)}, f16[448,512]{1,0:T(8,128)(2,1)S(1)}, u32[]{:S(2)}, u32[]{:S(2)}) %collective-permute-start.21) | collective-permute-done | bytes 458784 | tf_op jit(solution)/shard_map/ppermute | solution.py:167
  158.7 4.0 %collective-permute-done.22 = f16[448,512]{1,0:T(8,128)(2,1)S(1)} collective-permute-done((f16[448,512]{1,0:T(8,128)(2,1)S(1)}, f16[448,512]{1,0:T(8,128)(2,1)S(1)}, u32[]{:S(2)}, u32[]{:S(2)}) %collective-permute-start.22) | collective-permute-done | bytes 458784 | tf_op jit(solution)/shard_map/ppermute | solution.py:167
  163.0 14.1 %all_to_all.5 = f16[16,28,512]{2,1,0:T(8,128)(2,1)S(1)} all-to-all(f16[16,28,512]{2,1,0:T(8,128)(2,1)S(1)} %reshape.76), channel_id=1, replica_groups=mesh['ylo'=2,'x'=4,'yhi'=2,'z'=16,'core'=2] {'ylo','x','core'}, dimensions={0} | all-to-all | bytes 917504 | tf_op jit(solution)/shard_map/all_to_all | solution.py:180
  177.4 2.4 %shard_map.69 = (f32[28,512]{1,0:T(8,128)}, f32[28,512]{1,0:T(8,128)}, f32[28,512]{1,0:T(8,128)}) custom-call(f32[16,32,512]{2,1,0:T(8,128)S(1)} %pad.6.g_ref, bf16[28,512]{1,0:T(8,128)(2,1)S(1)} %copy-done.1), custom_call_target="tpu_custom_call" | custom-call | tf_op jit(solution)/shard_map/pallas_call | solution.py:112
  (55 shorter events, 36.1 us)
Async XLA Ops:
  0.6 11.9 %copy-start.3 = (s32[2]{0:T(128)S(1)}, s32[2]{0:T(128)}, u32[]{:S(2)}) copy-start(s32[2]{0:T(128)} %param.6) | copy-start | bytes 28
  0.6 12.0 %copy-start.2 = (bf16[2,64,512]{2,1,0:T(8,128)(2,1)S(1)}, bf16[2,64,512]{2,1,0:T(8,128)(2,1)}, u32[]{:S(2)}) copy-start(bf16[2,64,512]{2,1,0:T(8,128)(2,1)} %param.4) | copy-start | bytes 393220
  3.6 12.4 %collective-permute-start = (bf16[64,14336]{1,0:T(8,128)(2,1)}, bf16[64,14336]{1,0:T(8,128)(2,1)S(1)}, u32[]{:S(2)}, u32[]{:S(2)}) collective-permute-start(bf16[64,14336]{1,0:T(8,128)(2,1)} %dynamic-slice_bitcast_fusion), channel_id=1, source_target_pairs={{0,1},{1,0},{2,3},{3,2},{4,5},{5,4},{6,7},{7,6},{8,9},{9,8},{10,11... | collective-permute-start | bytes 5505032 | tf_op jit(solution)/shard_map/ppermute | solution.py:141
  15.9 2.0 %copy-start = (bf16[2,64,14336]{2,1,0:T(8,128)(2,1)S(1)}, bf16[2,64,14336]{2,1,0:T(8,128)(2,1)}, u32[]{:S(2)}) copy-start(bf16[2,64,14336]{2,1,0:T(8,128)(2,1)} %k1.3) | copy-start | bytes 11010052
  20.1 15.5 %collective-permute-start.2 = (bf16[3,4,112,128]{3,2,1,0:T(8,128)(2,1)S(1)}, bf16[3,4,112,128]{3,2,1,0:T(8,128)(2,1)S(1)}, u32[]{:S(2)}, u32[]{:S(2)}) collective-permute-start(bf16[3,4,112,128]{3,2,1,0:T(8,128)(2,1)S(1)} %get-tuple-element.26), channel_id=1, source_target_pairs={{0,32},{32,0},{1,33},{33,1},{2,34},{34,2},{3,35},{35,3},{4,36},{36... | collective-permute-start | bytes 1032200 | tf_op jit(solution)/shard_map/ppermute | solution.py:148
  22.0 3.2 %collective-permute-start.1 = (bf16[64,512]{1,0:T(8,128)(2,1)S(1)}, bf16[64,512]{1,0:T(8,128)(2,1)S(1)}, u32[]{:S(2)}, u32[]{:S(2)}) collective-permute-start(bf16[64,512]{1,0:T(8,128)(2,1)S(1)} %get-tuple-element.66), channel_id=1, source_target_pairs={{0,1},{1,0},{2,3},{3,2},{4,5},{5,4},{6,7},{7,6},{8,9},{9,8},{10,11... | collective-permute-start | bytes 196616 | tf_op jit(solution)/shard_map/ppermute | solution.py:142
  25.2 10.3 %collective-permute-start.3 = (bf16[128,512]{1,0:T(8,128)(2,1)S(1)}, bf16[128,512]{1,0:T(8,128)(2,1)S(1)}, u32[]{:S(2)}, u32[]{:S(2)}) collective-permute-start(bf16[128,512]{1,0:T(8,128)(2,1)S(1)} %pad_maximum_fusion), channel_id=1, source_target_pairs={{0,32},{32,0},{1,33},{33,1},{2,34},{34,2},{3,35},{35,3},{4,36},{36... | collective-permute-start | bytes 393224 | tf_op jit(solution)/shard_map/ppermute | solution.py:143
  36.7 12.5 %collective-permute-start.4 = (f16[224,512]{1,0:T(8,128)(2,1)S(1)}, f16[224,512]{1,0:T(8,128)(2,1)S(1)}, u32[]{:S(2)}, u32[]{:S(2)}) collective-permute-start(f16[224,512]{1,0:T(8,128)(2,1)S(1)} %get-tuple-element.64), channel_id=1, source_target_pairs={{0,2},{1,31},{2,4},{3,1},{4,6},{5,3},{6,8},{7,5},{8,10},{9,7},{10,... | collective-permute-start | bytes 688136 | tf_op jit(solution)/shard_map/ppermute | solution.py:167
  43.4 8.0 %collective-permute-start.5 = (f16[224,512]{1,0:T(8,128)(2,1)S(1)}, f16[224,512]{1,0:T(8,128)(2,1)S(1)}, u32[]{:S(2)}, u32[]{:S(2)}) collective-permute-start(f16[224,512]{1,0:T(8,128)(2,1)S(1)} %get-tuple-element.63), channel_id=1, source_target_pairs={{0,30},{1,3},{2,0},{3,5},{4,2},{5,7},{6,4},{7,9},{8,6},{9,11},{10,... | collective-permute-start | bytes 688136 | tf_op jit(solution)/shard_map/ppermute | solution.py:167
  45.3 14.0 %collective-permute-start.7 = (bf16[4,4,112,128]{3,2,1,0:T(8,128)(2,1)S(1)}, bf16[4,4,112,128]{3,2,1,0:T(8,128)(2,1)S(1)}, u32[]{:S(2)}, u32[]{:S(2)}) collective-permute-start(bf16[4,4,112,128]{3,2,1,0:T(8,128)(2,1)S(1)} %get-tuple-element.29), channel_id=1, source_target_pairs={{0,32},{32,0},{1,33},{33,1},{2,34},{34,2},{3,35},{35,3},{4,36},{36... | collective-permute-start | bytes 1376264 | tf_op jit(solution)/shard_map/ppermute | solution.py:148
  51.7 12.4 %collective-permute-start.6 = (f16[448,512]{1,0:T(8,128)(2,1)S(1)}, f16[448,512]{1,0:T(8,128)(2,1)S(1)}, u32[]{:S(2)}, u32[]{:S(2)}) collective-permute-start(f16[448,512]{1,0:T(8,128)(2,1)S(1)} %get-tuple-element.27), channel_id=1, source_target_pairs={{0,2},{1,31},{2,4},{3,1},{4,6},{5,3},{6,8},{7,5},{8,10},{9,7},{10,... | collective-permute-start | bytes 1376264 | tf_op jit(solution)/shard_map/ppermute | solution.py:167
  54.8 12.2 %collective-permute-start.8 = (f16[448,512]{1,0:T(8,128)(2,1)S(1)}, f16[448,512]{1,0:T(8,128)(2,1)S(1)}, u32[]{:S(2)}, u32[]{:S(2)}) collective-permute-start(f16[448,512]{1,0:T(8,128)(2,1)S(1)} %get-tuple-element.30), channel_id=1, source_target_pairs={{0,30},{1,3},{2,0},{3,5},{4,2},{5,7},{6,4},{7,9},{8,6},{9,11},{10,... | collective-permute-start | bytes 1376264 | tf_op jit(solution)/shard_map/ppermute | solution.py:167
  67.4 13.3 %collective-permute-start.10 = (f16[448,512]{1,0:T(8,128)(2,1)S(1)}, f16[448,512]{1,0:T(8,128)(2,1)S(1)}, u32[]{:S(2)}, u32[]{:S(2)}) collective-permute-start(f16[448,512]{1,0:T(8,128)(2,1)S(1)} %get-tuple-element.32), channel_id=1, source_target_pairs={{0,30},{1,3},{2,0},{3,5},{4,2},{5,7},{6,4},{7,9},{8,6},{9,11},{10,... | collective-permute-start | bytes 1376264 | tf_op jit(solution)/shard_map/ppermute | solution.py:167
  69.4 12.7 %collective-permute-start.9 = (f16[448,512]{1,0:T(8,128)(2,1)S(1)}, f16[448,512]{1,0:T(8,128)(2,1)S(1)}, u32[]{:S(2)}, u32[]{:S(2)}) collective-permute-start(f16[448,512]{1,0:T(8,128)(2,1)S(1)} %get-tuple-element.31), channel_id=1, source_target_pairs={{0,2},{1,31},{2,4},{3,1},{4,6},{5,3},{6,8},{7,5},{8,10},{9,7},{10,... | collective-permute-start | bytes 1376264 | tf_op jit(solution)/shard_map/ppermute | solution.py:167
  73.9 15.9 %collective-permute-start.12 = (bf16[4,4,112,128]{3,2,1,0:T(8,128)(2,1)S(1)}, bf16[4,4,112,128]{3,2,1,0:T(8,128)(2,1)S(1)}, u32[]{:S(2)}, u32[]{:S(2)}) collective-permute-start(bf16[4,4,112,128]{3,2,1,0:T(8,128)(2,1)S(1)} %get-tuple-element.35), channel_id=1, source_target_pairs={{0,32},{32,0},{1,33},{33,1},{2,34},{34,2},{3,35},{35,3},{4,36},{36... | collective-permute-start | bytes 1376264 | tf_op jit(solution)/shard_map/ppermute | solution.py:148
  77.6 28.0 %collective-permute-start.17 = (bf16[5,4,112,128]{3,2,1,0:T(8,128)(2,1)S(1)}, bf16[5,4,112,128]{3,2,1,0:T(8,128)(2,1)S(1)}, u32[]{:S(2)}, u32[]{:S(2)}) collective-permute-start(bf16[5,4,112,128]{3,2,1,0:T(8,128)(2,1)S(1)} %get-tuple-element.41), channel_id=1, source_target_pairs={{0,32},{32,0},{1,33},{33,1},{2,34},{34,2},{3,35},{35,3},{4,36},{36... | collective-permute-start | bytes 1720328 | tf_op jit(solution)/shard_map/ppermute | solution.py:148
  82.4 12.2 %collective-permute-start.11 = (f16[448,512]{1,0:T(8,128)(2,1)S(1)}, f16[448,512]{1,0:T(8,128)(2,1)S(1)}, u32[]{:S(2)}, u32[]{:S(2)}) collective-permute-start(f16[448,512]{1,0:T(8,128)(2,1)S(1)} %get-tuple-element.33), channel_id=1, source_target_pairs={{0,2},{1,31},{2,4},{3,1},{4,6},{5,3},{6,8},{7,5},{8,10},{9,7},{10,... | collective-permute-start | bytes 1376264 | tf_op jit(solution)/shard_map/ppermute | solution.py:167
  87.7 12.2 %collective-permute-start.13 = (f16[448,512]{1,0:T(8,128)(2,1)S(1)}, f16[448,512]{1,0:T(8,128)(2,1)S(1)}, u32[]{:S(2)}, u32[]{:S(2)}) collective-permute-start(f16[448,512]{1,0:T(8,128)(2,1)S(1)} %get-tuple-element.36), channel_id=1, source_target_pairs={{0,30},{1,3},{2,0},{3,5},{4,2},{5,7},{6,4},{7,9},{8,6},{9,11},{10,... | collective-permute-start | bytes 1376264 | tf_op jit(solution)/shard_map/ppermute | solution.py:167
  100.3 13.6 %collective-permute-start.14 = (f16[448,512]{1,0:T(8,128)(2,1)S(1)}, f16[448,512]{1,0:T(8,128)(2,1)S(1)}, u32[]{:S(2)}, u32[]{:S(2)}) collective-permute-start(f16[448,512]{1,0:T(8,128)(2,1)S(1)} %get-tuple-element.37), channel_id=1, source_target_pairs={{0,2},{1,31},{2,4},{3,1},{4,6},{5,3},{6,8},{7,5},{8,10},{9,7},{10,... | collective-permute-start | bytes 1376264 | tf_op jit(solution)/shard_map/ppermute | solution.py:167
  102.2 12.8 %collective-permute-start.15 = (f16[448,512]{1,0:T(8,128)(2,1)S(1)}, f16[448,512]{1,0:T(8,128)(2,1)S(1)}, u32[]{:S(2)}, u32[]{:S(2)}) collective-permute-start(f16[448,512]{1,0:T(8,128)(2,1)S(1)} %get-tuple-element.38), channel_id=1, source_target_pairs={{0,30},{1,3},{2,0},{3,5},{4,2},{5,7},{6,4},{7,9},{8,6},{9,11},{10,... | collective-permute-start | bytes 1376264 | tf_op jit(solution)/shard_map/ppermute | solution.py:167
  115.4 11.9 %collective-permute-start.16 = (f16[448,512]{1,0:T(8,128)(2,1)S(1)}, f16[448,512]{1,0:T(8,128)(2,1)S(1)}, u32[]{:S(2)}, u32[]{:S(2)}) collective-permute-start(f16[448,512]{1,0:T(8,128)(2,1)S(1)} %get-tuple-element.39), channel_id=1, source_target_pairs={{0,2},{1,31},{2,4},{3,1},{4,6},{5,3},{6,8},{7,5},{8,10},{9,7},{10,... | collective-permute-start | bytes 1376264 | tf_op jit(solution)/shard_map/ppermute | solution.py:167
  119.1 12.2 %collective-permute-start.18 = (f16[448,512]{1,0:T(8,128)(2,1)S(1)}, f16[448,512]{1,0:T(8,128)(2,1)S(1)}, u32[]{:S(2)}, u32[]{:S(2)}) collective-permute-start(f16[448,512]{1,0:T(8,128)(2,1)S(1)} %get-tuple-element.42), channel_id=1, source_target_pairs={{0,30},{1,3},{2,0},{3,5},{4,2},{5,7},{6,4},{7,9},{8,6},{9,11},{10,... | collective-permute-start | bytes 1376264 | tf_op jit(solution)/shard_map/ppermute | solution.py:167
  131.7 13.0 %collective-permute-start.19 = (f16[448,512]{1,0:T(8,128)(2,1)S(1)}, f16[448,512]{1,0:T(8,128)(2,1)S(1)}, u32[]{:S(2)}, u32[]{:S(2)}) collective-permute-start(f16[448,512]{1,0:T(8,128)(2,1)S(1)} %get-tuple-element.43), channel_id=1, source_target_pairs={{0,2},{1,31},{2,4},{3,1},{4,6},{5,3},{6,8},{7,5},{8,10},{9,7},{10,... | collective-permute-start | bytes 1376264 | tf_op jit(solution)/shard_map/ppermute | solution.py:167
  134.7 11.7 %collective-permute-start.20 = (f16[448,512]{1,0:T(8,128)(2,1)S(1)}, f16[448,512]{1,0:T(8,128)(2,1)S(1)}, u32[]{:S(2)}, u32[]{:S(2)}) collective-permute-start(f16[448,512]{1,0:T(8,128)(2,1)S(1)} %get-tuple-element.44), channel_id=1, source_target_pairs={{0,30},{1,3},{2,0},{3,5},{4,2},{5,7},{6,4},{7,9},{8,6},{9,11},{10,... | collective-permute-start | bytes 1376264 | tf_op jit(solution)/shard_map/ppermute | solution.py:167
  146.8 11.9 %collective-permute-start.21 = (f16[448,512]{1,0:T(8,128)(2,1)S(1)}, f16[448,512]{1,0:T(8,128)(2,1)S(1)}, u32[]{:S(2)}, u32[]{:S(2)}) collective-permute-start(f16[448,512]{1,0:T(8,128)(2,1)S(1)} %get-tuple-element.45), channel_id=1, source_target_pairs={{0,2},{1,31},{2,4},{3,1},{4,6},{5,3},{6,8},{7,5},{8,10},{9,7},{10,... | collective-permute-start | bytes 1376264 | tf_op jit(solution)/shard_map/ppermute | solution.py:167
  150.7 11.9 %collective-permute-start.22 = (f16[448,512]{1,0:T(8,128)(2,1)S(1)}, f16[448,512]{1,0:T(8,128)(2,1)S(1)}, u32[]{:S(2)}, u32[]{:S(2)}) collective-permute-start(f16[448,512]{1,0:T(8,128)(2,1)S(1)} %get-tuple-element.46), channel_id=1, source_target_pairs={{0,30},{1,3},{2,0},{3,5},{4,2},{5,7},{6,4},{7,9},{8,6},{9,11},{10,... | collective-permute-start | bytes 1376264 | tf_op jit(solution)/shard_map/ppermute | solution.py:167
  162.7 14.8 %copy-start.1 = (bf16[28,512]{1,0:T(8,128)(2,1)S(1)}, bf16[28,512]{1,0:T(8,128)(2,1)}, u32[]{:S(2)}) copy-start(bf16[28,512]{1,0:T(8,128)(2,1)} %w_ref.1) | copy-start | bytes 86020

commit v2 on v1

--- a/solution.py
+++ b/solution.py
@@ -139,8 +139,12 @@
 
     pick = lambda x, i: lax.dynamic_index_in_dim(x, i, 0, keepdims=False)
     other = lax.ppermute(pick(upstream, 1 - core), "core", SWAP)
-    mine = jnp.concatenate([pick(masked, core), lax.ppermute(pick(masked, 1 - core), "core", SWAP)], axis=0)
-    theirs = lax.ppermute(mine, "yhi", SWAP)
+    mine, rest = pick(masked, core), pick(masked, 1 - core)
+    theirs = jnp.concatenate([
+        lax.ppermute(mine, "yhi", SWAP),
+        lax.ppermute(rest, ("yhi", "core"), [(i, 3 - i) for i in range(4)]),
+    ], axis=0)
+    mine = jnp.concatenate([mine, lax.ppermute(rest, "core", SWAP)], axis=0)
 
     sign = 1 - 2 * core
     scalars = lambda half: jnp.stack([core, z, sign, half]).astype(jnp.int32)
@@ -162,18 +166,19 @@
     pairs = (ring_pairs(1), ring_pairs(-1))
     slot_of = (lambda d: d, lambda d: NZ - d)
     sums = [parts[8][:half].astype(f16), parts[8][half:].astype(f16)]
+    last = None
     for dist in range(7, -1, -1):
         for k in range(2):
             got = lax.ppermute(sums[k], ("z", "core"), pairs[k])
             if dist == 0:
                 sums[k] = got
                 continue
+            if last is not None:
+                got, _ = lax.optimization_barrier((got, last))
             if dist == 7:
                 empty = jnp.zeros_like(got)
                 got = jnp.concatenate([got, empty] if k == 0 else [empty, got], axis=0)
-            sums[k] = (got.astype(f32) + parts[slot_of[k](dist)]).astype(f16)
-        if dist:
-            sums = list(lax.optimization_barrier(tuple(sums)))
+            sums[k] = last = (got.astype(f32) + parts[slot_of[k](dist)]).astype(f16)
     length = pick(lengths, core).astype(f32)
     total = (sums[0].astype(f32) + sums[1].astype(f32) + parts[0]) * (4096.0 / length)
     pieces = total.astype(f16).reshape(2 * n_groups, -1, rows)

time: 181 us -> 188 us (1.039)
  waiting for transfers between devices: 65 us -> 55 us
  starting transfers between devices: 78.4 us -> 87.5 us
  blocking collectives: 14.1 us -> 22.5 us
    ppermute x16, starting transfers between devices: 49.6 us -> 58.5 us  [body(): got = lax.ppermute(sums[k], ('z', 'core'), pairs[k])]
    all_to_all x1, blocking collectives: 14.1 us -> 22.5 us  [body(): owned = lax.all_to_all(pieces, ('ylo', 'x', 'core'), 0, 0, tiled=True)]
    ppermute x16, waiting for transfers between devices: 55.3 us -> 47.4 us  [body(): got = lax.ppermute(sums[k], ('z', 'core'), pairs[k])]
    ppermute x4, waiting for transfers between devices: 2.54 us -> 0.01 us  [body(): arrived = [lax.ppermute(a, 'yhi', SWAP) for a in away]]
    ppermute x2 -> x3, starting transfers between devices: 7.43 us -> 9.63 us  [the longest x1 4.87 us: body(): lax.ppermute(mine, 'yhi', SWAP)]
    ppermute x4, starting transfers between devices: 12.6 us -> 10.6 us  [body(): arrived = [lax.ppermute(a, 'yhi', SWAP) for a in away]]
    ppermute x2 -> x3, waiting for transfers between devices: 3.97 us -> 4.38 us  [the longest x1 2.47 us: body(): lax.ppermute(mine, 'yhi', SWAP)]
  transfers between devices with their start and end apart: 23 -> 24, of which waited for: 19 -> 15; matrix products, arithmetic and copies ran while one was open for 3% -> 4% of each run, Pallas kernels for 1% -> 1%
where the time goes in v2:
time: 188 us; the launch traced here: 187 us
  starting transfers between devices  87.5 us (47%)
  waiting for transfers between devices  55 us (29%)
  blocking collectives  22.5 us (12%)
  Pallas kernels  6.58 us (4%)
  local copies, waits for them, and re-layouts  5.92 us (3%)
  matrix products  4.96 us (3%)
  other arithmetic  2.95 us (2%)
    ppermute x16, starting transfers between devices, body(): got = lax.ppermute(sums[k], ('z', 'core'), pairs[k])  58.5 us
    ppermute x16, waiting for transfers between devices, body(): got = lax.ppermute(sums[k], ('z', 'core'), pairs[k])  47.4 us
    all_to_all x1, blocking collectives, body(): owned = lax.all_to_all(pieces, ('ylo', 'x', 'core'), 0, 0, tiled=True)  22.5 us
    ppermute x4, starting transfers between devices, body(): arrived = [lax.ppermute(a, 'yhi', SWAP) for a in away]  10.6 us
    ppermute x1, starting transfers between devices, body(): other = lax.ppermute(pick(upstream, 1 - core), 'core', SWAP)  8.77 us
    ppermute x1, starting transfers between devices, body(): lax.ppermute(mine, 'yhi', SWAP)  4.87 us
    pallas_call x2, Pallas kernels, turn(): pl.pallas_call(turn_kernel, grid_spec=pltpu.PrefetchScalarGridSpec(num_sc...  4.17 us
  transfers between devices with their start and end apart: 24, of which 15 were waited for; matrix products, arithmetic and copies ran while one was open for 4% of the time, Pallas kernels for 1%

profile of v2, /device:TPU:1, one launch (start us, length us, event | category | flops | bytes accessed | tf_op | source)
XLA Modules:
  0.0 187.2 jit_solution(13780557761479201511)
XLA Ops:
  0.7 2.9 %dynamic-slice_bitcast_fusion = bf16[64,14336]{1,0:T(8,128)(2,1)} fusion(bf16[2,64,14336]{2,1,0:T(8,128)(2,1)} %k1.3, s32[]{:T(128)S(6)} %select_n.15), kind=kLoop, calls=%fused_computation.4 | loop fusion | bytes 3670020 | tf_op jit(solution)/shard_map/jit(dynamic_index_in_dim)/squeeze | solution.py:140
  3.6 8.8 %collective-permute-start = (bf16[64,14336]{1,0:T(8,128)(2,1)}, bf16[64,14336]{1,0:T(8,128)(2,1)S(1)}, u32[]{:S(2)}, u32[]{:S(2)}) collective-permute-start(bf16[64,14336]{1,0:T(8,128)(2,1)} %dynamic-slice_bitcast_fusion), channel_id=1, source_target_pairs={{0,1},{1,0},{2,3},{3,2},{4,5},{5,4},{6,7},{7,6},{8,9},{9,8},{10,11... | collective-permute-start | bytes 5505032 | tf_op jit(solution)/shard_map/ppermute | solution.py:141
  12.7 3.2 %collective-permute-done.r0.r1 = bf16[64,14336]{1,0:T(8,128)(2,1)S(1)} collective-permute-done((bf16[64,14336]{1,0:T(8,128)(2,1)}, bf16[64,14336]{1,0:T(8,128)(2,1)S(1)}, u32[]{:S(2)}, u32[]{:S(2)}) %collective-permute-start) | collective-permute-done | bytes 1835040 | tf_op jit(solution)/shard_map/ppermute | solution.py:141
  16.0 2.0 %copy-done = bf16[2,64,14336]{2,1,0:T(8,128)(2,1)S(1)} copy-done((bf16[2,64,14336]{2,1,0:T(8,128)(2,1)S(1)}, bf16[2,64,14336]{2,1,0:T(8,128)(2,1)}, u32[]{:S(2)}) %copy-start) | copy-done | bytes 3670040
  18.0 2.1 %shard_map.68 = (bf16[3,4,112,128]{3,2,1,0:T(8,128)(2,1)S(1)}, bf16[4,4,112,128]{3,2,1,0:T(8,128)(2,1)S(1)}, bf16[4,4,112,128]{3,2,1,0:T(8,128)(2,1)S(1)}, bf16[5,4,112,128]{3,2,1,0:T(8,128)(2,1)S(1)}) custom-call(s32[4]{0:T(128)S(1)} %pad_add_fusion.2.s_ref, bf16[2,64,14336]{2,1,0:T(8,128)(2,1)S(1)} %copy-done, bf16[2,64,14336]{2,1,0:T(8,128)(2,1)S(1)} %copy-done, ...), custom_call_target="tpu_custom_call" | custom-call | tf_op jit(solution)/shard_map/pallas_call | solution.py:42
  20.1 1.9 %collective-permute-start.2 = (bf16[3,4,112,128]{3,2,1,0:T(8,128)(2,1)S(1)}, bf16[3,4,112,128]{3,2,1,0:T(8,128)(2,1)S(1)}, u32[]{:S(2)}, u32[]{:S(2)}) collective-permute-start(bf16[3,4,112,128]{3,2,1,0:T(8,128)(2,1)S(1)} %get-tuple-element.25), channel_id=1, source_target_pairs={{0,32},{32,0},{1,33},{33,1},{2,34},{34,2},{3,35},{35,3},{4,36},{36... | collective-permute-start | bytes 1032200 | tf_op jit(solution)/shard_map/ppermute | solution.py:152
  22.0 4.9 %collective-permute-start.3 = (bf16[64,512]{1,0:T(8,128)(2,1)S(1)}, bf16[64,512]{1,0:T(8,128)(2,1)S(1)}, u32[]{:S(2)}, u32[]{:S(2)}) collective-permute-start(bf16[64,512]{1,0:T(8,128)(2,1)S(1)} %get-tuple-element.50), channel_id=1, source_target_pairs={{0,32},{32,0},{1,33},{33,1},{2,34},{34,2},{3,35},{35,3},{4,36},{36... | collective-permute-start | bytes 196616 | tf_op jit(solution)/shard_map/ppermute | solution.py:144
  26.9 2.5 %collective-permute-start.4 = (bf16[64,512]{1,0:T(8,128)(2,1)S(1)}, bf16[64,512]{1,0:T(8,128)(2,1)S(1)}, u32[]{:S(2)}, u32[]{:S(2)}) collective-permute-start(bf16[64,512]{1,0:T(8,128)(2,1)S(1)} %get-tuple-element.49), channel_id=1, source_target_pairs={{0,33},{1,32},{32,1},{33,0},{2,35},{3,34},{34,3},{35,2},{4,37},{5,... | collective-permute-start | bytes 196616 | tf_op jit(solution)/shard_map/ppermute | solution.py:145
  29.4 2.3 %collective-permute-start.1 = (bf16[64,512]{1,0:T(8,128)(2,1)S(1)}, bf16[64,512]{1,0:T(8,128)(2,1)S(1)}, u32[]{:S(2)}, u32[]{:S(2)}) collective-permute-start(bf16[64,512]{1,0:T(8,128)(2,1)S(1)} %get-tuple-element.49), channel_id=1, source_target_pairs={{0,1},{1,0},{2,3},{3,2},{4,5},{5,4},{6,7},{7,6},{8,9},{9,8},{10,11... | collective-permute-start | bytes 196616 | tf_op jit(solution)/shard_map/ppermute | solution.py:147
  31.7 2.5 %collective-permute-done.3 = bf16[64,512]{1,0:T(8,128)(2,1)S(1)} collective-permute-done((bf16[64,512]{1,0:T(8,128)(2,1)S(1)}, bf16[64,512]{1,0:T(8,128)(2,1)S(1)}, u32[]{:S(2)}, u32[]{:S(2)}) %collective-permute-start.3) | collective-permute-done | bytes 65568 | tf_op jit(solution)/shard_map/ppermute | solution.py:144
  38.0 4.9 %collective-permute-start.13 = (bf16[4,4,112,128]{3,2,1,0:T(8,128)(2,1)S(1)}, bf16[4,4,112,128]{3,2,1,0:T(8,128)(2,1)S(1)}, u32[]{:S(2)}, u32[]{:S(2)}) collective-permute-start(bf16[4,4,112,128]{3,2,1,0:T(8,128)(2,1)S(1)} %get-tuple-element.35), channel_id=1, source_target_pairs={{0,32},{32,0},{1,33},{33,1},{2,34},{34,2},{3,35},{35,3},{4,36},{36... | collective-permute-start | bytes 1376264 | tf_op jit(solution)/shard_map/ppermute | solution.py:152
  42.9 1.9 %collective-permute-start.18 = (bf16[5,4,112,128]{3,2,1,0:T(8,128)(2,1)S(1)}, bf16[5,4,112,128]{3,2,1,0:T(8,128)(2,1)S(1)}, u32[]{:S(2)}, u32[]{:S(2)}) collective-permute-start(bf16[5,4,112,128]{3,2,1,0:T(8,128)(2,1)S(1)} %get-tuple-element.41), channel_id=1, source_target_pairs={{0,32},{32,0},{1,33},{33,1},{2,34},{34,2},{3,35},{35,3},{4,36},{36... | collective-permute-start | bytes 1720328 | tf_op jit(solution)/shard_map/ppermute | solution.py:152
  44.8 2.1 %shard_map.67 = (bf16[3,4,112,128]{3,2,1,0:T(8,128)(2,1)S(1)}, bf16[4,4,112,128]{3,2,1,0:T(8,128)(2,1)S(1)}, bf16[4,4,112,128]{3,2,1,0:T(8,128)(2,1)S(1)}, bf16[5,4,112,128]{3,2,1,0:T(8,128)(2,1)S(1)}) custom-call(s32[4]{0:T(128)S(1)} %get-tuple-element.45.s_ref, bf16[2,64,14336]{2,1,0:T(8,128)(2,1)S(1)} %copy-done, bf16[2,64,14336]{2,1,0:T(8,128)(2,1)S(1)} %copy-done, ...), custom_call_target="tpu_custom_call" | custom-call | tf_op jit(solution)/shard_map/pallas_call | solution.py:42
  48.0 8.6 %collective-permute-start.5 = (f16[224,512]{1,0:T(8,128)(2,1)S(1)}, f16[224,512]{1,0:T(8,128)(2,1)S(1)}, u32[]{:S(2)}, u32[]{:S(2)}) collective-permute-start(f16[224,512]{1,0:T(8,128)(2,1)S(1)} %get-tuple-element.47), channel_id=1, source_target_pairs={{0,2},{1,31},{2,4},{3,1},{4,6},{5,3},{6,8},{7,5},{8,10},{9,7},{10,... | collective-permute-start | bytes 688136 | tf_op jit(solution)/shard_map/ppermute | solution.py:172
  59.8 5.3 %collective-permute-start.6 = (f16[448,512]{1,0:T(8,128)(2,1)S(1)}, f16[448,512]{1,0:T(8,128)(2,1)S(1)}, u32[]{:S(2)}, u32[]{:S(2)}) collective-permute-start(f16[448,512]{1,0:T(8,128)(2,1)S(1)} %fusion.15), channel_id=1, source_target_pairs={{0,2},{1,31},{2,4},{3,1},{4,6},{5,3},{6,8},{7,5},{8,10},{9,7},{10,... | collective-permute-start | bytes 1376264 | tf_op jit(solution)/shard_map/ppermute | solution.py:172
  67.8 3.3 %collective-permute-done.6 = f16[448,512]{1,0:T(8,128)(2,1)S(1)} collective-permute-done((f16[448,512]{1,0:T(8,128)(2,1)S(1)}, f16[448,512]{1,0:T(8,128)(2,1)S(1)}, u32[]{:S(2)}, u32[]{:S(2)}) %collective-permute-start.6) | collective-permute-done | bytes 458784 | tf_op jit(solution)/shard_map/ppermute | solution.py:172
  71.3 5.3 %collective-permute-start.9 = (f16[448,512]{1,0:T(8,128)(2,1)S(1)}, f16[448,512]{1,0:T(8,128)(2,1)S(1)}, u32[]{:S(2)}, u32[]{:S(2)}) collective-permute-start(f16[448,512]{1,0:T(8,128)(2,1)S(1)} %fusion.13), channel_id=1, source_target_pairs={{0,2},{1,31},{2,4},{3,1},{4,6},{5,3},{6,8},{7,5},{8,10},{9,7},{10,... | collective-permute-start | bytes 1376264 | tf_op jit(solution)/shard_map/ppermute | solution.py:172
  82.2 5.0 %collective-permute-start.11 = (f16[448,512]{1,0:T(8,128)(2,1)S(1)}, f16[448,512]{1,0:T(8,128)(2,1)S(1)}, u32[]{:S(2)}, u32[]{:S(2)}) collective-permute-start(f16[448,512]{1,0:T(8,128)(2,1)S(1)} %fusion.11), channel_id=1, source_target_pairs={{0,2},{1,31},{2,4},{3,1},{4,6},{5,3},{6,8},{7,5},{8,10},{9,7},{10,... | collective-permute-start | bytes 1376264 | tf_op jit(solution)/shard_map/ppermute | solution.py:172
  87.2 5.5 %collective-permute-done.12 = f16[448,512]{1,0:T(8,128)(2,1)S(1)} collective-permute-done((f16[448,512]{1,0:T(8,128)(2,1)S(1)}, f16[448,512]{1,0:T(8,128)(2,1)S(1)}, u32[]{:S(2)}, u32[]{:S(2)}) %collective-permute-start.12) | collective-permute-done | bytes 458784 | tf_op jit(solution)/shard_map/ppermute | solution.py:172
  95.6 4.6 %collective-permute-start.14 = (f16[448,512]{1,0:T(8,128)(2,1)S(1)}, f16[448,512]{1,0:T(8,128)(2,1)S(1)}, u32[]{:S(2)}, u32[]{:S(2)}) collective-permute-start(f16[448,512]{1,0:T(8,128)(2,1)S(1)} %fusion.9), channel_id=1, source_target_pairs={{0,2},{1,31},{2,4},{3,1},{4,6},{5,3},{6,8},{7,5},{8,10},{9,7},{10,... | collective-permute-start | bytes 1376264 | tf_op jit(solution)/shard_map/ppermute | solution.py:172
  100.1 7.8 %collective-permute-done.15 = f16[448,512]{1,0:T(8,128)(2,1)S(1)} collective-permute-done((f16[448,512]{1,0:T(8,128)(2,1)S(1)}, f16[448,512]{1,0:T(8,128)(2,1)S(1)}, u32[]{:S(2)}, u32[]{:S(2)}) %collective-permute-start.15) | collective-permute-done | bytes 458784 | tf_op jit(solution)/shard_map/ppermute | solution.py:172
  108.1 1.9 %collective-permute-start.17 = (f16[448,512]{1,0:T(8,128)(2,1)S(1)}, f16[448,512]{1,0:T(8,128)(2,1)S(1)}, u32[]{:S(2)}, u32[]{:S(2)}) collective-permute-start(f16[448,512]{1,0:T(8,128)(2,1)S(1)} %fusion.8), channel_id=1, source_target_pairs={{0,30},{1,3},{2,0},{3,5},{4,2},{5,7},{6,4},{7,9},{8,6},{9,11},{10,... | collective-permute-start | bytes 1376264 | tf_op jit(solution)/shard_map/ppermute | solution.py:172
  110.9 4.7 %collective-permute-start.16 = (f16[448,512]{1,0:T(8,128)(2,1)S(1)}, f16[448,512]{1,0:T(8,128)(2,1)S(1)}, u32[]{:S(2)}, u32[]{:S(2)}) collective-permute-start(f16[448,512]{1,0:T(8,128)(2,1)S(1)} %fusion.7), channel_id=1, source_target_pairs={{0,2},{1,31},{2,4},{3,1},{4,6},{5,3},{6,8},{7,5},{8,10},{9,7},{10,... | collective-permute-start | bytes 1376264 | tf_op jit(solution)/shard_map/ppermute | solution.py:172
  115.7 6.6 %collective-permute-done.17 = f16[448,512]{1,0:T(8,128)(2,1)S(1)} collective-permute-done((f16[448,512]{1,0:T(8,128)(2,1)S(1)}, f16[448,512]{1,0:T(8,128)(2,1)S(1)}, u32[]{:S(2)}, u32[]{:S(2)}) %collective-permute-start.17) | collective-permute-done | bytes 458784 | tf_op jit(solution)/shard_map/ppermute | solution.py:172
  125.3 5.0 %collective-permute-start.19 = (f16[448,512]{1,0:T(8,128)(2,1)S(1)}, f16[448,512]{1,0:T(8,128)(2,1)S(1)}, u32[]{:S(2)}, u32[]{:S(2)}) collective-permute-start(f16[448,512]{1,0:T(8,128)(2,1)S(1)} %fusion.5), channel_id=1, source_target_pairs={{0,2},{1,31},{2,4},{3,1},{4,6},{5,3},{6,8},{7,5},{8,10},{9,7},{10,... | collective-permute-start | bytes 1376264 | tf_op jit(solution)/shard_map/ppermute | solution.py:172
  130.3 5.5 %collective-permute-done.20 = f16[448,512]{1,0:T(8,128)(2,1)S(1)} collective-permute-done((f16[448,512]{1,0:T(8,128)(2,1)S(1)}, f16[448,512]{1,0:T(8,128)(2,1)S(1)}, u32[]{:S(2)}, u32[]{:S(2)}) %collective-permute-start.20) | collective-permute-done | bytes 458784 | tf_op jit(solution)/shard_map/ppermute | solution.py:172
  138.7 9.6 %collective-permute-done.22 = f16[448,512]{1,0:T(8,128)(2,1)S(1)} collective-permute-done((f16[448,512]{1,0:T(8,128)(2,1)S(1)}, f16[448,512]{1,0:T(8,128)(2,1)S(1)}, u32[]{:S(2)}, u32[]{:S(2)}) %collective-permute-start.22) | collective-permute-done | bytes 458784 | tf_op jit(solution)/shard_map/ppermute | solution.py:172
  150.4 4.6 %collective-permute-start.21 = (f16[448,512]{1,0:T(8,128)(2,1)S(1)}, f16[448,512]{1,0:T(8,128)(2,1)S(1)}, u32[]{:S(2)}, u32[]{:S(2)}) collective-permute-start(f16[448,512]{1,0:T(8,128)(2,1)S(1)} %fusion.3), channel_id=1, source_target_pairs={{0,2},{1,31},{2,4},{3,1},{4,6},{5,3},{6,8},{7,5},{8,10},{9,7},{10,... | collective-permute-start | bytes 1376264 | tf_op jit(solution)/shard_map/ppermute | solution.py:172
  156.2 2.6 %collective-permute-done.23 = f16[448,512]{1,0:T(8,128)(2,1)S(1)} collective-permute-done((f16[448,512]{1,0:T(8,128)(2,1)S(1)}, f16[448,512]{1,0:T(8,128)(2,1)S(1)}, u32[]{:S(2)}, u32[]{:S(2)}) %collective-permute-start.23) | collective-permute-done | bytes 458784 | tf_op jit(solution)/shard_map/ppermute | solution.py:172
  158.9 2.9 %collective-permute-done.21 = f16[448,512]{1,0:T(8,128)(2,1)S(1)} collective-permute-done((f16[448,512]{1,0:T(8,128)(2,1)S(1)}, f16[448,512]{1,0:T(8,128)(2,1)S(1)}, u32[]{:S(2)}, u32[]{:S(2)}) %collective-permute-start.21) | collective-permute-done | bytes 458784 | tf_op jit(solution)/shard_map/ppermute | solution.py:172
  162.1 22.5 %all_to_all.5 = f16[16,28,512]{2,1,0:T(8,128)(2,1)S(1)} all-to-all(f16[16,28,512]{2,1,0:T(8,128)(2,1)S(1)} %reshape.76), channel_id=1, replica_groups=mesh['ylo'=2,'x'=4,'yhi'=2,'z'=16,'core'=2] {'ylo','x','core'}, dimensions={0} | all-to-all | bytes 917504 | tf_op jit(solution)/shard_map/all_to_all | solution.py:185
  184.8 2.4 %shard_map.69 = (f32[28,512]{1,0:T(8,128)}, f32[28,512]{1,0:T(8,128)}, f32[28,512]{1,0:T(8,128)}) custom-call(f32[16,32,512]{2,1,0:T(8,128)S(1)} %pad.6.g_ref, bf16[28,512]{1,0:T(8,128)(2,1)S(1)} %copy-done.1), custom_call_target="tpu_custom_call" | custom-call | tf_op jit(solution)/shard_map/pallas_call | solution.py:112
  (65 shorter events, 29.9 us)
Async XLA Ops:
  0.6 11.9 %copy-start.3 = (s32[2]{0:T(128)S(1)}, s32[2]{0:T(128)}, u32[]{:S(2)}) copy-start(s32[2]{0:T(128)} %param.6) | copy-start | bytes 28
  0.6 12.0 %copy-start.2 = (bf16[2,64,512]{2,1,0:T(8,128)(2,1)S(1)}, bf16[2,64,512]{2,1,0:T(8,128)(2,1)}, u32[]{:S(2)}) copy-start(bf16[2,64,512]{2,1,0:T(8,128)(2,1)} %param.4) | copy-start | bytes 393220
  3.6 12.4 %collective-permute-start = (bf16[64,14336]{1,0:T(8,128)(2,1)}, bf16[64,14336]{1,0:T(8,128)(2,1)S(1)}, u32[]{:S(2)}, u32[]{:S(2)}) collective-permute-start(bf16[64,14336]{1,0:T(8,128)(2,1)} %dynamic-slice_bitcast_fusion), channel_id=1, source_target_pairs={{0,1},{1,0},{2,3},{3,2},{4,5},{5,4},{6,7},{7,6},{8,9},{9,8},{10,11... | collective-permute-start | bytes 5505032 | tf_op jit(solution)/shard_map/ppermute | solution.py:141
  16.0 2.0 %copy-start = (bf16[2,64,14336]{2,1,0:T(8,128)(2,1)S(1)}, bf16[2,64,14336]{2,1,0:T(8,128)(2,1)}, u32[]{:S(2)}) copy-start(bf16[2,64,14336]{2,1,0:T(8,128)(2,1)} %k1.3) | copy-start | bytes 11010052
  20.1 26.8 %collective-permute-start.2 = (bf16[3,4,112,128]{3,2,1,0:T(8,128)(2,1)S(1)}, bf16[3,4,112,128]{3,2,1,0:T(8,128)(2,1)S(1)}, u32[]{:S(2)}, u32[]{:S(2)}) collective-permute-start(bf16[3,4,112,128]{3,2,1,0:T(8,128)(2,1)S(1)} %get-tuple-element.25), channel_id=1, source_target_pairs={{0,32},{32,0},{1,33},{33,1},{2,34},{34,2},{3,35},{35,3},{4,36},{36... | collective-permute-start | bytes 1032200 | tf_op jit(solution)/shard_map/ppermute | solution.py:152
  22.0 12.1 %collective-permute-start.3 = (bf16[64,512]{1,0:T(8,128)(2,1)S(1)}, bf16[64,512]{1,0:T(8,128)(2,1)S(1)}, u32[]{:S(2)}, u32[]{:S(2)}) collective-permute-start(bf16[64,512]{1,0:T(8,128)(2,1)S(1)} %get-tuple-element.50), channel_id=1, source_target_pairs={{0,32},{32,0},{1,33},{33,1},{2,34},{34,2},{3,35},{35,3},{4,36},{36... | collective-permute-start | bytes 196616 | tf_op jit(solution)/shard_map/ppermute | solution.py:144
  26.9 9.2 %collective-permute-start.4 = (bf16[64,512]{1,0:T(8,128)(2,1)S(1)}, bf16[64,512]{1,0:T(8,128)(2,1)S(1)}, u32[]{:S(2)}, u32[]{:S(2)}) collective-permute-start(bf16[64,512]{1,0:T(8,128)(2,1)S(1)} %get-tuple-element.49), channel_id=1, source_target_pairs={{0,33},{1,32},{32,1},{33,0},{2,35},{3,34},{34,3},{35,2},{4,37},{5,... | collective-permute-start | bytes 196616 | tf_op jit(solution)/shard_map/ppermute | solution.py:145
  29.4 18.0 %collective-permute-start.1 = (bf16[64,512]{1,0:T(8,128)(2,1)S(1)}, bf16[64,512]{1,0:T(8,128)(2,1)S(1)}, u32[]{:S(2)}, u32[]{:S(2)}) collective-permute-start(bf16[64,512]{1,0:T(8,128)(2,1)S(1)} %get-tuple-element.49), channel_id=1, source_target_pairs={{0,1},{1,0},{2,3},{3,2},{4,5},{5,4},{6,7},{7,6},{8,9},{9,8},{10,11... | collective-permute-start | bytes 196616 | tf_op jit(solution)/shard_map/ppermute | solution.py:147
  36.1 22.5 %collective-permute-start.8 = (bf16[4,4,112,128]{3,2,1,0:T(8,128)(2,1)S(1)}, bf16[4,4,112,128]{3,2,1,0:T(8,128)(2,1)S(1)}, u32[]{:S(2)}, u32[]{:S(2)}) collective-permute-start(bf16[4,4,112,128]{3,2,1,0:T(8,128)(2,1)S(1)} %get-tuple-element.29), channel_id=1, source_target_pairs={{0,32},{32,0},{1,33},{33,1},{2,34},{34,2},{3,35},{35,3},{4,36},{36... | collective-permute-start | bytes 1376264 | tf_op jit(solution)/shard_map/ppermute | solution.py:152
  38.0 41.8 %collective-permute-start.13 = (bf16[4,4,112,128]{3,2,1,0:T(8,128)(2,1)S(1)}, bf16[4,4,112,128]{3,2,1,0:T(8,128)(2,1)S(1)}, u32[]{:S(2)}, u32[]{:S(2)}) collective-permute-start(bf16[4,4,112,128]{3,2,1,0:T(8,128)(2,1)S(1)} %get-tuple-element.35), channel_id=1, source_target_pairs={{0,32},{32,0},{1,33},{33,1},{2,34},{34,2},{3,35},{35,3},{4,36},{36... | collective-permute-start | bytes 1376264 | tf_op jit(solution)/shard_map/ppermute | solution.py:152
  42.9 67.2 %collective-permute-start.18 = (bf16[5,4,112,128]{3,2,1,0:T(8,128)(2,1)S(1)}, bf16[5,4,112,128]{3,2,1,0:T(8,128)(2,1)S(1)}, u32[]{:S(2)}, u32[]{:S(2)}) collective-permute-start(bf16[5,4,112,128]{3,2,1,0:T(8,128)(2,1)S(1)} %get-tuple-element.41), channel_id=1, source_target_pairs={{0,32},{32,0},{1,33},{33,1},{2,34},{34,2},{3,35},{35,3},{4,36},{36... | collective-permute-start | bytes 1720328 | tf_op jit(solution)/shard_map/ppermute | solution.py:152
  48.0 11.6 %collective-permute-start.5 = (f16[224,512]{1,0:T(8,128)(2,1)S(1)}, f16[224,512]{1,0:T(8,128)(2,1)S(1)}, u32[]{:S(2)}, u32[]{:S(2)}) collective-permute-start(f16[224,512]{1,0:T(8,128)(2,1)S(1)} %get-tuple-element.47), channel_id=1, source_target_pairs={{0,2},{1,31},{2,4},{3,1},{4,6},{5,3},{6,8},{7,5},{8,10},{9,7},{10,... | collective-permute-start | bytes 688136 | tf_op jit(solution)/shard_map/ppermute | solution.py:172
  56.7 8.4 %collective-permute-start.7 = (f16[224,512]{1,0:T(8,128)(2,1)S(1)}, f16[224,512]{1,0:T(8,128)(2,1)S(1)}, u32[]{:S(2)}, u32[]{:S(2)}) collective-permute-start(f16[224,512]{1,0:T(8,128)(2,1)S(1)} %get-tuple-element.48), channel_id=1, source_target_pairs={{0,30},{1,3},{2,0},{3,5},{4,2},{5,7},{6,4},{7,9},{8,6},{9,11},{10,... | collective-permute-start | bytes 688136 | tf_op jit(solution)/shard_map/ppermute | solution.py:172
  59.8 11.3 %collective-permute-start.6 = (f16[448,512]{1,0:T(8,128)(2,1)S(1)}, f16[448,512]{1,0:T(8,128)(2,1)S(1)}, u32[]{:S(2)}, u32[]{:S(2)}) collective-permute-start(f16[448,512]{1,0:T(8,128)(2,1)S(1)} %fusion.15), channel_id=1, source_target_pairs={{0,2},{1,31},{2,4},{3,1},{4,6},{5,3},{6,8},{7,5},{8,10},{9,7},{10,... | collective-permute-start | bytes 1376264 | tf_op jit(solution)/shard_map/ppermute | solution.py:172
  65.2 12.5 %collective-permute-start.10 = (f16[448,512]{1,0:T(8,128)(2,1)S(1)}, f16[448,512]{1,0:T(8,128)(2,1)S(1)}, u32[]{:S(2)}, u32[]{:S(2)}) collective-permute-start(f16[448,512]{1,0:T(8,128)(2,1)S(1)} %fusion.14), channel_id=1, source_target_pairs={{0,30},{1,3},{2,0},{3,5},{4,2},{5,7},{6,4},{7,9},{8,6},{9,11},{10,... | collective-permute-start | bytes 1376264 | tf_op jit(solution)/shard_map/ppermute | solution.py:172
  71.3 10.7 %collective-permute-start.9 = (f16[448,512]{1,0:T(8,128)(2,1)S(1)}, f16[448,512]{1,0:T(8,128)(2,1)S(1)}, u32[]{:S(2)}, u32[]{:S(2)}) collective-permute-start(f16[448,512]{1,0:T(8,128)(2,1)S(1)} %fusion.13), channel_id=1, source_target_pairs={{0,2},{1,31},{2,4},{3,1},{4,6},{5,3},{6,8},{7,5},{8,10},{9,7},{10,... | collective-permute-start | bytes 1376264 | tf_op jit(solution)/shard_map/ppermute | solution.py:172
  77.9 14.7 %collective-permute-start.12 = (f16[448,512]{1,0:T(8,128)(2,1)S(1)}, f16[448,512]{1,0:T(8,128)(2,1)S(1)}, u32[]{:S(2)}, u32[]{:S(2)}) collective-permute-start(f16[448,512]{1,0:T(8,128)(2,1)S(1)} %fusion.12), channel_id=1, source_target_pairs={{0,30},{1,3},{2,0},{3,5},{4,2},{5,7},{6,4},{7,9},{8,6},{9,11},{10,... | collective-permute-start | bytes 1376264 | tf_op jit(solution)/shard_map/ppermute | solution.py:172
  82.2 13.2 %collective-permute-start.11 = (f16[448,512]{1,0:T(8,128)(2,1)S(1)}, f16[448,512]{1,0:T(8,128)(2,1)S(1)}, u32[]{:S(2)}, u32[]{:S(2)}) collective-permute-start(f16[448,512]{1,0:T(8,128)(2,1)S(1)} %fusion.11), channel_id=1, source_target_pairs={{0,2},{1,31},{2,4},{3,1},{4,6},{5,3},{6,8},{7,5},{8,10},{9,7},{10,... | collective-permute-start | bytes 1376264 | tf_op jit(solution)/shard_map/ppermute | solution.py:172
  92.8 15.1 %collective-permute-start.15 = (f16[448,512]{1,0:T(8,128)(2,1)S(1)}, f16[448,512]{1,0:T(8,128)(2,1)S(1)}, u32[]{:S(2)}, u32[]{:S(2)}) collective-permute-start(f16[448,512]{1,0:T(8,128)(2,1)S(1)} %fusion.10), channel_id=1, source_target_pairs={{0,30},{1,3},{2,0},{3,5},{4,2},{5,7},{6,4},{7,9},{8,6},{9,11},{10,... | collective-permute-start | bytes 1376264 | tf_op jit(solution)/shard_map/ppermute | solution.py:172
  95.6 15.2 %collective-permute-start.14 = (f16[448,512]{1,0:T(8,128)(2,1)S(1)}, f16[448,512]{1,0:T(8,128)(2,1)S(1)}, u32[]{:S(2)}, u32[]{:S(2)}) collective-permute-start(f16[448,512]{1,0:T(8,128)(2,1)S(1)} %fusion.9), channel_id=1, source_target_pairs={{0,2},{1,31},{2,4},{3,1},{4,6},{5,3},{6,8},{7,5},{8,10},{9,7},{10,... | collective-permute-start | bytes 1376264 | tf_op jit(solution)/shard_map/ppermute | solution.py:172
  108.1 14.2 %collective-permute-start.17 = (f16[448,512]{1,0:T(8,128)(2,1)S(1)}, f16[448,512]{1,0:T(8,128)(2,1)S(1)}, u32[]{:S(2)}, u32[]{:S(2)}) collective-permute-start(f16[448,512]{1,0:T(8,128)(2,1)S(1)} %fusion.8), channel_id=1, source_target_pairs={{0,30},{1,3},{2,0},{3,5},{4,2},{5,7},{6,4},{7,9},{8,6},{9,11},{10,... | collective-permute-start | bytes 1376264 | tf_op jit(solution)/shard_map/ppermute | solution.py:172
  110.9 14.2 %collective-permute-start.16 = (f16[448,512]{1,0:T(8,128)(2,1)S(1)}, f16[448,512]{1,0:T(8,128)(2,1)S(1)}, u32[]{:S(2)}, u32[]{:S(2)}) collective-permute-start(f16[448,512]{1,0:T(8,128)(2,1)S(1)} %fusion.7), channel_id=1, source_target_pairs={{0,2},{1,31},{2,4},{3,1},{4,6},{5,3},{6,8},{7,5},{8,10},{9,7},{10,... | collective-permute-start | bytes 1376264 | tf_op jit(solution)/shard_map/ppermute | solution.py:172
  122.5 13.3 %collective-permute-start.20 = (f16[448,512]{1,0:T(8,128)(2,1)S(1)}, f16[448,512]{1,0:T(8,128)(2,1)S(1)}, u32[]{:S(2)}, u32[]{:S(2)}) collective-permute-start(f16[448,512]{1,0:T(8,128)(2,1)S(1)} %fusion.6), channel_id=1, source_target_pairs={{0,30},{1,3},{2,0},{3,5},{4,2},{5,7},{6,4},{7,9},{8,6},{9,11},{10,... | collective-permute-start | bytes 1376264 | tf_op jit(solution)/shard_map/ppermute | solution.py:172
  125.3 13.2 %collective-permute-start.19 = (f16[448,512]{1,0:T(8,128)(2,1)S(1)}, f16[448,512]{1,0:T(8,128)(2,1)S(1)}, u32[]{:S(2)}, u32[]{:S(2)}) collective-permute-start(f16[448,512]{1,0:T(8,128)(2,1)S(1)} %fusion.5), channel_id=1, source_target_pairs={{0,2},{1,31},{2,4},{3,1},{4,6},{5,3},{6,8},{7,5},{8,10},{9,7},{10,... | collective-permute-start | bytes 1376264 | tf_op jit(solution)/shard_map/ppermute | solution.py:172
  135.9 12.4 %collective-permute-start.22 = (f16[448,512]{1,0:T(8,128)(2,1)S(1)}, f16[448,512]{1,0:T(8,128)(2,1)S(1)}, u32[]{:S(2)}, u32[]{:S(2)}) collective-permute-start(f16[448,512]{1,0:T(8,128)(2,1)S(1)} %fusion.4), channel_id=1, source_target_pairs={{0,30},{1,3},{2,0},{3,5},{4,2},{5,7},{6,4},{7,9},{8,6},{9,11},{10,... | collective-permute-start | bytes 1376264 | tf_op jit(solution)/shard_map/ppermute | solution.py:172
  148.4 10.4 %collective-permute-start.23 = (f16[448,512]{1,0:T(8,128)(2,1)S(1)}, f16[448,512]{1,0:T(8,128)(2,1)S(1)}, u32[]{:S(2)}, u32[]{:S(2)}) collective-permute-start(f16[448,512]{1,0:T(8,128)(2,1)S(1)} %fusion.2), channel_id=1, source_target_pairs={{0,30},{1,3},{2,0},{3,5},{4,2},{5,7},{6,4},{7,9},{8,6},{9,11},{10,... | collective-permute-start | bytes 1376264 | tf_op jit(solution)/shard_map/ppermute | solution.py:172
  150.4 11.4 %collective-permute-start.21 = (f16[448,512]{1,0:T(8,128)(2,1)S(1)}, f16[448,512]{1,0:T(8,128)(2,1)S(1)}, u32[]{:S(2)}, u32[]{:S(2)}) collective-permute-start(f16[448,512]{1,0:T(8,128)(2,1)S(1)} %fusion.3), channel_id=1, source_target_pairs={{0,2},{1,31},{2,4},{3,1},{4,6},{5,3},{6,8},{7,5},{8,10},{9,7},{10,... | collective-permute-start | bytes 1376264 | tf_op jit(solution)/shard_map/ppermute | solution.py:172
  161.7 23.1 %copy-start.1 = (bf16[28,512]{1,0:T(8,128)(2,1)S(1)}, bf16[28,512]{1,0:T(8,128)(2,1)}, u32[]{:S(2)}) copy-start(bf16[28,512]{1,0:T(8,128)(2,1)} %w_ref.1) | copy-start | bytes 86020

commit v3 on v1

v3 whole, which is shorter than its diff:
```python
import functools

import jax
import jax.numpy as jnp
from jax import lax
from jax.experimental import pallas as pl
from jax.experimental.pallas import tpu as pltpu
from jax.sharding import Mesh, PartitionSpec as P

BLOCK = 128
AXES = ("ylo", "x", "yhi", "z", "core")
NZ = 16
FAR = NZ // 2
VMEM = 56 * 1024 * 1024
f32 = jnp.float32
f16 = jnp.float16


def turn_kernel(s_ref, up_ref, feat_ref, *rest):
    outs, hold = rest[:-1], rest[-1]
    step = pl.program_id(0)
    seg2, width = feat_ref.shape[0], up_ref.shape[2] // 4
    span = width // NZ
    for half in range(2):
        turned = []
        for j in range(2):
            x = up_ref[:, :, (2 * j + half) * width:(2 * j + half + 1) * width]
            turned.append(x.reshape(seg2, width).astype(f32).T)
        for dest in range(NZ):
            rows = [t[dest * span:(dest + 1) * span] for t in turned]
            hold[half, dest, step] = jnp.concatenate(rows, axis=0).astype(hold.dtype)

    @pl.when(step == pl.num_programs(0) - 1)
    def _():
        n, tall = hold.shape[2], hold.shape[3]
        yhi, z, core = s_ref[0], s_ref[1], s_ref[2]
        for other in range(4):
            half = yhi if other < 2 else 1 - yhi
            to = core if other % 2 == 0 else 1 - core
            first, second = outs[2 * other], outs[2 * other + 1]
            place = lambda dist: lax.rem(z + (1 - 2 * to) * dist + NZ, NZ)
            for p in range(n // 2):
                first[p * tall:(p + 1) * tall] = hold[half, place(FAR), (n // 2) * to + p]
            for p in range(n):
                at = (n // 2 + p) * tall
                first[at:at + tall] = hold[half, place(FAR - 1), p]
            at = (n // 2 + n) * tall
            for b in range(feat_ref.shape[1] // BLOCK):
                first[at + b * seg2:at + (b + 1) * seg2] = feat_ref[:, b * BLOCK:(b + 1) * BLOCK]
            for i in range(FAR - 1):
                for p in range(n):
                    at = (i * n + p) * tall
                    second[at:at + tall] = hold[half, place(FAR - 2 - i), p]


def turn(upstream, feats, scalars, n_groups):
    _, seg, units = upstream.shape
    seg2, rows = feats.shape
    n = n_groups // 2
    chunk = units // 2 // NZ
    tall = chunk // n
    shapes = [(chunk // 2 + chunk + rows // BLOCK * seg2, seg2), ((FAR - 1) * chunk, seg2)] * 4
    whole = lambda shape: pl.BlockSpec(shape, lambda i, s: (0,) * len(shape))
    return pl.pallas_call(
        turn_kernel,
        grid_spec=pltpu.PrefetchScalarGridSpec(
            num_scalar_prefetch=1,
            grid=(n,),
            in_specs=[pl.BlockSpec((2, seg, units // n), lambda i, s: (0, 0, i)), whole(feats.shape)],
            out_specs=[whole(shape) for shape in shapes],
            scratch_shapes=[pltpu.VMEM((2, NZ, n, tall, seg2), upstream.dtype)],
        ),
        out_shape=[jax.ShapeDtypeStruct(shape, upstream.dtype) for shape in shapes],
        compiler_params=pltpu.CompilerParams(vmem_limit_bytes=VMEM),
    )(scalars, upstream, feats)


def first_kernel(a_ref, b_ref, c_ref, d_ref, out_ref, right_ref):
    refs = (a_ref, b_ref, c_ref, d_ref)
    seg2 = a_ref.shape[1]
    height = out_ref.shape[0]
    n_lane = (a_ref.shape[0] - height) // seg2
    for k, ref in enumerate(refs):
        rows = [ref[height + b * seg2:height + (b + 1) * seg2] for b in range(n_lane)]
        feats = jnp.concatenate(rows, axis=1)
        half = seg2 // 2
        none = jnp.zeros((half, feats.shape[1]), feats.dtype)
        right_ref[k * seg2:k * seg2 + half] = jnp.concatenate([feats[:half], none], axis=1)
        right_ref[k * seg2 + half:(k + 1) * seg2] = jnp.concatenate([none, feats[half:]], axis=1)
    tile = height // 3

    @pl.loop(0, 3)
    def _(i):
        at = pl.ds(pl.multiple_of(i * tile, tile), tile)
        left = jnp.concatenate([ref[at] for ref in refs], axis=1)
        out_ref[at] = jnp.dot(left, right_ref[...], preferred_element_type=f32)


def first_product(pieces, height):
    seg2 = pieces[0].shape[1]
    wide = (pieces[0].shape[0] - height) // seg2 * BLOCK * 2
    return pl.pallas_call(
        first_kernel,
        out_shape=[
            jax.ShapeDtypeStruct((height, wide), f32),
            jax.ShapeDtypeStruct((4 * seg2, wide), pieces[0].dtype),
        ],
        cost_estimate=pl.CostEstimate(flops=2 * height * 4 * seg2 * wide, bytes_accessed=6 * height * wide, transcendentals=0),
        compiler_params=pltpu.CompilerParams(vmem_limit_bytes=40 * 1024 * 1024),
    )(*pieces)


def product_kernel(a_ref, b_ref, c_ref, d_ref, right_ref, out_ref):
    left = jnp.concatenate([ref[...] for ref in (a_ref, b_ref, c_ref, d_ref)], axis=1)
    out_ref[...] = jnp.dot(left, right_ref[...], preferred_element_type=f32)


def product(pieces, right, chunk, start, count):
    seg2 = pieces[0].shape[1]
    tile = chunk // 2
    wide = right.shape[1]
    return pl.pallas_call(
        product_kernel,
        grid=(2 * count,),
        in_specs=[pl.BlockSpec((tile, seg2), lambda i: (2 * start + i, 0))] * 4
        + [pl.BlockSpec(right.shape, lambda i: (0, 0))],
        out_specs=pl.BlockSpec((tile, wide), lambda i: (i, 0)),
        out_shape=jax.ShapeDtypeStruct((count * chunk, wide), f32),
        cost_estimate=pl.CostEstimate(
            flops=2 * count * chunk * 4 * seg2 * wide, bytes_accessed=6 * count * chunk * wide, transcendentals=0
        ),
        compiler_params=pltpu.CompilerParams(vmem_limit_bytes=40 * 1024 * 1024),
    )(*pieces, right)


def solve_kernel(shift, scale, g_ref, w_ref, inv_ref, sal_ref, step_ref, y_ref):
    n_ex = g_ref.shape[0]
    units = w_ref.shape[0]
    rows = w_ref.shape[1]
    pad = g_ref.shape[1]
    nb = rows // BLOCK

    def blocks(x):
        return jnp.concatenate([x[:, b * BLOCK:(b + 1) * BLOCK] for b in range(nb)], axis=0).T

    for e in range(n_ex):
        y_ref[e] = blocks(g_ref[e])
    weights = w_ref[...].astype(f32)
    w = blocks(jnp.concatenate([weights, jnp.zeros((pad - units, rows), f32)], axis=0))
    lane_rows = lax.broadcasted_iota(jnp.int32, (n_ex, BLOCK), 0)
    kern = []
    for i in range(n_ex):
        gi = y_ref[i]
        row = jnp.zeros((n_ex, BLOCK), f32)
        for j in range(i, n_ex):
            dot = jnp.sum(gi * y_ref[j], axis=0, keepdims=True)
            if j == i:
                dot = dot + shift
            row = jnp.where(lane_rows == j, dot, row)
        kern.append(row)
    diag = jnp.ones((BLOCK, BLOCK), f32)
    step = w
    for k in range(n_ex):
        pivot = kern[k]
        inv = 1.0 / pivot[k:k + 1]
        yk = y_ref[k]
        scaled = yk * inv
        diag = diag - yk * scaled
        step = step - scaled * jnp.sum(yk * w, axis=0, keepdims=True)
        for i in range(k + 1, n_ex):
            m = pivot[i:i + 1] * inv
            kern[i] = kern[i] - m * pivot
            y_ref[i] = y_ref[i] - m * yk
    diag = diag.T
    step = step.T * scale
    for b in range(nb):
        at = pl.ds(b * BLOCK, BLOCK)
        d = diag[b * pad:b * pad + units]
        wb = weights[:, b * BLOCK:(b + 1) * BLOCK]
        inv_ref[:, at] = d
        sal_ref[:, at] = rows * (wb * wb) / (2.0 * d)
        step_ref[:, at] = step[b * pad:b * pad + units]


def solve(grads, weights, shift):
    units, rows = weights.shape
    out = jax.ShapeDtypeStruct((units, rows), f32)
    return pl.pallas_call(
        functools.partial(solve_kernel, shift, float(rows) ** 0.5),
        out_shape=[out, out, out],
        scratch_shapes=[pltpu.VMEM((grads.shape[0], BLOCK, BLOCK), f32)],
        compiler_params=pltpu.CompilerParams(vmem_limit_bytes=40 * 1024 * 1024),
    )(grads, weights)


def ring_pairs(cross):
    pairs = []
    for z in range(NZ):
        for core in range(2):
            to = (z + 1 - 2 * core) % NZ
            pairs.append((z * 2 + core, to * 2 + (core ^ cross)))
    return pairs


def body(features, upstream, lengths, weights):
    yhi, z, core = lax.axis_index("yhi"), lax.axis_index("z"), lax.axis_index("core")
    n_ex, seg, rows = features.shape
    units = upstream.shape[2]
    n_groups = 8
    total_len = seg * 64
    shard = (yhi * NZ + z) * 2 + core
    positions = shard * seg + jnp.arange(seg, dtype=jnp.int32)
    kept_rows = positions[None, :] < lengths[:, None]
    masked = jnp.where(kept_rows[:, :, None], features, jnp.zeros_like(features)) * jnp.asarray(0.25, features.dtype)
    scalars = jnp.stack([yhi, z, core]).astype(jnp.int32)
    made = turn(upstream, masked.reshape(n_ex * seg, rows), scalars, n_groups)

    quad = lambda x, i: lax.ppermute(x, ("yhi", "core"), [(j, j ^ i) for j in range(4)])
    chunk = units // 2 // NZ
    half = chunk // 2
    order = (3, 2, 1)
    near = {i: quad(made[2 * i], i) for i in order}
    rest = {i: quad(made[2 * i + 1], i) for i in order}
    near, rest = [made[0]] + [near[i] for i in (1, 2, 3)], [made[1]] + [rest[i] for i in (1, 2, 3)]
    part, right = first_product(near, half + chunk)
    parts = {FAR: part[:half], FAR - 1: part[half:]}
    start = 0
    for count in (2, FAR - 3):
        part = product(rest, right, chunk, start, count)
        for i in range(count):
            parts[FAR - 2 - start - i] = part[i * chunk:(i + 1) * chunk]
        start += count

    ring = lambda x, cross=0: lax.ppermute(x, ("z", "core"), ring_pairs(cross))
    got = ring(parts[FAR].astype(f16)).astype(f32)
    sums = [
        (parts[FAR - 1][k * half:(k + 1) * half] + jnp.where(core == k, got, 0.0)).astype(f16) for k in range(2)
    ]
    last = sums[1]
    for dist in range(FAR - 2, 0, -1):
        for k in range(2):
            got = ring(sums[k])
            got, _ = lax.optimization_barrier((got, last))
            sums[k] = last = (got.astype(f32) + parts[dist][k * half:(k + 1) * half]).astype(f16)
    pick = lambda x, i: lax.dynamic_slice_in_dim(x, i * rows, rows, 1)
    ends = []
    for k in range(2):
        ends.append(ring(pick(sums[k], core)).astype(f32) + ring(pick(sums[k], 1 - core), 1).astype(f32))
    length = lax.dynamic_index_in_dim(lengths, core, 0, keepdims=False).astype(f32)
    total = (jnp.concatenate(ends, axis=0) + pick(parts[0], core)) * (4096.0 / length)
    pieces = total.astype(f16).reshape(2 * n_groups, -1, rows)
    owned = lax.all_to_all(pieces, ("ylo", "x", "core"), 0, 0, tiled=True)
    own_units = owned.shape[1]
    grads = owned.astype(f32) * (1.0 / 1024.0)
    grads = jnp.pad(grads, ((0, 0), (0, -own_units % 8), (0, 0)))
    return tuple(solve(grads, weights, BLOCK / total_len))


def solution(mesh):
    fine = Mesh(mesh.devices.reshape(2, 4, 2, NZ, 2), AXES)
    dp, shard = ("ylo", "x"), ("yhi", "z", "core")
    in_specs = (P(dp, shard, None), P(dp, shard, None), P(dp), P(dp + shard, None))
    out_specs = (P(dp + shard, None),) * 3
    return jax.shard_map(body, mesh=fine, in_specs=in_specs, out_specs=out_specs, check_vma=False)
```

time: 181 us -> 193 us (1.066)
  Pallas kernels: 6.58 us -> 19.7 us
  waiting for transfers between devices: 65 us -> 57.2 us
  other arithmetic: 3.16 us -> 10.4 us
  starting transfers between devices: 78.4 us -> 84.8 us
  matrix products: 4.95 us -> 0 us
  local copies, waits for them, and re-layouts: 5.89 us -> 2.03 us
    pallas_call x0 -> x3, Pallas kernels: none -> 10.8 us  [the longest x2 9.53 us: product(): pl.pallas_call(product_kernel, grid=(2 * count,), in_specs=[pl.BlockSpec(...]
    ppermute x23, waiting for transfers between devices: 65 us -> 57.2 us  [the longest x6 37.8 us: body(): lax.ppermute(x, ('yhi', 'core'), [(j, j ^ i) for j in range(4)])]
    ppermute x23, starting transfers between devices: 78.4 us -> 84.8 us  [the longest x17 59.5 us: body(): ring = lambda x, cross=0: lax.ppermute(x, ('z', 'core'), ring_pairs(cross))]
    dot_general x8 -> x0, matrix products: 4.95 us -> none  [the longest x4 2.48 us: body(): part = lax.dot_general(flat(a), mine, dims, preferred_element_type=f32)]
    convert_element_type x7 -> x13, other arithmetic: 2.48 us -> 6 us  [the longest x12 4.13 us: body(): (got.astype(f32) + parts[dist][k * half:(k + 1) * half]).astype(f16)]
    squeeze x2 -> x0, local copies, waits for them, and re-layouts: 2.92 us -> none  [body(): pick = lambda x, i: lax.dynamic_index_in_dim(x, i, 0, keepdims=False)]
    pallas_call x2 -> x1, Pallas kernels: 4.17 us -> 6.43 us  [turn(): pl.pallas_call(turn_kernel, grid_spec=pltpu.PrefetchScalarGridSpec(num_sc...]
  transfers between devices with their start and end apart: 23 -> 23, of which waited for: 19 -> 12; matrix products, arithmetic and copies ran while one was open for 3% -> 4% of each run, Pallas kernels for 1% -> 5%
where the time goes in v3:
time: 193 us; the launch traced here: 191 us
  starting transfers between devices  84.8 us (44%)
  waiting for transfers between devices  57.2 us (30%)
  Pallas kernels  19.7 us (10%)
  blocking collectives  14.9 us (8%)
  other arithmetic  10.4 us (5%)
  local copies, waits for them, and re-layouts  2.03 us (1%)
    ppermute x17, starting transfers between devices, body(): ring = lambda x, cross=0: lax.ppermute(x, ('z', 'core'), ring_pairs(cross))  59.5 us
    ppermute x6, waiting for transfers between devices, body(): lax.ppermute(x, ('yhi', 'core'), [(j, j ^ i) for j in range(4)])  37.8 us
    ppermute x6, starting transfers between devices, body(): lax.ppermute(x, ('yhi', 'core'), [(j, j ^ i) for j in range(4)])  25.2 us
    ppermute x17, waiting for transfers between devices, body(): ring = lambda x, cross=0: lax.ppermute(x, ('z', 'core'), ring_pairs(cross))  19.4 us
    all_to_all x1, blocking collectives, body(): owned = lax.all_to_all(pieces, ('ylo', 'x', 'core'), 0, 0, tiled=True)  14.9 us
    pallas_call x2, Pallas kernels, product(): pl.pallas_call(product_kernel, grid=(2 * count,), in_specs=[pl.BlockSpec(...  9.53 us
    pallas_call x1, Pallas kernels, turn(): pl.pallas_call(turn_kernel, grid_spec=pltpu.PrefetchScalarGridSpec(num_sc...  6.43 us
    convert_element_type x12, other arithmetic, body(): (got.astype(f32) + parts[dist][k * half:(k + 1) * half]).astype(f16)  4.13 us
  transfers between devices with their start and end apart: 23, of which 12 were waited for; matrix products, arithmetic and copies ran while one was open for 4% of the time, Pallas kernels for 5%

profile of v3, /device:TPU:1, one launch (start us, length us, event | category | flops | bytes accessed | tf_op | source)
XLA Modules:
  0.0 191.0 jit_solution(16251510364513209504)
XLA Ops:
  3.6 6.4 %shard_map.67 = (bf16[1184,128]{1,0:T(8,128)(2,1)}, bf16[3136,128]{1,0:T(8,128)(2,1)}, bf16[1184,128]{1,0:T(8,128)(2,1)}, bf16[3136,128]{1,0:T(8,128)(2,1)}, bf1...) custom-call(s32[3]{0:T(128)} %pad_add_fusion.s_ref, ...), custom_call_target="tpu_custom_call" | custom-call | tf_op jit(solution)/shard_map/pallas_call | solution.py:64
  10.1 8.9 %collective-permute-start = (bf16[1184,128]{1,0:T(8,128)(2,1)}, bf16[1184,128]{1,0:T(8,128)(2,1)S(1)}, u32[]{:S(2)}, u32[]{:S(2)}) collective-permute-start(bf16[1184,128]{1,0:T(8,128)(2,1)} %get-tuple-element.26), channel_id=1, source_target_pairs={{0,1},{1,0},{32,33},{33,32},{2,3},{3,2},{34,35},{35,34},{4,5},{5,4... | collective-permute-start | bytes 909320 | tf_op jit(solution)/shard_map/ppermute | solution.py:218
  20.9 5.0 %collective-permute-start.2 = (bf16[1184,128]{1,0:T(8,128)(2,1)}, bf16[1184,128]{1,0:T(8,128)(2,1)S(1)}, u32[]{:S(2)}, u32[]{:S(2)}) collective-permute-start(bf16[1184,128]{1,0:T(8,128)(2,1)} %get-tuple-element.28), channel_id=1, source_target_pairs={{0,33},{1,32},{32,1},{33,0},{2,35},{3,34},{34,3},{35,2},{4,37},{5,... | collective-permute-start | bytes 909320 | tf_op jit(solution)/shard_map/ppermute | solution.py:218
  26.0 5.4 %collective-permute-done.1.c_ref = bf16[1184,128]{1,0:T(8,128)(2,1)S(1)} collective-permute-done((bf16[1184,128]{1,0:T(8,128)(2,1)}, bf16[1184,128]{1,0:T(8,128)(2,1)S(1)}, u32[]{:S(2)}, u32[]{:S(2)}) %collective-permute-start.1) | collective-permute-done | bytes 303136 | tf_op jit(solution)/shard_map/ppermute | solution.py:218
  31.4 6.6 %collective-permute-done.2.d_ref = bf16[1184,128]{1,0:T(8,128)(2,1)S(1)} collective-permute-done((bf16[1184,128]{1,0:T(8,128)(2,1)}, bf16[1184,128]{1,0:T(8,128)(2,1)S(1)}, u32[]{:S(2)}, u32[]{:S(2)}) %collective-permute-start.2) | collective-permute-done | bytes 303136 | tf_op jit(solution)/shard_map/ppermute | solution.py:218
  41.2 5.7 %collective-permute-start.3 = (f16[224,1024]{1,0:T(8,128)(2,1)}, f16[224,1024]{1,0:T(8,128)(2,1)}, u32[]{:S(2)}, u32[]{:S(2)}) collective-permute-start(f16[224,1024]{1,0:T(8,128)(2,1)} %slice_convert_fusion), channel_id=1, source_target_pairs={{0,2},{1,31},{2,4},{3,1},{4,6},{5,3},{6,8},{7,5},{8,10},{9,7},{10,... | collective-permute-start | bytes 1376264 | tf_op jit(solution)/shard_map/ppermute | solution.py:234
  48.9 4.8 %collective-permute-start.6 = (bf16[3136,128]{1,0:T(8,128)(2,1)}, bf16[3136,128]{1,0:T(8,128)(2,1)S(1)}, u32[]{:S(2)}, u32[]{:S(2)}) collective-permute-start(bf16[3136,128]{1,0:T(8,128)(2,1)} %get-tuple-element.33), channel_id=1, source_target_pairs={{0,32},{1,33},{32,0},{33,1},{2,34},{3,35},{34,2},{35,3},{4,36},{5,... | collective-permute-start | bytes 2408456 | tf_op jit(solution)/shard_map/ppermute | solution.py:218
  53.7 2.6 %collective-permute-start.7 = (bf16[3136,128]{1,0:T(8,128)(2,1)}, bf16[3136,128]{1,0:T(8,128)(2,1)}, u32[]{:S(2)}, u32[]{:S(2)}) collective-permute-start(bf16[3136,128]{1,0:T(8,128)(2,1)} %get-tuple-element.34), channel_id=1, source_target_pairs={{0,33},{1,32},{32,1},{33,0},{2,35},{3,34},{34,3},{35,2},{4,37},{5,... | collective-permute-start | bytes 2408456 | tf_op jit(solution)/shard_map/ppermute | solution.py:218
  58.3 2.6 %collective-permute-start.4 = (f16[224,1024]{1,0:T(8,128)(2,1)S(1)}, f16[224,1024]{1,0:T(8,128)(2,1)S(1)}, u32[]{:S(2)}, u32[]{:S(2)}) collective-permute-start(f16[224,1024]{1,0:T(8,128)(2,1)S(1)} %get-tuple-element.47), channel_id=1, source_target_pairs={{0,2},{1,31},{2,4},{3,1},{4,6},{5,3},{6,8},{7,5},{8,10},{9,7},{10,... | collective-permute-start | bytes 1376264 | tf_op jit(solution)/shard_map/ppermute | solution.py:234
  60.9 2.7 %collective-permute-start.9 = (f16[224,1024]{1,0:T(8,128)(2,1)S(1)}, f16[224,1024]{1,0:T(8,128)(2,1)S(1)}, u32[]{:S(2)}, u32[]{:S(2)}) collective-permute-start(f16[224,1024]{1,0:T(8,128)(2,1)S(1)} %get-tuple-element.48), channel_id=1, source_target_pairs={{0,2},{1,31},{2,4},{3,1},{4,6},{5,3},{6,8},{7,5},{8,10},{9,7},{10,... | collective-permute-start | bytes 1376264 | tf_op jit(solution)/shard_map/ppermute | solution.py:234
  63.7 7.8 %collective-permute-done.6.c_ref = bf16[3136,128]{1,0:T(8,128)(2,1)S(1)} collective-permute-done((bf16[3136,128]{1,0:T(8,128)(2,1)}, bf16[3136,128]{1,0:T(8,128)(2,1)S(1)}, u32[]{:S(2)}, u32[]{:S(2)}) %collective-permute-start.6) | collective-permute-done | bytes 802848 | tf_op jit(solution)/shard_map/ppermute | solution.py:218
  71.5 18.0 %collective-permute-done.7.d_ref = bf16[3136,128]{1,0:T(8,128)(2,1)} collective-permute-done((bf16[3136,128]{1,0:T(8,128)(2,1)}, bf16[3136,128]{1,0:T(8,128)(2,1)}, u32[]{:S(2)}, u32[]{:S(2)}) %collective-permute-start.7) | collective-permute-done | bytes 802848 | tf_op jit(solution)/shard_map/ppermute | solution.py:218
  89.5 2.9 %shard_map.69 = f32[896,1024]{1,0:T(8,128)S(1)} custom-call(bf16[3136,128]{1,0:T(8,128)(2,1)S(1)} %copy-done.1, bf16[3136,128]{1,0:T(8,128)(2,1)S(1)} %collective-permute-done.5.b_ref, bf16[3136,128]{1,0:T(8,128)(2,1)S(1)} %collective-permute-done.6.c_ref, bf16[3136,128]{1,0:T(8,128)(2,1)} %collective-permute-done.7.d_ref, ...), custom_call_target="tpu_custom_call" | custom-call | flops 939524096 | bytes 5505024 | tf_op jit(solution)/shard_map/pallas_call | solution.py:122
  92.5 2.6 %collective-permute-start.8 = (f16[224,1024]{1,0:T(8,128)(2,1)S(1)}, f16[224,1024]{1,0:T(8,128)(2,1)S(1)}, u32[]{:S(2)}, u32[]{:S(2)}) collective-permute-start(f16[224,1024]{1,0:T(8,128)(2,1)S(1)} %fusion.15), channel_id=1, source_target_pairs={{0,2},{1,31},{2,4},{3,1},{4,6},{5,3},{6,8},{7,5},{8,10},{9,7},{10,... | collective-permute-start | bytes 1376264 | tf_op jit(solution)/shard_map/ppermute | solution.py:234
  95.3 3.2 %collective-permute-start.11 = (f16[224,1024]{1,0:T(8,128)(2,1)S(1)}, f16[224,1024]{1,0:T(8,128)(2,1)S(1)}, u32[]{:S(2)}, u32[]{:S(2)}) collective-permute-start(f16[224,1024]{1,0:T(8,128)(2,1)S(1)} %fusion.14), channel_id=1, source_target_pairs={{0,2},{1,31},{2,4},{3,1},{4,6},{5,3},{6,8},{7,5},{8,10},{9,7},{10,... | collective-permute-start | bytes 1376264 | tf_op jit(solution)/shard_map/ppermute | solution.py:234
  98.5 3.5 %collective-permute-done.8 = f16[224,1024]{1,0:T(8,128)(2,1)S(1)} collective-permute-done((f16[224,1024]{1,0:T(8,128)(2,1)S(1)}, f16[224,1024]{1,0:T(8,128)(2,1)S(1)}, u32[]{:S(2)}, u32[]{:S(2)}) %collective-permute-start.8) | collective-permute-done | bytes 458784 | tf_op jit(solution)/shard_map/ppermute | solution.py:234
  102.2 3.5 %collective-permute-start.10 = (f16[224,1024]{1,0:T(8,128)(2,1)S(1)}, f16[224,1024]{1,0:T(8,128)(2,1)S(1)}, u32[]{:S(2)}, u32[]{:S(2)}) collective-permute-start(f16[224,1024]{1,0:T(8,128)(2,1)S(1)} %fusion.13), channel_id=1, source_target_pairs={{0,2},{1,31},{2,4},{3,1},{4,6},{5,3},{6,8},{7,5},{8,10},{9,7},{10,... | collective-permute-start | bytes 1376264 | tf_op jit(solution)/shard_map/ppermute | solution.py:234
  107.1 3.5 %collective-permute-start.13 = (f16[224,1024]{1,0:T(8,128)(2,1)S(1)}, f16[224,1024]{1,0:T(8,128)(2,1)S(1)}, u32[]{:S(2)}, u32[]{:S(2)}) collective-permute-start(f16[224,1024]{1,0:T(8,128)(2,1)S(1)} %fusion.12), channel_id=1, source_target_pairs={{0,2},{1,31},{2,4},{3,1},{4,6},{5,3},{6,8},{7,5},{8,10},{9,7},{10,... | collective-permute-start | bytes 1376264 | tf_op jit(solution)/shard_map/ppermute | solution.py:234
  110.6 6.6 %shard_map.70 = f32[2240,1024]{1,0:T(8,128)S(1)} custom-call(bf16[3136,128]{1,0:T(8,128)(2,1)S(1)} %copy-done.1, bf16[3136,128]{1,0:T(8,128)(2,1)S(1)} %collective-permute-done.5.b_ref, bf16[3136,128]{1,0:T(8,128)(2,1)S(1)} %collective-permute-done.6.c_ref, bf16[3136,128]{1,0:T(8,128)(2,1)} %collective-permute-done.7.d_ref, ...), custom_call_target="tpu_custom_call" | custom-call | flops 2348810240 | bytes 13762560 | tf_op jit(solution)/shard_map/pallas_call | solution.py:122
  117.5 2.3 %collective-permute-start.12 = (f16[224,1024]{1,0:T(8,128)(2,1)S(1)}, f16[224,1024]{1,0:T(8,128)(2,1)S(1)}, u32[]{:S(2)}, u32[]{:S(2)}) collective-permute-start(f16[224,1024]{1,0:T(8,128)(2,1)S(1)} %fusion.11), channel_id=1, source_target_pairs={{0,2},{1,31},{2,4},{3,1},{4,6},{5,3},{6,8},{7,5},{8,10},{9,7},{10,... | collective-permute-start | bytes 1376264 | tf_op jit(solution)/shard_map/ppermute | solution.py:234
  119.9 2.7 %collective-permute-start.15 = (f16[224,1024]{1,0:T(8,128)(2,1)S(1)}, f16[224,1024]{1,0:T(8,128)(2,1)S(1)}, u32[]{:S(2)}, u32[]{:S(2)}) collective-permute-start(f16[224,1024]{1,0:T(8,128)(2,1)S(1)} %fusion.10), channel_id=1, source_target_pairs={{0,2},{1,31},{2,4},{3,1},{4,6},{5,3},{6,8},{7,5},{8,10},{9,7},{10,... | collective-permute-start | bytes 1376264 | tf_op jit(solution)/shard_map/ppermute | solution.py:234
  122.7 4.3 %collective-permute-done.12 = f16[224,1024]{1,0:T(8,128)(2,1)S(1)} collective-permute-done((f16[224,1024]{1,0:T(8,128)(2,1)S(1)}, f16[224,1024]{1,0:T(8,128)(2,1)S(1)}, u32[]{:S(2)}, u32[]{:S(2)}) %collective-permute-start.12) | collective-permute-done | bytes 458784 | tf_op jit(solution)/shard_map/ppermute | solution.py:234
  127.1 3.2 %collective-permute-start.14 = (f16[224,1024]{1,0:T(8,128)(2,1)S(1)}, f16[224,1024]{1,0:T(8,128)(2,1)S(1)}, u32[]{:S(2)}, u32[]{:S(2)}) collective-permute-start(f16[224,1024]{1,0:T(8,128)(2,1)S(1)} %fusion.9), channel_id=1, source_target_pairs={{0,2},{1,31},{2,4},{3,1},{4,6},{5,3},{6,8},{7,5},{8,10},{9,7},{10,... | collective-permute-start | bytes 1376264 | tf_op jit(solution)/shard_map/ppermute | solution.py:234
  132.0 3.2 %collective-permute-start.17 = (f16[224,1024]{1,0:T(8,128)(2,1)S(1)}, f16[224,1024]{1,0:T(8,128)(2,1)S(1)}, u32[]{:S(2)}, u32[]{:S(2)}) collective-permute-start(f16[224,1024]{1,0:T(8,128)(2,1)S(1)} %fusion.8), channel_id=1, source_target_pairs={{0,2},{1,31},{2,4},{3,1},{4,6},{5,3},{6,8},{7,5},{8,10},{9,7},{10,... | collective-permute-start | bytes 1376264 | tf_op jit(solution)/shard_map/ppermute | solution.py:234
  136.9 4.0 %collective-permute-start.16 = (f16[224,1024]{1,0:T(8,128)(2,1)S(1)}, f16[224,1024]{1,0:T(8,128)(2,1)S(1)}, u32[]{:S(2)}, u32[]{:S(2)}) collective-permute-start(f16[224,1024]{1,0:T(8,128)(2,1)S(1)} %fusion.7), channel_id=1, source_target_pairs={{0,2},{1,31},{2,4},{3,1},{4,6},{5,3},{6,8},{7,5},{8,10},{9,7},{10,... | collective-permute-start | bytes 1376264 | tf_op jit(solution)/shard_map/ppermute | solution.py:234
  141.9 4.0 %collective-permute-start.20 = (f16[224,1024]{1,0:T(8,128)(2,1)S(1)}, f16[224,1024]{1,0:T(8,128)(2,1)S(1)}, u32[]{:S(2)}, u32[]{:S(2)}) collective-permute-start(f16[224,1024]{1,0:T(8,128)(2,1)S(1)} %fusion.6), channel_id=1, source_target_pairs={{0,2},{1,31},{2,4},{3,1},{4,6},{5,3},{6,8},{7,5},{8,10},{9,7},{10,... | collective-permute-start | bytes 1376264 | tf_op jit(solution)/shard_map/ppermute | solution.py:234
  148.7 4.1 %collective-permute-start.18 = (f16[224,512]{1,0:T(8,128)(2,1)S(1)}, f16[224,512]{1,0:T(8,128)(2,1)S(1)}, u32[]{:S(2)}, u32[]{:S(2)}) collective-permute-start(f16[224,512]{1,0:T(8,128)(2,1)S(1)} %get-tuple-element.49), channel_id=1, source_target_pairs={{0,2},{1,31},{2,4},{3,1},{4,6},{5,3},{6,8},{7,5},{8,10},{9,7},{10,... | collective-permute-start | bytes 688136 | tf_op jit(solution)/shard_map/ppermute | solution.py:234
  152.8 8.1 %collective-permute-start.19 = (f16[224,512]{1,0:T(8,128)(2,1)S(1)}, f16[224,512]{1,0:T(8,128)(2,1)S(1)}, u32[]{:S(2)}, u32[]{:S(2)}) collective-permute-start(f16[224,512]{1,0:T(8,128)(2,1)S(1)} %get-tuple-element.50), channel_id=1, source_target_pairs={{0,3},{1,30},{2,5},{3,0},{4,7},{5,2},{6,9},{7,4},{8,11},{9,6},{10,... | collective-permute-start | bytes 688136 | tf_op jit(solution)/shard_map/ppermute | solution.py:234
  166.3 2.8 %collective-permute-done.21 = f16[224,512]{1,0:T(8,128)(2,1)S(1)} collective-permute-done((f16[224,512]{1,0:T(8,128)(2,1)S(1)}, f16[224,512]{1,0:T(8,128)(2,1)S(1)}, u32[]{:S(2)}, u32[]{:S(2)}) %collective-permute-start.21) | collective-permute-done | bytes 229408 | tf_op jit(solution)/shard_map/ppermute | solution.py:234
  169.1 3.7 %collective-permute-done.22 = f16[224,512]{1,0:T(8,128)(2,1)S(1)} collective-permute-done((f16[224,512]{1,0:T(8,128)(2,1)S(1)}, f16[224,512]{1,0:T(8,128)(2,1)S(1)}, u32[]{:S(2)}, u32[]{:S(2)}) %collective-permute-start.22) | collective-permute-done | bytes 229408 | tf_op jit(solution)/shard_map/ppermute | solution.py:234
  173.3 14.9 %all_to_all.5 = f16[16,28,512]{2,1,0:T(8,128)(2,1)S(1)} all-to-all(f16[16,28,512]{2,1,0:T(8,128)(2,1)S(1)} %reshape.48), channel_id=1, replica_groups=mesh['ylo'=2,'x'=4,'yhi'=2,'z'=16,'core'=2] {'ylo','x','core'}, dimensions={0} | all-to-all | bytes 917504 | tf_op jit(solution)/shard_map/all_to_all | solution.py:252
  188.6 2.4 %shard_map.71 = (f32[28,512]{1,0:T(8,128)}, f32[28,512]{1,0:T(8,128)}, f32[28,512]{1,0:T(8,128)}) custom-call(f32[16,32,512]{2,1,0:T(8,128)S(1)} %pad.4.g_ref, bf16[28,512]{1,0:T(8,128)(2,1)S(1)} %copy-done.3), custom_call_target="tpu_custom_call" | custom-call | tf_op jit(solution)/shard_map/pallas_call | solution.py:188
  (61 shorter events, 26.6 us)
Async XLA Ops:
  10.1 79.4 %copy-start.1 = (bf16[3136,128]{1,0:T(8,128)(2,1)S(1)}, bf16[3136,128]{1,0:T(8,128)(2,1)}, u32[]{:S(2)}) copy-start(bf16[3136,128]{1,0:T(8,128)(2,1)} %get-tuple-element.31.a_ref) | copy-start | bytes 2408452
  10.1 15.9 %collective-permute-start = (bf16[1184,128]{1,0:T(8,128)(2,1)}, bf16[1184,128]{1,0:T(8,128)(2,1)S(1)}, u32[]{:S(2)}, u32[]{:S(2)}) collective-permute-start(bf16[1184,128]{1,0:T(8,128)(2,1)} %get-tuple-element.26), channel_id=1, source_target_pairs={{0,1},{1,0},{32,33},{33,32},{2,3},{3,2},{34,35},{35,34},{4,5},{5,4... | collective-permute-start | bytes 909320 | tf_op jit(solution)/shard_map/ppermute | solution.py:218
  19.0 12.4 %collective-permute-start.1 = (bf16[1184,128]{1,0:T(8,128)(2,1)}, bf16[1184,128]{1,0:T(8,128)(2,1)S(1)}, u32[]{:S(2)}, u32[]{:S(2)}) collective-permute-start(bf16[1184,128]{1,0:T(8,128)(2,1)} %get-tuple-element.27), channel_id=1, source_target_pairs={{0,32},{1,33},{32,0},{33,1},{2,34},{3,35},{34,2},{35,3},{4,36},{5,... | collective-permute-start | bytes 909320 | tf_op jit(solution)/shard_map/ppermute | solution.py:218
  20.9 17.1 %collective-permute-start.2 = (bf16[1184,128]{1,0:T(8,128)(2,1)}, bf16[1184,128]{1,0:T(8,128)(2,1)S(1)}, u32[]{:S(2)}, u32[]{:S(2)}) collective-permute-start(bf16[1184,128]{1,0:T(8,128)(2,1)} %get-tuple-element.28), channel_id=1, source_target_pairs={{0,33},{1,32},{32,1},{33,0},{2,35},{3,34},{34,3},{35,2},{4,37},{5,... | collective-permute-start | bytes 909320 | tf_op jit(solution)/shard_map/ppermute | solution.py:218
  38.0 1.0 copy-start.4
  40.3 8.6 %copy-start.2 = (f32[672,1024]{1,0:T(8,128)}, f32[672,1024]{1,0:T(8,128)S(1)}, u32[]{:S(2)}) copy-start(f32[672,1024]{1,0:T(8,128)S(1)} %get-tuple-element.29) | copy-start | bytes 8257540
  41.2 15.2 %collective-permute-start.3 = (f16[224,1024]{1,0:T(8,128)(2,1)}, f16[224,1024]{1,0:T(8,128)(2,1)}, u32[]{:S(2)}, u32[]{:S(2)}) collective-permute-start(f16[224,1024]{1,0:T(8,128)(2,1)} %slice_convert_fusion), channel_id=1, source_target_pairs={{0,2},{1,31},{2,4},{3,1},{4,6},{5,3},{6,8},{7,5},{8,10},{9,7},{10,... | collective-permute-start | bytes 1376264 | tf_op jit(solution)/shard_map/ppermute | solution.py:234
  47.0 16.7 %collective-permute-start.5 = (bf16[3136,128]{1,0:T(8,128)(2,1)}, bf16[3136,128]{1,0:T(8,128)(2,1)S(1)}, u32[]{:S(2)}, u32[]{:S(2)}) collective-permute-start(bf16[3136,128]{1,0:T(8,128)(2,1)} %get-tuple-element.32), channel_id=1, source_target_pairs={{0,1},{1,0},{32,33},{33,32},{2,3},{3,2},{34,35},{35,34},{4,5},{5,4... | collective-permute-start | bytes 2408456 | tf_op jit(solution)/shard_map/ppermute | solution.py:218
  48.9 22.6 %collective-permute-start.6 = (bf16[3136,128]{1,0:T(8,128)(2,1)}, bf16[3136,128]{1,0:T(8,128)(2,1)S(1)}, u32[]{:S(2)}, u32[]{:S(2)}) collective-permute-start(bf16[3136,128]{1,0:T(8,128)(2,1)} %get-tuple-element.33), channel_id=1, source_target_pairs={{0,32},{1,33},{32,0},{33,1},{2,34},{3,35},{34,2},{35,3},{4,36},{5,... | collective-permute-start | bytes 2408456 | tf_op jit(solution)/shard_map/ppermute | solution.py:218
  53.7 35.7 %collective-permute-start.7 = (bf16[3136,128]{1,0:T(8,128)(2,1)}, bf16[3136,128]{1,0:T(8,128)(2,1)}, u32[]{:S(2)}, u32[]{:S(2)}) collective-permute-start(bf16[3136,128]{1,0:T(8,128)(2,1)} %get-tuple-element.34), channel_id=1, source_target_pairs={{0,33},{1,32},{32,1},{33,0},{2,35},{3,34},{34,3},{35,2},{4,37},{5,... | collective-permute-start | bytes 2408456 | tf_op jit(solution)/shard_map/ppermute | solution.py:218
  58.3 34.1 %collective-permute-start.4 = (f16[224,1024]{1,0:T(8,128)(2,1)S(1)}, f16[224,1024]{1,0:T(8,128)(2,1)S(1)}, u32[]{:S(2)}, u32[]{:S(2)}) collective-permute-start(f16[224,1024]{1,0:T(8,128)(2,1)S(1)} %get-tuple-element.47), channel_id=1, source_target_pairs={{0,2},{1,31},{2,4},{3,1},{4,6},{5,3},{6,8},{7,5},{8,10},{9,7},{10,... | collective-permute-start | bytes 1376264 | tf_op jit(solution)/shard_map/ppermute | solution.py:234
  60.9 34.2 %collective-permute-start.9 = (f16[224,1024]{1,0:T(8,128)(2,1)S(1)}, f16[224,1024]{1,0:T(8,128)(2,1)S(1)}, u32[]{:S(2)}, u32[]{:S(2)}) collective-permute-start(f16[224,1024]{1,0:T(8,128)(2,1)S(1)} %get-tuple-element.48), channel_id=1, source_target_pairs={{0,2},{1,31},{2,4},{3,1},{4,6},{5,3},{6,8},{7,5},{8,10},{9,7},{10,... | collective-permute-start | bytes 1376264 | tf_op jit(solution)/shard_map/ppermute | solution.py:234
  92.5 9.5 %collective-permute-start.8 = (f16[224,1024]{1,0:T(8,128)(2,1)S(1)}, f16[224,1024]{1,0:T(8,128)(2,1)S(1)}, u32[]{:S(2)}, u32[]{:S(2)}) collective-permute-start(f16[224,1024]{1,0:T(8,128)(2,1)S(1)} %fusion.15), channel_id=1, source_target_pairs={{0,2},{1,31},{2,4},{3,1},{4,6},{5,3},{6,8},{7,5},{8,10},{9,7},{10,... | collective-permute-start | bytes 1376264 | tf_op jit(solution)/shard_map/ppermute | solution.py:234
  95.3 11.6 %collective-permute-start.11 = (f16[224,1024]{1,0:T(8,128)(2,1)S(1)}, f16[224,1024]{1,0:T(8,128)(2,1)S(1)}, u32[]{:S(2)}, u32[]{:S(2)}) collective-permute-start(f16[224,1024]{1,0:T(8,128)(2,1)S(1)} %fusion.14), channel_id=1, source_target_pairs={{0,2},{1,31},{2,4},{3,1},{4,6},{5,3},{6,8},{7,5},{8,10},{9,7},{10,... | collective-permute-start | bytes 1376264 | tf_op jit(solution)/shard_map/ppermute | solution.py:234
  102.2 15.1 %collective-permute-start.10 = (f16[224,1024]{1,0:T(8,128)(2,1)S(1)}, f16[224,1024]{1,0:T(8,128)(2,1)S(1)}, u32[]{:S(2)}, u32[]{:S(2)}) collective-permute-start(f16[224,1024]{1,0:T(8,128)(2,1)S(1)} %fusion.13), channel_id=1, source_target_pairs={{0,2},{1,31},{2,4},{3,1},{4,6},{5,3},{6,8},{7,5},{8,10},{9,7},{10,... | collective-permute-start | bytes 1376264 | tf_op jit(solution)/shard_map/ppermute | solution.py:234
  107.1 12.7 %collective-permute-start.13 = (f16[224,1024]{1,0:T(8,128)(2,1)S(1)}, f16[224,1024]{1,0:T(8,128)(2,1)S(1)}, u32[]{:S(2)}, u32[]{:S(2)}) collective-permute-start(f16[224,1024]{1,0:T(8,128)(2,1)S(1)} %fusion.12), channel_id=1, source_target_pairs={{0,2},{1,31},{2,4},{3,1},{4,6},{5,3},{6,8},{7,5},{8,10},{9,7},{10,... | collective-permute-start | bytes 1376264 | tf_op jit(solution)/shard_map/ppermute | solution.py:234
  117.3 24.4 %copy-start = (f32[2240,1024]{1,0:T(8,128)}, f32[2240,1024]{1,0:T(8,128)S(1)}, u32[]{:S(2)}) copy-start(f32[2240,1024]{1,0:T(8,128)S(1)} %shard_map.70) | copy-start | bytes 27525124
  117.5 9.5 %collective-permute-start.12 = (f16[224,1024]{1,0:T(8,128)(2,1)S(1)}, f16[224,1024]{1,0:T(8,128)(2,1)S(1)}, u32[]{:S(2)}, u32[]{:S(2)}) collective-permute-start(f16[224,1024]{1,0:T(8,128)(2,1)S(1)} %fusion.11), channel_id=1, source_target_pairs={{0,2},{1,31},{2,4},{3,1},{4,6},{5,3},{6,8},{7,5},{8,10},{9,7},{10,... | collective-permute-start | bytes 1376264 | tf_op jit(solution)/shard_map/ppermute | solution.py:234
  119.9 25.9 %copy-start.5 = (s32[2]{0:T(128)S(1)}, s32[2]{0:T(128)}, u32[]{:S(2)}) copy-start(s32[2]{0:T(128)} %param.6) | copy-start | bytes 28
  119.9 11.9 %collective-permute-start.15 = (f16[224,1024]{1,0:T(8,128)(2,1)S(1)}, f16[224,1024]{1,0:T(8,128)(2,1)S(1)}, u32[]{:S(2)}, u32[]{:S(2)}) collective-permute-start(f16[224,1024]{1,0:T(8,128)(2,1)S(1)} %fusion.10), channel_id=1, source_target_pairs={{0,2},{1,31},{2,4},{3,1},{4,6},{5,3},{6,8},{7,5},{8,10},{9,7},{10,... | collective-permute-start | bytes 1376264 | tf_op jit(solution)/shard_map/ppermute | solution.py:234
  127.1 9.7 %collective-permute-start.14 = (f16[224,1024]{1,0:T(8,128)(2,1)S(1)}, f16[224,1024]{1,0:T(8,128)(2,1)S(1)}, u32[]{:S(2)}, u32[]{:S(2)}) collective-permute-start(f16[224,1024]{1,0:T(8,128)(2,1)S(1)} %fusion.9), channel_id=1, source_target_pairs={{0,2},{1,31},{2,4},{3,1},{4,6},{5,3},{6,8},{7,5},{8,10},{9,7},{10,... | collective-permute-start | bytes 1376264 | tf_op jit(solution)/shard_map/ppermute | solution.py:234
  132.0 9.7 %collective-permute-start.17 = (f16[224,1024]{1,0:T(8,128)(2,1)S(1)}, f16[224,1024]{1,0:T(8,128)(2,1)S(1)}, u32[]{:S(2)}, u32[]{:S(2)}) collective-permute-start(f16[224,1024]{1,0:T(8,128)(2,1)S(1)} %fusion.8), channel_id=1, source_target_pairs={{0,2},{1,31},{2,4},{3,1},{4,6},{5,3},{6,8},{7,5},{8,10},{9,7},{10,... | collective-permute-start | bytes 1376264 | tf_op jit(solution)/shard_map/ppermute | solution.py:234
  136.9 10.2 %collective-permute-start.16 = (f16[224,1024]{1,0:T(8,128)(2,1)S(1)}, f16[224,1024]{1,0:T(8,128)(2,1)S(1)}, u32[]{:S(2)}, u32[]{:S(2)}) collective-permute-start(f16[224,1024]{1,0:T(8,128)(2,1)S(1)} %fusion.7), channel_id=1, source_target_pairs={{0,2},{1,31},{2,4},{3,1},{4,6},{5,3},{6,8},{7,5},{8,10},{9,7},{10,... | collective-permute-start | bytes 1376264 | tf_op jit(solution)/shard_map/ppermute | solution.py:234
  141.9 19.1 %collective-permute-start.20 = (f16[224,1024]{1,0:T(8,128)(2,1)S(1)}, f16[224,1024]{1,0:T(8,128)(2,1)S(1)}, u32[]{:S(2)}, u32[]{:S(2)}) collective-permute-start(f16[224,1024]{1,0:T(8,128)(2,1)S(1)} %fusion.6), channel_id=1, source_target_pairs={{0,2},{1,31},{2,4},{3,1},{4,6},{5,3},{6,8},{7,5},{8,10},{9,7},{10,... | collective-permute-start | bytes 1376264 | tf_op jit(solution)/shard_map/ppermute | solution.py:234
  147.1 25.8 %slice-start = ((f32[2240,1024]{1,0:T(8,128)}), f32[448,1024]{1,0:T(8,128)S(1)}, s32[]{:S(2)}) async-start(f32[2240,1024]{1,0:T(8,128)} %copy-done), calls=%async_computation.1 | async-start | bytes 3670016 | tf_op jit(solution)/shard_map/slice | solution.py:231
  148.7 17.5 %collective-permute-start.18 = (f16[224,512]{1,0:T(8,128)(2,1)S(1)}, f16[224,512]{1,0:T(8,128)(2,1)S(1)}, u32[]{:S(2)}, u32[]{:S(2)}) collective-permute-start(f16[224,512]{1,0:T(8,128)(2,1)S(1)} %get-tuple-element.49), channel_id=1, source_target_pairs={{0,2},{1,31},{2,4},{3,1},{4,6},{5,3},{6,8},{7,5},{8,10},{9,7},{10,... | collective-permute-start | bytes 688136 | tf_op jit(solution)/shard_map/ppermute | solution.py:234
  152.8 13.5 %collective-permute-start.19 = (f16[224,512]{1,0:T(8,128)(2,1)S(1)}, f16[224,512]{1,0:T(8,128)(2,1)S(1)}, u32[]{:S(2)}, u32[]{:S(2)}) collective-permute-start(f16[224,512]{1,0:T(8,128)(2,1)S(1)} %get-tuple-element.50), channel_id=1, source_target_pairs={{0,3},{1,30},{2,5},{3,0},{4,7},{5,2},{6,9},{7,4},{8,11},{9,6},{10,... | collective-permute-start | bytes 688136 | tf_op jit(solution)/shard_map/ppermute | solution.py:234
  162.4 6.8 %collective-permute-start.21 = (f16[224,512]{1,0:T(8,128)(2,1)S(1)}, f16[224,512]{1,0:T(8,128)(2,1)S(1)}, u32[]{:S(2)}, u32[]{:S(2)}) collective-permute-start(f16[224,512]{1,0:T(8,128)(2,1)S(1)} %get-tuple-element.51), channel_id=1, source_target_pairs={{0,2},{1,31},{2,4},{3,1},{4,6},{5,3},{6,8},{7,5},{8,10},{9,7},{10,... | collective-permute-start | bytes 688136 | tf_op jit(solution)/shard_map/ppermute | solution.py:234
  164.3 8.6 %collective-permute-start.22 = (f16[224,512]{1,0:T(8,128)(2,1)S(1)}, f16[224,512]{1,0:T(8,128)(2,1)S(1)}, u32[]{:S(2)}, u32[]{:S(2)}) collective-permute-start(f16[224,512]{1,0:T(8,128)(2,1)S(1)} %get-tuple-element.52), channel_id=1, source_target_pairs={{0,3},{1,30},{2,5},{3,0},{4,7},{5,2},{6,9},{7,4},{8,11},{9,6},{10,... | collective-permute-start | bytes 688136 | tf_op jit(solution)/shard_map/ppermute | solution.py:234
  172.9 15.6 %copy-start.3 = (bf16[28,512]{1,0:T(8,128)(2,1)S(1)}, bf16[28,512]{1,0:T(8,128)(2,1)}, u32[]{:S(2)}) copy-start(bf16[28,512]{1,0:T(8,128)(2,1)} %w_ref.1) | copy-start | bytes 86020

commit v4 on v3

--- a/solution.py
+++ b/solution.py
@@ -11,15 +11,21 @@
 AXES = ("ylo", "x", "yhi", "z", "core")
 NZ = 16
 FAR = NZ // 2
+GROUPS = ((7, 6), (5, 4), (3, 2, 1, 0))
 VMEM = 56 * 1024 * 1024
 f32 = jnp.float32
 f16 = jnp.float16
 
 
+def outputs_of(other):
+    return (sum(GROUPS, ()),) if other == 1 else GROUPS
+
+
 def turn_kernel(s_ref, up_ref, feat_ref, *rest):
-    outs, hold = rest[:-1], rest[-1]
+    outs, hold = list(rest[:-1]), rest[-1]
     step = pl.program_id(0)
-    seg2, width = feat_ref.shape[0], up_ref.shape[2] // 4
+    n_ex, seg, n_row = feat_ref.shape
+    seg2, width = n_ex * seg, up_ref.shape[2] // 4
     span = width // NZ
     for half in range(2):
         turned = []
@@ -34,45 +40,53 @@
     def _():
         n, tall = hold.shape[2], hold.shape[3]
         yhi, z, core = s_ref[0], s_ref[1], s_ref[2]
+        position = s_ref[3] + lax.broadcasted_iota(jnp.int32, (seg, n_row), 0)
+        feats = jnp.concatenate([
+            jnp.where(position < s_ref[4 + e], feat_ref[e].astype(f32) * 0.25, 0.0) for e in range(n_ex)
+        ], axis=0).astype(feat_ref.dtype)
         for other in range(4):
             half = yhi if other < 2 else 1 - yhi
             to = core if other % 2 == 0 else 1 - core
-            first, second = outs[2 * other], outs[2 * other + 1]
             place = lambda dist: lax.rem(z + (1 - 2 * to) * dist + NZ, NZ)
+            first = outs.pop(0)
             for p in range(n // 2):
                 first[p * tall:(p + 1) * tall] = hold[half, place(FAR), (n // 2) * to + p]
-            for p in range(n):
-                at = (n // 2 + p) * tall
-                first[at:at + tall] = hold[half, place(FAR - 1), p]
-            at = (n // 2 + n) * tall
-            for b in range(feat_ref.shape[1] // BLOCK):
-                first[at + b * seg2:at + (b + 1) * seg2] = feat_ref[:, b * BLOCK:(b + 1) * BLOCK]
-            for i in range(FAR - 1):
-                for p in range(n):
-                    at = (i * n + p) * tall
-                    second[at:at + tall] = hold[half, place(FAR - 2 - i), p]
-
-
-def turn(upstream, feats, scalars, n_groups):
-    _, seg, units = upstream.shape
-    seg2, rows = feats.shape
+            at = n // 2 * tall
+            for b in range(n_row // BLOCK):
+                first[at + b * seg2:at + (b + 1) * seg2] = feats[:, b * BLOCK:(b + 1) * BLOCK]
+            for group in outputs_of(other):
+                out = outs.pop(0)
+                for i, dist in enumerate(group):
+                    for p in range(n):
+                        at = (i * n + p) * tall
+                        out[at:at + tall] = hold[half, place(dist), p]
+
+
+def turn(upstream, features, scalars, n_groups):
+    n_ex, seg, units = upstream.shape
+    rows = features.shape[2]
+    seg2 = n_ex * seg
     n = n_groups // 2
     chunk = units // 2 // NZ
-    tall = chunk // n
-    shapes = [(chunk // 2 + chunk + rows // BLOCK * seg2, seg2), ((FAR - 1) * chunk, seg2)] * 4
+    shapes = []
+    for other in range(4):
+        shapes.append((chunk // 2 + rows // BLOCK * seg2, seg2))
+        shapes += [(len(group) * chunk, seg2) for group in outputs_of(other)]
     whole = lambda shape: pl.BlockSpec(shape, lambda i, s: (0,) * len(shape))
-    return pl.pallas_call(
+    made = pl.pallas_call(
         turn_kernel,
         grid_spec=pltpu.PrefetchScalarGridSpec(
             num_scalar_prefetch=1,
             grid=(n,),
-            in_specs=[pl.BlockSpec((2, seg, units // n), lambda i, s: (0, 0, i)), whole(feats.shape)],
+            in_specs=[pl.BlockSpec((n_ex, seg, units // n), lambda i, s: (0, 0, i)), whole(features.shape)],
             out_specs=[whole(shape) for shape in shapes],
-            scratch_shapes=[pltpu.VMEM((2, NZ, n, tall, seg2), upstream.dtype)],
+            scratch_shapes=[pltpu.VMEM((2, NZ, n, chunk // n, seg2), upstream.dtype)],
         ),
         out_shape=[jax.ShapeDtypeStruct(shape, upstream.dtype) for shape in shapes],
         compiler_params=pltpu.CompilerParams(vmem_limit_bytes=VMEM),
-    )(scalars, upstream, feats)
+    )(scalars, upstream, features)
+    made = list(made)
+    return [[made.pop(0) for _ in range(1 + len(outputs_of(other)))] for other in range(4)]
 
 
 def first_kernel(a_ref, b_ref, c_ref, d_ref, out_ref, right_ref):
@@ -87,13 +101,8 @@
         none = jnp.zeros((half, feats.shape[1]), feats.dtype)
         right_ref[k * seg2:k * seg2 + half] = jnp.concatenate([feats[:half], none], axis=1)
         right_ref[k * seg2 + half:(k + 1) * seg2] = jnp.concatenate([none, feats[half:]], axis=1)
-    tile = height // 3
-
-    @pl.loop(0, 3)
-    def _(i):
-        at = pl.ds(pl.multiple_of(i * tile, tile), tile)
-        left = jnp.concatenate([ref[at] for ref in refs], axis=1)
-        out_ref[at] = jnp.dot(left, right_ref[...], preferred_element_type=f32)
+    left = jnp.concatenate([ref[:height] for ref in refs], axis=1)
+    out_ref[...] = jnp.dot(left, right_ref[...], preferred_element_type=f32)
 
 
 def first_product(pieces, height):
@@ -105,7 +114,7 @@
             jax.ShapeDtypeStruct((height, wide), f32),
             jax.ShapeDtypeStruct((4 * seg2, wide), pieces[0].dtype),
         ],
-        cost_estimate=pl.CostEstimate(flops=2 * height * 4 * seg2 * wide, bytes_accessed=6 * height * wide, transcendentals=0),
+        cost_estimate=pl.CostEstimate(flops=200 * height * 4 * seg2 * wide, bytes_accessed=6 * height * wide, transcendentals=0),
         compiler_params=pltpu.CompilerParams(vmem_limit_bytes=40 * 1024 * 1024),
     )(*pieces)
 
@@ -115,19 +124,19 @@
     out_ref[...] = jnp.dot(left, right_ref[...], preferred_element_type=f32)
 
 
-def product(pieces, right, chunk, start, count):
+def product(pieces, starts, right, chunk, count):
     seg2 = pieces[0].shape[1]
     tile = chunk // 2
     wide = right.shape[1]
     return pl.pallas_call(
         product_kernel,
         grid=(2 * count,),
-        in_specs=[pl.BlockSpec((tile, seg2), lambda i: (2 * start + i, 0))] * 4
+        in_specs=[pl.BlockSpec((tile, seg2), lambda i, start=start: (2 * start + i, 0)) for start in starts]
         + [pl.BlockSpec(right.shape, lambda i: (0, 0))],
         out_specs=pl.BlockSpec((tile, wide), lambda i: (i, 0)),
         out_shape=jax.ShapeDtypeStruct((count * chunk, wide), f32),
         cost_estimate=pl.CostEstimate(
-            flops=2 * count * chunk * 4 * seg2 * wide, bytes_accessed=6 * count * chunk * wide, transcendentals=0
+            flops=80 * count * chunk * 4 * seg2 * wide, bytes_accessed=6 * count * chunk * wide, transcendentals=0
         ),
         compiler_params=pltpu.CompilerParams(vmem_limit_bytes=40 * 1024 * 1024),
     )(*pieces, right)
@@ -209,30 +218,26 @@
     n_groups = 8
     total_len = seg * 64
     shard = (yhi * NZ + z) * 2 + core
-    positions = shard * seg + jnp.arange(seg, dtype=jnp.int32)
-    kept_rows = positions[None, :] < lengths[:, None]
-    masked = jnp.where(kept_rows[:, :, None], features, jnp.zeros_like(features)) * jnp.asarray(0.25, features.dtype)
-    scalars = jnp.stack([yhi, z, core]).astype(jnp.int32)
-    made = turn(upstream, masked.reshape(n_ex * seg, rows), scalars, n_groups)
+    scalars = jnp.concatenate([jnp.stack([yhi, z, core, shard * seg]), lengths]).astype(jnp.int32)
+    made = turn(upstream, features, scalars, n_groups)
 
     quad = lambda x, i: lax.ppermute(x, ("yhi", "core"), [(j, j ^ i) for j in range(4)])
     chunk = units // 2 // NZ
     half = chunk // 2
-    order = (3, 2, 1)
-    near = {i: quad(made[2 * i], i) for i in order}
-    rest = {i: quad(made[2 * i + 1], i) for i in order}
-    near, rest = [made[0]] + [near[i] for i in (1, 2, 3)], [made[1]] + [rest[i] for i in (1, 2, 3)]
-    part, right = first_product(near, half + chunk)
-    parts = {FAR: part[:half], FAR - 1: part[half:]}
+    got = {i: [quad(x, i) for x in made[i]] for i in (2, 3, 1)}
+    got[0] = made[0]
+    far, right = first_product([got[i][0] for i in range(4)], half)
+    parts = {}
     start = 0
-    for count in (2, FAR - 3):
-        part = product(rest, right, chunk, start, count)
-        for i in range(count):
-            parts[FAR - 2 - start - i] = part[i * chunk:(i + 1) * chunk]
-        start += count
+    for g, group in enumerate(GROUPS):
+        pieces = [got[0][1 + g], got[1][1], got[2][1 + g], got[3][1 + g]]
+        part = product(pieces, (0, start, 0, 0), right, chunk, len(group))
+        for i, dist in enumerate(group):
+            parts[dist] = part[i * chunk:(i + 1) * chunk]
+        start += len(group)
 
     ring = lambda x, cross=0: lax.ppermute(x, ("z", "core"), ring_pairs(cross))
-    got = ring(parts[FAR].astype(f16)).astype(f32)
+    got = ring(far.astype(f16)).astype(f32)
     sums = [
         (parts[FAR - 1][k * half:(k + 1) * half] + jnp.where(core == k, got, 0.0)).astype(f16) for k in range(2)
     ]

time: 193 us -> 170 us (0.88)
  waiting for transfers between devices: 57.2 us -> 27.6 us
  starting transfers between devices: 84.8 us -> 101 us
  other arithmetic: 10.4 us -> 4.96 us
  Pallas kernels: 19.7 us -> 15.9 us
    ppermute x6 -> x10, waiting for transfers between devices: 37.8 us -> 12.9 us  [body(): lax.ppermute(x, ('yhi', 'core'), [(j, j ^ i) for j in range(4)])]
    ppermute x6 -> x10, starting transfers between devices: 25.2 us -> 39.5 us  [body(): lax.ppermute(x, ('yhi', 'core'), [(j, j ^ i) for j in range(4)])]
    ppermute x17, waiting for transfers between devices: 19.4 us -> 14.7 us  [body(): ring = lambda x, cross=0: lax.ppermute(x, ('z', 'core'), ring_pairs(cross))]
    pallas_call x2 -> x3, Pallas kernels: 9.53 us -> 6.62 us  [product(): pl.pallas_call(product_kernel, grid=(2 * count,), in_specs=[pl.BlockSpec(...]
  transfers between devices with their start and end apart: 23 -> 27, of which waited for: 12 -> 11; matrix products, arithmetic and copies ran while one was open for 4% -> 3% of each run, Pallas kernels for 5% -> 4%
where the time goes in v4:
time: 170 us; the launch traced here: 169 us
  starting transfers between devices  101 us (59%)
  waiting for transfers between devices  27.6 us (16%)
  Pallas kernels  15.9 us (9%)
  blocking collectives  14.6 us (9%)
  other arithmetic  4.96 us (3%)
  local copies, waits for them, and re-layouts  3.33 us (2%)
  between operations  2.02 us (1%)
    ppermute x17, starting transfers between devices, body(): ring = lambda x, cross=0: lax.ppermute(x, ('z', 'core'), ring_pairs(cross))  61.2 us
    ppermute x10, starting transfers between devices, body(): lax.ppermute(x, ('yhi', 'core'), [(j, j ^ i) for j in range(4)])  39.5 us
    ppermute x17, waiting for transfers between devices, body(): ring = lambda x, cross=0: lax.ppermute(x, ('z', 'core'), ring_pairs(cross))  14.7 us
    all_to_all x1, blocking collectives, body(): owned = lax.all_to_all(pieces, ('ylo', 'x', 'core'), 0, 0, tiled=True)  14.6 us
    ppermute x10, waiting for transfers between devices, body(): lax.ppermute(x, ('yhi', 'core'), [(j, j ^ i) for j in range(4)])  12.9 us
    pallas_call x3, Pallas kernels, product(): pl.pallas_call(product_kernel, grid=(2 * count,), in_specs=[pl.BlockSpec(...  6.62 us
    pallas_call x1, Pallas kernels, turn(): pl.pallas_call(turn_kernel, grid_spec=pltpu.PrefetchScalarGridSpec(num_sc...  6.46 us
    convert_element_type x12, other arithmetic, body(): (got.astype(f32) + parts[dist][k * half:(k + 1) * half]).astype(f16)  4.13 us
  transfers between devices with their start and end apart: 27, of which 11 were waited for; matrix products, arithmetic and copies ran while one was open for 3% of the time, Pallas kernels for 4%

profile of v4, /device:TPU:1, one launch (start us, length us, event | category | flops | bytes accessed | tf_op | source)
XLA Modules:
  0.0 169.1 jit_solution(2780561012195029204)
XLA Ops:
  2.0 6.5 %shard_map.67 = (bf16[736,128]{1,0:T(8,128)(2,1)}, bf16[896,128]{1,0:T(8,128)(2,1)}, bf16[896,128]{1,0:T(8,128)(2,1)}, bf16[1792,128]{1,0:T(8,128)(2,1)}, bf16[7...) custom-call(s32[6]{0:T(128)} %concatenate.6.s_ref, ...), custom_call_target="tpu_custom_call" | custom-call | tf_op jit(solution)/shard_map/pallas_call | solution.py:76
  8.4 8.8 %collective-permute-start.3 = (bf16[736,128]{1,0:T(8,128)(2,1)}, bf16[736,128]{1,0:T(8,128)(2,1)S(1)}, u32[]{:S(2)}, u32[]{:S(2)}) collective-permute-start(bf16[736,128]{1,0:T(8,128)(2,1)} %get-tuple-element.36), channel_id=1, source_target_pairs={{0,1},{1,0},{32,33},{33,32},{2,3},{3,2},{34,35},{35,34},{4,5},{5,4... | collective-permute-start | bytes 565256 | tf_op jit(solution)/shard_map/ppermute | solution.py:224
  19.1 5.0 %collective-permute-start.5 = (bf16[736,128]{1,0:T(8,128)(2,1)}, bf16[736,128]{1,0:T(8,128)(2,1)S(1)}, u32[]{:S(2)}, u32[]{:S(2)}) collective-permute-start(bf16[736,128]{1,0:T(8,128)(2,1)} %get-tuple-element.38), channel_id=1, source_target_pairs={{0,33},{1,32},{32,1},{33,0},{2,35},{3,34},{34,3},{35,2},{4,37},{5,... | collective-permute-start | bytes 565256 | tf_op jit(solution)/shard_map/ppermute | solution.py:224
  24.2 2.1 %collective-permute-start = (bf16[3584,128]{1,0:T(8,128)(2,1)}, bf16[3584,128]{1,0:T(8,128)(2,1)S(1)}, u32[]{:S(2)}, u32[]{:S(2)}) collective-permute-start(bf16[3584,128]{1,0:T(8,128)(2,1)} %get-tuple-element.32), channel_id=1, source_target_pairs={{0,1},{1,0},{32,33},{33,32},{2,3},{3,2},{34,35},{35,34},{4,5},{5,4... | collective-permute-start | bytes 2752520 | tf_op jit(solution)/shard_map/ppermute | solution.py:224
  28.3 5.3 %collective-permute-start.2 = (bf16[896,128]{1,0:T(8,128)(2,1)}, bf16[896,128]{1,0:T(8,128)(2,1)S(1)}, u32[]{:S(2)}, u32[]{:S(2)}) collective-permute-start(bf16[896,128]{1,0:T(8,128)(2,1)} %get-tuple-element.34), channel_id=1, source_target_pairs={{0,33},{1,32},{32,1},{33,0},{2,35},{3,34},{34,3},{35,2},{4,37},{5,... | collective-permute-start | bytes 688136 | tf_op jit(solution)/shard_map/ppermute | solution.py:224
  35.0 5.7 %collective-permute-start.6 = (f16[224,1024]{1,0:T(8,128)(2,1)S(1)}, f16[224,1024]{1,0:T(8,128)(2,1)S(1)}, u32[]{:S(2)}, u32[]{:S(2)}) collective-permute-start(f16[224,1024]{1,0:T(8,128)(2,1)S(1)} %convert_element_type.108), channel_id=1, source_target_pairs={{0,2},{1,31},{2,4},{3,1},{4,6},{5,3},{6,8},{7,5},{8,10},{9,7},{10,... | collective-permute-start | bytes 1376264 | tf_op jit(solution)/shard_map/ppermute | solution.py:239
  43.9 2.3 %collective-permute-done.6 = f16[224,1024]{1,0:T(8,128)(2,1)S(1)} collective-permute-done((f16[224,1024]{1,0:T(8,128)(2,1)S(1)}, f16[224,1024]{1,0:T(8,128)(2,1)S(1)}, u32[]{:S(2)}, u32[]{:S(2)}) %collective-permute-start.6) | collective-permute-done | bytes 458784 | tf_op jit(solution)/shard_map/ppermute | solution.py:239
  46.5 5.0 %collective-permute-start.7 = (f16[224,1024]{1,0:T(8,128)(2,1)S(1)}, f16[224,1024]{1,0:T(8,128)(2,1)S(1)}, u32[]{:S(2)}, u32[]{:S(2)}) collective-permute-start(f16[224,1024]{1,0:T(8,128)(2,1)S(1)} %get-tuple-element.59), channel_id=1, source_target_pairs={{0,2},{1,31},{2,4},{3,1},{4,6},{5,3},{6,8},{7,5},{8,10},{9,7},{10,... | collective-permute-start | bytes 1376264 | tf_op jit(solution)/shard_map/ppermute | solution.py:239
  51.5 1.9 %collective-permute-start.9 = (f16[224,1024]{1,0:T(8,128)(2,1)S(1)}, f16[224,1024]{1,0:T(8,128)(2,1)S(1)}, u32[]{:S(2)}, u32[]{:S(2)}) collective-permute-start(f16[224,1024]{1,0:T(8,128)(2,1)S(1)} %get-tuple-element.60), channel_id=1, source_target_pairs={{0,2},{1,31},{2,4},{3,1},{4,6},{5,3},{6,8},{7,5},{8,10},{9,7},{10,... | collective-permute-start | bytes 1376264 | tf_op jit(solution)/shard_map/ppermute | solution.py:239
  53.5 4.8 %collective-permute-start.10 = (bf16[896,128]{1,0:T(8,128)(2,1)S(1)}, bf16[896,128]{1,0:T(8,128)(2,1)S(1)}, u32[]{:S(2)}, u32[]{:S(2)}) collective-permute-start(bf16[896,128]{1,0:T(8,128)(2,1)S(1)} %copy-done.10), channel_id=1, source_target_pairs={{0,32},{1,33},{32,0},{33,1},{2,34},{3,35},{34,2},{35,3},{4,36},{5,... | collective-permute-start | bytes 688136 | tf_op jit(solution)/shard_map/ppermute | solution.py:224
  60.4 3.4 %collective-permute-start.8 = (f16[224,1024]{1,0:T(8,128)(2,1)S(1)}, f16[224,1024]{1,0:T(8,128)(2,1)S(1)}, u32[]{:S(2)}, u32[]{:S(2)}) collective-permute-start(f16[224,1024]{1,0:T(8,128)(2,1)S(1)} %fusion.15), channel_id=1, source_target_pairs={{0,2},{1,31},{2,4},{3,1},{4,6},{5,3},{6,8},{7,5},{8,10},{9,7},{10,... | collective-permute-start | bytes 1376264 | tf_op jit(solution)/shard_map/ppermute | solution.py:239
  63.9 3.6 %collective-permute-start.13 = (f16[224,1024]{1,0:T(8,128)(2,1)S(1)}, f16[224,1024]{1,0:T(8,128)(2,1)S(1)}, u32[]{:S(2)}, u32[]{:S(2)}) collective-permute-start(f16[224,1024]{1,0:T(8,128)(2,1)S(1)} %fusion.14), channel_id=1, source_target_pairs={{0,2},{1,31},{2,4},{3,1},{4,6},{5,3},{6,8},{7,5},{8,10},{9,7},{10,... | collective-permute-start | bytes 1376264 | tf_op jit(solution)/shard_map/ppermute | solution.py:239
  70.1 4.3 %collective-permute-start.12 = (f16[224,1024]{1,0:T(8,128)(2,1)S(1)}, f16[224,1024]{1,0:T(8,128)(2,1)S(1)}, u32[]{:S(2)}, u32[]{:S(2)}) collective-permute-start(f16[224,1024]{1,0:T(8,128)(2,1)S(1)} %fusion.13), channel_id=1, source_target_pairs={{0,2},{1,31},{2,4},{3,1},{4,6},{5,3},{6,8},{7,5},{8,10},{9,7},{10,... | collective-permute-start | bytes 1376264 | tf_op jit(solution)/shard_map/ppermute | solution.py:239
  75.0 4.3 %collective-permute-start.15 = (f16[224,1024]{1,0:T(8,128)(2,1)S(1)}, f16[224,1024]{1,0:T(8,128)(2,1)S(1)}, u32[]{:S(2)}, u32[]{:S(2)}) collective-permute-start(f16[224,1024]{1,0:T(8,128)(2,1)S(1)} %fusion.12), channel_id=1, source_target_pairs={{0,2},{1,31},{2,4},{3,1},{4,6},{5,3},{6,8},{7,5},{8,10},{9,7},{10,... | collective-permute-start | bytes 1376264 | tf_op jit(solution)/shard_map/ppermute | solution.py:239
  79.3 4.7 %collective-permute-start.16 = (bf16[1792,128]{1,0:T(8,128)(2,1)S(1)}, bf16[1792,128]{1,0:T(8,128)(2,1)S(1)}, u32[]{:S(2)}, u32[]{:S(2)}) collective-permute-start(bf16[1792,128]{1,0:T(8,128)(2,1)S(1)} %copy-done.8), channel_id=1, source_target_pairs={{0,32},{1,33},{32,0},{33,1},{2,34},{3,35},{34,2},{35,3},{4,36},{5,... | collective-permute-start | bytes 1376264 | tf_op jit(solution)/shard_map/ppermute | solution.py:224
  84.0 2.9 %collective-permute-start.17 = (bf16[1792,128]{1,0:T(8,128)(2,1)S(1)}, bf16[1792,128]{1,0:T(8,128)(2,1)S(1)}, u32[]{:S(2)}, u32[]{:S(2)}) collective-permute-start(bf16[1792,128]{1,0:T(8,128)(2,1)S(1)} %copy-done.7), channel_id=1, source_target_pairs={{0,33},{1,32},{32,1},{33,0},{2,35},{3,34},{34,3},{35,2},{4,37},{5,... | collective-permute-start | bytes 1376264 | tf_op jit(solution)/shard_map/ppermute | solution.py:224
  87.1 4.3 %collective-permute-start.14 = (f16[224,1024]{1,0:T(8,128)(2,1)S(1)}, f16[224,1024]{1,0:T(8,128)(2,1)S(1)}, u32[]{:S(2)}, u32[]{:S(2)}) collective-permute-start(f16[224,1024]{1,0:T(8,128)(2,1)S(1)} %fusion.11), channel_id=1, source_target_pairs={{0,2},{1,31},{2,4},{3,1},{4,6},{5,3},{6,8},{7,5},{8,10},{9,7},{10,... | collective-permute-start | bytes 1376264 | tf_op jit(solution)/shard_map/ppermute | solution.py:239
  94.1 10.7 %collective-permute-done.17.d_ref = bf16[1792,128]{1,0:T(8,128)(2,1)S(1)} collective-permute-done((bf16[1792,128]{1,0:T(8,128)(2,1)S(1)}, bf16[1792,128]{1,0:T(8,128)(2,1)S(1)}, u32[]{:S(2)}, u32[]{:S(2)}) %collective-permute-start.17) | collective-permute-done | bytes 458784 | tf_op jit(solution)/shard_map/ppermute | solution.py:224
  104.7 3.3 %shard_map.71 = f32[1792,1024]{1,0:T(8,128)S(1)} custom-call(bf16[1792,128]{1,0:T(8,128)(2,1)S(1)} %copy-done.2, bf16[3584,128]{1,0:T(8,128)(2,1)S(1)} %collective-permute-done.b_ref, bf16[1792,128]{1,0:T(8,128)(2,1)S(1)} %collective-permute-done.16.c_ref, bf16[1792,128]{1,0:T(8,128)(2,1)S(1)} %collective-permute-done.17.d_ref, ...), custom_call_target="tpu_custom_call" | custom-call | flops 75161927680 | bytes 11010048 | tf_op jit(solution)/shard_map/pallas_call | solution.py:131
  108.2 2.7 %collective-permute-start.18 = (f16[224,1024]{1,0:T(8,128)(2,1)S(1)}, f16[224,1024]{1,0:T(8,128)(2,1)S(1)}, u32[]{:S(2)}, u32[]{:S(2)}) collective-permute-start(f16[224,1024]{1,0:T(8,128)(2,1)S(1)} %fusion.9), channel_id=1, source_target_pairs={{0,2},{1,31},{2,4},{3,1},{4,6},{5,3},{6,8},{7,5},{8,10},{9,7},{10,... | collective-permute-start | bytes 1376264 | tf_op jit(solution)/shard_map/ppermute | solution.py:239
  111.1 2.9 %collective-permute-start.21 = (f16[224,1024]{1,0:T(8,128)(2,1)S(1)}, f16[224,1024]{1,0:T(8,128)(2,1)S(1)}, u32[]{:S(2)}, u32[]{:S(2)}) collective-permute-start(f16[224,1024]{1,0:T(8,128)(2,1)S(1)} %fusion.8), channel_id=1, source_target_pairs={{0,2},{1,31},{2,4},{3,1},{4,6},{5,3},{6,8},{7,5},{8,10},{9,7},{10,... | collective-permute-start | bytes 1376264 | tf_op jit(solution)/shard_map/ppermute | solution.py:239
  114.0 3.8 %collective-permute-done.18 = f16[224,1024]{1,0:T(8,128)(2,1)S(1)} collective-permute-done((f16[224,1024]{1,0:T(8,128)(2,1)S(1)}, f16[224,1024]{1,0:T(8,128)(2,1)S(1)}, u32[]{:S(2)}, u32[]{:S(2)}) %collective-permute-start.18) | collective-permute-done | bytes 458784 | tf_op jit(solution)/shard_map/ppermute | solution.py:239
  117.9 3.6 %collective-permute-start.20 = (f16[224,1024]{1,0:T(8,128)(2,1)S(1)}, f16[224,1024]{1,0:T(8,128)(2,1)S(1)}, u32[]{:S(2)}, u32[]{:S(2)}) collective-permute-start(f16[224,1024]{1,0:T(8,128)(2,1)S(1)} %fusion.7), channel_id=1, source_target_pairs={{0,2},{1,31},{2,4},{3,1},{4,6},{5,3},{6,8},{7,5},{8,10},{9,7},{10,... | collective-permute-start | bytes 1376264 | tf_op jit(solution)/shard_map/ppermute | solution.py:239
  122.8 3.6 %collective-permute-start.24 = (f16[224,1024]{1,0:T(8,128)(2,1)S(1)}, f16[224,1024]{1,0:T(8,128)(2,1)S(1)}, u32[]{:S(2)}, u32[]{:S(2)}) collective-permute-start(f16[224,1024]{1,0:T(8,128)(2,1)S(1)} %fusion.6), channel_id=1, source_target_pairs={{0,2},{1,31},{2,4},{3,1},{4,6},{5,3},{6,8},{7,5},{8,10},{9,7},{10,... | collective-permute-start | bytes 1376264 | tf_op jit(solution)/shard_map/ppermute | solution.py:239
  129.3 4.1 %collective-permute-start.22 = (f16[224,512]{1,0:T(8,128)(2,1)S(1)}, f16[224,512]{1,0:T(8,128)(2,1)S(1)}, u32[]{:S(2)}, u32[]{:S(2)}) collective-permute-start(f16[224,512]{1,0:T(8,128)(2,1)S(1)} %get-tuple-element.61), channel_id=1, source_target_pairs={{0,2},{1,31},{2,4},{3,1},{4,6},{5,3},{6,8},{7,5},{8,10},{9,7},{10,... | collective-permute-start | bytes 688136 | tf_op jit(solution)/shard_map/ppermute | solution.py:239
  133.4 6.0 %collective-permute-start.23 = (f16[224,512]{1,0:T(8,128)(2,1)S(1)}, f16[224,512]{1,0:T(8,128)(2,1)S(1)}, u32[]{:S(2)}, u32[]{:S(2)}) collective-permute-start(f16[224,512]{1,0:T(8,128)(2,1)S(1)} %get-tuple-element.62), channel_id=1, source_target_pairs={{0,3},{1,30},{2,5},{3,0},{4,7},{5,2},{6,9},{7,4},{8,11},{9,6},{10,... | collective-permute-start | bytes 688136 | tf_op jit(solution)/shard_map/ppermute | solution.py:239
  140.8 1.9 %collective-permute-start.25 = (f16[224,512]{1,0:T(8,128)(2,1)S(1)}, f16[224,512]{1,0:T(8,128)(2,1)S(1)}, u32[]{:S(2)}, u32[]{:S(2)}) collective-permute-start(f16[224,512]{1,0:T(8,128)(2,1)S(1)} %get-tuple-element.63), channel_id=1, source_target_pairs={{0,2},{1,31},{2,4},{3,1},{4,6},{5,3},{6,8},{7,5},{8,10},{9,7},{10,... | collective-permute-start | bytes 688136 | tf_op jit(solution)/shard_map/ppermute | solution.py:239
  142.8 1.9 %collective-permute-start.26 = (f16[224,512]{1,0:T(8,128)(2,1)S(1)}, f16[224,512]{1,0:T(8,128)(2,1)S(1)}, u32[]{:S(2)}, u32[]{:S(2)}) collective-permute-start(f16[224,512]{1,0:T(8,128)(2,1)S(1)} %get-tuple-element.64), channel_id=1, source_target_pairs={{0,3},{1,30},{2,5},{3,0},{4,7},{5,2},{6,9},{7,4},{8,11},{9,6},{10,... | collective-permute-start | bytes 688136 | tf_op jit(solution)/shard_map/ppermute | solution.py:239
  144.8 2.8 %collective-permute-done.25 = f16[224,512]{1,0:T(8,128)(2,1)S(1)} collective-permute-done((f16[224,512]{1,0:T(8,128)(2,1)S(1)}, f16[224,512]{1,0:T(8,128)(2,1)S(1)}, u32[]{:S(2)}, u32[]{:S(2)}) %collective-permute-start.25) | collective-permute-done | bytes 229408 | tf_op jit(solution)/shard_map/ppermute | solution.py:239
  147.6 3.7 %collective-permute-done.26 = f16[224,512]{1,0:T(8,128)(2,1)S(1)} collective-permute-done((f16[224,512]{1,0:T(8,128)(2,1)S(1)}, f16[224,512]{1,0:T(8,128)(2,1)S(1)}, u32[]{:S(2)}, u32[]{:S(2)}) %collective-permute-start.26) | collective-permute-done | bytes 229408 | tf_op jit(solution)/shard_map/ppermute | solution.py:239
  151.8 14.6 %all_to_all.5 = f16[16,28,512]{2,1,0:T(8,128)(2,1)S(1)} all-to-all(f16[16,28,512]{2,1,0:T(8,128)(2,1)S(1)} %reshape.12), channel_id=1, replica_groups=mesh['ylo'=2,'x'=4,'yhi'=2,'z'=16,'core'=2] {'ylo','x','core'}, dimensions={0} | all-to-all | bytes 917504 | tf_op jit(solution)/shard_map/all_to_all | solution.py:257
  166.7 2.4 %shard_map.72 = (f32[28,512]{1,0:T(8,128)}, f32[28,512]{1,0:T(8,128)}, f32[28,512]{1,0:T(8,128)}) custom-call(f32[16,32,512]{2,1,0:T(8,128)S(1)} %pad.4.g_ref, bf16[28,512]{1,0:T(8,128)(2,1)S(1)} %copy-done.1), custom_call_target="tpu_custom_call" | custom-call | tf_op jit(solution)/shard_map/pallas_call | solution.py:197
  (77 shorter events, 23.9 us)
Async XLA Ops:
  8.4 19.8 %collective-permute-start.3 = (bf16[736,128]{1,0:T(8,128)(2,1)}, bf16[736,128]{1,0:T(8,128)(2,1)S(1)}, u32[]{:S(2)}, u32[]{:S(2)}) collective-permute-start(bf16[736,128]{1,0:T(8,128)(2,1)} %get-tuple-element.36), channel_id=1, source_target_pairs={{0,1},{1,0},{32,33},{33,32},{2,3},{3,2},{34,35},{35,34},{4,5},{5,4... | collective-permute-start | bytes 565256 | tf_op jit(solution)/shard_map/ppermute | solution.py:224
  17.2 16.4 %collective-permute-start.4 = (bf16[736,128]{1,0:T(8,128)(2,1)}, bf16[736,128]{1,0:T(8,128)(2,1)S(1)}, u32[]{:S(2)}, u32[]{:S(2)}) collective-permute-start(bf16[736,128]{1,0:T(8,128)(2,1)} %get-tuple-element.37), channel_id=1, source_target_pairs={{0,32},{1,33},{32,0},{33,1},{2,34},{3,35},{34,2},{35,3},{4,36},{5,... | collective-permute-start | bytes 565256 | tf_op jit(solution)/shard_map/ppermute | solution.py:224
  19.1 14.5 %collective-permute-start.5 = (bf16[736,128]{1,0:T(8,128)(2,1)}, bf16[736,128]{1,0:T(8,128)(2,1)S(1)}, u32[]{:S(2)}, u32[]{:S(2)}) collective-permute-start(bf16[736,128]{1,0:T(8,128)(2,1)} %get-tuple-element.38), channel_id=1, source_target_pairs={{0,33},{1,32},{32,1},{33,0},{2,35},{3,34},{34,3},{35,2},{4,37},{5,... | collective-permute-start | bytes 565256 | tf_op jit(solution)/shard_map/ppermute | solution.py:224
  24.2 18.0 %collective-permute-start = (bf16[3584,128]{1,0:T(8,128)(2,1)}, bf16[3584,128]{1,0:T(8,128)(2,1)S(1)}, u32[]{:S(2)}, u32[]{:S(2)}) collective-permute-start(bf16[3584,128]{1,0:T(8,128)(2,1)} %get-tuple-element.32), channel_id=1, source_target_pairs={{0,1},{1,0},{32,33},{33,32},{2,3},{3,2},{34,35},{35,34},{4,5},{5,4... | collective-permute-start | bytes 2752520 | tf_op jit(solution)/shard_map/ppermute | solution.py:224
  26.3 14.5 %collective-permute-start.1 = (bf16[896,128]{1,0:T(8,128)(2,1)}, bf16[896,128]{1,0:T(8,128)(2,1)S(1)}, u32[]{:S(2)}, u32[]{:S(2)}) collective-permute-start(bf16[896,128]{1,0:T(8,128)(2,1)} %get-tuple-element.33), channel_id=1, source_target_pairs={{0,32},{1,33},{32,0},{33,1},{2,34},{3,35},{34,2},{35,3},{4,36},{5,... | collective-permute-start | bytes 688136 | tf_op jit(solution)/shard_map/ppermute | solution.py:224
  28.3 13.9 %collective-permute-start.2 = (bf16[896,128]{1,0:T(8,128)(2,1)}, bf16[896,128]{1,0:T(8,128)(2,1)S(1)}, u32[]{:S(2)}, u32[]{:S(2)}) collective-permute-start(bf16[896,128]{1,0:T(8,128)(2,1)} %get-tuple-element.34), channel_id=1, source_target_pairs={{0,33},{1,32},{32,1},{33,0},{2,35},{3,34},{34,3},{35,2},{4,37},{5,... | collective-permute-start | bytes 688136 | tf_op jit(solution)/shard_map/ppermute | solution.py:224
  35.0 11.2 %collective-permute-start.6 = (f16[224,1024]{1,0:T(8,128)(2,1)S(1)}, f16[224,1024]{1,0:T(8,128)(2,1)S(1)}, u32[]{:S(2)}, u32[]{:S(2)}) collective-permute-start(f16[224,1024]{1,0:T(8,128)(2,1)S(1)} %convert_element_type.108), channel_id=1, source_target_pairs={{0,2},{1,31},{2,4},{3,1},{4,6},{5,3},{6,8},{7,5},{8,10},{9,7},{10,... | collective-permute-start | bytes 1376264 | tf_op jit(solution)/shard_map/ppermute | solution.py:239
  42.2 16.1 %copy-start.9 = (bf16[896,128]{1,0:T(8,128)(2,1)S(1)}, bf16[896,128]{1,0:T(8,128)(2,1)}, u32[]{:S(2)}) copy-start(bf16[896,128]{1,0:T(8,128)(2,1)} %get-tuple-element.46) | copy-start | bytes 688132
  43.9 24.0 %copy-start.3 = (bf16[896,128]{1,0:T(8,128)(2,1)S(1)}, bf16[896,128]{1,0:T(8,128)(2,1)}, u32[]{:S(2)}) copy-start(bf16[896,128]{1,0:T(8,128)(2,1)} %get-tuple-element.44.a_ref) | copy-start | bytes 688132
  46.5 13.7 %collective-permute-start.7 = (f16[224,1024]{1,0:T(8,128)(2,1)S(1)}, f16[224,1024]{1,0:T(8,128)(2,1)S(1)}, u32[]{:S(2)}, u32[]{:S(2)}) collective-permute-start(f16[224,1024]{1,0:T(8,128)(2,1)S(1)} %get-tuple-element.59), channel_id=1, source_target_pairs={{0,2},{1,31},{2,4},{3,1},{4,6},{5,3},{6,8},{7,5},{8,10},{9,7},{10,... | collective-permute-start | bytes 1376264 | tf_op jit(solution)/shard_map/ppermute | solution.py:239
  51.5 12.2 %collective-permute-start.9 = (f16[224,1024]{1,0:T(8,128)(2,1)S(1)}, f16[224,1024]{1,0:T(8,128)(2,1)S(1)}, u32[]{:S(2)}, u32[]{:S(2)}) collective-permute-start(f16[224,1024]{1,0:T(8,128)(2,1)S(1)} %get-tuple-element.60), channel_id=1, source_target_pairs={{0,2},{1,31},{2,4},{3,1},{4,6},{5,3},{6,8},{7,5},{8,10},{9,7},{10,... | collective-permute-start | bytes 1376264 | tf_op jit(solution)/shard_map/ppermute | solution.py:239
  53.5 14.1 %collective-permute-start.10 = (bf16[896,128]{1,0:T(8,128)(2,1)S(1)}, bf16[896,128]{1,0:T(8,128)(2,1)S(1)}, u32[]{:S(2)}, u32[]{:S(2)}) collective-permute-start(bf16[896,128]{1,0:T(8,128)(2,1)S(1)} %copy-done.10), channel_id=1, source_target_pairs={{0,32},{1,33},{32,0},{33,1},{2,34},{3,35},{34,2},{35,3},{4,36},{5,... | collective-permute-start | bytes 688136 | tf_op jit(solution)/shard_map/ppermute | solution.py:224
  58.3 9.6 %collective-permute-start.11 = (bf16[896,128]{1,0:T(8,128)(2,1)S(1)}, bf16[896,128]{1,0:T(8,128)(2,1)S(1)}, u32[]{:S(2)}, u32[]{:S(2)}) collective-permute-start(bf16[896,128]{1,0:T(8,128)(2,1)S(1)} %copy-done.9), channel_id=1, source_target_pairs={{0,33},{1,32},{32,1},{33,0},{2,35},{3,34},{34,3},{35,2},{4,37},{5,... | collective-permute-start | bytes 688136 | tf_op jit(solution)/shard_map/ppermute | solution.py:224
  60.4 9.5 %collective-permute-start.8 = (f16[224,1024]{1,0:T(8,128)(2,1)S(1)}, f16[224,1024]{1,0:T(8,128)(2,1)S(1)}, u32[]{:S(2)}, u32[]{:S(2)}) collective-permute-start(f16[224,1024]{1,0:T(8,128)(2,1)S(1)} %fusion.15), channel_id=1, source_target_pairs={{0,2},{1,31},{2,4},{3,1},{4,6},{5,3},{6,8},{7,5},{8,10},{9,7},{10,... | collective-permute-start | bytes 1376264 | tf_op jit(solution)/shard_map/ppermute | solution.py:239
  63.9 10.9 %collective-permute-start.13 = (f16[224,1024]{1,0:T(8,128)(2,1)S(1)}, f16[224,1024]{1,0:T(8,128)(2,1)S(1)}, u32[]{:S(2)}, u32[]{:S(2)}) collective-permute-start(f16[224,1024]{1,0:T(8,128)(2,1)S(1)} %fusion.14), channel_id=1, source_target_pairs={{0,2},{1,31},{2,4},{3,1},{4,6},{5,3},{6,8},{7,5},{8,10},{9,7},{10,... | collective-permute-start | bytes 1376264 | tf_op jit(solution)/shard_map/ppermute | solution.py:239
  69.5 35.2 %copy-start.2 = (bf16[1792,128]{1,0:T(8,128)(2,1)S(1)}, bf16[1792,128]{1,0:T(8,128)(2,1)}, u32[]{:S(2)}) copy-start(bf16[1792,128]{1,0:T(8,128)(2,1)} %get-tuple-element.51.a_ref) | copy-start | bytes 1376260
  70.1 16.8 %collective-permute-start.12 = (f16[224,1024]{1,0:T(8,128)(2,1)S(1)}, f16[224,1024]{1,0:T(8,128)(2,1)S(1)}, u32[]{:S(2)}, u32[]{:S(2)}) collective-permute-start(f16[224,1024]{1,0:T(8,128)(2,1)S(1)} %fusion.13), channel_id=1, source_target_pairs={{0,2},{1,31},{2,4},{3,1},{4,6},{5,3},{6,8},{7,5},{8,10},{9,7},{10,... | collective-permute-start | bytes 1376264 | tf_op jit(solution)/shard_map/ppermute | solution.py:239
  75.0 16.4 %collective-permute-start.15 = (f16[224,1024]{1,0:T(8,128)(2,1)S(1)}, f16[224,1024]{1,0:T(8,128)(2,1)S(1)}, u32[]{:S(2)}, u32[]{:S(2)}) collective-permute-start(f16[224,1024]{1,0:T(8,128)(2,1)S(1)} %fusion.12), channel_id=1, source_target_pairs={{0,2},{1,31},{2,4},{3,1},{4,6},{5,3},{6,8},{7,5},{8,10},{9,7},{10,... | collective-permute-start | bytes 1376264 | tf_op jit(solution)/shard_map/ppermute | solution.py:239
  79.3 14.8 %collective-permute-start.16 = (bf16[1792,128]{1,0:T(8,128)(2,1)S(1)}, bf16[1792,128]{1,0:T(8,128)(2,1)S(1)}, u32[]{:S(2)}, u32[]{:S(2)}) collective-permute-start(bf16[1792,128]{1,0:T(8,128)(2,1)S(1)} %copy-done.8), channel_id=1, source_target_pairs={{0,32},{1,33},{32,0},{33,1},{2,34},{3,35},{34,2},{35,3},{4,36},{5,... | collective-permute-start | bytes 1376264 | tf_op jit(solution)/shard_map/ppermute | solution.py:224
  84.0 20.8 %collective-permute-start.17 = (bf16[1792,128]{1,0:T(8,128)(2,1)S(1)}, bf16[1792,128]{1,0:T(8,128)(2,1)S(1)}, u32[]{:S(2)}, u32[]{:S(2)}) collective-permute-start(bf16[1792,128]{1,0:T(8,128)(2,1)S(1)} %copy-done.7), channel_id=1, source_target_pairs={{0,33},{1,32},{32,1},{33,0},{2,35},{3,34},{34,3},{35,2},{4,37},{5,... | collective-permute-start | bytes 1376264 | tf_op jit(solution)/shard_map/ppermute | solution.py:224
  87.1 21.0 %collective-permute-start.14 = (f16[224,1024]{1,0:T(8,128)(2,1)S(1)}, f16[224,1024]{1,0:T(8,128)(2,1)S(1)}, u32[]{:S(2)}, u32[]{:S(2)}) collective-permute-start(f16[224,1024]{1,0:T(8,128)(2,1)S(1)} %fusion.11), channel_id=1, source_target_pairs={{0,2},{1,31},{2,4},{3,1},{4,6},{5,3},{6,8},{7,5},{8,10},{9,7},{10,... | collective-permute-start | bytes 1376264 | tf_op jit(solution)/shard_map/ppermute | solution.py:239
  91.6 19.4 %collective-permute-start.19 = (f16[224,1024]{1,0:T(8,128)(2,1)S(1)}, f16[224,1024]{1,0:T(8,128)(2,1)S(1)}, u32[]{:S(2)}, u32[]{:S(2)}) collective-permute-start(f16[224,1024]{1,0:T(8,128)(2,1)S(1)} %fusion.10), channel_id=1, source_target_pairs={{0,2},{1,31},{2,4},{3,1},{4,6},{5,3},{6,8},{7,5},{8,10},{9,7},{10,... | collective-permute-start | bytes 1376264 | tf_op jit(solution)/shard_map/ppermute | solution.py:239
  108.0 18.4 %copy-start.6 = (s32[2]{0:T(128)S(1)}, s32[2]{0:T(128)}, u32[]{:S(2)}) copy-start(s32[2]{0:T(128)} %param.6) | copy-start | bytes 28
  108.2 9.5 %collective-permute-start.18 = (f16[224,1024]{1,0:T(8,128)(2,1)S(1)}, f16[224,1024]{1,0:T(8,128)(2,1)S(1)}, u32[]{:S(2)}, u32[]{:S(2)}) collective-permute-start(f16[224,1024]{1,0:T(8,128)(2,1)S(1)} %fusion.9), channel_id=1, source_target_pairs={{0,2},{1,31},{2,4},{3,1},{4,6},{5,3},{6,8},{7,5},{8,10},{9,7},{10,... | collective-permute-start | bytes 1376264 | tf_op jit(solution)/shard_map/ppermute | solution.py:239
  111.1 11.6 %collective-permute-start.21 = (f16[224,1024]{1,0:T(8,128)(2,1)S(1)}, f16[224,1024]{1,0:T(8,128)(2,1)S(1)}, u32[]{:S(2)}, u32[]{:S(2)}) collective-permute-start(f16[224,1024]{1,0:T(8,128)(2,1)S(1)} %fusion.8), channel_id=1, source_target_pairs={{0,2},{1,31},{2,4},{3,1},{4,6},{5,3},{6,8},{7,5},{8,10},{9,7},{10,... | collective-permute-start | bytes 1376264 | tf_op jit(solution)/shard_map/ppermute | solution.py:239
  117.9 9.9 %collective-permute-start.20 = (f16[224,1024]{1,0:T(8,128)(2,1)S(1)}, f16[224,1024]{1,0:T(8,128)(2,1)S(1)}, u32[]{:S(2)}, u32[]{:S(2)}) collective-permute-start(f16[224,1024]{1,0:T(8,128)(2,1)S(1)} %fusion.7), channel_id=1, source_target_pairs={{0,2},{1,31},{2,4},{3,1},{4,6},{5,3},{6,8},{7,5},{8,10},{9,7},{10,... | collective-permute-start | bytes 1376264 | tf_op jit(solution)/shard_map/ppermute | solution.py:239
  122.8 16.6 %collective-permute-start.24 = (f16[224,1024]{1,0:T(8,128)(2,1)S(1)}, f16[224,1024]{1,0:T(8,128)(2,1)S(1)}, u32[]{:S(2)}, u32[]{:S(2)}) collective-permute-start(f16[224,1024]{1,0:T(8,128)(2,1)S(1)} %fusion.6), channel_id=1, source_target_pairs={{0,2},{1,31},{2,4},{3,1},{4,6},{5,3},{6,8},{7,5},{8,10},{9,7},{10,... | collective-permute-start | bytes 1376264 | tf_op jit(solution)/shard_map/ppermute | solution.py:239
  127.7 23.7 %slice-start = ((f32[1792,1024]{1,0:T(8,128)}), f32[448,1024]{1,0:T(8,128)S(1)}, s32[]{:S(2)}) async-start(f32[1792,1024]{1,0:T(8,128)} %copy-done), calls=%async_computation.1 | async-start | bytes 3670016 | tf_op jit(solution)/shard_map/slice | solution.py:236
  129.3 15.4 %collective-permute-start.22 = (f16[224,512]{1,0:T(8,128)(2,1)S(1)}, f16[224,512]{1,0:T(8,128)(2,1)S(1)}, u32[]{:S(2)}, u32[]{:S(2)}) collective-permute-start(f16[224,512]{1,0:T(8,128)(2,1)S(1)} %get-tuple-element.61), channel_id=1, source_target_pairs={{0,2},{1,31},{2,4},{3,1},{4,6},{5,3},{6,8},{7,5},{8,10},{9,7},{10,... | collective-permute-start | bytes 688136 | tf_op jit(solution)/shard_map/ppermute | solution.py:239
  133.4 11.3 %collective-permute-start.23 = (f16[224,512]{1,0:T(8,128)(2,1)S(1)}, f16[224,512]{1,0:T(8,128)(2,1)S(1)}, u32[]{:S(2)}, u32[]{:S(2)}) collective-permute-start(f16[224,512]{1,0:T(8,128)(2,1)S(1)} %get-tuple-element.62), channel_id=1, source_target_pairs={{0,3},{1,30},{2,5},{3,0},{4,7},{5,2},{6,9},{7,4},{8,11},{9,6},{10,... | collective-permute-start | bytes 688136 | tf_op jit(solution)/shard_map/ppermute | solution.py:239
  140.8 6.8 %collective-permute-start.25 = (f16[224,512]{1,0:T(8,128)(2,1)S(1)}, f16[224,512]{1,0:T(8,128)(2,1)S(1)}, u32[]{:S(2)}, u32[]{:S(2)}) collective-permute-start(f16[224,512]{1,0:T(8,128)(2,1)S(1)} %get-tuple-element.63), channel_id=1, source_target_pairs={{0,2},{1,31},{2,4},{3,1},{4,6},{5,3},{6,8},{7,5},{8,10},{9,7},{10,... | collective-permute-start | bytes 688136 | tf_op jit(solution)/shard_map/ppermute | solution.py:239
  142.8 8.6 %collective-permute-start.26 = (f16[224,512]{1,0:T(8,128)(2,1)S(1)}, f16[224,512]{1,0:T(8,128)(2,1)S(1)}, u32[]{:S(2)}, u32[]{:S(2)}) collective-permute-start(f16[224,512]{1,0:T(8,128)(2,1)S(1)} %get-tuple-element.64), channel_id=1, source_target_pairs={{0,3},{1,30},{2,5},{3,0},{4,7},{5,2},{6,9},{7,4},{8,11},{9,6},{10,... | collective-permute-start | bytes 688136 | tf_op jit(solution)/shard_map/ppermute | solution.py:239
  (7 other events, 73.9 us)

commit v5 on v4

--- a/solution.py
+++ b/solution.py
@@ -12,16 +12,14 @@
 NZ = 16
 FAR = NZ // 2
 GROUPS = ((7, 6), (5, 4), (3, 2, 1, 0))
+LATER = {6: (1, 0), 4: (2, 0), 3: (2, 2)}
+CHAINS = ((0, 160), (160, 304), (304, 448))
 VMEM = 56 * 1024 * 1024
 f32 = jnp.float32
 f16 = jnp.float16
 
 
-def outputs_of(other):
-    return (sum(GROUPS, ()),) if other == 1 else GROUPS
-
-
-def turn_kernel(s_ref, up_ref, feat_ref, *rest):
+def turn_kernel(len_ref, up_ref, feat_ref, *rest):
     outs, hold = list(rest[:-1]), rest[-1]
     step = pl.program_id(0)
     n_ex, seg, n_row = feat_ref.shape
@@ -39,54 +37,65 @@
     @pl.when(step == pl.num_programs(0) - 1)
     def _():
         n, tall = hold.shape[2], hold.shape[3]
-        yhi, z, core = s_ref[0], s_ref[1], s_ref[2]
-        position = s_ref[3] + lax.broadcasted_iota(jnp.int32, (seg, n_row), 0)
+        yhi, z, core = lax.axis_index("yhi"), lax.axis_index("z"), lax.axis_index("core")
+        first_position = ((yhi * NZ + z) * 2 + core) * seg
+        position = first_position + lax.broadcasted_iota(jnp.int32, (seg, n_row), 0)
         feats = jnp.concatenate([
-            jnp.where(position < s_ref[4 + e], feat_ref[e].astype(f32) * 0.25, 0.0) for e in range(n_ex)
+            jnp.where(position < len_ref[e], feat_ref[e].astype(f32) * 0.25, 0.0) for e in range(n_ex)
         ], axis=0).astype(feat_ref.dtype)
-        for other in range(4):
-            half = yhi if other < 2 else 1 - yhi
-            to = core if other % 2 == 0 else 1 - core
-            place = lambda dist: lax.rem(z + (1 - 2 * to) * dist + NZ, NZ)
-            first = outs.pop(0)
-            for p in range(n // 2):
-                first[p * tall:(p + 1) * tall] = hold[half, place(FAR), (n // 2) * to + p]
-            at = n // 2 * tall
+
+        def put(out, at, half, to, dist, pairs):
+            dest = lax.rem(z + (1 - 2 * to) * dist + NZ, NZ)
+            for i, p in enumerate(pairs):
+                out[at + i * tall:at + (i + 1) * tall] = hold[half, dest, p]
+            return at + len(pairs) * tall
+
+        def put_far(out, at, half, to):
+            return put(out, at, half, to, FAR, [n // 2 * to + p for p in range(n // 2)])
+
+        def put_features(out, at):
             for b in range(n_row // BLOCK):
-                first[at + b * seg2:at + (b + 1) * seg2] = feats[:, b * BLOCK:(b + 1) * BLOCK]
-            for group in outputs_of(other):
-                out = outs.pop(0)
-                for i, dist in enumerate(group):
-                    for p in range(n):
-                        at = (i * n + p) * tall
-                        out[at:at + tall] = hold[half, place(dist), p]
-
-
-def turn(upstream, features, scalars, n_groups):
+                out[at + b * seg2:at + (b + 1) * seg2] = feats[:, b * BLOCK:(b + 1) * BLOCK]
+
+        for i, half in enumerate((yhi, 1 - yhi)):
+            n_out = 1 + len(GROUPS)
+            first, *others = outs[n_out * i:n_out * (i + 1)]
+            put_features(first, put_far(first, 0, half, core))
+            for out, group in zip(others, GROUPS):
+                at = 0
+                for dist in group:
+                    at = put(out, at, half, core, dist, range(n))
+        first, other = outs[2 * n_out:]
+        at = put_far(first, 0, yhi, 1 - core)
+        put_features(first, put_far(first, at, 1 - yhi, 1 - core))
+        at = 0
+        for half in (yhi, 1 - yhi):
+            for dist in sum(GROUPS, ()):
+                at = put(other, at, half, 1 - core, dist, range(n))
+
+
+def turn(upstream, features, lengths, n_groups):
     n_ex, seg, units = upstream.shape
     rows = features.shape[2]
     seg2 = n_ex * seg
     n = n_groups // 2
     chunk = units // 2 // NZ
-    shapes = []
-    for other in range(4):
-        shapes.append((chunk // 2 + rows // BLOCK * seg2, seg2))
-        shapes += [(len(group) * chunk, seg2) for group in outputs_of(other)]
+    extra = rows // BLOCK * seg2
+    heights = 2 * [chunk // 2 + extra, *(len(group) * chunk for group in GROUPS)]
+    heights += [chunk + extra, 2 * FAR * chunk]
     whole = lambda shape: pl.BlockSpec(shape, lambda i, s: (0,) * len(shape))
-    made = pl.pallas_call(
+    return pl.pallas_call(
         turn_kernel,
         grid_spec=pltpu.PrefetchScalarGridSpec(
             num_scalar_prefetch=1,
             grid=(n,),
             in_specs=[pl.BlockSpec((n_ex, seg, units // n), lambda i, s: (0, 0, i)), whole(features.shape)],
-            out_specs=[whole(shape) for shape in shapes],
+            out_specs=[whole((height, seg2)) for height in heights],
             scratch_shapes=[pltpu.VMEM((2, NZ, n, chunk // n, seg2), upstream.dtype)],
         ),
-        out_shape=[jax.ShapeDtypeStruct(shape, upstream.dtype) for shape in shapes],
+        out_shape=[jax.ShapeDtypeStruct((height, seg2), upstream.dtype) for height in heights],
         compiler_params=pltpu.CompilerParams(vmem_limit_bytes=VMEM),
-    )(scalars, upstream, features)
-    made = list(made)
-    return [[made.pop(0) for _ in range(1 + len(outputs_of(other)))] for other in range(4)]
+    )(lengths, upstream, features)
 
 
 def first_kernel(a_ref, b_ref, c_ref, d_ref, out_ref, right_ref):
@@ -95,7 +104,8 @@
     height = out_ref.shape[0]
     n_lane = (a_ref.shape[0] - height) // seg2
     for k, ref in enumerate(refs):
-        rows = [ref[height + b * seg2:height + (b + 1) * seg2] for b in range(n_lane)]
+        at = ref.shape[0] - n_lane * seg2
+        rows = [ref[at + b * seg2:at + (b + 1) * seg2] for b in range(n_lane)]
         feats = jnp.concatenate(rows, axis=1)
         half = seg2 // 2
         none = jnp.zeros((half, feats.shape[1]), feats.dtype)
@@ -212,47 +222,62 @@
 
 
 def body(features, upstream, lengths, weights):
-    yhi, z, core = lax.axis_index("yhi"), lax.axis_index("z"), lax.axis_index("core")
-    n_ex, seg, rows = features.shape
+    core = lax.axis_index("core")
+    _, seg, rows = features.shape
     units = upstream.shape[2]
     n_groups = 8
     total_len = seg * 64
-    shard = (yhi * NZ + z) * 2 + core
-    scalars = jnp.concatenate([jnp.stack([yhi, z, core, shard * seg]), lengths]).astype(jnp.int32)
-    made = turn(upstream, features, scalars, n_groups)
-
+    made = turn(upstream, features, lengths, n_groups)
     quad = lambda x, i: lax.ppermute(x, ("yhi", "core"), [(j, j ^ i) for j in range(4)])
     chunk = units // 2 // NZ
     half = chunk // 2
-    got = {i: [quad(x, i) for x in made[i]] for i in (2, 3, 1)}
-    got[0] = made[0]
-    far, right = first_product([got[i][0] for i in range(4)], half)
+    n_out = 1 + len(GROUPS)
+    after = lambda x, *events: lax.optimization_barrier((x, *events))[0]
+    sizes = [len(group) * chunk for group in GROUPS]
+    sib_far = quad(made[2 * n_out], 1)
+    near = [quad(made[n_out], 2)]
+    diag = [quad(sib_far[half:], 2)]
+    far, right = first_product([made[0], sib_far, near[0], diag[0]], half)
+    sib = quad(after(made[2 * n_out + 1], sib_far), 1)
     parts = {}
-    start = 0
-    for g, group in enumerate(GROUPS):
-        pieces = [got[0][1 + g], got[1][1], got[2][1 + g], got[3][1 + g]]
-        part = product(pieces, (0, start, 0, 0), right, chunk, len(group))
-        for i, dist in enumerate(group):
-            parts[dist] = part[i * chunk:(i + 1) * chunk]
-        start += len(group)
+
+    def send(g, event):
+        at = FAR * chunk + sum(sizes[:g])
+        near.append(quad(after(made[n_out + 1 + g], event), 2))
+        diag.append(quad(after(sib[at:at + sizes[g]], event), 2))
+
+    def multiply(g, at, event):
+        group = GROUPS[g]
+        start = sum(map(len, GROUPS[:g])) + at
+        pieces = [made[1 + g], sib, near[1 + g], after(diag[1 + g], event)]
+        part = product(pieces, (at, start, at, at), right, chunk, 2)
+        for i in range(2):
+            parts[group[at + i]] = part[i * chunk:(i + 1) * chunk]
+        return part
 
     ring = lambda x, cross=0: lax.ppermute(x, ("z", "core"), ring_pairs(cross))
-    got = ring(far.astype(f16)).astype(f32)
-    sums = [
-        (parts[FAR - 1][k * half:(k + 1) * half] + jnp.where(core == k, got, 0.0)).astype(f16) for k in range(2)
-    ]
-    last = sums[1]
+    send(0, sib_far)
+    send(1, far)
+    nearest = multiply(0, 0, far)
+    send(2, nearest)
+    got, _ = lax.optimization_barrier((ring(far.astype(f16)), nearest))
+    got = got.astype(f32)
+    none = jnp.zeros_like(got)
+    got = jnp.where(core == 0, jnp.concatenate([got, none], axis=0), jnp.concatenate([none, got], axis=0))
+    sums = [(parts[FAR - 1][a:b] + got[a:b]).astype(f16) for a, b in CHAINS]
+    last = sums[-1]
     for dist in range(FAR - 2, 0, -1):
-        for k in range(2):
+        for k, (a, b) in enumerate(CHAINS):
             got = ring(sums[k])
-            got, _ = lax.optimization_barrier((got, last))
-            sums[k] = last = (got.astype(f32) + parts[dist][k * half:(k + 1) * half]).astype(f16)
+            got = after(got, last)
+            sums[k] = last = (got.astype(f32) + parts[dist][a:b]).astype(f16)
+            if k == 0 and dist in LATER:
+                multiply(*LATER[dist], last)
     pick = lambda x, i: lax.dynamic_slice_in_dim(x, i * rows, rows, 1)
-    ends = []
-    for k in range(2):
-        ends.append(ring(pick(sums[k], core)).astype(f32) + ring(pick(sums[k], 1 - core), 1).astype(f32))
+    same = [ring(pick(x, core)).astype(f32) for x in sums]
+    cross = ring(jnp.concatenate([pick(x, 1 - core) for x in sums], axis=0), 1).astype(f32)
     length = lax.dynamic_index_in_dim(lengths, core, 0, keepdims=False).astype(f32)
-    total = (jnp.concatenate(ends, axis=0) + pick(parts[0], core)) * (4096.0 / length)
+    total = (jnp.concatenate(same, axis=0) + cross + pick(parts[0], core)) * (4096.0 / length)
     pieces = total.astype(f16).reshape(2 * n_groups, -1, rows)
     owned = lax.all_to_all(pieces, ("ylo", "x", "core"), 0, 0, tiled=True)
     own_units = owned.shape[1]

time: 170 us -> 177 us (1.041)
  starting transfers between devices: 101 us -> 118 us
  waiting for transfers between devices: 27.6 us -> 15.1 us
  other arithmetic: 4.96 us -> 7.72 us
    ppermute x17 -> x23, starting transfers between devices: 61.2 us -> 77.5 us  [body(): ring = lambda x, cross=0: lax.ppermute(x, ('z', 'core'), ring_pairs(cross))]
    ppermute x10, waiting for transfers between devices: 12.9 us -> 4.48 us  [body(): lax.ppermute(x, ('yhi', 'core'), [(j, j ^ i) for j in range(4)])]
    ppermute x17 -> x23, waiting for transfers between devices: 14.7 us -> 10.6 us  [body(): ring = lambda x, cross=0: lax.ppermute(x, ('z', 'core'), ring_pairs(cross))]
    convert_element_type x14 -> x22, other arithmetic: 4.47 us -> 6.97 us  [the longest x18 4.94 us: body(): sums[k] = last = (got.astype(f32) + parts[dist][a:b]).astype(f16)]
    pallas_call x3 -> x4, Pallas kernels: 6.62 us -> 6.66 us  [product(): pl.pallas_call(product_kernel, grid=(2 * count,), in_specs=[pl.BlockSpec(...]
  transfers between devices with their start and end apart: 27 -> 33, of which waited for: 11 -> 13; matrix products, arithmetic and copies ran while one was open for 3% -> 4% of each run, Pallas kernels for 4% -> 4%
where the time goes in v5:
time: 177 us; the launch traced here: 176 us
  starting transfers between devices  118 us (67%)
  Pallas kernels  15.9 us (9%)
  waiting for transfers between devices  15.1 us (9%)
  blocking collectives  14.4 us (8%)
  other arithmetic  7.72 us (4%)
  local copies, waits for them, and re-layouts  2.74 us (2%)
  between operations  2.09 us (1%)
    ppermute x23, starting transfers between devices, body(): ring = lambda x, cross=0: lax.ppermute(x, ('z', 'core'), ring_pairs(cross))  77.5 us
    ppermute x10, starting transfers between devices, body(): lax.ppermute(x, ('yhi', 'core'), [(j, j ^ i) for j in range(4)])  40.5 us
    all_to_all x1, blocking collectives, body(): owned = lax.all_to_all(pieces, ('ylo', 'x', 'core'), 0, 0, tiled=True)  14.4 us
    ppermute x23, waiting for transfers between devices, body(): ring = lambda x, cross=0: lax.ppermute(x, ('z', 'core'), ring_pairs(cross))  10.6 us
    pallas_call x4, Pallas kernels, product(): pl.pallas_call(product_kernel, grid=(2 * count,), in_specs=[pl.BlockSpec(...  6.66 us
    pallas_call x1, Pallas kernels, turn(): pl.pallas_call(turn_kernel, grid_spec=pltpu.PrefetchScalarGridSpec(num_sc...  6.43 us
    convert_element_type x18, other arithmetic, body(): sums[k] = last = (got.astype(f32) + parts[dist][a:b]).astype(f16)  4.94 us
    ppermute x10, waiting for transfers between devices, body(): lax.ppermute(x, ('yhi', 'core'), [(j, j ^ i) for j in range(4)])  4.48 us
  transfers between devices with their start and end apart: 33, of which 13 were waited for; matrix products, arithmetic and copies ran while one was open for 4% of the time, Pallas kernels for 4%

profile of v5, /device:TPU:1, one launch (start us, length us, event | category | flops | bytes accessed | tf_op | source)
XLA Modules:
  0.0 176.0 jit_solution(2648606400980661162)
XLA Ops:
  0.6 6.4 %shard_map.67 = (bf16[736,128]{1,0:T(8,128)(2,1)}, bf16[896,128]{1,0:T(8,128)(2,1)}, bf16[896,128]{1,0:T(8,128)(2,1)}, bf16[1792,128]{1,0:T(8,128)(2,1)}, bf16[7...) custom-call(s32[2]{0:T(128)} %len_ref.1, ...), custom_call_target="tpu_custom_call" | custom-call | tf_op jit(solution)/shard_map/pallas_call | solution.py:87
  7.1 8.8 %collective-permute-start = (bf16[960,128]{1,0:T(8,128)(2,1)}, bf16[960,128]{1,0:T(8,128)(2,1)S(1)}, u32[]{:S(2)}, u32[]{:S(2)}) collective-permute-start(bf16[960,128]{1,0:T(8,128)(2,1)} %get-tuple-element.47), channel_id=1, source_target_pairs={{0,1},{1,0},{32,33},{33,32},{2,3},{3,2},{34,35},{35,34},{4,5},{5,4... | collective-permute-start | bytes 737288 | tf_op jit(solution)/shard_map/ppermute | solution.py:231
  17.2 2.3 %collective-permute-start.1 = (bf16[7168,128]{1,0:T(8,128)(2,1)}, bf16[7168,128]{1,0:T(8,128)(2,1)S(1)}, u32[]{:S(2)}, u32[]{:S(2)}) collective-permute-start(bf16[7168,128]{1,0:T(8,128)(2,1)} %get-tuple-element.48), channel_id=1, source_target_pairs={{0,1},{1,0},{32,33},{33,32},{2,3},{3,2},{34,35},{35,34},{4,5},{5,4... | collective-permute-start | bytes 5505032 | tf_op jit(solution)/shard_map/ppermute | solution.py:231
  21.4 4.9 %collective-permute-start.5 = (bf16[736,128]{1,0:T(8,128)(2,1)S(1)}, bf16[736,128]{1,0:T(8,128)(2,1)S(1)}, u32[]{:S(2)}, u32[]{:S(2)}) collective-permute-start(bf16[736,128]{1,0:T(8,128)(2,1)S(1)} %slice.145), channel_id=1, source_target_pairs={{0,32},{1,33},{32,0},{33,1},{2,34},{3,35},{34,2},{35,3},{4,36},{5,... | collective-permute-start | bytes 565256 | tf_op jit(solution)/shard_map/ppermute | solution.py:231
  28.3 4.9 %collective-permute-start.3 = (bf16[896,128]{1,0:T(8,128)(2,1)S(1)}, bf16[896,128]{1,0:T(8,128)(2,1)S(1)}, u32[]{:S(2)}, u32[]{:S(2)}) collective-permute-start(bf16[896,128]{1,0:T(8,128)(2,1)S(1)} %get-tuple-element.51), channel_id=1, source_target_pairs={{0,32},{1,33},{32,0},{33,1},{2,34},{3,35},{34,2},{35,3},{4,36},{5,... | collective-permute-start | bytes 688136 | tf_op jit(solution)/shard_map/ppermute | solution.py:231
  34.7 6.0 %collective-permute-start.6 = (f16[224,1024]{1,0:T(8,128)(2,1)S(1)}, f16[224,1024]{1,0:T(8,128)(2,1)S(1)}, u32[]{:S(2)}, u32[]{:S(2)}) collective-permute-start(f16[224,1024]{1,0:T(8,128)(2,1)S(1)} %convert_element_type.141), channel_id=1, source_target_pairs={{0,2},{1,31},{2,4},{3,1},{4,6},{5,3},{6,8},{7,5},{8,10},{9,7},{10,... | collective-permute-start | bytes 1376264 | tf_op jit(solution)/shard_map/ppermute | solution.py:258
  40.8 2.3 %collective-permute-done.3.d_ref = bf16[896,128]{1,0:T(8,128)(2,1)S(1)} collective-permute-done((bf16[896,128]{1,0:T(8,128)(2,1)S(1)}, bf16[896,128]{1,0:T(8,128)(2,1)S(1)}, u32[]{:S(2)}, u32[]{:S(2)}) %collective-permute-start.3) | collective-permute-done | bytes 229408 | tf_op jit(solution)/shard_map/ppermute | solution.py:231
  47.3 5.6 %collective-permute-start.7 = (f16[160,1024]{1,0:T(8,128)(2,1)}, f16[160,1024]{1,0:T(8,128)(2,1)}, u32[]{:S(2)}, u32[]{:S(2)}) collective-permute-start(f16[160,1024]{1,0:T(8,128)(2,1)} %fusion.6), channel_id=1, source_target_pairs={{0,2},{1,31},{2,4},{3,1},{4,6},{5,3},{6,8},{7,5},{8,10},{9,7},{10,... | collective-permute-start | bytes 983048 | tf_op jit(solution)/shard_map/ppermute | solution.py:258
  54.0 2.2 %collective-permute-start.10 = (f16[144,1024]{1,0:T(8,128)(2,1)}, f16[144,1024]{1,0:T(8,128)(2,1)}, u32[]{:S(2)}, u32[]{:S(2)}) collective-permute-start(f16[144,1024]{1,0:T(8,128)(2,1)} %get-tuple-element.87), channel_id=1, source_target_pairs={{0,2},{1,31},{2,4},{3,1},{4,6},{5,3},{6,8},{7,5},{8,10},{9,7},{10,... | collective-permute-start | bytes 884744 | tf_op jit(solution)/shard_map/ppermute | solution.py:258
  56.1 4.5 %collective-permute-start.11 = (bf16[896,128]{1,0:T(8,128)(2,1)}, bf16[896,128]{1,0:T(8,128)(2,1)S(1)}, u32[]{:S(2)}, u32[]{:S(2)}) collective-permute-start(bf16[896,128]{1,0:T(8,128)(2,1)} %get-tuple-element.64), channel_id=1, source_target_pairs={{0,32},{1,33},{32,0},{33,1},{2,34},{3,35},{34,2},{35,3},{4,36},{5,... | collective-permute-start | bytes 688136 | tf_op jit(solution)/shard_map/ppermute | solution.py:231
  60.7 2.3 %collective-permute-start.12 = (bf16[896,128]{1,0:T(8,128)(2,1)S(1)}, bf16[896,128]{1,0:T(8,128)(2,1)S(1)}, u32[]{:S(2)}, u32[]{:S(2)}) collective-permute-start(bf16[896,128]{1,0:T(8,128)(2,1)S(1)} %get-tuple-element.65), channel_id=1, source_target_pairs={{0,32},{1,33},{32,0},{33,1},{2,34},{3,35},{34,2},{35,3},{4,36},{5,... | collective-permute-start | bytes 688136 | tf_op jit(solution)/shard_map/ppermute | solution.py:231
  63.0 4.5 %collective-permute-start.20 = (bf16[1792,128]{1,0:T(8,128)(2,1)S(1)}, bf16[1792,128]{1,0:T(8,128)(2,1)S(1)}, u32[]{:S(2)}, u32[]{:S(2)}) collective-permute-start(bf16[1792,128]{1,0:T(8,128)(2,1)S(1)} %slice.162), channel_id=1, source_target_pairs={{0,32},{1,33},{32,0},{33,1},{2,34},{3,35},{34,2},{35,3},{4,36},{5,... | collective-permute-start | bytes 1376264 | tf_op jit(solution)/shard_map/ppermute | solution.py:231
  67.5 2.6 %collective-permute-start.9 = (f16[144,1024]{1,0:T(8,128)(2,1)}, f16[144,1024]{1,0:T(8,128)(2,1)S(1)}, u32[]{:S(2)}, u32[]{:S(2)}) collective-permute-start(f16[144,1024]{1,0:T(8,128)(2,1)} %get-tuple-element.88), channel_id=1, source_target_pairs={{0,2},{1,31},{2,4},{3,1},{4,6},{5,3},{6,8},{7,5},{8,10},{9,7},{10,... | collective-permute-start | bytes 884744 | tf_op jit(solution)/shard_map/ppermute | solution.py:258
  72.1 4.6 %collective-permute-start.19 = (bf16[1792,128]{1,0:T(8,128)(2,1)}, bf16[1792,128]{1,0:T(8,128)(2,1)S(1)}, u32[]{:S(2)}, u32[]{:S(2)}) collective-permute-start(bf16[1792,128]{1,0:T(8,128)(2,1)} %get-tuple-element.75), channel_id=1, source_target_pairs={{0,32},{1,33},{32,0},{33,1},{2,34},{3,35},{34,2},{35,3},{4,36},{5,... | collective-permute-start | bytes 1376264 | tf_op jit(solution)/shard_map/ppermute | solution.py:231
  83.1 4.9 %collective-permute-start.14 = (f16[144,1024]{1,0:T(8,128)(2,1)S(1)}, f16[144,1024]{1,0:T(8,128)(2,1)S(1)}, u32[]{:S(2)}, u32[]{:S(2)}) collective-permute-start(f16[144,1024]{1,0:T(8,128)(2,1)S(1)} %fusion.17), channel_id=1, source_target_pairs={{0,2},{1,31},{2,4},{3,1},{4,6},{5,3},{6,8},{7,5},{8,10},{9,7},{10,... | collective-permute-start | bytes 884744 | tf_op jit(solution)/shard_map/ppermute | solution.py:258
  89.8 2.1 %collective-permute-start.13 = (f16[160,1024]{1,0:T(8,128)(2,1)S(1)}, f16[160,1024]{1,0:T(8,128)(2,1)S(1)}, u32[]{:S(2)}, u32[]{:S(2)}) collective-permute-start(f16[160,1024]{1,0:T(8,128)(2,1)S(1)} %fusion.4), channel_id=1, source_target_pairs={{0,2},{1,31},{2,4},{3,1},{4,6},{5,3},{6,8},{7,5},{8,10},{9,7},{10,... | collective-permute-start | bytes 983048 | tf_op jit(solution)/shard_map/ppermute | solution.py:258
  94.0 2.8 %collective-permute-start.17 = (f16[144,1024]{1,0:T(8,128)(2,1)S(1)}, f16[144,1024]{1,0:T(8,128)(2,1)S(1)}, u32[]{:S(2)}, u32[]{:S(2)}) collective-permute-start(f16[144,1024]{1,0:T(8,128)(2,1)S(1)} %fusion.15), channel_id=1, source_target_pairs={{0,2},{1,31},{2,4},{3,1},{4,6},{5,3},{6,8},{7,5},{8,10},{9,7},{10,... | collective-permute-start | bytes 884744 | tf_op jit(solution)/shard_map/ppermute | solution.py:258
  98.1 2.8 %collective-permute-start.16 = (f16[160,1024]{1,0:T(8,128)(2,1)S(1)}, f16[160,1024]{1,0:T(8,128)(2,1)S(1)}, u32[]{:S(2)}, u32[]{:S(2)}) collective-permute-start(f16[160,1024]{1,0:T(8,128)(2,1)S(1)} %fusion.3), channel_id=1, source_target_pairs={{0,2},{1,31},{2,4},{3,1},{4,6},{5,3},{6,8},{7,5},{8,10},{9,7},{10,... | collective-permute-start | bytes 983048 | tf_op jit(solution)/shard_map/ppermute | solution.py:258
  101.3 2.8 %collective-permute-start.23 = (f16[144,1024]{1,0:T(8,128)(2,1)S(1)}, f16[144,1024]{1,0:T(8,128)(2,1)S(1)}, u32[]{:S(2)}, u32[]{:S(2)}) collective-permute-start(f16[144,1024]{1,0:T(8,128)(2,1)S(1)} %fusion.14), channel_id=1, source_target_pairs={{0,2},{1,31},{2,4},{3,1},{4,6},{5,3},{6,8},{7,5},{8,10},{9,7},{10,... | collective-permute-start | bytes 884744 | tf_op jit(solution)/shard_map/ppermute | solution.py:258
  104.2 3.0 %collective-permute-start.22 = (f16[144,1024]{1,0:T(8,128)(2,1)S(1)}, f16[144,1024]{1,0:T(8,128)(2,1)S(1)}, u32[]{:S(2)}, u32[]{:S(2)}) collective-permute-start(f16[144,1024]{1,0:T(8,128)(2,1)S(1)} %fusion.13), channel_id=1, source_target_pairs={{0,2},{1,31},{2,4},{3,1},{4,6},{5,3},{6,8},{7,5},{8,10},{9,7},{10,... | collective-permute-start | bytes 884744 | tf_op jit(solution)/shard_map/ppermute | solution.py:258
  111.1 2.8 %collective-permute-start.26 = (f16[144,1024]{1,0:T(8,128)(2,1)S(1)}, f16[144,1024]{1,0:T(8,128)(2,1)S(1)}, u32[]{:S(2)}, u32[]{:S(2)}) collective-permute-start(f16[144,1024]{1,0:T(8,128)(2,1)S(1)} %fusion.12), channel_id=1, source_target_pairs={{0,2},{1,31},{2,4},{3,1},{4,6},{5,3},{6,8},{7,5},{8,10},{9,7},{10,... | collective-permute-start | bytes 884744 | tf_op jit(solution)/shard_map/ppermute | solution.py:258
  114.3 2.8 %collective-permute-start.25 = (f16[144,1024]{1,0:T(8,128)(2,1)S(1)}, f16[144,1024]{1,0:T(8,128)(2,1)S(1)}, u32[]{:S(2)}, u32[]{:S(2)}) collective-permute-start(f16[144,1024]{1,0:T(8,128)(2,1)S(1)} %fusion.11), channel_id=1, source_target_pairs={{0,2},{1,31},{2,4},{3,1},{4,6},{5,3},{6,8},{7,5},{8,10},{9,7},{10,... | collective-permute-start | bytes 884744 | tf_op jit(solution)/shard_map/ppermute | solution.py:258
  121.0 2.8 %collective-permute-start.28 = (f16[144,1024]{1,0:T(8,128)(2,1)S(1)}, f16[144,1024]{1,0:T(8,128)(2,1)S(1)}, u32[]{:S(2)}, u32[]{:S(2)}) collective-permute-start(f16[144,1024]{1,0:T(8,128)(2,1)S(1)} %fusion.10), channel_id=1, source_target_pairs={{0,2},{1,31},{2,4},{3,1},{4,6},{5,3},{6,8},{7,5},{8,10},{9,7},{10,... | collective-permute-start | bytes 884744 | tf_op jit(solution)/shard_map/ppermute | solution.py:258
  124.1 4.2 %collective-permute-start.30 = (f16[144,1024]{1,0:T(8,128)(2,1)S(1)}, f16[144,1024]{1,0:T(8,128)(2,1)S(1)}, u32[]{:S(2)}, u32[]{:S(2)}) collective-permute-start(f16[144,1024]{1,0:T(8,128)(2,1)S(1)} %fusion.9), channel_id=1, source_target_pairs={{0,2},{1,31},{2,4},{3,1},{4,6},{5,3},{6,8},{7,5},{8,10},{9,7},{10,... | collective-permute-start | bytes 884744 | tf_op jit(solution)/shard_map/ppermute | solution.py:258
  128.5 2.2 %collective-permute-done.28 = f16[144,1024]{1,0:T(8,128)(2,1)S(1)} collective-permute-done((f16[144,1024]{1,0:T(8,128)(2,1)S(1)}, f16[144,1024]{1,0:T(8,128)(2,1)S(1)}, u32[]{:S(2)}, u32[]{:S(2)}) %collective-permute-start.28) | collective-permute-done | bytes 294944 | tf_op jit(solution)/shard_map/ppermute | solution.py:258
  130.9 2.9 %collective-permute-done.30 = f16[144,1024]{1,0:T(8,128)(2,1)S(1)} collective-permute-done((f16[144,1024]{1,0:T(8,128)(2,1)S(1)}, f16[144,1024]{1,0:T(8,128)(2,1)S(1)}, u32[]{:S(2)}, u32[]{:S(2)}) %collective-permute-start.30) | collective-permute-done | bytes 294944 | tf_op jit(solution)/shard_map/ppermute | solution.py:258
  134.8 11.8 %collective-permute-start.32 = (f16[448,512]{1,0:T(8,128)(2,1)S(1)}, f16[448,512]{1,0:T(8,128)(2,1)S(1)}, u32[]{:S(2)}, u32[]{:S(2)}) collective-permute-start(f16[448,512]{1,0:T(8,128)(2,1)S(1)} %pad_maximum_fusion), channel_id=1, source_target_pairs={{0,3},{1,30},{2,5},{3,0},{4,7},{5,2},{6,9},{7,4},{8,11},{9,6},{10,... | collective-permute-start | bytes 1376264 | tf_op jit(solution)/shard_map/ppermute | solution.py:258
  146.6 2.5 %collective-permute-start.27 = (f16[160,512]{1,0:T(8,128)(2,1)S(1)}, f16[160,512]{1,0:T(8,128)(2,1)S(1)}, u32[]{:S(2)}, u32[]{:S(2)}) collective-permute-start(f16[160,512]{1,0:T(8,128)(2,1)S(1)} %get-tuple-element.91), channel_id=1, source_target_pairs={{0,2},{1,31},{2,4},{3,1},{4,6},{5,3},{6,8},{7,5},{8,10},{9,7},{10,... | collective-permute-start | bytes 491528 | tf_op jit(solution)/shard_map/ppermute | solution.py:258
  149.1 2.4 %collective-permute-start.31 = (f16[144,512]{1,0:T(8,128)(2,1)}, f16[144,512]{1,0:T(8,128)(2,1)S(1)}, u32[]{:S(2)}, u32[]{:S(2)}) collective-permute-start(f16[144,512]{1,0:T(8,128)(2,1)} %get-tuple-element.95), channel_id=1, source_target_pairs={{0,2},{1,31},{2,4},{3,1},{4,6},{5,3},{6,8},{7,5},{8,10},{9,7},{10,... | collective-permute-start | bytes 442376 | tf_op jit(solution)/shard_map/ppermute | solution.py:258
  151.6 3.5 %collective-permute-start.29 = (f16[144,512]{1,0:T(8,128)(2,1)S(1)}, f16[144,512]{1,0:T(8,128)(2,1)S(1)}, u32[]{:S(2)}, u32[]{:S(2)}) collective-permute-start(f16[144,512]{1,0:T(8,128)(2,1)S(1)} %get-tuple-element.93), channel_id=1, source_target_pairs={{0,2},{1,31},{2,4},{3,1},{4,6},{5,3},{6,8},{7,5},{8,10},{9,7},{10,... | collective-permute-start | bytes 442376 | tf_op jit(solution)/shard_map/ppermute | solution.py:258
  158.8 14.4 %all_to_all.5 = f16[16,28,512]{2,1,0:T(8,128)(2,1)S(1)} all-to-all(f16[16,28,512]{2,1,0:T(8,128)(2,1)S(1)} %reshape.12), channel_id=1, replica_groups=mesh['ylo'=2,'x'=4,'yhi'=2,'z'=16,'core'=2] {'ylo','x','core'}, dimensions={0} | all-to-all | bytes 917504 | tf_op jit(solution)/shard_map/all_to_all | solution.py:282
  173.6 2.4 %shard_map.73 = (f32[28,512]{1,0:T(8,128)}, f32[28,512]{1,0:T(8,128)}, f32[28,512]{1,0:T(8,128)}) custom-call(f32[16,32,512]{2,1,0:T(8,128)S(1)} %pad.6.g_ref, bf16[28,512]{1,0:T(8,128)(2,1)S(1)} %copy-done.2), custom_call_target="tpu_custom_call" | custom-call | tf_op jit(solution)/shard_map/pallas_call | solution.py:207
  (95 shorter events, 38.7 us)
Async XLA Ops:
  7.1 10.1 %collective-permute-start = (bf16[960,128]{1,0:T(8,128)(2,1)}, bf16[960,128]{1,0:T(8,128)(2,1)S(1)}, u32[]{:S(2)}, u32[]{:S(2)}) collective-permute-start(bf16[960,128]{1,0:T(8,128)(2,1)} %get-tuple-element.47), channel_id=1, source_target_pairs={{0,1},{1,0},{32,33},{33,32},{2,3},{3,2},{34,35},{35,34},{4,5},{5,4... | collective-permute-start | bytes 737288 | tf_op jit(solution)/shard_map/ppermute | solution.py:231
  17.2 11.0 %collective-permute-start.1 = (bf16[7168,128]{1,0:T(8,128)(2,1)}, bf16[7168,128]{1,0:T(8,128)(2,1)S(1)}, u32[]{:S(2)}, u32[]{:S(2)}) collective-permute-start(bf16[7168,128]{1,0:T(8,128)(2,1)} %get-tuple-element.48), channel_id=1, source_target_pairs={{0,1},{1,0},{32,33},{33,32},{2,3},{3,2},{34,35},{35,34},{4,5},{5,4... | collective-permute-start | bytes 5505032 | tf_op jit(solution)/shard_map/ppermute | solution.py:231
  19.4 13.7 %collective-permute-start.4 = (bf16[736,128]{1,0:T(8,128)(2,1)}, bf16[736,128]{1,0:T(8,128)(2,1)S(1)}, u32[]{:S(2)}, u32[]{:S(2)}) collective-permute-start(bf16[736,128]{1,0:T(8,128)(2,1)} %get-tuple-element.53), channel_id=1, source_target_pairs={{0,32},{1,33},{32,0},{33,1},{2,34},{3,35},{34,2},{35,3},{4,36},{5,... | collective-permute-start | bytes 565256 | tf_op jit(solution)/shard_map/ppermute | solution.py:231
  21.4 11.9 %collective-permute-start.5 = (bf16[736,128]{1,0:T(8,128)(2,1)S(1)}, bf16[736,128]{1,0:T(8,128)(2,1)S(1)}, u32[]{:S(2)}, u32[]{:S(2)}) collective-permute-start(bf16[736,128]{1,0:T(8,128)(2,1)S(1)} %slice.145), channel_id=1, source_target_pairs={{0,32},{1,33},{32,0},{33,1},{2,34},{3,35},{34,2},{35,3},{4,36},{5,... | collective-permute-start | bytes 565256 | tf_op jit(solution)/shard_map/ppermute | solution.py:231
  26.3 16.8 %collective-permute-start.2 = (bf16[896,128]{1,0:T(8,128)(2,1)}, bf16[896,128]{1,0:T(8,128)(2,1)S(1)}, u32[]{:S(2)}, u32[]{:S(2)}) collective-permute-start(bf16[896,128]{1,0:T(8,128)(2,1)} %get-tuple-element.50), channel_id=1, source_target_pairs={{0,32},{1,33},{32,0},{33,1},{2,34},{3,35},{34,2},{35,3},{4,36},{5,... | collective-permute-start | bytes 688136 | tf_op jit(solution)/shard_map/ppermute | solution.py:231
  28.3 14.9 %collective-permute-start.3 = (bf16[896,128]{1,0:T(8,128)(2,1)S(1)}, bf16[896,128]{1,0:T(8,128)(2,1)S(1)}, u32[]{:S(2)}, u32[]{:S(2)}) collective-permute-start(bf16[896,128]{1,0:T(8,128)(2,1)S(1)} %get-tuple-element.51), channel_id=1, source_target_pairs={{0,32},{1,33},{32,0},{33,1},{2,34},{3,35},{34,2},{35,3},{4,36},{5,... | collective-permute-start | bytes 688136 | tf_op jit(solution)/shard_map/ppermute | solution.py:231
  34.7 11.4 %collective-permute-start.6 = (f16[224,1024]{1,0:T(8,128)(2,1)S(1)}, f16[224,1024]{1,0:T(8,128)(2,1)S(1)}, u32[]{:S(2)}, u32[]{:S(2)}) collective-permute-start(f16[224,1024]{1,0:T(8,128)(2,1)S(1)} %convert_element_type.141), channel_id=1, source_target_pairs={{0,2},{1,31},{2,4},{3,1},{4,6},{5,3},{6,8},{7,5},{8,10},{9,7},{10,... | collective-permute-start | bytes 1376264 | tf_op jit(solution)/shard_map/ppermute | solution.py:258
  47.3 20.2 %collective-permute-start.7 = (f16[160,1024]{1,0:T(8,128)(2,1)}, f16[160,1024]{1,0:T(8,128)(2,1)}, u32[]{:S(2)}, u32[]{:S(2)}) collective-permute-start(f16[160,1024]{1,0:T(8,128)(2,1)} %fusion.6), channel_id=1, source_target_pairs={{0,2},{1,31},{2,4},{3,1},{4,6},{5,3},{6,8},{7,5},{8,10},{9,7},{10,... | collective-permute-start | bytes 983048 | tf_op jit(solution)/shard_map/ppermute | solution.py:258
  54.0 22.8 %collective-permute-start.10 = (f16[144,1024]{1,0:T(8,128)(2,1)}, f16[144,1024]{1,0:T(8,128)(2,1)}, u32[]{:S(2)}, u32[]{:S(2)}) collective-permute-start(f16[144,1024]{1,0:T(8,128)(2,1)} %get-tuple-element.87), channel_id=1, source_target_pairs={{0,2},{1,31},{2,4},{3,1},{4,6},{5,3},{6,8},{7,5},{8,10},{9,7},{10,... | collective-permute-start | bytes 884744 | tf_op jit(solution)/shard_map/ppermute | solution.py:258
  56.1 27.0 %collective-permute-start.11 = (bf16[896,128]{1,0:T(8,128)(2,1)}, bf16[896,128]{1,0:T(8,128)(2,1)S(1)}, u32[]{:S(2)}, u32[]{:S(2)}) collective-permute-start(bf16[896,128]{1,0:T(8,128)(2,1)} %get-tuple-element.64), channel_id=1, source_target_pairs={{0,32},{1,33},{32,0},{33,1},{2,34},{3,35},{34,2},{35,3},{4,36},{5,... | collective-permute-start | bytes 688136 | tf_op jit(solution)/shard_map/ppermute | solution.py:231
  60.7 11.4 %collective-permute-start.12 = (bf16[896,128]{1,0:T(8,128)(2,1)S(1)}, bf16[896,128]{1,0:T(8,128)(2,1)S(1)}, u32[]{:S(2)}, u32[]{:S(2)}) collective-permute-start(bf16[896,128]{1,0:T(8,128)(2,1)S(1)} %get-tuple-element.65), channel_id=1, source_target_pairs={{0,32},{1,33},{32,0},{33,1},{2,34},{3,35},{34,2},{35,3},{4,36},{5,... | collective-permute-start | bytes 688136 | tf_op jit(solution)/shard_map/ppermute | solution.py:231
  63.0 38.0 %collective-permute-start.20 = (bf16[1792,128]{1,0:T(8,128)(2,1)S(1)}, bf16[1792,128]{1,0:T(8,128)(2,1)S(1)}, u32[]{:S(2)}, u32[]{:S(2)}) collective-permute-start(bf16[1792,128]{1,0:T(8,128)(2,1)S(1)} %slice.162), channel_id=1, source_target_pairs={{0,32},{1,33},{32,0},{33,1},{2,34},{3,35},{34,2},{35,3},{4,36},{5,... | collective-permute-start | bytes 1376264 | tf_op jit(solution)/shard_map/ppermute | solution.py:231
  67.5 12.4 %collective-permute-start.9 = (f16[144,1024]{1,0:T(8,128)(2,1)}, f16[144,1024]{1,0:T(8,128)(2,1)S(1)}, u32[]{:S(2)}, u32[]{:S(2)}) collective-permute-start(f16[144,1024]{1,0:T(8,128)(2,1)} %get-tuple-element.88), channel_id=1, source_target_pairs={{0,2},{1,31},{2,4},{3,1},{4,6},{5,3},{6,8},{7,5},{8,10},{9,7},{10,... | collective-permute-start | bytes 884744 | tf_op jit(solution)/shard_map/ppermute | solution.py:258
  72.1 35.2 %collective-permute-start.19 = (bf16[1792,128]{1,0:T(8,128)(2,1)}, bf16[1792,128]{1,0:T(8,128)(2,1)S(1)}, u32[]{:S(2)}, u32[]{:S(2)}) collective-permute-start(bf16[1792,128]{1,0:T(8,128)(2,1)} %get-tuple-element.75), channel_id=1, source_target_pairs={{0,32},{1,33},{32,0},{33,1},{2,34},{3,35},{34,2},{35,3},{4,36},{5,... | collective-permute-start | bytes 1376264 | tf_op jit(solution)/shard_map/ppermute | solution.py:231
  76.7 13.0 %collective-permute-start.8 = (f16[160,1024]{1,0:T(8,128)(2,1)S(1)}, f16[160,1024]{1,0:T(8,128)(2,1)S(1)}, u32[]{:S(2)}, u32[]{:S(2)}) collective-permute-start(f16[160,1024]{1,0:T(8,128)(2,1)S(1)} %fusion.5), channel_id=1, source_target_pairs={{0,2},{1,31},{2,4},{3,1},{4,6},{5,3},{6,8},{7,5},{8,10},{9,7},{10,... | collective-permute-start | bytes 983048 | tf_op jit(solution)/shard_map/ppermute | solution.py:258
  79.9 12.0 %collective-permute-start.15 = (f16[144,1024]{1,0:T(8,128)(2,1)S(1)}, f16[144,1024]{1,0:T(8,128)(2,1)S(1)}, u32[]{:S(2)}, u32[]{:S(2)}) collective-permute-start(f16[144,1024]{1,0:T(8,128)(2,1)S(1)} %fusion.18), channel_id=1, source_target_pairs={{0,2},{1,31},{2,4},{3,1},{4,6},{5,3},{6,8},{7,5},{8,10},{9,7},{10,... | collective-permute-start | bytes 884744 | tf_op jit(solution)/shard_map/ppermute | solution.py:258
  83.1 10.8 %collective-permute-start.14 = (f16[144,1024]{1,0:T(8,128)(2,1)S(1)}, f16[144,1024]{1,0:T(8,128)(2,1)S(1)}, u32[]{:S(2)}, u32[]{:S(2)}) collective-permute-start(f16[144,1024]{1,0:T(8,128)(2,1)S(1)} %fusion.17), channel_id=1, source_target_pairs={{0,2},{1,31},{2,4},{3,1},{4,6},{5,3},{6,8},{7,5},{8,10},{9,7},{10,... | collective-permute-start | bytes 884744 | tf_op jit(solution)/shard_map/ppermute | solution.py:258
  89.8 8.2 %collective-permute-start.13 = (f16[160,1024]{1,0:T(8,128)(2,1)S(1)}, f16[160,1024]{1,0:T(8,128)(2,1)S(1)}, u32[]{:S(2)}, u32[]{:S(2)}) collective-permute-start(f16[160,1024]{1,0:T(8,128)(2,1)S(1)} %fusion.4), channel_id=1, source_target_pairs={{0,2},{1,31},{2,4},{3,1},{4,6},{5,3},{6,8},{7,5},{8,10},{9,7},{10,... | collective-permute-start | bytes 983048 | tf_op jit(solution)/shard_map/ppermute | solution.py:258
  92.0 9.2 %collective-permute-start.18 = (f16[144,1024]{1,0:T(8,128)(2,1)S(1)}, f16[144,1024]{1,0:T(8,128)(2,1)S(1)}, u32[]{:S(2)}, u32[]{:S(2)}) collective-permute-start(f16[144,1024]{1,0:T(8,128)(2,1)S(1)} %fusion.16), channel_id=1, source_target_pairs={{0,2},{1,31},{2,4},{3,1},{4,6},{5,3},{6,8},{7,5},{8,10},{9,7},{10,... | collective-permute-start | bytes 884744 | tf_op jit(solution)/shard_map/ppermute | solution.py:258
  94.0 10.1 %collective-permute-start.17 = (f16[144,1024]{1,0:T(8,128)(2,1)S(1)}, f16[144,1024]{1,0:T(8,128)(2,1)S(1)}, u32[]{:S(2)}, u32[]{:S(2)}) collective-permute-start(f16[144,1024]{1,0:T(8,128)(2,1)S(1)} %fusion.15), channel_id=1, source_target_pairs={{0,2},{1,31},{2,4},{3,1},{4,6},{5,3},{6,8},{7,5},{8,10},{9,7},{10,... | collective-permute-start | bytes 884744 | tf_op jit(solution)/shard_map/ppermute | solution.py:258
  98.1 10.9 %collective-permute-start.16 = (f16[160,1024]{1,0:T(8,128)(2,1)S(1)}, f16[160,1024]{1,0:T(8,128)(2,1)S(1)}, u32[]{:S(2)}, u32[]{:S(2)}) collective-permute-start(f16[160,1024]{1,0:T(8,128)(2,1)S(1)} %fusion.3), channel_id=1, source_target_pairs={{0,2},{1,31},{2,4},{3,1},{4,6},{5,3},{6,8},{7,5},{8,10},{9,7},{10,... | collective-permute-start | bytes 983048 | tf_op jit(solution)/shard_map/ppermute | solution.py:258
  101.3 9.8 %collective-permute-start.23 = (f16[144,1024]{1,0:T(8,128)(2,1)S(1)}, f16[144,1024]{1,0:T(8,128)(2,1)S(1)}, u32[]{:S(2)}, u32[]{:S(2)}) collective-permute-start(f16[144,1024]{1,0:T(8,128)(2,1)S(1)} %fusion.14), channel_id=1, source_target_pairs={{0,2},{1,31},{2,4},{3,1},{4,6},{5,3},{6,8},{7,5},{8,10},{9,7},{10,... | collective-permute-start | bytes 884744 | tf_op jit(solution)/shard_map/ppermute | solution.py:258
  104.2 10.0 %collective-permute-start.22 = (f16[144,1024]{1,0:T(8,128)(2,1)S(1)}, f16[144,1024]{1,0:T(8,128)(2,1)S(1)}, u32[]{:S(2)}, u32[]{:S(2)}) collective-permute-start(f16[144,1024]{1,0:T(8,128)(2,1)S(1)} %fusion.13), channel_id=1, source_target_pairs={{0,2},{1,31},{2,4},{3,1},{4,6},{5,3},{6,8},{7,5},{8,10},{9,7},{10,... | collective-permute-start | bytes 884744 | tf_op jit(solution)/shard_map/ppermute | solution.py:258
  109.1 9.7 %collective-permute-start.21 = (f16[160,1024]{1,0:T(8,128)(2,1)S(1)}, f16[160,1024]{1,0:T(8,128)(2,1)S(1)}, u32[]{:S(2)}, u32[]{:S(2)}) collective-permute-start(f16[160,1024]{1,0:T(8,128)(2,1)S(1)} %fusion.2), channel_id=1, source_target_pairs={{0,2},{1,31},{2,4},{3,1},{4,6},{5,3},{6,8},{7,5},{8,10},{9,7},{10,... | collective-permute-start | bytes 983048 | tf_op jit(solution)/shard_map/ppermute | solution.py:258
  111.1 9.7 %collective-permute-start.26 = (f16[144,1024]{1,0:T(8,128)(2,1)S(1)}, f16[144,1024]{1,0:T(8,128)(2,1)S(1)}, u32[]{:S(2)}, u32[]{:S(2)}) collective-permute-start(f16[144,1024]{1,0:T(8,128)(2,1)S(1)} %fusion.12), channel_id=1, source_target_pairs={{0,2},{1,31},{2,4},{3,1},{4,6},{5,3},{6,8},{7,5},{8,10},{9,7},{10,... | collective-permute-start | bytes 884744 | tf_op jit(solution)/shard_map/ppermute | solution.py:258
  114.3 9.7 %collective-permute-start.25 = (f16[144,1024]{1,0:T(8,128)(2,1)S(1)}, f16[144,1024]{1,0:T(8,128)(2,1)S(1)}, u32[]{:S(2)}, u32[]{:S(2)}) collective-permute-start(f16[144,1024]{1,0:T(8,128)(2,1)S(1)} %fusion.11), channel_id=1, source_target_pairs={{0,2},{1,31},{2,4},{3,1},{4,6},{5,3},{6,8},{7,5},{8,10},{9,7},{10,... | collective-permute-start | bytes 884744 | tf_op jit(solution)/shard_map/ppermute | solution.py:258
  118.9 9.4 %collective-permute-start.24 = (f16[160,1024]{1,0:T(8,128)(2,1)S(1)}, f16[160,1024]{1,0:T(8,128)(2,1)S(1)}, u32[]{:S(2)}, u32[]{:S(2)}) collective-permute-start(f16[160,1024]{1,0:T(8,128)(2,1)S(1)} %fusion.1), channel_id=1, source_target_pairs={{0,2},{1,31},{2,4},{3,1},{4,6},{5,3},{6,8},{7,5},{8,10},{9,7},{10,... | collective-permute-start | bytes 983048 | tf_op jit(solution)/shard_map/ppermute | solution.py:258
  121.0 9.7 %collective-permute-start.28 = (f16[144,1024]{1,0:T(8,128)(2,1)S(1)}, f16[144,1024]{1,0:T(8,128)(2,1)S(1)}, u32[]{:S(2)}, u32[]{:S(2)}) collective-permute-start(f16[144,1024]{1,0:T(8,128)(2,1)S(1)} %fusion.10), channel_id=1, source_target_pairs={{0,2},{1,31},{2,4},{3,1},{4,6},{5,3},{6,8},{7,5},{8,10},{9,7},{10,... | collective-permute-start | bytes 884744 | tf_op jit(solution)/shard_map/ppermute | solution.py:258
  124.1 9.7 %collective-permute-start.30 = (f16[144,1024]{1,0:T(8,128)(2,1)S(1)}, f16[144,1024]{1,0:T(8,128)(2,1)S(1)}, u32[]{:S(2)}, u32[]{:S(2)}) collective-permute-start(f16[144,1024]{1,0:T(8,128)(2,1)S(1)} %fusion.9), channel_id=1, source_target_pairs={{0,2},{1,31},{2,4},{3,1},{4,6},{5,3},{6,8},{7,5},{8,10},{9,7},{10,... | collective-permute-start | bytes 884744 | tf_op jit(solution)/shard_map/ppermute | solution.py:258
  134.8 23.6 %collective-permute-start.32 = (f16[448,512]{1,0:T(8,128)(2,1)S(1)}, f16[448,512]{1,0:T(8,128)(2,1)S(1)}, u32[]{:S(2)}, u32[]{:S(2)}) collective-permute-start(f16[448,512]{1,0:T(8,128)(2,1)S(1)} %pad_maximum_fusion), channel_id=1, source_target_pairs={{0,3},{1,30},{2,5},{3,0},{4,7},{5,2},{6,9},{7,4},{8,11},{9,6},{10,... | collective-permute-start | bytes 1376264 | tf_op jit(solution)/shard_map/ppermute | solution.py:258
  146.6 11.8 %collective-permute-start.27 = (f16[160,512]{1,0:T(8,128)(2,1)S(1)}, f16[160,512]{1,0:T(8,128)(2,1)S(1)}, u32[]{:S(2)}, u32[]{:S(2)}) collective-permute-start(f16[160,512]{1,0:T(8,128)(2,1)S(1)} %get-tuple-element.91), channel_id=1, source_target_pairs={{0,2},{1,31},{2,4},{3,1},{4,6},{5,3},{6,8},{7,5},{8,10},{9,7},{10,... | collective-permute-start | bytes 491528 | tf_op jit(solution)/shard_map/ppermute | solution.py:258
  149.1 7.8 %collective-permute-start.31 = (f16[144,512]{1,0:T(8,128)(2,1)}, f16[144,512]{1,0:T(8,128)(2,1)S(1)}, u32[]{:S(2)}, u32[]{:S(2)}) collective-permute-start(f16[144,512]{1,0:T(8,128)(2,1)} %get-tuple-element.95), channel_id=1, source_target_pairs={{0,2},{1,31},{2,4},{3,1},{4,6},{5,3},{6,8},{7,5},{8,10},{9,7},{10,... | collective-permute-start | bytes 442376 | tf_op jit(solution)/shard_map/ppermute | solution.py:258
  (10 other events, 172.9 us)

commit v6 on v5

--- a/solution.py
+++ b/solution.py
@@ -13,6 +13,7 @@
 FAR = NZ // 2
 GROUPS = ((7, 6), (5, 4), (3, 2, 1, 0))
 LATER = {6: (1, 0), 4: (2, 0), 3: (2, 2)}
+DUE = {6: 1, 4: 2}
 CHAINS = ((0, 160), (160, 304), (304, 448))
 VMEM = 56 * 1024 * 1024
 f32 = jnp.float32
@@ -67,10 +68,13 @@
                     at = put(out, at, half, core, dist, range(n))
         first, other = outs[2 * n_out:]
         at = put_far(first, 0, yhi, 1 - core)
+        for half in (1 - yhi, yhi):
+            for dist in GROUPS[0]:
+                at = put(first, at, half, 1 - core, dist, range(n))
         put_features(first, put_far(first, at, 1 - yhi, 1 - core))
         at = 0
         for half in (yhi, 1 - yhi):
-            for dist in sum(GROUPS, ()):
+            for dist in sum(GROUPS[1:], ()):
                 at = put(other, at, half, 1 - core, dist, range(n))
 
 
@@ -82,7 +86,7 @@
     chunk = units // 2 // NZ
     extra = rows // BLOCK * seg2
     heights = 2 * [chunk // 2 + extra, *(len(group) * chunk for group in GROUPS)]
-    heights += [chunk + extra, 2 * FAR * chunk]
+    heights += [chunk + 2 * len(GROUPS[0]) * chunk + extra, 2 * (FAR - len(GROUPS[0])) * chunk]
     whole = lambda shape: pl.BlockSpec(shape, lambda i, s: (0,) * len(shape))
     return pl.pallas_call(
         turn_kernel,
@@ -125,7 +129,7 @@
             jax.ShapeDtypeStruct((4 * seg2, wide), pieces[0].dtype),
         ],
         cost_estimate=pl.CostEstimate(flops=200 * height * 4 * seg2 * wide, bytes_accessed=6 * height * wide, transcendentals=0),
-        compiler_params=pltpu.CompilerParams(vmem_limit_bytes=40 * 1024 * 1024),
+        compiler_params=pltpu.CompilerParams(vmem_limit_bytes=12 * 1024 * 1024),
     )(*pieces)
 
 
@@ -141,14 +145,14 @@
     return pl.pallas_call(
         product_kernel,
         grid=(2 * count,),
-        in_specs=[pl.BlockSpec((tile, seg2), lambda i, start=start: (2 * start + i, 0)) for start in starts]
+        in_specs=[pl.BlockSpec((tile, seg2), lambda i, start=start: (start + i, 0)) for start in starts]
         + [pl.BlockSpec(right.shape, lambda i: (0, 0))],
         out_specs=pl.BlockSpec((tile, wide), lambda i: (i, 0)),
         out_shape=jax.ShapeDtypeStruct((count * chunk, wide), f32),
         cost_estimate=pl.CostEstimate(
             flops=80 * count * chunk * 4 * seg2 * wide, bytes_accessed=6 * count * chunk * wide, transcendentals=0
         ),
-        compiler_params=pltpu.CompilerParams(vmem_limit_bytes=40 * 1024 * 1024),
+        compiler_params=pltpu.CompilerParams(vmem_limit_bytes=12 * 1024 * 1024),
     )(*pieces, right)
 
 
@@ -234,33 +238,35 @@
     n_out = 1 + len(GROUPS)
     after = lambda x, *events: lax.optimization_barrier((x, *events))[0]
     sizes = [len(group) * chunk for group in GROUPS]
-    sib_far = quad(made[2 * n_out], 1)
-    near = [quad(made[n_out], 2)]
-    diag = [quad(sib_far[half:], 2)]
-    far, right = first_product([made[0], sib_far, near[0], diag[0]], half)
-    sib = quad(after(made[2 * n_out + 1], sib_far), 1)
-    parts = {}
-
-    def send(g, event):
-        at = FAR * chunk + sum(sizes[:g])
-        near.append(quad(after(made[n_out + 1 + g], event), 2))
-        diag.append(quad(after(sib[at:at + sizes[g]], event), 2))
+    sib_first = quad(made[2 * n_out], 1)
+    far_at = sib_first.shape[0] - made[0].shape[0]
+    far, right = first_product([made[0], sib_first, quad(made[n_out], 2), quad(sib_first[far_at:], 2)], half)
+    sib_rest = quad(after(made[2 * n_out + 1], far), 1)
+
+    def send(g, *events):
+        at = half if g == 0 else sum(sizes[1:]) + sum(sizes[1:g])
+        forward = (sib_first if g == 0 else sib_rest)[at:at + sizes[g]]
+        both = after(jnp.concatenate([made[n_out + 1 + g], forward], axis=0), *events)
+        sent.append(both)
+        return quad(both, 2)
+
+    parts, sent = {}, []
 
     def multiply(g, at, event):
         group = GROUPS[g]
-        start = sum(map(len, GROUPS[:g])) + at
-        pieces = [made[1 + g], sib, near[1 + g], after(diag[1 + g], event)]
-        part = product(pieces, (at, start, at, at), right, chunk, 2)
+        sib, sib_at = (sib_first, 1 + 2 * len(group)) if g == 0 else (sib_rest, 2 * sum(map(len, GROUPS[1:g])))
+        away = after(arrived[g], event)
+        starts = (2 * at, sib_at + 2 * at, 2 * at, 2 * len(group) + 2 * at)
+        part = product([made[1 + g], sib, away, away], starts, right, chunk, 2)
         for i in range(2):
             parts[group[at + i]] = part[i * chunk:(i + 1) * chunk]
         return part
 
     ring = lambda x, cross=0: lax.ppermute(x, ("z", "core"), ring_pairs(cross))
-    send(0, sib_far)
-    send(1, far)
+    arrived = [send(0), send(1)]
     nearest = multiply(0, 0, far)
-    send(2, nearest)
-    got, _ = lax.optimization_barrier((ring(far.astype(f16)), nearest))
+    arrived.append(send(2, far))
+    got = after(ring(far.astype(f16)), nearest, *sent[1:])
     got = got.astype(f32)
     none = jnp.zeros_like(got)
     got = jnp.where(core == 0, jnp.concatenate([got, none], axis=0), jnp.concatenate([none, got], axis=0))
@@ -269,7 +275,8 @@
     for dist in range(FAR - 2, 0, -1):
         for k, (a, b) in enumerate(CHAINS):
             got = ring(sums[k])
-            got = after(got, last)
+            due = [arrived[DUE[dist]]] if k == 0 and dist in DUE else []
+            got = after(got, last, *due)
             sums[k] = last = (got.astype(f32) + parts[dist][a:b]).astype(f16)
             if k == 0 and dist in LATER:
                 multiply(*LATER[dist], last)

time: 177 us -> 165 us (0.932)
  starting transfers between devices: 118 us -> 104 us
  other arithmetic: 7.72 us -> 10.8 us
  waiting for transfers between devices: 15.1 us -> 12.9 us
    ppermute x10 -> x7, starting transfers between devices: 40.5 us -> 27 us  [body(): lax.ppermute(x, ('yhi', 'core'), [(j, j ^ i) for j in range(4)])]
    concatenate x0 -> x3, other arithmetic: none -> 3.13 us  [send(): jnp.concatenate([made[n_out + 1 + g], forward], axis=0)]
    ppermute x23, waiting for transfers between devices: 10.6 us -> 8.64 us  [body(): ring = lambda x, cross=0: lax.ppermute(x, ('z', 'core'), ring_pairs(cross))]
    ppermute x10 -> x7, waiting for transfers between devices: 4.48 us -> 4.25 us  [body(): lax.ppermute(x, ('yhi', 'core'), [(j, j ^ i) for j in range(4)])]
  transfers between devices with their start and end apart: 33 -> 30, of which waited for: 13 -> 8; matrix products, arithmetic and copies ran while one was open for 4% -> 7% of each run, Pallas kernels for 4% -> 4%
where the time goes in v6:
time: 165 us; the launch traced here: 164 us
  starting transfers between devices  104 us (63%)
  Pallas kernels  15.9 us (10%)
  blocking collectives  14.8 us (9%)
  waiting for transfers between devices  12.9 us (8%)
  other arithmetic  10.8 us (7%)
  local copies, waits for them, and re-layouts  3.55 us (2%)
  between operations  2.13 us (1%)
    ppermute x23, starting transfers between devices, body(): ring = lambda x, cross=0: lax.ppermute(x, ('z', 'core'), ring_pairs(cross))  76.8 us
    ppermute x7, starting transfers between devices, body(): lax.ppermute(x, ('yhi', 'core'), [(j, j ^ i) for j in range(4)])  27 us
    all_to_all x1, blocking collectives, body(): owned = lax.all_to_all(pieces, ('ylo', 'x', 'core'), 0, 0, tiled=True)  14.8 us
    ppermute x23, waiting for transfers between devices, body(): ring = lambda x, cross=0: lax.ppermute(x, ('z', 'core'), ring_pairs(cross))  8.64 us
    pallas_call x4, Pallas kernels, product(): pl.pallas_call(product_kernel, grid=(2 * count,), in_specs=[pl.BlockSpec(...  6.68 us
    pallas_call x1, Pallas kernels, turn(): pl.pallas_call(turn_kernel, grid_spec=pltpu.PrefetchScalarGridSpec(num_sc...  6.41 us
    convert_element_type x18, other arithmetic, body(): sums[k] = last = (got.astype(f32) + parts[dist][a:b]).astype(f16)  4.86 us
    ppermute x7, waiting for transfers between devices, body(): lax.ppermute(x, ('yhi', 'core'), [(j, j ^ i) for j in range(4)])  4.25 us
  transfers between devices with their start and end apart: 30, of which 8 were waited for; matrix products, arithmetic and copies ran while one was open for 7% of the time, Pallas kernels for 4%

profile of v6, /device:TPU:1, one launch (start us, length us, event | category | flops | bytes accessed | tf_op | source)
XLA Modules:
  0.0 163.8 jit_solution(9150658426292851441)
XLA Ops:
  0.6 6.4 %shard_map.67 = (bf16[736,128]{1,0:T(8,128)(2,1)}, bf16[896,128]{1,0:T(8,128)(2,1)}, bf16[896,128]{1,0:T(8,128)(2,1)}, bf16[1792,128]{1,0:T(8,128)(2,1)}, bf16[7...) custom-call(s32[2]{0:T(128)} %len_ref.1, ...), custom_call_target="tpu_custom_call" | custom-call | tf_op jit(solution)/shard_map/pallas_call | solution.py:91
  7.0 8.8 %collective-permute-start = (bf16[2752,128]{1,0:T(8,128)(2,1)}, bf16[2752,128]{1,0:T(8,128)(2,1)S(1)}, u32[]{:S(2)}, u32[]{:S(2)}) collective-permute-start(bf16[2752,128]{1,0:T(8,128)(2,1)} %get-tuple-element.41), channel_id=1, source_target_pairs={{0,1},{1,0},{32,33},{33,32},{2,3},{3,2},{34,35},{35,34},{4,5},{5,4... | collective-permute-start | bytes 2113544 | tf_op jit(solution)/shard_map/ppermute | solution.py:235
  17.8 4.8 %collective-permute-start.3 = (bf16[736,128]{1,0:T(8,128)(2,1)S(1)}, bf16[736,128]{1,0:T(8,128)(2,1)S(1)}, u32[]{:S(2)}, u32[]{:S(2)}) collective-permute-start(bf16[736,128]{1,0:T(8,128)(2,1)S(1)} %slice.145), channel_id=1, source_target_pairs={{0,32},{1,33},{32,0},{33,1},{2,34},{3,35},{34,2},{35,3},{4,36},{5,... | collective-permute-start | bytes 565256 | tf_op jit(solution)/shard_map/ppermute | solution.py:235
  23.7 2.0 %collective-permute-start.1 = (bf16[1792,128]{1,0:T(8,128)(2,1)S(1)}, bf16[1792,128]{1,0:T(8,128)(2,1)S(1)}, u32[]{:S(2)}, u32[]{:S(2)}) collective-permute-start(bf16[1792,128]{1,0:T(8,128)(2,1)S(1)} %pad_maximum_fusion.1), channel_id=1, source_target_pairs={{0,32},{1,33},{32,0},{33,1},{2,34},{3,35},{34,2},{35,3},{4,36},{5,... | collective-permute-start | bytes 1376264 | tf_op jit(solution)/shard_map/ppermute | solution.py:235
  25.8 4.0 %collective-permute-done.3.d_ref = bf16[736,128]{1,0:T(8,128)(2,1)S(1)} collective-permute-done((bf16[736,128]{1,0:T(8,128)(2,1)S(1)}, bf16[736,128]{1,0:T(8,128)(2,1)S(1)}, u32[]{:S(2)}, u32[]{:S(2)}) %collective-permute-start.3) | collective-permute-done | bytes 188448 | tf_op jit(solution)/shard_map/ppermute | solution.py:235
  32.1 3.1 %collective-permute-start.5 = (bf16[5376,128]{1,0:T(8,128)(2,1)S(1)}, bf16[5376,128]{1,0:T(8,128)(2,1)S(1)}, u32[]{:S(2)}, u32[]{:S(2)}) collective-permute-start(bf16[5376,128]{1,0:T(8,128)(2,1)S(1)} %copy-done.10), channel_id=1, source_target_pairs={{0,1},{1,0},{32,33},{33,32},{2,3},{3,2},{34,35},{35,34},{4,5},{5,4... | collective-permute-start | bytes 4128776 | tf_op jit(solution)/shard_map/ppermute | solution.py:235
  35.2 6.7 %collective-permute-start.4 = (f16[224,1024]{1,0:T(8,128)(2,1)S(1)}, f16[224,1024]{1,0:T(8,128)(2,1)S(1)}, u32[]{:S(2)}, u32[]{:S(2)}) collective-permute-start(f16[224,1024]{1,0:T(8,128)(2,1)S(1)} %convert_element_type.141), channel_id=1, source_target_pairs={{0,2},{1,31},{2,4},{3,1},{4,6},{5,3},{6,8},{7,5},{8,10},{9,7},{10,... | collective-permute-start | bytes 1376264 | tf_op jit(solution)/shard_map/ppermute | solution.py:265
  45.8 3.9 %collective-permute-start.7 = (bf16[1792,128]{1,0:T(8,128)(2,1)}, bf16[1792,128]{1,0:T(8,128)(2,1)S(1)}, u32[]{:S(2)}, u32[]{:S(2)}) collective-permute-start(bf16[1792,128]{1,0:T(8,128)(2,1)} %pad_maximum_fusion.2), channel_id=1, source_target_pairs={{0,32},{1,33},{32,0},{33,1},{2,34},{3,35},{34,2},{35,3},{4,36},{5,... | collective-permute-start | bytes 1376264 | tf_op jit(solution)/shard_map/ppermute | solution.py:235
  50.9 4.3 %collective-permute-start.6 = (f16[160,1024]{1,0:T(8,128)(2,1)}, f16[160,1024]{1,0:T(8,128)(2,1)S(1)}, u32[]{:S(2)}, u32[]{:S(2)}) collective-permute-start(f16[160,1024]{1,0:T(8,128)(2,1)} %fusion.6), channel_id=1, source_target_pairs={{0,2},{1,31},{2,4},{3,1},{4,6},{5,3},{6,8},{7,5},{8,10},{9,7},{10,... | collective-permute-start | bytes 983048 | tf_op jit(solution)/shard_map/ppermute | solution.py:265
  56.3 2.6 %collective-permute-start.10 = (f16[144,1024]{1,0:T(8,128)(2,1)}, f16[144,1024]{1,0:T(8,128)(2,1)}, u32[]{:S(2)}, u32[]{:S(2)}) collective-permute-start(f16[144,1024]{1,0:T(8,128)(2,1)} %get-tuple-element.77), channel_id=1, source_target_pairs={{0,2},{1,31},{2,4},{3,1},{4,6},{5,3},{6,8},{7,5},{8,10},{9,7},{10,... | collective-permute-start | bytes 884744 | tf_op jit(solution)/shard_map/ppermute | solution.py:265
  58.9 2.5 %collective-permute-start.14 = (bf16[3584,128]{1,0:T(8,128)(2,1)}, bf16[3584,128]{1,0:T(8,128)(2,1)S(1)}, u32[]{:S(2)}, u32[]{:S(2)}) collective-permute-start(bf16[3584,128]{1,0:T(8,128)(2,1)} %pad_maximum_fusion), channel_id=1, source_target_pairs={{0,32},{1,33},{32,0},{33,1},{2,34},{3,35},{34,2},{35,3},{4,36},{5,... | collective-permute-start | bytes 2752520 | tf_op jit(solution)/shard_map/ppermute | solution.py:235
  61.4 2.6 %collective-permute-start.9 = (f16[144,1024]{1,0:T(8,128)(2,1)}, f16[144,1024]{1,0:T(8,128)(2,1)S(1)}, u32[]{:S(2)}, u32[]{:S(2)}) collective-permute-start(f16[144,1024]{1,0:T(8,128)(2,1)} %get-tuple-element.78), channel_id=1, source_target_pairs={{0,2},{1,31},{2,4},{3,1},{4,6},{5,3},{6,8},{7,5},{8,10},{9,7},{10,... | collective-permute-start | bytes 884744 | tf_op jit(solution)/shard_map/ppermute | solution.py:265
  65.3 2.7 %collective-permute-start.8 = (f16[160,1024]{1,0:T(8,128)(2,1)S(1)}, f16[160,1024]{1,0:T(8,128)(2,1)S(1)}, u32[]{:S(2)}, u32[]{:S(2)}) collective-permute-start(f16[160,1024]{1,0:T(8,128)(2,1)S(1)} %fusion.5), channel_id=1, source_target_pairs={{0,2},{1,31},{2,4},{3,1},{4,6},{5,3},{6,8},{7,5},{8,10},{9,7},{10,... | collective-permute-start | bytes 983048 | tf_op jit(solution)/shard_map/ppermute | solution.py:265
  69.2 3.8 %collective-permute-start.13 = (f16[144,1024]{1,0:T(8,128)(2,1)S(1)}, f16[144,1024]{1,0:T(8,128)(2,1)S(1)}, u32[]{:S(2)}, u32[]{:S(2)}) collective-permute-start(f16[144,1024]{1,0:T(8,128)(2,1)S(1)} %fusion.18), channel_id=1, source_target_pairs={{0,2},{1,31},{2,4},{3,1},{4,6},{5,3},{6,8},{7,5},{8,10},{9,7},{10,... | collective-permute-start | bytes 884744 | tf_op jit(solution)/shard_map/ppermute | solution.py:265
  74.2 2.6 %collective-permute-start.12 = (f16[144,1024]{1,0:T(8,128)(2,1)S(1)}, f16[144,1024]{1,0:T(8,128)(2,1)S(1)}, u32[]{:S(2)}, u32[]{:S(2)}) collective-permute-start(f16[144,1024]{1,0:T(8,128)(2,1)S(1)} %fusion.17), channel_id=1, source_target_pairs={{0,2},{1,31},{2,4},{3,1},{4,6},{5,3},{6,8},{7,5},{8,10},{9,7},{10,... | collective-permute-start | bytes 884744 | tf_op jit(solution)/shard_map/ppermute | solution.py:265
  78.7 2.8 %collective-permute-start.11 = (f16[160,1024]{1,0:T(8,128)(2,1)S(1)}, f16[160,1024]{1,0:T(8,128)(2,1)S(1)}, u32[]{:S(2)}, u32[]{:S(2)}) collective-permute-start(f16[160,1024]{1,0:T(8,128)(2,1)S(1)} %fusion.4), channel_id=1, source_target_pairs={{0,2},{1,31},{2,4},{3,1},{4,6},{5,3},{6,8},{7,5},{8,10},{9,7},{10,... | collective-permute-start | bytes 983048 | tf_op jit(solution)/shard_map/ppermute | solution.py:265
  81.5 2.6 %collective-permute-start.17 = (f16[144,1024]{1,0:T(8,128)(2,1)S(1)}, f16[144,1024]{1,0:T(8,128)(2,1)S(1)}, u32[]{:S(2)}, u32[]{:S(2)}) collective-permute-start(f16[144,1024]{1,0:T(8,128)(2,1)S(1)} %fusion.16), channel_id=1, source_target_pairs={{0,2},{1,31},{2,4},{3,1},{4,6},{5,3},{6,8},{7,5},{8,10},{9,7},{10,... | collective-permute-start | bytes 884744 | tf_op jit(solution)/shard_map/ppermute | solution.py:265
  87.0 3.5 %collective-permute-start.15 = (f16[160,1024]{1,0:T(8,128)(2,1)S(1)}, f16[160,1024]{1,0:T(8,128)(2,1)S(1)}, u32[]{:S(2)}, u32[]{:S(2)}) collective-permute-start(f16[160,1024]{1,0:T(8,128)(2,1)S(1)} %fusion.3), channel_id=1, source_target_pairs={{0,2},{1,31},{2,4},{3,1},{4,6},{5,3},{6,8},{7,5},{8,10},{9,7},{10,... | collective-permute-start | bytes 983048 | tf_op jit(solution)/shard_map/ppermute | solution.py:265
  90.7 3.0 %collective-permute-start.20 = (f16[144,1024]{1,0:T(8,128)(2,1)S(1)}, f16[144,1024]{1,0:T(8,128)(2,1)S(1)}, u32[]{:S(2)}, u32[]{:S(2)}) collective-permute-start(f16[144,1024]{1,0:T(8,128)(2,1)S(1)} %fusion.14), channel_id=1, source_target_pairs={{0,2},{1,31},{2,4},{3,1},{4,6},{5,3},{6,8},{7,5},{8,10},{9,7},{10,... | collective-permute-start | bytes 884744 | tf_op jit(solution)/shard_map/ppermute | solution.py:265
  93.8 3.0 %collective-permute-start.19 = (f16[144,1024]{1,0:T(8,128)(2,1)S(1)}, f16[144,1024]{1,0:T(8,128)(2,1)S(1)}, u32[]{:S(2)}, u32[]{:S(2)}) collective-permute-start(f16[144,1024]{1,0:T(8,128)(2,1)S(1)} %fusion.13), channel_id=1, source_target_pairs={{0,2},{1,31},{2,4},{3,1},{4,6},{5,3},{6,8},{7,5},{8,10},{9,7},{10,... | collective-permute-start | bytes 884744 | tf_op jit(solution)/shard_map/ppermute | solution.py:265
  100.7 2.8 %collective-permute-start.23 = (f16[144,1024]{1,0:T(8,128)(2,1)S(1)}, f16[144,1024]{1,0:T(8,128)(2,1)S(1)}, u32[]{:S(2)}, u32[]{:S(2)}) collective-permute-start(f16[144,1024]{1,0:T(8,128)(2,1)S(1)} %fusion.12), channel_id=1, source_target_pairs={{0,2},{1,31},{2,4},{3,1},{4,6},{5,3},{6,8},{7,5},{8,10},{9,7},{10,... | collective-permute-start | bytes 884744 | tf_op jit(solution)/shard_map/ppermute | solution.py:265
  103.6 3.0 %collective-permute-start.22 = (f16[144,1024]{1,0:T(8,128)(2,1)S(1)}, f16[144,1024]{1,0:T(8,128)(2,1)S(1)}, u32[]{:S(2)}, u32[]{:S(2)}) collective-permute-start(f16[144,1024]{1,0:T(8,128)(2,1)S(1)} %fusion.11), channel_id=1, source_target_pairs={{0,2},{1,31},{2,4},{3,1},{4,6},{5,3},{6,8},{7,5},{8,10},{9,7},{10,... | collective-permute-start | bytes 884744 | tf_op jit(solution)/shard_map/ppermute | solution.py:265
  110.5 3.1 %collective-permute-start.25 = (f16[144,1024]{1,0:T(8,128)(2,1)S(1)}, f16[144,1024]{1,0:T(8,128)(2,1)S(1)}, u32[]{:S(2)}, u32[]{:S(2)}) collective-permute-start(f16[144,1024]{1,0:T(8,128)(2,1)S(1)} %fusion.10), channel_id=1, source_target_pairs={{0,2},{1,31},{2,4},{3,1},{4,6},{5,3},{6,8},{7,5},{8,10},{9,7},{10,... | collective-permute-start | bytes 884744 | tf_op jit(solution)/shard_map/ppermute | solution.py:265
  113.7 2.8 %collective-permute-start.27 = (f16[144,1024]{1,0:T(8,128)(2,1)S(1)}, f16[144,1024]{1,0:T(8,128)(2,1)S(1)}, u32[]{:S(2)}, u32[]{:S(2)}) collective-permute-start(f16[144,1024]{1,0:T(8,128)(2,1)S(1)} %fusion.9), channel_id=1, source_target_pairs={{0,2},{1,31},{2,4},{3,1},{4,6},{5,3},{6,8},{7,5},{8,10},{9,7},{10,... | collective-permute-start | bytes 884744 | tf_op jit(solution)/shard_map/ppermute | solution.py:265
  116.7 2.8 %collective-permute-done.25 = f16[144,1024]{1,0:T(8,128)(2,1)S(1)} collective-permute-done((f16[144,1024]{1,0:T(8,128)(2,1)S(1)}, f16[144,1024]{1,0:T(8,128)(2,1)S(1)}, u32[]{:S(2)}, u32[]{:S(2)}) %collective-permute-start.25) | collective-permute-done | bytes 294944 | tf_op jit(solution)/shard_map/ppermute | solution.py:265
  119.7 3.2 %collective-permute-done.27 = f16[144,1024]{1,0:T(8,128)(2,1)S(1)} collective-permute-done((f16[144,1024]{1,0:T(8,128)(2,1)S(1)}, f16[144,1024]{1,0:T(8,128)(2,1)S(1)}, u32[]{:S(2)}, u32[]{:S(2)}) %collective-permute-start.27) | collective-permute-done | bytes 294944 | tf_op jit(solution)/shard_map/ppermute | solution.py:265
  123.9 10.2 %collective-permute-start.29 = (f16[448,512]{1,0:T(8,128)(2,1)S(1)}, f16[448,512]{1,0:T(8,128)(2,1)S(1)}, u32[]{:S(2)}, u32[]{:S(2)}) collective-permute-start(f16[448,512]{1,0:T(8,128)(2,1)S(1)} %pad_maximum_fusion.3), channel_id=1, source_target_pairs={{0,3},{1,30},{2,5},{3,0},{4,7},{5,2},{6,9},{7,4},{8,11},{9,6},{10,... | collective-permute-start | bytes 1376264 | tf_op jit(solution)/shard_map/ppermute | solution.py:265
  134.1 2.5 %collective-permute-start.24 = (f16[160,512]{1,0:T(8,128)(2,1)S(1)}, f16[160,512]{1,0:T(8,128)(2,1)S(1)}, u32[]{:S(2)}, u32[]{:S(2)}) collective-permute-start(f16[160,512]{1,0:T(8,128)(2,1)S(1)} %get-tuple-element.79), channel_id=1, source_target_pairs={{0,2},{1,31},{2,4},{3,1},{4,6},{5,3},{6,8},{7,5},{8,10},{9,7},{10,... | collective-permute-start | bytes 491528 | tf_op jit(solution)/shard_map/ppermute | solution.py:265
  136.7 2.2 %collective-permute-start.28 = (f16[144,512]{1,0:T(8,128)(2,1)}, f16[144,512]{1,0:T(8,128)(2,1)S(1)}, u32[]{:S(2)}, u32[]{:S(2)}) collective-permute-start(f16[144,512]{1,0:T(8,128)(2,1)} %get-tuple-element.83), channel_id=1, source_target_pairs={{0,2},{1,31},{2,4},{3,1},{4,6},{5,3},{6,8},{7,5},{8,10},{9,7},{10,... | collective-permute-start | bytes 442376 | tf_op jit(solution)/shard_map/ppermute | solution.py:265
  138.8 3.9 %collective-permute-start.26 = (f16[144,512]{1,0:T(8,128)(2,1)S(1)}, f16[144,512]{1,0:T(8,128)(2,1)S(1)}, u32[]{:S(2)}, u32[]{:S(2)}) collective-permute-start(f16[144,512]{1,0:T(8,128)(2,1)S(1)} %get-tuple-element.81), channel_id=1, source_target_pairs={{0,2},{1,31},{2,4},{3,1},{4,6},{5,3},{6,8},{7,5},{8,10},{9,7},{10,... | collective-permute-start | bytes 442376 | tf_op jit(solution)/shard_map/ppermute | solution.py:265
  146.4 14.8 %all_to_all.5 = f16[16,28,512]{2,1,0:T(8,128)(2,1)S(1)} all-to-all(f16[16,28,512]{2,1,0:T(8,128)(2,1)S(1)} %reshape.12), channel_id=1, replica_groups=mesh['ylo'=2,'x'=4,'yhi'=2,'z'=16,'core'=2] {'ylo','x','core'}, dimensions={0} | all-to-all | bytes 917504 | tf_op jit(solution)/shard_map/all_to_all | solution.py:289
  161.4 2.4 %shard_map.73 = (f32[28,512]{1,0:T(8,128)}, f32[28,512]{1,0:T(8,128)}, f32[28,512]{1,0:T(8,128)}) custom-call(f32[16,32,512]{2,1,0:T(8,128)S(1)} %pad.6.g_ref, bf16[28,512]{1,0:T(8,128)(2,1)S(1)} %copy-done.2), custom_call_target="tpu_custom_call" | custom-call | tf_op jit(solution)/shard_map/pallas_call | solution.py:211
  (99 shorter events, 32.0 us)
Async XLA Ops:
  7.0 10.8 %collective-permute-start = (bf16[2752,128]{1,0:T(8,128)(2,1)}, bf16[2752,128]{1,0:T(8,128)(2,1)S(1)}, u32[]{:S(2)}, u32[]{:S(2)}) collective-permute-start(bf16[2752,128]{1,0:T(8,128)(2,1)} %get-tuple-element.41), channel_id=1, source_target_pairs={{0,1},{1,0},{32,33},{33,32},{2,3},{3,2},{34,35},{35,34},{4,5},{5,4... | collective-permute-start | bytes 2113544 | tf_op jit(solution)/shard_map/ppermute | solution.py:235
  15.8 10.0 %collective-permute-start.2 = (bf16[736,128]{1,0:T(8,128)(2,1)}, bf16[736,128]{1,0:T(8,128)(2,1)S(1)}, u32[]{:S(2)}, u32[]{:S(2)}) collective-permute-start(bf16[736,128]{1,0:T(8,128)(2,1)} %get-tuple-element.44), channel_id=1, source_target_pairs={{0,32},{1,33},{32,0},{33,1},{2,34},{3,35},{34,2},{35,3},{4,36},{5,... | collective-permute-start | bytes 565256 | tf_op jit(solution)/shard_map/ppermute | solution.py:235
  17.8 12.0 %collective-permute-start.3 = (bf16[736,128]{1,0:T(8,128)(2,1)S(1)}, bf16[736,128]{1,0:T(8,128)(2,1)S(1)}, u32[]{:S(2)}, u32[]{:S(2)}) collective-permute-start(bf16[736,128]{1,0:T(8,128)(2,1)S(1)} %slice.145), channel_id=1, source_target_pairs={{0,32},{1,33},{32,0},{33,1},{2,34},{3,35},{34,2},{35,3},{4,36},{5,... | collective-permute-start | bytes 565256 | tf_op jit(solution)/shard_map/ppermute | solution.py:235
  23.7 18.2 %collective-permute-start.1 = (bf16[1792,128]{1,0:T(8,128)(2,1)S(1)}, bf16[1792,128]{1,0:T(8,128)(2,1)S(1)}, u32[]{:S(2)}, u32[]{:S(2)}) collective-permute-start(bf16[1792,128]{1,0:T(8,128)(2,1)S(1)} %pad_maximum_fusion.1), channel_id=1, source_target_pairs={{0,32},{1,33},{32,0},{33,1},{2,34},{3,35},{34,2},{35,3},{4,36},{5,... | collective-permute-start | bytes 1376264 | tf_op jit(solution)/shard_map/ppermute | solution.py:235
  32.1 11.5 %collective-permute-start.5 = (bf16[5376,128]{1,0:T(8,128)(2,1)S(1)}, bf16[5376,128]{1,0:T(8,128)(2,1)S(1)}, u32[]{:S(2)}, u32[]{:S(2)}) collective-permute-start(bf16[5376,128]{1,0:T(8,128)(2,1)S(1)} %copy-done.10), channel_id=1, source_target_pairs={{0,1},{1,0},{32,33},{33,32},{2,3},{3,2},{34,35},{35,34},{4,5},{5,4... | collective-permute-start | bytes 4128776 | tf_op jit(solution)/shard_map/ppermute | solution.py:235
  35.2 14.6 %collective-permute-start.4 = (f16[224,1024]{1,0:T(8,128)(2,1)S(1)}, f16[224,1024]{1,0:T(8,128)(2,1)S(1)}, u32[]{:S(2)}, u32[]{:S(2)}) collective-permute-start(f16[224,1024]{1,0:T(8,128)(2,1)S(1)} %convert_element_type.141), channel_id=1, source_target_pairs={{0,2},{1,31},{2,4},{3,1},{4,6},{5,3},{6,8},{7,5},{8,10},{9,7},{10,... | collective-permute-start | bytes 1376264 | tf_op jit(solution)/shard_map/ppermute | solution.py:265
  45.8 18.3 %collective-permute-start.7 = (bf16[1792,128]{1,0:T(8,128)(2,1)}, bf16[1792,128]{1,0:T(8,128)(2,1)S(1)}, u32[]{:S(2)}, u32[]{:S(2)}) collective-permute-start(bf16[1792,128]{1,0:T(8,128)(2,1)} %pad_maximum_fusion.2), channel_id=1, source_target_pairs={{0,32},{1,33},{32,0},{33,1},{2,34},{3,35},{34,2},{35,3},{4,36},{5,... | collective-permute-start | bytes 1376264 | tf_op jit(solution)/shard_map/ppermute | solution.py:235
  50.9 26.0 %copy-start.4 = (bf16[896,128]{1,0:T(8,128)(2,1)S(1)}, bf16[896,128]{1,0:T(8,128)(2,1)}, u32[]{:S(2)}) copy-start(bf16[896,128]{1,0:T(8,128)(2,1)} %get-tuple-element.58.a_ref) | copy-start | bytes 688132
  50.9 13.2 %collective-permute-start.6 = (f16[160,1024]{1,0:T(8,128)(2,1)}, f16[160,1024]{1,0:T(8,128)(2,1)S(1)}, u32[]{:S(2)}, u32[]{:S(2)}) collective-permute-start(f16[160,1024]{1,0:T(8,128)(2,1)} %fusion.6), channel_id=1, source_target_pairs={{0,2},{1,31},{2,4},{3,1},{4,6},{5,3},{6,8},{7,5},{8,10},{9,7},{10,... | collective-permute-start | bytes 983048 | tf_op jit(solution)/shard_map/ppermute | solution.py:265
  56.3 11.7 %collective-permute-start.10 = (f16[144,1024]{1,0:T(8,128)(2,1)}, f16[144,1024]{1,0:T(8,128)(2,1)}, u32[]{:S(2)}, u32[]{:S(2)}) collective-permute-start(f16[144,1024]{1,0:T(8,128)(2,1)} %get-tuple-element.77), channel_id=1, source_target_pairs={{0,2},{1,31},{2,4},{3,1},{4,6},{5,3},{6,8},{7,5},{8,10},{9,7},{10,... | collective-permute-start | bytes 884744 | tf_op jit(solution)/shard_map/ppermute | solution.py:265
  58.9 27.3 %collective-permute-start.14 = (bf16[3584,128]{1,0:T(8,128)(2,1)}, bf16[3584,128]{1,0:T(8,128)(2,1)S(1)}, u32[]{:S(2)}, u32[]{:S(2)}) collective-permute-start(bf16[3584,128]{1,0:T(8,128)(2,1)} %pad_maximum_fusion), channel_id=1, source_target_pairs={{0,32},{1,33},{32,0},{33,1},{2,34},{3,35},{34,2},{35,3},{4,36},{5,... | collective-permute-start | bytes 2752520 | tf_op jit(solution)/shard_map/ppermute | solution.py:235
  61.4 11.6 %collective-permute-start.9 = (f16[144,1024]{1,0:T(8,128)(2,1)}, f16[144,1024]{1,0:T(8,128)(2,1)S(1)}, u32[]{:S(2)}, u32[]{:S(2)}) collective-permute-start(f16[144,1024]{1,0:T(8,128)(2,1)} %get-tuple-element.78), channel_id=1, source_target_pairs={{0,2},{1,31},{2,4},{3,1},{4,6},{5,3},{6,8},{7,5},{8,10},{9,7},{10,... | collective-permute-start | bytes 884744 | tf_op jit(solution)/shard_map/ppermute | solution.py:265
  65.3 13.2 %collective-permute-start.8 = (f16[160,1024]{1,0:T(8,128)(2,1)S(1)}, f16[160,1024]{1,0:T(8,128)(2,1)S(1)}, u32[]{:S(2)}, u32[]{:S(2)}) collective-permute-start(f16[160,1024]{1,0:T(8,128)(2,1)S(1)} %fusion.5), channel_id=1, source_target_pairs={{0,2},{1,31},{2,4},{3,1},{4,6},{5,3},{6,8},{7,5},{8,10},{9,7},{10,... | collective-permute-start | bytes 983048 | tf_op jit(solution)/shard_map/ppermute | solution.py:265
  69.2 12.2 %collective-permute-start.13 = (f16[144,1024]{1,0:T(8,128)(2,1)S(1)}, f16[144,1024]{1,0:T(8,128)(2,1)S(1)}, u32[]{:S(2)}, u32[]{:S(2)}) collective-permute-start(f16[144,1024]{1,0:T(8,128)(2,1)S(1)} %fusion.18), channel_id=1, source_target_pairs={{0,2},{1,31},{2,4},{3,1},{4,6},{5,3},{6,8},{7,5},{8,10},{9,7},{10,... | collective-permute-start | bytes 884744 | tf_op jit(solution)/shard_map/ppermute | solution.py:265
  74.2 10.0 %collective-permute-start.12 = (f16[144,1024]{1,0:T(8,128)(2,1)S(1)}, f16[144,1024]{1,0:T(8,128)(2,1)S(1)}, u32[]{:S(2)}, u32[]{:S(2)}) collective-permute-start(f16[144,1024]{1,0:T(8,128)(2,1)S(1)} %fusion.17), channel_id=1, source_target_pairs={{0,2},{1,31},{2,4},{3,1},{4,6},{5,3},{6,8},{7,5},{8,10},{9,7},{10,... | collective-permute-start | bytes 884744 | tf_op jit(solution)/shard_map/ppermute | solution.py:265
  78.7 8.2 %collective-permute-start.11 = (f16[160,1024]{1,0:T(8,128)(2,1)S(1)}, f16[160,1024]{1,0:T(8,128)(2,1)S(1)}, u32[]{:S(2)}, u32[]{:S(2)}) collective-permute-start(f16[160,1024]{1,0:T(8,128)(2,1)S(1)} %fusion.4), channel_id=1, source_target_pairs={{0,2},{1,31},{2,4},{3,1},{4,6},{5,3},{6,8},{7,5},{8,10},{9,7},{10,... | collective-permute-start | bytes 983048 | tf_op jit(solution)/shard_map/ppermute | solution.py:265
  81.5 9.0 %collective-permute-start.17 = (f16[144,1024]{1,0:T(8,128)(2,1)S(1)}, f16[144,1024]{1,0:T(8,128)(2,1)S(1)}, u32[]{:S(2)}, u32[]{:S(2)}) collective-permute-start(f16[144,1024]{1,0:T(8,128)(2,1)S(1)} %fusion.16), channel_id=1, source_target_pairs={{0,2},{1,31},{2,4},{3,1},{4,6},{5,3},{6,8},{7,5},{8,10},{9,7},{10,... | collective-permute-start | bytes 884744 | tf_op jit(solution)/shard_map/ppermute | solution.py:265
  84.3 9.4 %collective-permute-start.16 = (f16[144,1024]{1,0:T(8,128)(2,1)S(1)}, f16[144,1024]{1,0:T(8,128)(2,1)S(1)}, u32[]{:S(2)}, u32[]{:S(2)}) collective-permute-start(f16[144,1024]{1,0:T(8,128)(2,1)S(1)} %fusion.15), channel_id=1, source_target_pairs={{0,2},{1,31},{2,4},{3,1},{4,6},{5,3},{6,8},{7,5},{8,10},{9,7},{10,... | collective-permute-start | bytes 884744 | tf_op jit(solution)/shard_map/ppermute | solution.py:265
  87.0 11.6 %collective-permute-start.15 = (f16[160,1024]{1,0:T(8,128)(2,1)S(1)}, f16[160,1024]{1,0:T(8,128)(2,1)S(1)}, u32[]{:S(2)}, u32[]{:S(2)}) collective-permute-start(f16[160,1024]{1,0:T(8,128)(2,1)S(1)} %fusion.3), channel_id=1, source_target_pairs={{0,2},{1,31},{2,4},{3,1},{4,6},{5,3},{6,8},{7,5},{8,10},{9,7},{10,... | collective-permute-start | bytes 983048 | tf_op jit(solution)/shard_map/ppermute | solution.py:265
  90.7 9.9 %collective-permute-start.20 = (f16[144,1024]{1,0:T(8,128)(2,1)S(1)}, f16[144,1024]{1,0:T(8,128)(2,1)S(1)}, u32[]{:S(2)}, u32[]{:S(2)}) collective-permute-start(f16[144,1024]{1,0:T(8,128)(2,1)S(1)} %fusion.14), channel_id=1, source_target_pairs={{0,2},{1,31},{2,4},{3,1},{4,6},{5,3},{6,8},{7,5},{8,10},{9,7},{10,... | collective-permute-start | bytes 884744 | tf_op jit(solution)/shard_map/ppermute | solution.py:265
  93.8 9.7 %collective-permute-start.19 = (f16[144,1024]{1,0:T(8,128)(2,1)S(1)}, f16[144,1024]{1,0:T(8,128)(2,1)S(1)}, u32[]{:S(2)}, u32[]{:S(2)}) collective-permute-start(f16[144,1024]{1,0:T(8,128)(2,1)S(1)} %fusion.13), channel_id=1, source_target_pairs={{0,2},{1,31},{2,4},{3,1},{4,6},{5,3},{6,8},{7,5},{8,10},{9,7},{10,... | collective-permute-start | bytes 884744 | tf_op jit(solution)/shard_map/ppermute | solution.py:265
  98.7 9.7 %collective-permute-start.18 = (f16[160,1024]{1,0:T(8,128)(2,1)S(1)}, f16[160,1024]{1,0:T(8,128)(2,1)S(1)}, u32[]{:S(2)}, u32[]{:S(2)}) collective-permute-start(f16[160,1024]{1,0:T(8,128)(2,1)S(1)} %fusion.2), channel_id=1, source_target_pairs={{0,2},{1,31},{2,4},{3,1},{4,6},{5,3},{6,8},{7,5},{8,10},{9,7},{10,... | collective-permute-start | bytes 983048 | tf_op jit(solution)/shard_map/ppermute | solution.py:265
  100.7 9.7 %collective-permute-start.23 = (f16[144,1024]{1,0:T(8,128)(2,1)S(1)}, f16[144,1024]{1,0:T(8,128)(2,1)S(1)}, u32[]{:S(2)}, u32[]{:S(2)}) collective-permute-start(f16[144,1024]{1,0:T(8,128)(2,1)S(1)} %fusion.12), channel_id=1, source_target_pairs={{0,2},{1,31},{2,4},{3,1},{4,6},{5,3},{6,8},{7,5},{8,10},{9,7},{10,... | collective-permute-start | bytes 884744 | tf_op jit(solution)/shard_map/ppermute | solution.py:265
  103.6 10.0 %collective-permute-start.22 = (f16[144,1024]{1,0:T(8,128)(2,1)S(1)}, f16[144,1024]{1,0:T(8,128)(2,1)S(1)}, u32[]{:S(2)}, u32[]{:S(2)}) collective-permute-start(f16[144,1024]{1,0:T(8,128)(2,1)S(1)} %fusion.11), channel_id=1, source_target_pairs={{0,2},{1,31},{2,4},{3,1},{4,6},{5,3},{6,8},{7,5},{8,10},{9,7},{10,... | collective-permute-start | bytes 884744 | tf_op jit(solution)/shard_map/ppermute | solution.py:265
  108.5 8.1 %collective-permute-start.21 = (f16[160,1024]{1,0:T(8,128)(2,1)S(1)}, f16[160,1024]{1,0:T(8,128)(2,1)S(1)}, u32[]{:S(2)}, u32[]{:S(2)}) collective-permute-start(f16[160,1024]{1,0:T(8,128)(2,1)S(1)} %fusion.1), channel_id=1, source_target_pairs={{0,2},{1,31},{2,4},{3,1},{4,6},{5,3},{6,8},{7,5},{8,10},{9,7},{10,... | collective-permute-start | bytes 983048 | tf_op jit(solution)/shard_map/ppermute | solution.py:265
  110.5 32.3 %copy-start.9 = (s32[2]{0:T(128)S(1)}, s32[2]{0:T(128)}, u32[]{:S(2)}) copy-start(s32[2]{0:T(128)} %len_ref.1) | copy-start | bytes 28
  110.5 8.9 %collective-permute-start.25 = (f16[144,1024]{1,0:T(8,128)(2,1)S(1)}, f16[144,1024]{1,0:T(8,128)(2,1)S(1)}, u32[]{:S(2)}, u32[]{:S(2)}) collective-permute-start(f16[144,1024]{1,0:T(8,128)(2,1)S(1)} %fusion.10), channel_id=1, source_target_pairs={{0,2},{1,31},{2,4},{3,1},{4,6},{5,3},{6,8},{7,5},{8,10},{9,7},{10,... | collective-permute-start | bytes 884744 | tf_op jit(solution)/shard_map/ppermute | solution.py:265
  113.7 9.2 %collective-permute-start.27 = (f16[144,1024]{1,0:T(8,128)(2,1)S(1)}, f16[144,1024]{1,0:T(8,128)(2,1)S(1)}, u32[]{:S(2)}, u32[]{:S(2)}) collective-permute-start(f16[144,1024]{1,0:T(8,128)(2,1)S(1)} %fusion.9), channel_id=1, source_target_pairs={{0,2},{1,31},{2,4},{3,1},{4,6},{5,3},{6,8},{7,5},{8,10},{9,7},{10,... | collective-permute-start | bytes 884744 | tf_op jit(solution)/shard_map/ppermute | solution.py:265
  123.9 22.0 %collective-permute-start.29 = (f16[448,512]{1,0:T(8,128)(2,1)S(1)}, f16[448,512]{1,0:T(8,128)(2,1)S(1)}, u32[]{:S(2)}, u32[]{:S(2)}) collective-permute-start(f16[448,512]{1,0:T(8,128)(2,1)S(1)} %pad_maximum_fusion.3), channel_id=1, source_target_pairs={{0,3},{1,30},{2,5},{3,0},{4,7},{5,2},{6,9},{7,4},{8,11},{9,6},{10,... | collective-permute-start | bytes 1376264 | tf_op jit(solution)/shard_map/ppermute | solution.py:265
  134.1 11.8 %collective-permute-start.24 = (f16[160,512]{1,0:T(8,128)(2,1)S(1)}, f16[160,512]{1,0:T(8,128)(2,1)S(1)}, u32[]{:S(2)}, u32[]{:S(2)}) collective-permute-start(f16[160,512]{1,0:T(8,128)(2,1)S(1)} %get-tuple-element.79), channel_id=1, source_target_pairs={{0,2},{1,31},{2,4},{3,1},{4,6},{5,3},{6,8},{7,5},{8,10},{9,7},{10,... | collective-permute-start | bytes 491528 | tf_op jit(solution)/shard_map/ppermute | solution.py:265
  136.7 7.8 %collective-permute-start.28 = (f16[144,512]{1,0:T(8,128)(2,1)}, f16[144,512]{1,0:T(8,128)(2,1)S(1)}, u32[]{:S(2)}, u32[]{:S(2)}) collective-permute-start(f16[144,512]{1,0:T(8,128)(2,1)} %get-tuple-element.83), channel_id=1, source_target_pairs={{0,2},{1,31},{2,4},{3,1},{4,6},{5,3},{6,8},{7,5},{8,10},{9,7},{10,... | collective-permute-start | bytes 442376 | tf_op jit(solution)/shard_map/ppermute | solution.py:265
  138.8 7.1 %collective-permute-start.26 = (f16[144,512]{1,0:T(8,128)(2,1)S(1)}, f16[144,512]{1,0:T(8,128)(2,1)S(1)}, u32[]{:S(2)}, u32[]{:S(2)}) collective-permute-start(f16[144,512]{1,0:T(8,128)(2,1)S(1)} %get-tuple-element.81), channel_id=1, source_target_pairs={{0,2},{1,31},{2,4},{3,1},{4,6},{5,3},{6,8},{7,5},{8,10},{9,7},{10,... | collective-permute-start | bytes 442376 | tf_op jit(solution)/shard_map/ppermute | solution.py:265
  (10 other events, 100.9 us)

commit v7 on v6

--- a/solution.py
+++ b/solution.py
@@ -13,8 +13,8 @@
 FAR = NZ // 2
 GROUPS = ((7, 6), (5, 4), (3, 2, 1, 0))
 LATER = {6: (1, 0), 4: (2, 0), 3: (2, 2)}
-DUE = {6: 1, 4: 2}
-CHAINS = ((0, 160), (160, 304), (304, 448))
+DUE = {(6, 0): 1, (4, 0): 2}
+CHAINS = ((0, 224), (224, 448))
 VMEM = 56 * 1024 * 1024
 f32 = jnp.float32
 f16 = jnp.float16
@@ -212,7 +212,7 @@
         functools.partial(solve_kernel, shift, float(rows) ** 0.5),
         out_shape=[out, out, out],
         scratch_shapes=[pltpu.VMEM((grads.shape[0], BLOCK, BLOCK), f32)],
-        compiler_params=pltpu.CompilerParams(vmem_limit_bytes=40 * 1024 * 1024),
+        compiler_params=pltpu.CompilerParams(vmem_limit_bytes=12 * 1024 * 1024),
     )(grads, weights)
 
 
@@ -241,7 +241,6 @@
     sib_first = quad(made[2 * n_out], 1)
     far_at = sib_first.shape[0] - made[0].shape[0]
     far, right = first_product([made[0], sib_first, quad(made[n_out], 2), quad(sib_first[far_at:], 2)], half)
-    sib_rest = quad(after(made[2 * n_out + 1], far), 1)
 
     def send(g, *events):
         at = half if g == 0 else sum(sizes[1:]) + sum(sizes[1:g])
@@ -263,10 +262,12 @@
         return part
 
     ring = lambda x, cross=0: lax.ppermute(x, ("z", "core"), ring_pairs(cross))
-    arrived = [send(0), send(1)]
+    arrived = [send(0)]
+    sib_rest = quad(after(made[2 * n_out + 1], far), 1)
+    arrived.append(send(1))
     nearest = multiply(0, 0, far)
     arrived.append(send(2, far))
-    got = after(ring(far.astype(f16)), nearest, *sent[1:])
+    got = after(ring(far.astype(f16)), nearest, sent[1])
     got = got.astype(f32)
     none = jnp.zeros_like(got)
     got = jnp.where(core == 0, jnp.concatenate([got, none], axis=0), jnp.concatenate([none, got], axis=0))
@@ -275,7 +276,7 @@
     for dist in range(FAR - 2, 0, -1):
         for k, (a, b) in enumerate(CHAINS):
             got = ring(sums[k])
-            due = [arrived[DUE[dist]]] if k == 0 and dist in DUE else []
+            due = [arrived[DUE[dist, k]]] if (dist, k) in DUE else []
             got = after(got, last, *due)
             sums[k] = last = (got.astype(f32) + parts[dist][a:b]).astype(f16)
             if k == 0 and dist in LATER:

time: 165 us -> 161 us (0.976)
  starting transfers between devices: 104 us -> 101 us
  waiting for transfers between devices: 12.9 us -> 14.8 us
    ppermute x23 -> x16, starting transfers between devices: 76.8 us -> 72.7 us  [body(): ring = lambda x, cross=0: lax.ppermute(x, ('z', 'core'), ring_pairs(cross))]
    concatenate x3, other arithmetic: 3.13 us -> 1.06 us  [send(): jnp.concatenate([made[n_out + 1 + g], forward], axis=0)]
    ppermute x23 -> x16, waiting for transfers between devices: 8.64 us -> 10.6 us  [body(): ring = lambda x, cross=0: lax.ppermute(x, ('z', 'core'), ring_pairs(cross))]
    convert_element_type x18 -> x12, other arithmetic: 4.86 us -> 5.91 us  [body(): sums[k] = last = (got.astype(f32) + parts[dist][a:b]).astype(f16)]
  transfers between devices with their start and end apart: 30 -> 23, of which waited for: 8 -> 8; matrix products, arithmetic and copies ran while one was open for 7% -> 5% of each run, Pallas kernels for 4% -> 4%
where the time goes in v7:
time: 161 us; the launch traced here: 160 us
  starting transfers between devices  101 us (63%)
  Pallas kernels  16 us (10%)
  waiting for transfers between devices  14.8 us (9%)
  blocking collectives  14.2 us (9%)
  other arithmetic  9.18 us (6%)
  local copies, waits for them, and re-layouts  2.9 us (2%)
  between operations  2.03 us (1%)
    ppermute x16, starting transfers between devices, body(): ring = lambda x, cross=0: lax.ppermute(x, ('z', 'core'), ring_pairs(cross))  72.7 us
    ppermute x7, starting transfers between devices, body(): lax.ppermute(x, ('yhi', 'core'), [(j, j ^ i) for j in range(4)])  28.2 us
    all_to_all x1, blocking collectives, body(): owned = lax.all_to_all(pieces, ('ylo', 'x', 'core'), 0, 0, tiled=True)  14.2 us
    ppermute x16, waiting for transfers between devices, body(): ring = lambda x, cross=0: lax.ppermute(x, ('z', 'core'), ring_pairs(cross))  10.6 us
    pallas_call x4, Pallas kernels, product(): pl.pallas_call(product_kernel, grid=(2 * count,), in_specs=[pl.BlockSpec(...  6.67 us
    pallas_call x1, Pallas kernels, turn(): pl.pallas_call(turn_kernel, grid_spec=pltpu.PrefetchScalarGridSpec(num_sc...  6.48 us
    convert_element_type x12, other arithmetic, body(): sums[k] = last = (got.astype(f32) + parts[dist][a:b]).astype(f16)  5.91 us
    ppermute x7, waiting for transfers between devices, body(): lax.ppermute(x, ('yhi', 'core'), [(j, j ^ i) for j in range(4)])  4.25 us
  transfers between devices with their start and end apart: 23, of which 8 were waited for; matrix products, arithmetic and copies ran while one was open for 5% of the time, Pallas kernels for 4%

profile of v7, /device:TPU:1, one launch (start us, length us, event | category | flops | bytes accessed | tf_op | source)
XLA Modules:
  0.0 160.1 jit_solution(2343165333325814056)
XLA Ops:
  0.6 6.5 %shard_map.67 = (bf16[736,128]{1,0:T(8,128)(2,1)}, bf16[896,128]{1,0:T(8,128)(2,1)}, bf16[896,128]{1,0:T(8,128)(2,1)}, bf16[1792,128]{1,0:T(8,128)(2,1)}, bf16[7...) custom-call(s32[2]{0:T(128)} %len_ref.1, ...), custom_call_target="tpu_custom_call" | custom-call | tf_op jit(solution)/shard_map/pallas_call | solution.py:91
  7.1 8.8 %collective-permute-start = (bf16[2752,128]{1,0:T(8,128)(2,1)}, bf16[2752,128]{1,0:T(8,128)(2,1)S(1)}, u32[]{:S(2)}, u32[]{:S(2)}) collective-permute-start(bf16[2752,128]{1,0:T(8,128)(2,1)} %get-tuple-element.35), channel_id=1, source_target_pairs={{0,1},{1,0},{32,33},{33,32},{2,3},{3,2},{34,35},{35,34},{4,5},{5,4... | collective-permute-start | bytes 2113544 | tf_op jit(solution)/shard_map/ppermute | solution.py:235
  15.9 1.9 %collective-permute-start.2 = (bf16[736,128]{1,0:T(8,128)(2,1)}, bf16[736,128]{1,0:T(8,128)(2,1)S(1)}, u32[]{:S(2)}, u32[]{:S(2)}) collective-permute-start(bf16[736,128]{1,0:T(8,128)(2,1)} %get-tuple-element.38), channel_id=1, source_target_pairs={{0,32},{1,33},{32,0},{33,1},{2,34},{3,35},{34,2},{35,3},{4,36},{5,... | collective-permute-start | bytes 565256 | tf_op jit(solution)/shard_map/ppermute | solution.py:235
  17.9 4.8 %collective-permute-start.3 = (bf16[736,128]{1,0:T(8,128)(2,1)S(1)}, bf16[736,128]{1,0:T(8,128)(2,1)S(1)}, u32[]{:S(2)}, u32[]{:S(2)}) collective-permute-start(bf16[736,128]{1,0:T(8,128)(2,1)S(1)} %slice.106), channel_id=1, source_target_pairs={{0,32},{1,33},{32,0},{33,1},{2,34},{3,35},{34,2},{35,3},{4,36},{5,... | collective-permute-start | bytes 565256 | tf_op jit(solution)/shard_map/ppermute | solution.py:235
  23.7 2.0 %collective-permute-start.1 = (bf16[1792,128]{1,0:T(8,128)(2,1)S(1)}, bf16[1792,128]{1,0:T(8,128)(2,1)S(1)}, u32[]{:S(2)}, u32[]{:S(2)}) collective-permute-start(bf16[1792,128]{1,0:T(8,128)(2,1)S(1)} %pad_maximum_fusion.1), channel_id=1, source_target_pairs={{0,32},{1,33},{32,0},{33,1},{2,34},{3,35},{34,2},{35,3},{4,36},{5,... | collective-permute-start | bytes 1376264 | tf_op jit(solution)/shard_map/ppermute | solution.py:235
  25.8 4.0 %collective-permute-done.3.d_ref = bf16[736,128]{1,0:T(8,128)(2,1)S(1)} collective-permute-done((bf16[736,128]{1,0:T(8,128)(2,1)S(1)}, bf16[736,128]{1,0:T(8,128)(2,1)S(1)}, u32[]{:S(2)}, u32[]{:S(2)}) %collective-permute-start.3) | collective-permute-done | bytes 188448 | tf_op jit(solution)/shard_map/ppermute | solution.py:235
  32.1 3.1 %collective-permute-start.5 = (bf16[5376,128]{1,0:T(8,128)(2,1)S(1)}, bf16[5376,128]{1,0:T(8,128)(2,1)S(1)}, u32[]{:S(2)}, u32[]{:S(2)}) collective-permute-start(bf16[5376,128]{1,0:T(8,128)(2,1)S(1)} %copy-done.12), channel_id=1, source_target_pairs={{0,1},{1,0},{32,33},{33,32},{2,3},{3,2},{34,35},{35,34},{4,5},{5,4... | collective-permute-start | bytes 4128776 | tf_op jit(solution)/shard_map/ppermute | solution.py:235
  35.2 6.7 %collective-permute-start.4 = (f16[224,1024]{1,0:T(8,128)(2,1)S(1)}, f16[224,1024]{1,0:T(8,128)(2,1)S(1)}, u32[]{:S(2)}, u32[]{:S(2)}) collective-permute-start(f16[224,1024]{1,0:T(8,128)(2,1)S(1)} %convert_element_type.101), channel_id=1, source_target_pairs={{0,2},{1,31},{2,4},{3,1},{4,6},{5,3},{6,8},{7,5},{8,10},{9,7},{10,... | collective-permute-start | bytes 1376264 | tf_op jit(solution)/shard_map/ppermute | solution.py:264
  42.0 1.7 %shard_map.69 = f32[896,1024]{1,0:T(8,128)S(1)} custom-call(bf16[896,128]{1,0:T(8,128)(2,1)S(1)} %copy-done.5, bf16[2752,128]{1,0:T(8,128)(2,1)S(1)} %collective-permute-done.b_ref, bf16[1792,128]{1,0:T(8,128)(2,1)S(1)} %collective-permute-done.1.c_ref.d_ref, bf16[1792,128]{1,0:T(8,128)(2,1)S(1)} %collective-permute-done.1.c_ref.d_ref, ...), custom_call_target="tpu_custom_call" | custom-call | flops 37580963840 | bytes 5505024 | tf_op jit(solution)/shard_map/pallas_call | solution.py:145
  43.7 3.9 %collective-permute-start.7 = (bf16[1792,128]{1,0:T(8,128)(2,1)S(1)}, bf16[1792,128]{1,0:T(8,128)(2,1)S(1)}, u32[]{:S(2)}, u32[]{:S(2)}) collective-permute-start(bf16[1792,128]{1,0:T(8,128)(2,1)S(1)} %pad_maximum_fusion.2), channel_id=1, source_target_pairs={{0,32},{1,33},{32,0},{33,1},{2,34},{3,35},{34,2},{35,3},{4,36},{5,... | collective-permute-start | bytes 1376264 | tf_op jit(solution)/shard_map/ppermute | solution.py:235
  48.4 4.9 %collective-permute-start.6 = (f16[224,1024]{1,0:T(8,128)(2,1)S(1)}, f16[224,1024]{1,0:T(8,128)(2,1)S(1)}, u32[]{:S(2)}, u32[]{:S(2)}) collective-permute-start(f16[224,1024]{1,0:T(8,128)(2,1)S(1)} %get-tuple-element.66), channel_id=1, source_target_pairs={{0,2},{1,31},{2,4},{3,1},{4,6},{5,3},{6,8},{7,5},{8,10},{9,7},{10,... | collective-permute-start | bytes 1376264 | tf_op jit(solution)/shard_map/ppermute | solution.py:264
  53.2 2.1 %collective-permute-start.9 = (f16[224,1024]{1,0:T(8,128)(2,1)S(1)}, f16[224,1024]{1,0:T(8,128)(2,1)S(1)}, u32[]{:S(2)}, u32[]{:S(2)}) collective-permute-start(f16[224,1024]{1,0:T(8,128)(2,1)S(1)} %get-tuple-element.65), channel_id=1, source_target_pairs={{0,2},{1,31},{2,4},{3,1},{4,6},{5,3},{6,8},{7,5},{8,10},{9,7},{10,... | collective-permute-start | bytes 1376264 | tf_op jit(solution)/shard_map/ppermute | solution.py:264
  55.4 3.7 %collective-permute-start.12 = (bf16[3584,128]{1,0:T(8,128)(2,1)S(1)}, bf16[3584,128]{1,0:T(8,128)(2,1)S(1)}, u32[]{:S(2)}, u32[]{:S(2)}) collective-permute-start(bf16[3584,128]{1,0:T(8,128)(2,1)S(1)} %pad_maximum_fusion), channel_id=1, source_target_pairs={{0,32},{1,33},{32,0},{33,1},{2,34},{3,35},{34,2},{35,3},{4,36},{5,... | collective-permute-start | bytes 2752520 | tf_op jit(solution)/shard_map/ppermute | solution.py:235
  59.4 4.5 %collective-permute-start.8 = (f16[224,1024]{1,0:T(8,128)(2,1)S(1)}, f16[224,1024]{1,0:T(8,128)(2,1)S(1)}, u32[]{:S(2)}, u32[]{:S(2)}) collective-permute-start(f16[224,1024]{1,0:T(8,128)(2,1)S(1)} %fusion.11), channel_id=1, source_target_pairs={{0,2},{1,31},{2,4},{3,1},{4,6},{5,3},{6,8},{7,5},{8,10},{9,7},{10,... | collective-permute-start | bytes 1376264 | tf_op jit(solution)/shard_map/ppermute | solution.py:264
  64.0 5.0 %collective-permute-start.11 = (f16[224,1024]{1,0:T(8,128)(2,1)S(1)}, f16[224,1024]{1,0:T(8,128)(2,1)S(1)}, u32[]{:S(2)}, u32[]{:S(2)}) collective-permute-start(f16[224,1024]{1,0:T(8,128)(2,1)S(1)} %fusion.10), channel_id=1, source_target_pairs={{0,2},{1,31},{2,4},{3,1},{4,6},{5,3},{6,8},{7,5},{8,10},{9,7},{10,... | collective-permute-start | bytes 1376264 | tf_op jit(solution)/shard_map/ppermute | solution.py:264
  70.9 3.8 %collective-permute-start.10 = (f16[224,1024]{1,0:T(8,128)(2,1)S(1)}, f16[224,1024]{1,0:T(8,128)(2,1)S(1)}, u32[]{:S(2)}, u32[]{:S(2)}) collective-permute-start(f16[224,1024]{1,0:T(8,128)(2,1)S(1)} %fusion.9), channel_id=1, source_target_pairs={{0,2},{1,31},{2,4},{3,1},{4,6},{5,3},{6,8},{7,5},{8,10},{9,7},{10,... | collective-permute-start | bytes 1376264 | tf_op jit(solution)/shard_map/ppermute | solution.py:264
  74.9 5.0 %collective-permute-start.14 = (f16[224,1024]{1,0:T(8,128)(2,1)S(1)}, f16[224,1024]{1,0:T(8,128)(2,1)S(1)}, u32[]{:S(2)}, u32[]{:S(2)}) collective-permute-start(f16[224,1024]{1,0:T(8,128)(2,1)S(1)} %fusion.8), channel_id=1, source_target_pairs={{0,2},{1,31},{2,4},{3,1},{4,6},{5,3},{6,8},{7,5},{8,10},{9,7},{10,... | collective-permute-start | bytes 1376264 | tf_op jit(solution)/shard_map/ppermute | solution.py:264
  80.6 4.7 %collective-permute-start.13 = (f16[224,1024]{1,0:T(8,128)(2,1)S(1)}, f16[224,1024]{1,0:T(8,128)(2,1)S(1)}, u32[]{:S(2)}, u32[]{:S(2)}) collective-permute-start(f16[224,1024]{1,0:T(8,128)(2,1)S(1)} %fusion.7), channel_id=1, source_target_pairs={{0,2},{1,31},{2,4},{3,1},{4,6},{5,3},{6,8},{7,5},{8,10},{9,7},{10,... | collective-permute-start | bytes 1376264 | tf_op jit(solution)/shard_map/ppermute | solution.py:264
  85.5 5.0 %collective-permute-start.16 = (f16[224,1024]{1,0:T(8,128)(2,1)S(1)}, f16[224,1024]{1,0:T(8,128)(2,1)S(1)}, u32[]{:S(2)}, u32[]{:S(2)}) collective-permute-start(f16[224,1024]{1,0:T(8,128)(2,1)S(1)} %fusion.6), channel_id=1, source_target_pairs={{0,2},{1,31},{2,4},{3,1},{4,6},{5,3},{6,8},{7,5},{8,10},{9,7},{10,... | collective-permute-start | bytes 1376264 | tf_op jit(solution)/shard_map/ppermute | solution.py:264
  90.5 1.7 %shard_map.71 = f32[896,1024]{1,0:T(8,128)S(1)} custom-call(bf16[1792,128]{1,0:T(8,128)(2,1)S(1)} %copy-done.3, bf16[5376,128]{1,0:T(8,128)(2,1)S(1)} %collective-permute-done.5.b_ref, bf16[3584,128]{1,0:T(8,128)(2,1)S(1)} %collective-permute-done.12.c_ref.d_ref, bf16[3584,128]{1,0:T(8,128)(2,1)S(1)} %collective-permute-done.12.c_ref.d_ref, ...), custom_call_target="tpu_custom_call" | custom-call | flops 37580963840 | bytes 5505024 | tf_op jit(solution)/shard_map/pallas_call | solution.py:145
  93.3 3.3 %collective-permute-start.15 = (f16[224,1024]{1,0:T(8,128)(2,1)}, f16[224,1024]{1,0:T(8,128)(2,1)}, u32[]{:S(2)}, u32[]{:S(2)}) collective-permute-start(f16[224,1024]{1,0:T(8,128)(2,1)} %fusion.5), channel_id=1, source_target_pairs={{0,2},{1,31},{2,4},{3,1},{4,6},{5,3},{6,8},{7,5},{8,10},{9,7},{10,... | collective-permute-start | bytes 1376264 | tf_op jit(solution)/shard_map/ppermute | solution.py:264
  97.6 4.3 %collective-permute-start.18 = (f16[224,1024]{1,0:T(8,128)(2,1)}, f16[224,1024]{1,0:T(8,128)(2,1)S(1)}, u32[]{:S(2)}, u32[]{:S(2)}) collective-permute-start(f16[224,1024]{1,0:T(8,128)(2,1)} %fusion.4), channel_id=1, source_target_pairs={{0,2},{1,31},{2,4},{3,1},{4,6},{5,3},{6,8},{7,5},{8,10},{9,7},{10,... | collective-permute-start | bytes 1376264 | tf_op jit(solution)/shard_map/ppermute | solution.py:264
  104.3 4.5 %collective-permute-start.17 = (f16[224,1024]{1,0:T(8,128)(2,1)S(1)}, f16[224,1024]{1,0:T(8,128)(2,1)S(1)}, u32[]{:S(2)}, u32[]{:S(2)}) collective-permute-start(f16[224,1024]{1,0:T(8,128)(2,1)S(1)} %fusion.3), channel_id=1, source_target_pairs={{0,2},{1,31},{2,4},{3,1},{4,6},{5,3},{6,8},{7,5},{8,10},{9,7},{10,... | collective-permute-start | bytes 1376264 | tf_op jit(solution)/shard_map/ppermute | solution.py:264
  110.2 3.7 %collective-permute-start.20 = (f16[224,1024]{1,0:T(8,128)(2,1)S(1)}, f16[224,1024]{1,0:T(8,128)(2,1)S(1)}, u32[]{:S(2)}, u32[]{:S(2)}) collective-permute-start(f16[224,1024]{1,0:T(8,128)(2,1)S(1)} %fusion.2), channel_id=1, source_target_pairs={{0,2},{1,31},{2,4},{3,1},{4,6},{5,3},{6,8},{7,5},{8,10},{9,7},{10,... | collective-permute-start | bytes 1376264 | tf_op jit(solution)/shard_map/ppermute | solution.py:264
  115.7 4.0 %collective-permute-done.20 = f16[224,1024]{1,0:T(8,128)(2,1)S(1)} collective-permute-done((f16[224,1024]{1,0:T(8,128)(2,1)S(1)}, f16[224,1024]{1,0:T(8,128)(2,1)S(1)}, u32[]{:S(2)}, u32[]{:S(2)}) %collective-permute-start.20) | collective-permute-done | bytes 458784 | tf_op jit(solution)/shard_map/ppermute | solution.py:264
  120.2 9.4 %collective-permute-start.22 = (f16[448,512]{1,0:T(8,128)(2,1)S(1)}, f16[448,512]{1,0:T(8,128)(2,1)S(1)}, u32[]{:S(2)}, u32[]{:S(2)}) collective-permute-start(f16[448,512]{1,0:T(8,128)(2,1)S(1)} %pad_maximum_fusion.3), channel_id=1, source_target_pairs={{0,3},{1,30},{2,5},{3,0},{4,7},{5,2},{6,9},{7,4},{8,11},{9,6},{10,... | collective-permute-start | bytes 1376264 | tf_op jit(solution)/shard_map/ppermute | solution.py:264
  129.6 1.9 %collective-permute-start.21 = (f16[224,512]{1,0:T(8,128)(2,1)S(1)}, f16[224,512]{1,0:T(8,128)(2,1)S(1)}, u32[]{:S(2)}, u32[]{:S(2)}) collective-permute-start(f16[224,512]{1,0:T(8,128)(2,1)S(1)} %get-tuple-element.69), channel_id=1, source_target_pairs={{0,2},{1,31},{2,4},{3,1},{4,6},{5,3},{6,8},{7,5},{8,10},{9,7},{10,... | collective-permute-start | bytes 688136 | tf_op jit(solution)/shard_map/ppermute | solution.py:264
  131.5 4.0 %collective-permute-start.19 = (f16[224,512]{1,0:T(8,128)(2,1)S(1)}, f16[224,512]{1,0:T(8,128)(2,1)}, u32[]{:S(2)}, u32[]{:S(2)}) collective-permute-start(f16[224,512]{1,0:T(8,128)(2,1)S(1)} %get-tuple-element.67), channel_id=1, source_target_pairs={{0,2},{1,31},{2,4},{3,1},{4,6},{5,3},{6,8},{7,5},{8,10},{9,7},{10,... | collective-permute-start | bytes 688136 | tf_op jit(solution)/shard_map/ppermute | solution.py:264
  136.8 2.9 %collective-permute-done.21 = f16[224,512]{1,0:T(8,128)(2,1)S(1)} collective-permute-done((f16[224,512]{1,0:T(8,128)(2,1)S(1)}, f16[224,512]{1,0:T(8,128)(2,1)S(1)}, u32[]{:S(2)}, u32[]{:S(2)}) %collective-permute-start.21) | collective-permute-done | bytes 229408 | tf_op jit(solution)/shard_map/ppermute | solution.py:264
  139.7 2.2 %collective-permute-done.19 = f16[224,512]{1,0:T(8,128)(2,1)} collective-permute-done((f16[224,512]{1,0:T(8,128)(2,1)S(1)}, f16[224,512]{1,0:T(8,128)(2,1)}, u32[]{:S(2)}, u32[]{:S(2)}) %collective-permute-start.19) | collective-permute-done | bytes 229408 | tf_op jit(solution)/shard_map/ppermute | solution.py:264
  143.2 14.2 %all_to_all.5 = f16[16,28,512]{2,1,0:T(8,128)(2,1)S(1)} all-to-all(f16[16,28,512]{2,1,0:T(8,128)(2,1)S(1)} %reshape.12), channel_id=1, replica_groups=mesh['ylo'=2,'x'=4,'yhi'=2,'z'=16,'core'=2] {'ylo','x','core'}, dimensions={0} | all-to-all | bytes 917504 | tf_op jit(solution)/shard_map/all_to_all | solution.py:290
  157.7 2.4 %shard_map.73 = (f32[28,512]{1,0:T(8,128)}, f32[28,512]{1,0:T(8,128)}, f32[28,512]{1,0:T(8,128)}) custom-call(f32[16,32,512]{2,1,0:T(8,128)S(1)} %pad.6.g_ref, bf16[28,512]{1,0:T(8,128)(2,1)S(1)} %copy-done.2), custom_call_target="tpu_custom_call" | custom-call | tf_op jit(solution)/shard_map/pallas_call | solution.py:211
  (81 shorter events, 17.6 us)
Async XLA Ops:
  7.1 10.8 %collective-permute-start = (bf16[2752,128]{1,0:T(8,128)(2,1)}, bf16[2752,128]{1,0:T(8,128)(2,1)S(1)}, u32[]{:S(2)}, u32[]{:S(2)}) collective-permute-start(bf16[2752,128]{1,0:T(8,128)(2,1)} %get-tuple-element.35), channel_id=1, source_target_pairs={{0,1},{1,0},{32,33},{33,32},{2,3},{3,2},{34,35},{35,34},{4,5},{5,4... | collective-permute-start | bytes 2113544 | tf_op jit(solution)/shard_map/ppermute | solution.py:235
  15.9 10.0 %collective-permute-start.2 = (bf16[736,128]{1,0:T(8,128)(2,1)}, bf16[736,128]{1,0:T(8,128)(2,1)S(1)}, u32[]{:S(2)}, u32[]{:S(2)}) collective-permute-start(bf16[736,128]{1,0:T(8,128)(2,1)} %get-tuple-element.38), channel_id=1, source_target_pairs={{0,32},{1,33},{32,0},{33,1},{2,34},{3,35},{34,2},{35,3},{4,36},{5,... | collective-permute-start | bytes 565256 | tf_op jit(solution)/shard_map/ppermute | solution.py:235
  17.9 12.0 %collective-permute-start.3 = (bf16[736,128]{1,0:T(8,128)(2,1)S(1)}, bf16[736,128]{1,0:T(8,128)(2,1)S(1)}, u32[]{:S(2)}, u32[]{:S(2)}) collective-permute-start(bf16[736,128]{1,0:T(8,128)(2,1)S(1)} %slice.106), channel_id=1, source_target_pairs={{0,32},{1,33},{32,0},{33,1},{2,34},{3,35},{34,2},{35,3},{4,36},{5,... | collective-permute-start | bytes 565256 | tf_op jit(solution)/shard_map/ppermute | solution.py:235
  23.7 18.2 %collective-permute-start.1 = (bf16[1792,128]{1,0:T(8,128)(2,1)S(1)}, bf16[1792,128]{1,0:T(8,128)(2,1)S(1)}, u32[]{:S(2)}, u32[]{:S(2)}) collective-permute-start(bf16[1792,128]{1,0:T(8,128)(2,1)S(1)} %pad_maximum_fusion.1), channel_id=1, source_target_pairs={{0,32},{1,33},{32,0},{33,1},{2,34},{3,35},{34,2},{35,3},{4,36},{5,... | collective-permute-start | bytes 1376264 | tf_op jit(solution)/shard_map/ppermute | solution.py:235
  30.8 11.1 %copy-start.5 = (bf16[896,128]{1,0:T(8,128)(2,1)S(1)}, bf16[896,128]{1,0:T(8,128)(2,1)}, u32[]{:S(2)}) copy-start(bf16[896,128]{1,0:T(8,128)(2,1)} %get-tuple-element.34.a_ref) | copy-start | bytes 688132
  31.3 59.2 %copy-start.7 = (bf16[512,1024]{1,0:T(8,128)(2,1)}, bf16[512,1024]{1,0:T(8,128)(2,1)S(1)}, u32[]{:S(2)}) copy-start(bf16[512,1024]{1,0:T(8,128)(2,1)S(1)} %get-tuple-element.41.right_ref) | copy-start | bytes 3145732
  32.1 11.5 %collective-permute-start.5 = (bf16[5376,128]{1,0:T(8,128)(2,1)S(1)}, bf16[5376,128]{1,0:T(8,128)(2,1)S(1)}, u32[]{:S(2)}, u32[]{:S(2)}) collective-permute-start(bf16[5376,128]{1,0:T(8,128)(2,1)S(1)} %copy-done.12), channel_id=1, source_target_pairs={{0,1},{1,0},{32,33},{33,32},{2,3},{3,2},{34,35},{35,34},{4,5},{5,4... | collective-permute-start | bytes 4128776 | tf_op jit(solution)/shard_map/ppermute | solution.py:235
  35.2 12.4 %collective-permute-start.4 = (f16[224,1024]{1,0:T(8,128)(2,1)S(1)}, f16[224,1024]{1,0:T(8,128)(2,1)S(1)}, u32[]{:S(2)}, u32[]{:S(2)}) collective-permute-start(f16[224,1024]{1,0:T(8,128)(2,1)S(1)} %convert_element_type.101), channel_id=1, source_target_pairs={{0,2},{1,31},{2,4},{3,1},{4,6},{5,3},{6,8},{7,5},{8,10},{9,7},{10,... | collective-permute-start | bytes 1376264 | tf_op jit(solution)/shard_map/ppermute | solution.py:264
  43.7 15.5 %collective-permute-start.7 = (bf16[1792,128]{1,0:T(8,128)(2,1)S(1)}, bf16[1792,128]{1,0:T(8,128)(2,1)S(1)}, u32[]{:S(2)}, u32[]{:S(2)}) collective-permute-start(bf16[1792,128]{1,0:T(8,128)(2,1)S(1)} %pad_maximum_fusion.2), channel_id=1, source_target_pairs={{0,32},{1,33},{32,0},{33,1},{2,34},{3,35},{34,2},{35,3},{4,36},{5,... | collective-permute-start | bytes 1376264 | tf_op jit(solution)/shard_map/ppermute | solution.py:235
  47.7 7.7 %copy-start.9 = (bf16[1792,128]{1,0:T(8,128)(2,1)S(1)}, bf16[1792,128]{1,0:T(8,128)(2,1)}, u32[]{:S(2)}) copy-start(bf16[1792,128]{1,0:T(8,128)(2,1)} %get-tuple-element.52) | copy-start | bytes 1376260
  48.4 20.7 %copy-start.4 = (bf16[896,128]{1,0:T(8,128)(2,1)S(1)}, bf16[896,128]{1,0:T(8,128)(2,1)}, u32[]{:S(2)}) copy-start(bf16[896,128]{1,0:T(8,128)(2,1)} %get-tuple-element.49.a_ref) | copy-start | bytes 688132
  48.4 10.8 %collective-permute-start.6 = (f16[224,1024]{1,0:T(8,128)(2,1)S(1)}, f16[224,1024]{1,0:T(8,128)(2,1)S(1)}, u32[]{:S(2)}, u32[]{:S(2)}) collective-permute-start(f16[224,1024]{1,0:T(8,128)(2,1)S(1)} %get-tuple-element.66), channel_id=1, source_target_pairs={{0,2},{1,31},{2,4},{3,1},{4,6},{5,3},{6,8},{7,5},{8,10},{9,7},{10,... | collective-permute-start | bytes 1376264 | tf_op jit(solution)/shard_map/ppermute | solution.py:264
  53.2 10.6 %collective-permute-start.9 = (f16[224,1024]{1,0:T(8,128)(2,1)S(1)}, f16[224,1024]{1,0:T(8,128)(2,1)S(1)}, u32[]{:S(2)}, u32[]{:S(2)}) collective-permute-start(f16[224,1024]{1,0:T(8,128)(2,1)S(1)} %get-tuple-element.65), channel_id=1, source_target_pairs={{0,2},{1,31},{2,4},{3,1},{4,6},{5,3},{6,8},{7,5},{8,10},{9,7},{10,... | collective-permute-start | bytes 1376264 | tf_op jit(solution)/shard_map/ppermute | solution.py:264
  55.4 24.5 %collective-permute-start.12 = (bf16[3584,128]{1,0:T(8,128)(2,1)S(1)}, bf16[3584,128]{1,0:T(8,128)(2,1)S(1)}, u32[]{:S(2)}, u32[]{:S(2)}) collective-permute-start(bf16[3584,128]{1,0:T(8,128)(2,1)S(1)} %pad_maximum_fusion), channel_id=1, source_target_pairs={{0,32},{1,33},{32,0},{33,1},{2,34},{3,35},{34,2},{35,3},{4,36},{5,... | collective-permute-start | bytes 2752520 | tf_op jit(solution)/shard_map/ppermute | solution.py:235
  59.4 11.4 %collective-permute-start.8 = (f16[224,1024]{1,0:T(8,128)(2,1)S(1)}, f16[224,1024]{1,0:T(8,128)(2,1)S(1)}, u32[]{:S(2)}, u32[]{:S(2)}) collective-permute-start(f16[224,1024]{1,0:T(8,128)(2,1)S(1)} %fusion.11), channel_id=1, source_target_pairs={{0,2},{1,31},{2,4},{3,1},{4,6},{5,3},{6,8},{7,5},{8,10},{9,7},{10,... | collective-permute-start | bytes 1376264 | tf_op jit(solution)/shard_map/ppermute | solution.py:264
  64.0 10.7 %collective-permute-start.11 = (f16[224,1024]{1,0:T(8,128)(2,1)S(1)}, f16[224,1024]{1,0:T(8,128)(2,1)S(1)}, u32[]{:S(2)}, u32[]{:S(2)}) collective-permute-start(f16[224,1024]{1,0:T(8,128)(2,1)S(1)} %fusion.10), channel_id=1, source_target_pairs={{0,2},{1,31},{2,4},{3,1},{4,6},{5,3},{6,8},{7,5},{8,10},{9,7},{10,... | collective-permute-start | bytes 1376264 | tf_op jit(solution)/shard_map/ppermute | solution.py:264
  70.7 19.8 %copy-start.3 = (bf16[1792,128]{1,0:T(8,128)(2,1)S(1)}, bf16[1792,128]{1,0:T(8,128)(2,1)}, u32[]{:S(2)}) copy-start(bf16[1792,128]{1,0:T(8,128)(2,1)} %get-tuple-element.57.a_ref) | copy-start | bytes 1376260
  70.9 9.5 %collective-permute-start.10 = (f16[224,1024]{1,0:T(8,128)(2,1)S(1)}, f16[224,1024]{1,0:T(8,128)(2,1)S(1)}, u32[]{:S(2)}, u32[]{:S(2)}) collective-permute-start(f16[224,1024]{1,0:T(8,128)(2,1)S(1)} %fusion.9), channel_id=1, source_target_pairs={{0,2},{1,31},{2,4},{3,1},{4,6},{5,3},{6,8},{7,5},{8,10},{9,7},{10,... | collective-permute-start | bytes 1376264 | tf_op jit(solution)/shard_map/ppermute | solution.py:264
  74.9 10.5 %collective-permute-start.14 = (f16[224,1024]{1,0:T(8,128)(2,1)S(1)}, f16[224,1024]{1,0:T(8,128)(2,1)S(1)}, u32[]{:S(2)}, u32[]{:S(2)}) collective-permute-start(f16[224,1024]{1,0:T(8,128)(2,1)S(1)} %fusion.8), channel_id=1, source_target_pairs={{0,2},{1,31},{2,4},{3,1},{4,6},{5,3},{6,8},{7,5},{8,10},{9,7},{10,... | collective-permute-start | bytes 1376264 | tf_op jit(solution)/shard_map/ppermute | solution.py:264
  80.6 11.6 %collective-permute-start.13 = (f16[224,1024]{1,0:T(8,128)(2,1)S(1)}, f16[224,1024]{1,0:T(8,128)(2,1)S(1)}, u32[]{:S(2)}, u32[]{:S(2)}) collective-permute-start(f16[224,1024]{1,0:T(8,128)(2,1)S(1)} %fusion.7), channel_id=1, source_target_pairs={{0,2},{1,31},{2,4},{3,1},{4,6},{5,3},{6,8},{7,5},{8,10},{9,7},{10,... | collective-permute-start | bytes 1376264 | tf_op jit(solution)/shard_map/ppermute | solution.py:264
  85.5 11.1 %collective-permute-start.16 = (f16[224,1024]{1,0:T(8,128)(2,1)S(1)}, f16[224,1024]{1,0:T(8,128)(2,1)S(1)}, u32[]{:S(2)}, u32[]{:S(2)}) collective-permute-start(f16[224,1024]{1,0:T(8,128)(2,1)S(1)} %fusion.6), channel_id=1, source_target_pairs={{0,2},{1,31},{2,4},{3,1},{4,6},{5,3},{6,8},{7,5},{8,10},{9,7},{10,... | collective-permute-start | bytes 1376264 | tf_op jit(solution)/shard_map/ppermute | solution.py:264
  93.3 9.5 %collective-permute-start.15 = (f16[224,1024]{1,0:T(8,128)(2,1)}, f16[224,1024]{1,0:T(8,128)(2,1)}, u32[]{:S(2)}, u32[]{:S(2)}) collective-permute-start(f16[224,1024]{1,0:T(8,128)(2,1)} %fusion.5), channel_id=1, source_target_pairs={{0,2},{1,31},{2,4},{3,1},{4,6},{5,3},{6,8},{7,5},{8,10},{9,7},{10,... | collective-permute-start | bytes 1376264 | tf_op jit(solution)/shard_map/ppermute | solution.py:264
  97.6 11.2 %collective-permute-start.18 = (f16[224,1024]{1,0:T(8,128)(2,1)}, f16[224,1024]{1,0:T(8,128)(2,1)S(1)}, u32[]{:S(2)}, u32[]{:S(2)}) collective-permute-start(f16[224,1024]{1,0:T(8,128)(2,1)} %fusion.4), channel_id=1, source_target_pairs={{0,2},{1,31},{2,4},{3,1},{4,6},{5,3},{6,8},{7,5},{8,10},{9,7},{10,... | collective-permute-start | bytes 1376264 | tf_op jit(solution)/shard_map/ppermute | solution.py:264
  101.9 12.0 %copy-start.8 = (bf16[512,1024]{1,0:T(8,128)(2,1)S(1)}, bf16[512,1024]{1,0:T(8,128)(2,1)}, u32[]{:S(2)}) copy-start(bf16[512,1024]{1,0:T(8,128)(2,1)} %copy-done.7) | copy-start | bytes 3145732
  104.3 11.3 %collective-permute-start.17 = (f16[224,1024]{1,0:T(8,128)(2,1)S(1)}, f16[224,1024]{1,0:T(8,128)(2,1)S(1)}, u32[]{:S(2)}, u32[]{:S(2)}) collective-permute-start(f16[224,1024]{1,0:T(8,128)(2,1)S(1)} %fusion.3), channel_id=1, source_target_pairs={{0,2},{1,31},{2,4},{3,1},{4,6},{5,3},{6,8},{7,5},{8,10},{9,7},{10,... | collective-permute-start | bytes 1376264 | tf_op jit(solution)/shard_map/ppermute | solution.py:264
  110.2 9.5 %collective-permute-start.20 = (f16[224,1024]{1,0:T(8,128)(2,1)S(1)}, f16[224,1024]{1,0:T(8,128)(2,1)S(1)}, u32[]{:S(2)}, u32[]{:S(2)}) collective-permute-start(f16[224,1024]{1,0:T(8,128)(2,1)S(1)} %fusion.2), channel_id=1, source_target_pairs={{0,2},{1,31},{2,4},{3,1},{4,6},{5,3},{6,8},{7,5},{8,10},{9,7},{10,... | collective-permute-start | bytes 1376264 | tf_op jit(solution)/shard_map/ppermute | solution.py:264
  115.5 20.0 %copy-start.11 = (s32[2]{0:T(128)S(1)}, s32[2]{0:T(128)}, u32[]{:S(2)}) copy-start(s32[2]{0:T(128)} %len_ref.1) | copy-start | bytes 28
  119.8 22.0 %slice-start = ((f32[896,1024]{1,0:T(8,128)}), f32[448,1024]{1,0:T(8,128)S(1)}, s32[]{:S(2)}) async-start(f32[896,1024]{1,0:T(8,128)} %copy-done), calls=%async_computation.1 | async-start | bytes 3670016 | tf_op jit(solution)/shard_map/slice | solution.py:261
  120.2 21.7 %collective-permute-start.22 = (f16[448,512]{1,0:T(8,128)(2,1)S(1)}, f16[448,512]{1,0:T(8,128)(2,1)S(1)}, u32[]{:S(2)}, u32[]{:S(2)}) collective-permute-start(f16[448,512]{1,0:T(8,128)(2,1)S(1)} %pad_maximum_fusion.3), channel_id=1, source_target_pairs={{0,3},{1,30},{2,5},{3,0},{4,7},{5,2},{6,9},{7,4},{8,11},{9,6},{10,... | collective-permute-start | bytes 1376264 | tf_op jit(solution)/shard_map/ppermute | solution.py:264
  129.6 10.1 %collective-permute-start.21 = (f16[224,512]{1,0:T(8,128)(2,1)S(1)}, f16[224,512]{1,0:T(8,128)(2,1)S(1)}, u32[]{:S(2)}, u32[]{:S(2)}) collective-permute-start(f16[224,512]{1,0:T(8,128)(2,1)S(1)} %get-tuple-element.69), channel_id=1, source_target_pairs={{0,2},{1,31},{2,4},{3,1},{4,6},{5,3},{6,8},{7,5},{8,10},{9,7},{10,... | collective-permute-start | bytes 688136 | tf_op jit(solution)/shard_map/ppermute | solution.py:264
  131.5 10.3 %collective-permute-start.19 = (f16[224,512]{1,0:T(8,128)(2,1)S(1)}, f16[224,512]{1,0:T(8,128)(2,1)}, u32[]{:S(2)}, u32[]{:S(2)}) collective-permute-start(f16[224,512]{1,0:T(8,128)(2,1)S(1)} %get-tuple-element.67), channel_id=1, source_target_pairs={{0,2},{1,31},{2,4},{3,1},{4,6},{5,3},{6,8},{7,5},{8,10},{9,7},{10,... | collective-permute-start | bytes 688136 | tf_op jit(solution)/shard_map/ppermute | solution.py:264
  141.8 15.8 %copy-start.2 = (bf16[28,512]{1,0:T(8,128)(2,1)S(1)}, bf16[28,512]{1,0:T(8,128)(2,1)}, u32[]{:S(2)}) copy-start(bf16[28,512]{1,0:T(8,128)(2,1)} %w_ref.1) | copy-start | bytes 86020
  (5 other events, 12.6 us)

commit v8 on v7

--- a/solution.py
+++ b/solution.py
@@ -13,7 +13,7 @@
 FAR = NZ // 2
 GROUPS = ((7, 6), (5, 4), (3, 2, 1, 0))
 LATER = {6: (1, 0), 4: (2, 0), 3: (2, 2)}
-DUE = {(6, 0): 1, (4, 0): 2}
+DUE = {(6, 1): 1, (4, 0): 2}
 CHAINS = ((0, 224), (224, 448))
 VMEM = 56 * 1024 * 1024
 f32 = jnp.float32
@@ -263,11 +263,12 @@
 
     ring = lambda x, cross=0: lax.ppermute(x, ("z", "core"), ring_pairs(cross))
     arrived = [send(0)]
-    sib_rest = quad(after(made[2 * n_out + 1], far), 1)
-    arrived.append(send(1))
     nearest = multiply(0, 0, far)
-    arrived.append(send(2, far))
-    got = after(ring(far.astype(f16)), nearest, sent[1])
+    quarter = half // 2
+    got = [ring(far[i * quarter:(i + 1) * quarter].astype(f16)) for i in range(2)]
+    sib_rest = quad(after(made[2 * n_out + 1], got[0]), 1)
+    arrived += [send(1), send(2)]
+    got = after(jnp.concatenate(got, axis=0), nearest)
     got = got.astype(f32)
     none = jnp.zeros_like(got)
     got = jnp.where(core == 0, jnp.concatenate([got, none], axis=0), jnp.concatenate([none, got], axis=0))
@@ -277,6 +278,8 @@
         for k, (a, b) in enumerate(CHAINS):
             got = ring(sums[k])
             due = [arrived[DUE[dist, k]]] if (dist, k) in DUE else []
+            if (dist, k) == (FAR - 2, 0):
+                due.append(sent[1])
             got = after(got, last, *due)
             sums[k] = last = (got.astype(f32) + parts[dist][a:b]).astype(f16)
             if k == 0 and dist in LATER:

time: 161 us -> 169 us (1.050)
  waiting for transfers between devices: 14.8 us -> 19.9 us
  local copies, waits for them, and re-layouts: 2.9 us -> 5.05 us
    ppermute x7, waiting for transfers between devices: 4.25 us -> 10.2 us  [body(): lax.ppermute(x, ('yhi', 'core'), [(j, j ^ i) for j in range(4)])]
    ppermute x16 -> x17, starting transfers between devices: 72.7 us -> 69.8 us  [body(): ring = lambda x, cross=0: lax.ppermute(x, ('z', 'core'), ring_pairs(cross))]
    ppermute x7, starting transfers between devices: 28.2 us -> 30.4 us  [body(): lax.ppermute(x, ('yhi', 'core'), [(j, j ^ i) for j in range(4)])]
    unnamed x26 -> x30, local copies, waits for them, and re-layouts: 1.78 us -> 3.85 us
    ppermute x16 -> x17, waiting for transfers between devices: 10.6 us -> 9.73 us  [body(): ring = lambda x, cross=0: lax.ppermute(x, ('z', 'core'), ring_pairs(cross))]
  transfers between devices with their start and end apart: 23 -> 24, of which waited for: 8 -> 11; matrix products, arithmetic and copies ran while one was open for 5% -> 6% of each run, Pallas kernels for 4% -> 4%
where the time goes in v8:
time: 169 us; the launch traced here: 168 us
  starting transfers between devices  100 us (59%)
  waiting for transfers between devices  19.9 us (12%)
  Pallas kernels  16 us (9%)
  blocking collectives  14.2 us (8%)
  other arithmetic  10.4 us (6%)
  local copies, waits for them, and re-layouts  5.05 us (3%)
  between operations  2.06 us (1%)
    ppermute x17, starting transfers between devices, body(): ring = lambda x, cross=0: lax.ppermute(x, ('z', 'core'), ring_pairs(cross))  69.8 us
    ppermute x7, starting transfers between devices, body(): lax.ppermute(x, ('yhi', 'core'), [(j, j ^ i) for j in range(4)])  30.4 us
    all_to_all x1, blocking collectives, body(): owned = lax.all_to_all(pieces, ('ylo', 'x', 'core'), 0, 0, tiled=True)  14.2 us
    ppermute x7, waiting for transfers between devices, body(): lax.ppermute(x, ('yhi', 'core'), [(j, j ^ i) for j in range(4)])  10.2 us
    ppermute x17, waiting for transfers between devices, body(): ring = lambda x, cross=0: lax.ppermute(x, ('z', 'core'), ring_pairs(cross))  9.73 us
    pallas_call x4, Pallas kernels, product(): pl.pallas_call(product_kernel, grid=(2 * count,), in_specs=[pl.BlockSpec(...  6.67 us
    pallas_call x1, Pallas kernels, turn(): pl.pallas_call(turn_kernel, grid_spec=pltpu.PrefetchScalarGridSpec(num_sc...  6.45 us
    convert_element_type x12, other arithmetic, body(): sums[k] = last = (got.astype(f32) + parts[dist][a:b]).astype(f16)  5.96 us
  transfers between devices with their start and end apart: 24, of which 11 were waited for; matrix products, arithmetic and copies ran while one was open for 6% of the time, Pallas kernels for 4%

profile of v8, /device:TPU:1, one launch (start us, length us, event | category | flops | bytes accessed | tf_op | source)
XLA Modules:
  0.0 167.8 jit_solution(5759233171886359038)
XLA Ops:
  0.6 6.4 %shard_map.67 = (bf16[736,128]{1,0:T(8,128)(2,1)}, bf16[896,128]{1,0:T(8,128)(2,1)}, bf16[896,128]{1,0:T(8,128)(2,1)}, bf16[1792,128]{1,0:T(8,128)(2,1)}, bf16[7...) custom-call(s32[2]{0:T(128)} %len_ref.1, ...), custom_call_target="tpu_custom_call" | custom-call | tf_op jit(solution)/shard_map/pallas_call | solution.py:91
  7.1 8.8 %collective-permute-start = (bf16[2752,128]{1,0:T(8,128)(2,1)}, bf16[2752,128]{1,0:T(8,128)(2,1)S(1)}, u32[]{:S(2)}, u32[]{:S(2)}) collective-permute-start(bf16[2752,128]{1,0:T(8,128)(2,1)} %get-tuple-element.34), channel_id=1, source_target_pairs={{0,1},{1,0},{32,33},{33,32},{2,3},{3,2},{34,35},{35,34},{4,5},{5,4... | collective-permute-start | bytes 2113544 | tf_op jit(solution)/shard_map/ppermute | solution.py:235
  15.9 1.9 %collective-permute-start.2 = (bf16[736,128]{1,0:T(8,128)(2,1)}, bf16[736,128]{1,0:T(8,128)(2,1)S(1)}, u32[]{:S(2)}, u32[]{:S(2)}) collective-permute-start(bf16[736,128]{1,0:T(8,128)(2,1)} %get-tuple-element.37), channel_id=1, source_target_pairs={{0,32},{1,33},{32,0},{33,1},{2,34},{3,35},{34,2},{35,3},{4,36},{5,... | collective-permute-start | bytes 565256 | tf_op jit(solution)/shard_map/ppermute | solution.py:235
  17.9 4.8 %collective-permute-start.3 = (bf16[736,128]{1,0:T(8,128)(2,1)S(1)}, bf16[736,128]{1,0:T(8,128)(2,1)S(1)}, u32[]{:S(2)}, u32[]{:S(2)}) collective-permute-start(bf16[736,128]{1,0:T(8,128)(2,1)S(1)} %slice.116), channel_id=1, source_target_pairs={{0,32},{1,33},{32,0},{33,1},{2,34},{3,35},{34,2},{35,3},{4,36},{5,... | collective-permute-start | bytes 565256 | tf_op jit(solution)/shard_map/ppermute | solution.py:235
  23.7 2.0 %collective-permute-start.1 = (bf16[1792,128]{1,0:T(8,128)(2,1)S(1)}, bf16[1792,128]{1,0:T(8,128)(2,1)S(1)}, u32[]{:S(2)}, u32[]{:S(2)}) collective-permute-start(bf16[1792,128]{1,0:T(8,128)(2,1)S(1)} %pad_maximum_fusion.1), channel_id=1, source_target_pairs={{0,32},{1,33},{32,0},{33,1},{2,34},{3,35},{34,2},{35,3},{4,36},{5,... | collective-permute-start | bytes 1376264 | tf_op jit(solution)/shard_map/ppermute | solution.py:235
  25.8 4.0 %collective-permute-done.3.d_ref = bf16[736,128]{1,0:T(8,128)(2,1)S(1)} collective-permute-done((bf16[736,128]{1,0:T(8,128)(2,1)S(1)}, bf16[736,128]{1,0:T(8,128)(2,1)S(1)}, u32[]{:S(2)}, u32[]{:S(2)}) %collective-permute-start.3) | collective-permute-done | bytes 188448 | tf_op jit(solution)/shard_map/ppermute | solution.py:235
  32.4 6.0 %collective-permute-start.4 = (f16[112,1024]{1,0:T(8,128)(2,1)S(1)}, f16[112,1024]{1,0:T(8,128)(2,1)S(1)}, u32[]{:S(2)}, u32[]{:S(2)}) collective-permute-start(f16[112,1024]{1,0:T(8,128)(2,1)S(1)} %get-tuple-element.70), channel_id=1, source_target_pairs={{0,2},{1,31},{2,4},{3,1},{4,6},{5,3},{6,8},{7,5},{8,10},{9,7},{10,... | collective-permute-start | bytes 688136 | tf_op jit(solution)/shard_map/ppermute | solution.py:264
  38.4 2.6 %collective-permute-start.5 = (f16[112,1024]{1,0:T(8,128)(2,1)S(1)}, f16[112,1024]{1,0:T(8,128)(2,1)}, u32[]{:S(2)}, u32[]{:S(2)}) collective-permute-start(f16[112,1024]{1,0:T(8,128)(2,1)S(1)} %get-tuple-element.69), channel_id=1, source_target_pairs={{0,2},{1,31},{2,4},{3,1},{4,6},{5,3},{6,8},{7,5},{8,10},{9,7},{10,... | collective-permute-start | bytes 688136 | tf_op jit(solution)/shard_map/ppermute | solution.py:264
  42.1 5.0 %collective-permute-start.7 = (bf16[5376,128]{1,0:T(8,128)(2,1)}, bf16[5376,128]{1,0:T(8,128)(2,1)S(1)}, u32[]{:S(2)}, u32[]{:S(2)}) collective-permute-start(bf16[5376,128]{1,0:T(8,128)(2,1)} %get-tuple-element.44), channel_id=1, source_target_pairs={{0,1},{1,0},{32,33},{33,32},{2,3},{3,2},{34,35},{35,34},{4,5},{5,4... | collective-permute-start | bytes 4128776 | tf_op jit(solution)/shard_map/ppermute | solution.py:235
  51.9 3.6 %collective-permute-start.6 = (f16[224,1024]{1,0:T(8,128)(2,1)S(1)}, f16[224,1024]{1,0:T(8,128)(2,1)S(1)}, u32[]{:S(2)}, u32[]{:S(2)}) collective-permute-start(f16[224,1024]{1,0:T(8,128)(2,1)S(1)} %get-tuple-element.64), channel_id=1, source_target_pairs={{0,2},{1,31},{2,4},{3,1},{4,6},{5,3},{6,8},{7,5},{8,10},{9,7},{10,... | collective-permute-start | bytes 1376264 | tf_op jit(solution)/shard_map/ppermute | solution.py:264
  55.6 2.6 %collective-permute-start.9 = (f16[224,1024]{1,0:T(8,128)(2,1)S(1)}, f16[224,1024]{1,0:T(8,128)(2,1)S(1)}, u32[]{:S(2)}, u32[]{:S(2)}) collective-permute-start(f16[224,1024]{1,0:T(8,128)(2,1)S(1)} %get-tuple-element.63), channel_id=1, source_target_pairs={{0,2},{1,31},{2,4},{3,1},{4,6},{5,3},{6,8},{7,5},{8,10},{9,7},{10,... | collective-permute-start | bytes 1376264 | tf_op jit(solution)/shard_map/ppermute | solution.py:264
  58.3 4.0 %collective-permute-start.10 = (bf16[1792,128]{1,0:T(8,128)(2,1)S(1)}, bf16[1792,128]{1,0:T(8,128)(2,1)S(1)}, u32[]{:S(2)}, u32[]{:S(2)}) collective-permute-start(bf16[1792,128]{1,0:T(8,128)(2,1)S(1)} %pad_maximum_fusion.3), channel_id=1, source_target_pairs={{0,32},{1,33},{32,0},{33,1},{2,34},{3,35},{34,2},{35,3},{4,36},{5,... | collective-permute-start | bytes 1376264 | tf_op jit(solution)/shard_map/ppermute | solution.py:235
  62.5 3.6 %collective-permute-start.8 = (f16[224,1024]{1,0:T(8,128)(2,1)S(1)}, f16[224,1024]{1,0:T(8,128)(2,1)S(1)}, u32[]{:S(2)}, u32[]{:S(2)}) collective-permute-start(f16[224,1024]{1,0:T(8,128)(2,1)S(1)} %fusion.11), channel_id=1, source_target_pairs={{0,2},{1,31},{2,4},{3,1},{4,6},{5,3},{6,8},{7,5},{8,10},{9,7},{10,... | collective-permute-start | bytes 1376264 | tf_op jit(solution)/shard_map/ppermute | solution.py:264
  66.3 3.9 %collective-permute-start.13 = (bf16[3584,128]{1,0:T(8,128)(2,1)S(1)}, bf16[3584,128]{1,0:T(8,128)(2,1)S(1)}, u32[]{:S(2)}, u32[]{:S(2)}) collective-permute-start(bf16[3584,128]{1,0:T(8,128)(2,1)S(1)} %pad_maximum_fusion), channel_id=1, source_target_pairs={{0,32},{1,33},{32,0},{33,1},{2,34},{3,35},{34,2},{35,3},{4,36},{5,... | collective-permute-start | bytes 2752520 | tf_op jit(solution)/shard_map/ppermute | solution.py:235
  70.2 2.3 %collective-permute-done.10.c_ref.d_ref = bf16[1792,128]{1,0:T(8,128)(2,1)S(1)} collective-permute-done((bf16[1792,128]{1,0:T(8,128)(2,1)S(1)}, bf16[1792,128]{1,0:T(8,128)(2,1)S(1)}, u32[]{:S(2)}, u32[]{:S(2)}) %collective-permute-start.10) | collective-permute-done | bytes 458784 | tf_op jit(solution)/shard_map/ppermute | solution.py:235
  72.7 4.3 %collective-permute-start.12 = (f16[224,1024]{1,0:T(8,128)(2,1)S(1)}, f16[224,1024]{1,0:T(8,128)(2,1)S(1)}, u32[]{:S(2)}, u32[]{:S(2)}) collective-permute-start(f16[224,1024]{1,0:T(8,128)(2,1)S(1)} %fusion.10), channel_id=1, source_target_pairs={{0,2},{1,31},{2,4},{3,1},{4,6},{5,3},{6,8},{7,5},{8,10},{9,7},{10,... | collective-permute-start | bytes 1376264 | tf_op jit(solution)/shard_map/ppermute | solution.py:264
  78.8 4.0 %collective-permute-start.11 = (f16[224,1024]{1,0:T(8,128)(2,1)S(1)}, f16[224,1024]{1,0:T(8,128)(2,1)S(1)}, u32[]{:S(2)}, u32[]{:S(2)}) collective-permute-start(f16[224,1024]{1,0:T(8,128)(2,1)S(1)} %fusion.9), channel_id=1, source_target_pairs={{0,2},{1,31},{2,4},{3,1},{4,6},{5,3},{6,8},{7,5},{8,10},{9,7},{10,... | collective-permute-start | bytes 1376264 | tf_op jit(solution)/shard_map/ppermute | solution.py:264
  83.0 4.8 %collective-permute-start.15 = (f16[224,1024]{1,0:T(8,128)(2,1)S(1)}, f16[224,1024]{1,0:T(8,128)(2,1)S(1)}, u32[]{:S(2)}, u32[]{:S(2)}) collective-permute-start(f16[224,1024]{1,0:T(8,128)(2,1)S(1)} %fusion.8), channel_id=1, source_target_pairs={{0,2},{1,31},{2,4},{3,1},{4,6},{5,3},{6,8},{7,5},{8,10},{9,7},{10,... | collective-permute-start | bytes 1376264 | tf_op jit(solution)/shard_map/ppermute | solution.py:264
  88.4 3.7 %collective-permute-done.13.c_ref.d_ref = bf16[3584,128]{1,0:T(8,128)(2,1)S(1)} collective-permute-done((bf16[3584,128]{1,0:T(8,128)(2,1)S(1)}, bf16[3584,128]{1,0:T(8,128)(2,1)S(1)}, u32[]{:S(2)}, u32[]{:S(2)}) %collective-permute-start.13) | collective-permute-done | bytes 917536 | tf_op jit(solution)/shard_map/ppermute | solution.py:235
  92.2 4.4 %collective-permute-start.14 = (f16[224,1024]{1,0:T(8,128)(2,1)S(1)}, f16[224,1024]{1,0:T(8,128)(2,1)S(1)}, u32[]{:S(2)}, u32[]{:S(2)}) collective-permute-start(f16[224,1024]{1,0:T(8,128)(2,1)S(1)} %fusion.7), channel_id=1, source_target_pairs={{0,2},{1,31},{2,4},{3,1},{4,6},{5,3},{6,8},{7,5},{8,10},{9,7},{10,... | collective-permute-start | bytes 1376264 | tf_op jit(solution)/shard_map/ppermute | solution.py:264
  96.7 4.0 %collective-permute-start.17 = (f16[224,1024]{1,0:T(8,128)(2,1)S(1)}, f16[224,1024]{1,0:T(8,128)(2,1)S(1)}, u32[]{:S(2)}, u32[]{:S(2)}) collective-permute-start(f16[224,1024]{1,0:T(8,128)(2,1)S(1)} %fusion.6), channel_id=1, source_target_pairs={{0,2},{1,31},{2,4},{3,1},{4,6},{5,3},{6,8},{7,5},{8,10},{9,7},{10,... | collective-permute-start | bytes 1376264 | tf_op jit(solution)/shard_map/ppermute | solution.py:264
  103.6 4.3 %collective-permute-start.16 = (f16[224,1024]{1,0:T(8,128)(2,1)}, f16[224,1024]{1,0:T(8,128)(2,1)}, u32[]{:S(2)}, u32[]{:S(2)}) collective-permute-start(f16[224,1024]{1,0:T(8,128)(2,1)} %fusion.5), channel_id=1, source_target_pairs={{0,2},{1,31},{2,4},{3,1},{4,6},{5,3},{6,8},{7,5},{8,10},{9,7},{10,... | collective-permute-start | bytes 1376264 | tf_op jit(solution)/shard_map/ppermute | solution.py:264
  108.9 4.0 %collective-permute-start.19 = (f16[224,1024]{1,0:T(8,128)(2,1)}, f16[224,1024]{1,0:T(8,128)(2,1)S(1)}, u32[]{:S(2)}, u32[]{:S(2)}) collective-permute-start(f16[224,1024]{1,0:T(8,128)(2,1)} %fusion.4), channel_id=1, source_target_pairs={{0,2},{1,31},{2,4},{3,1},{4,6},{5,3},{6,8},{7,5},{8,10},{9,7},{10,... | collective-permute-start | bytes 1376264 | tf_op jit(solution)/shard_map/ppermute | solution.py:264
  115.1 5.0 %collective-permute-start.18 = (f16[224,1024]{1,0:T(8,128)(2,1)S(1)}, f16[224,1024]{1,0:T(8,128)(2,1)S(1)}, u32[]{:S(2)}, u32[]{:S(2)}) collective-permute-start(f16[224,1024]{1,0:T(8,128)(2,1)S(1)} %fusion.3), channel_id=1, source_target_pairs={{0,2},{1,31},{2,4},{3,1},{4,6},{5,3},{6,8},{7,5},{8,10},{9,7},{10,... | collective-permute-start | bytes 1376264 | tf_op jit(solution)/shard_map/ppermute | solution.py:264
  121.4 3.4 %collective-permute-start.21 = (f16[224,1024]{1,0:T(8,128)(2,1)S(1)}, f16[224,1024]{1,0:T(8,128)(2,1)S(1)}, u32[]{:S(2)}, u32[]{:S(2)}) collective-permute-start(f16[224,1024]{1,0:T(8,128)(2,1)S(1)} %fusion.2), channel_id=1, source_target_pairs={{0,2},{1,31},{2,4},{3,1},{4,6},{5,3},{6,8},{7,5},{8,10},{9,7},{10,... | collective-permute-start | bytes 1376264 | tf_op jit(solution)/shard_map/ppermute | solution.py:264
  126.8 4.1 %collective-permute-done.21 = f16[224,1024]{1,0:T(8,128)(2,1)S(1)} collective-permute-done((f16[224,1024]{1,0:T(8,128)(2,1)S(1)}, f16[224,1024]{1,0:T(8,128)(2,1)S(1)}, u32[]{:S(2)}, u32[]{:S(2)}) %collective-permute-start.21) | collective-permute-done | bytes 458784 | tf_op jit(solution)/shard_map/ppermute | solution.py:264
  131.3 5.9 %collective-permute-start.23 = (f16[448,512]{1,0:T(8,128)(2,1)S(1)}, f16[448,512]{1,0:T(8,128)(2,1)S(1)}, u32[]{:S(2)}, u32[]{:S(2)}) collective-permute-start(f16[448,512]{1,0:T(8,128)(2,1)S(1)} %pad_maximum_fusion.4), channel_id=1, source_target_pairs={{0,3},{1,30},{2,5},{3,0},{4,7},{5,2},{6,9},{7,4},{8,11},{9,6},{10,... | collective-permute-start | bytes 1376264 | tf_op jit(solution)/shard_map/ppermute | solution.py:264
  137.3 2.9 %collective-permute-start.20 = (f16[224,512]{1,0:T(8,128)(2,1)S(1)}, f16[224,512]{1,0:T(8,128)(2,1)S(1)}, u32[]{:S(2)}, u32[]{:S(2)}) collective-permute-start(f16[224,512]{1,0:T(8,128)(2,1)S(1)} %get-tuple-element.65), channel_id=1, source_target_pairs={{0,2},{1,31},{2,4},{3,1},{4,6},{5,3},{6,8},{7,5},{8,10},{9,7},{10,... | collective-permute-start | bytes 688136 | tf_op jit(solution)/shard_map/ppermute | solution.py:264
  140.2 4.1 %collective-permute-start.22 = (f16[224,512]{1,0:T(8,128)(2,1)S(1)}, f16[224,512]{1,0:T(8,128)(2,1)}, u32[]{:S(2)}, u32[]{:S(2)}) collective-permute-start(f16[224,512]{1,0:T(8,128)(2,1)S(1)} %get-tuple-element.67), channel_id=1, source_target_pairs={{0,2},{1,31},{2,4},{3,1},{4,6},{5,3},{6,8},{7,5},{8,10},{9,7},{10,... | collective-permute-start | bytes 688136 | tf_op jit(solution)/shard_map/ppermute | solution.py:264
  147.4 2.2 %collective-permute-done.22 = f16[224,512]{1,0:T(8,128)(2,1)} collective-permute-done((f16[224,512]{1,0:T(8,128)(2,1)S(1)}, f16[224,512]{1,0:T(8,128)(2,1)}, u32[]{:S(2)}, u32[]{:S(2)}) %collective-permute-start.22) | collective-permute-done | bytes 229408 | tf_op jit(solution)/shard_map/ppermute | solution.py:264
  150.9 14.2 %all_to_all.5 = f16[16,28,512]{2,1,0:T(8,128)(2,1)S(1)} all-to-all(f16[16,28,512]{2,1,0:T(8,128)(2,1)S(1)} %reshape.12), channel_id=1, replica_groups=mesh['ylo'=2,'x'=4,'yhi'=2,'z'=16,'core'=2] {'ylo','x','core'}, dimensions={0} | all-to-all | bytes 917504 | tf_op jit(solution)/shard_map/all_to_all | solution.py:293
  165.4 2.4 %shard_map.73 = (f32[28,512]{1,0:T(8,128)}, f32[28,512]{1,0:T(8,128)}, f32[28,512]{1,0:T(8,128)}) custom-call(f32[16,32,512]{2,1,0:T(8,128)S(1)} %pad.6.g_ref, bf16[28,512]{1,0:T(8,128)(2,1)S(1)} %copy-done.2), custom_call_target="tpu_custom_call" | custom-call | tf_op jit(solution)/shard_map/pallas_call | solution.py:211
  (89 shorter events, 26.2 us)
Async XLA Ops:
  7.1 10.8 %collective-permute-start = (bf16[2752,128]{1,0:T(8,128)(2,1)}, bf16[2752,128]{1,0:T(8,128)(2,1)S(1)}, u32[]{:S(2)}, u32[]{:S(2)}) collective-permute-start(bf16[2752,128]{1,0:T(8,128)(2,1)} %get-tuple-element.34), channel_id=1, source_target_pairs={{0,1},{1,0},{32,33},{33,32},{2,3},{3,2},{34,35},{35,34},{4,5},{5,4... | collective-permute-start | bytes 2113544 | tf_op jit(solution)/shard_map/ppermute | solution.py:235
  15.9 10.0 %collective-permute-start.2 = (bf16[736,128]{1,0:T(8,128)(2,1)}, bf16[736,128]{1,0:T(8,128)(2,1)S(1)}, u32[]{:S(2)}, u32[]{:S(2)}) collective-permute-start(bf16[736,128]{1,0:T(8,128)(2,1)} %get-tuple-element.37), channel_id=1, source_target_pairs={{0,32},{1,33},{32,0},{33,1},{2,34},{3,35},{34,2},{35,3},{4,36},{5,... | collective-permute-start | bytes 565256 | tf_op jit(solution)/shard_map/ppermute | solution.py:235
  17.9 12.0 %collective-permute-start.3 = (bf16[736,128]{1,0:T(8,128)(2,1)S(1)}, bf16[736,128]{1,0:T(8,128)(2,1)S(1)}, u32[]{:S(2)}, u32[]{:S(2)}) collective-permute-start(bf16[736,128]{1,0:T(8,128)(2,1)S(1)} %slice.116), channel_id=1, source_target_pairs={{0,32},{1,33},{32,0},{33,1},{2,34},{3,35},{34,2},{35,3},{4,36},{5,... | collective-permute-start | bytes 565256 | tf_op jit(solution)/shard_map/ppermute | solution.py:235
  23.7 24.6 %collective-permute-start.1 = (bf16[1792,128]{1,0:T(8,128)(2,1)S(1)}, bf16[1792,128]{1,0:T(8,128)(2,1)S(1)}, u32[]{:S(2)}, u32[]{:S(2)}) collective-permute-start(bf16[1792,128]{1,0:T(8,128)(2,1)S(1)} %pad_maximum_fusion.1), channel_id=1, source_target_pairs={{0,32},{1,33},{32,0},{33,1},{2,34},{3,35},{34,2},{35,3},{4,36},{5,... | collective-permute-start | bytes 1376264 | tf_op jit(solution)/shard_map/ppermute | solution.py:235
  30.8 17.5 %copy-start.5 = (bf16[896,128]{1,0:T(8,128)(2,1)S(1)}, bf16[896,128]{1,0:T(8,128)(2,1)}, u32[]{:S(2)}) copy-start(bf16[896,128]{1,0:T(8,128)(2,1)} %get-tuple-element.33.a_ref) | copy-start | bytes 688132
  32.4 9.0 %collective-permute-start.4 = (f16[112,1024]{1,0:T(8,128)(2,1)S(1)}, f16[112,1024]{1,0:T(8,128)(2,1)S(1)}, u32[]{:S(2)}, u32[]{:S(2)}) collective-permute-start(f16[112,1024]{1,0:T(8,128)(2,1)S(1)} %get-tuple-element.70), channel_id=1, source_target_pairs={{0,2},{1,31},{2,4},{3,1},{4,6},{5,3},{6,8},{7,5},{8,10},{9,7},{10,... | collective-permute-start | bytes 688136 | tf_op jit(solution)/shard_map/ppermute | solution.py:264
  38.4 8.7 %collective-permute-start.5 = (f16[112,1024]{1,0:T(8,128)(2,1)S(1)}, f16[112,1024]{1,0:T(8,128)(2,1)}, u32[]{:S(2)}, u32[]{:S(2)}) collective-permute-start(f16[112,1024]{1,0:T(8,128)(2,1)S(1)} %get-tuple-element.69), channel_id=1, source_target_pairs={{0,2},{1,31},{2,4},{3,1},{4,6},{5,3},{6,8},{7,5},{8,10},{9,7},{10,... | collective-permute-start | bytes 688136 | tf_op jit(solution)/shard_map/ppermute | solution.py:264
  42.1 16.2 %collective-permute-start.7 = (bf16[5376,128]{1,0:T(8,128)(2,1)}, bf16[5376,128]{1,0:T(8,128)(2,1)S(1)}, u32[]{:S(2)}, u32[]{:S(2)}) collective-permute-start(bf16[5376,128]{1,0:T(8,128)(2,1)} %get-tuple-element.44), channel_id=1, source_target_pairs={{0,1},{1,0},{32,33},{33,32},{2,3},{3,2},{34,35},{35,34},{4,5},{5,4... | collective-permute-start | bytes 4128776 | tf_op jit(solution)/shard_map/ppermute | solution.py:235
  51.5 14.7 %copy-start.11 = (bf16[1792,128]{1,0:T(8,128)(2,1)S(1)}, bf16[1792,128]{1,0:T(8,128)(2,1)}, u32[]{:S(2)}) copy-start(bf16[1792,128]{1,0:T(8,128)(2,1)} %get-tuple-element.51) | copy-start | bytes 1376260
  51.9 10.4 %collective-permute-start.6 = (f16[224,1024]{1,0:T(8,128)(2,1)S(1)}, f16[224,1024]{1,0:T(8,128)(2,1)S(1)}, u32[]{:S(2)}, u32[]{:S(2)}) collective-permute-start(f16[224,1024]{1,0:T(8,128)(2,1)S(1)} %get-tuple-element.64), channel_id=1, source_target_pairs={{0,2},{1,31},{2,4},{3,1},{4,6},{5,3},{6,8},{7,5},{8,10},{9,7},{10,... | collective-permute-start | bytes 1376264 | tf_op jit(solution)/shard_map/ppermute | solution.py:264
  55.6 14.6 %collective-permute-start.9 = (f16[224,1024]{1,0:T(8,128)(2,1)S(1)}, f16[224,1024]{1,0:T(8,128)(2,1)S(1)}, u32[]{:S(2)}, u32[]{:S(2)}) collective-permute-start(f16[224,1024]{1,0:T(8,128)(2,1)S(1)} %get-tuple-element.63), channel_id=1, source_target_pairs={{0,2},{1,31},{2,4},{3,1},{4,6},{5,3},{6,8},{7,5},{8,10},{9,7},{10,... | collective-permute-start | bytes 1376264 | tf_op jit(solution)/shard_map/ppermute | solution.py:264
  58.3 18.7 %copy-start.4 = (bf16[896,128]{1,0:T(8,128)(2,1)S(1)}, bf16[896,128]{1,0:T(8,128)(2,1)}, u32[]{:S(2)}) copy-start(bf16[896,128]{1,0:T(8,128)(2,1)} %get-tuple-element.48.a_ref) | copy-start | bytes 688132
  58.3 18.7 %copy-start.9 = (bf16[512,1024]{1,0:T(8,128)(2,1)S(1)}, bf16[512,1024]{1,0:T(8,128)(2,1)}, u32[]{:S(2)}) copy-start(bf16[512,1024]{1,0:T(8,128)(2,1)} %copy-done.7) | copy-start | bytes 3145732
  58.3 14.2 %collective-permute-start.10 = (bf16[1792,128]{1,0:T(8,128)(2,1)S(1)}, bf16[1792,128]{1,0:T(8,128)(2,1)S(1)}, u32[]{:S(2)}, u32[]{:S(2)}) collective-permute-start(bf16[1792,128]{1,0:T(8,128)(2,1)S(1)} %pad_maximum_fusion.3), channel_id=1, source_target_pairs={{0,32},{1,33},{32,0},{33,1},{2,34},{3,35},{34,2},{35,3},{4,36},{5,... | collective-permute-start | bytes 1376264 | tf_op jit(solution)/shard_map/ppermute | solution.py:235
  62.5 16.1 %collective-permute-start.8 = (f16[224,1024]{1,0:T(8,128)(2,1)S(1)}, f16[224,1024]{1,0:T(8,128)(2,1)S(1)}, u32[]{:S(2)}, u32[]{:S(2)}) collective-permute-start(f16[224,1024]{1,0:T(8,128)(2,1)S(1)} %fusion.11), channel_id=1, source_target_pairs={{0,2},{1,31},{2,4},{3,1},{4,6},{5,3},{6,8},{7,5},{8,10},{9,7},{10,... | collective-permute-start | bytes 1376264 | tf_op jit(solution)/shard_map/ppermute | solution.py:264
  66.3 25.7 %collective-permute-start.13 = (bf16[3584,128]{1,0:T(8,128)(2,1)S(1)}, bf16[3584,128]{1,0:T(8,128)(2,1)S(1)}, u32[]{:S(2)}, u32[]{:S(2)}) collective-permute-start(bf16[3584,128]{1,0:T(8,128)(2,1)S(1)} %pad_maximum_fusion), channel_id=1, source_target_pairs={{0,32},{1,33},{32,0},{33,1},{2,34},{3,35},{34,2},{35,3},{4,36},{5,... | collective-permute-start | bytes 2752520 | tf_op jit(solution)/shard_map/ppermute | solution.py:235
  72.7 10.2 %collective-permute-start.12 = (f16[224,1024]{1,0:T(8,128)(2,1)S(1)}, f16[224,1024]{1,0:T(8,128)(2,1)S(1)}, u32[]{:S(2)}, u32[]{:S(2)}) collective-permute-start(f16[224,1024]{1,0:T(8,128)(2,1)S(1)} %fusion.10), channel_id=1, source_target_pairs={{0,2},{1,31},{2,4},{3,1},{4,6},{5,3},{6,8},{7,5},{8,10},{9,7},{10,... | collective-permute-start | bytes 1376264 | tf_op jit(solution)/shard_map/ppermute | solution.py:264
  78.7 22.1 %copy-start.3 = (bf16[1792,128]{1,0:T(8,128)(2,1)S(1)}, bf16[1792,128]{1,0:T(8,128)(2,1)}, u32[]{:S(2)}) copy-start(bf16[1792,128]{1,0:T(8,128)(2,1)} %get-tuple-element.55.a_ref) | copy-start | bytes 1376260
  78.8 9.5 %collective-permute-start.11 = (f16[224,1024]{1,0:T(8,128)(2,1)S(1)}, f16[224,1024]{1,0:T(8,128)(2,1)S(1)}, u32[]{:S(2)}, u32[]{:S(2)}) collective-permute-start(f16[224,1024]{1,0:T(8,128)(2,1)S(1)} %fusion.9), channel_id=1, source_target_pairs={{0,2},{1,31},{2,4},{3,1},{4,6},{5,3},{6,8},{7,5},{8,10},{9,7},{10,... | collective-permute-start | bytes 1376264 | tf_op jit(solution)/shard_map/ppermute | solution.py:264
  83.0 13.5 %collective-permute-start.15 = (f16[224,1024]{1,0:T(8,128)(2,1)S(1)}, f16[224,1024]{1,0:T(8,128)(2,1)S(1)}, u32[]{:S(2)}, u32[]{:S(2)}) collective-permute-start(f16[224,1024]{1,0:T(8,128)(2,1)S(1)} %fusion.8), channel_id=1, source_target_pairs={{0,2},{1,31},{2,4},{3,1},{4,6},{5,3},{6,8},{7,5},{8,10},{9,7},{10,... | collective-permute-start | bytes 1376264 | tf_op jit(solution)/shard_map/ppermute | solution.py:264
  92.2 10.3 %collective-permute-start.14 = (f16[224,1024]{1,0:T(8,128)(2,1)S(1)}, f16[224,1024]{1,0:T(8,128)(2,1)S(1)}, u32[]{:S(2)}, u32[]{:S(2)}) collective-permute-start(f16[224,1024]{1,0:T(8,128)(2,1)S(1)} %fusion.7), channel_id=1, source_target_pairs={{0,2},{1,31},{2,4},{3,1},{4,6},{5,3},{6,8},{7,5},{8,10},{9,7},{10,... | collective-permute-start | bytes 1376264 | tf_op jit(solution)/shard_map/ppermute | solution.py:264
  96.7 11.2 %collective-permute-start.17 = (f16[224,1024]{1,0:T(8,128)(2,1)S(1)}, f16[224,1024]{1,0:T(8,128)(2,1)S(1)}, u32[]{:S(2)}, u32[]{:S(2)}) collective-permute-start(f16[224,1024]{1,0:T(8,128)(2,1)S(1)} %fusion.6), channel_id=1, source_target_pairs={{0,2},{1,31},{2,4},{3,1},{4,6},{5,3},{6,8},{7,5},{8,10},{9,7},{10,... | collective-permute-start | bytes 1376264 | tf_op jit(solution)/shard_map/ppermute | solution.py:264
  103.6 10.1 %collective-permute-start.16 = (f16[224,1024]{1,0:T(8,128)(2,1)}, f16[224,1024]{1,0:T(8,128)(2,1)}, u32[]{:S(2)}, u32[]{:S(2)}) collective-permute-start(f16[224,1024]{1,0:T(8,128)(2,1)} %fusion.5), channel_id=1, source_target_pairs={{0,2},{1,31},{2,4},{3,1},{4,6},{5,3},{6,8},{7,5},{8,10},{9,7},{10,... | collective-permute-start | bytes 1376264 | tf_op jit(solution)/shard_map/ppermute | solution.py:264
  108.9 11.2 %collective-permute-start.19 = (f16[224,1024]{1,0:T(8,128)(2,1)}, f16[224,1024]{1,0:T(8,128)(2,1)S(1)}, u32[]{:S(2)}, u32[]{:S(2)}) collective-permute-start(f16[224,1024]{1,0:T(8,128)(2,1)} %fusion.4), channel_id=1, source_target_pairs={{0,2},{1,31},{2,4},{3,1},{4,6},{5,3},{6,8},{7,5},{8,10},{9,7},{10,... | collective-permute-start | bytes 1376264 | tf_op jit(solution)/shard_map/ppermute | solution.py:264
  115.1 11.5 %collective-permute-start.18 = (f16[224,1024]{1,0:T(8,128)(2,1)S(1)}, f16[224,1024]{1,0:T(8,128)(2,1)S(1)}, u32[]{:S(2)}, u32[]{:S(2)}) collective-permute-start(f16[224,1024]{1,0:T(8,128)(2,1)S(1)} %fusion.3), channel_id=1, source_target_pairs={{0,2},{1,31},{2,4},{3,1},{4,6},{5,3},{6,8},{7,5},{8,10},{9,7},{10,... | collective-permute-start | bytes 1376264 | tf_op jit(solution)/shard_map/ppermute | solution.py:264
  121.4 9.5 %collective-permute-start.21 = (f16[224,1024]{1,0:T(8,128)(2,1)S(1)}, f16[224,1024]{1,0:T(8,128)(2,1)S(1)}, u32[]{:S(2)}, u32[]{:S(2)}) collective-permute-start(f16[224,1024]{1,0:T(8,128)(2,1)S(1)} %fusion.2), channel_id=1, source_target_pairs={{0,2},{1,31},{2,4},{3,1},{4,6},{5,3},{6,8},{7,5},{8,10},{9,7},{10,... | collective-permute-start | bytes 1376264 | tf_op jit(solution)/shard_map/ppermute | solution.py:264
  126.6 17.7 %copy-start.14 = (s32[2]{0:T(128)S(1)}, s32[2]{0:T(128)}, u32[]{:S(2)}) copy-start(s32[2]{0:T(128)} %len_ref.1) | copy-start | bytes 28
  131.1 18.4 %slice-start = ((f32[896,1024]{1,0:T(8,128)}), f32[448,1024]{1,0:T(8,128)S(1)}, s32[]{:S(2)}) async-start(f32[896,1024]{1,0:T(8,128)} %copy-done), calls=%async_computation.1 | async-start | bytes 3670016 | tf_op jit(solution)/shard_map/slice | solution.py:261
  131.3 18.2 %collective-permute-start.23 = (f16[448,512]{1,0:T(8,128)(2,1)S(1)}, f16[448,512]{1,0:T(8,128)(2,1)S(1)}, u32[]{:S(2)}, u32[]{:S(2)}) collective-permute-start(f16[448,512]{1,0:T(8,128)(2,1)S(1)} %pad_maximum_fusion.4), channel_id=1, source_target_pairs={{0,3},{1,30},{2,5},{3,0},{4,7},{5,2},{6,9},{7,4},{8,11},{9,6},{10,... | collective-permute-start | bytes 1376264 | tf_op jit(solution)/shard_map/ppermute | solution.py:264
  137.3 10.1 %collective-permute-start.20 = (f16[224,512]{1,0:T(8,128)(2,1)S(1)}, f16[224,512]{1,0:T(8,128)(2,1)S(1)}, u32[]{:S(2)}, u32[]{:S(2)}) collective-permute-start(f16[224,512]{1,0:T(8,128)(2,1)S(1)} %get-tuple-element.65), channel_id=1, source_target_pairs={{0,2},{1,31},{2,4},{3,1},{4,6},{5,3},{6,8},{7,5},{8,10},{9,7},{10,... | collective-permute-start | bytes 688136 | tf_op jit(solution)/shard_map/ppermute | solution.py:264
  140.2 9.4 %collective-permute-start.22 = (f16[224,512]{1,0:T(8,128)(2,1)S(1)}, f16[224,512]{1,0:T(8,128)(2,1)}, u32[]{:S(2)}, u32[]{:S(2)}) collective-permute-start(f16[224,512]{1,0:T(8,128)(2,1)S(1)} %get-tuple-element.67), channel_id=1, source_target_pairs={{0,2},{1,31},{2,4},{3,1},{4,6},{5,3},{6,8},{7,5},{8,10},{9,7},{10,... | collective-permute-start | bytes 688136 | tf_op jit(solution)/shard_map/ppermute | solution.py:264
  149.5 15.8 %copy-start.2 = (bf16[28,512]{1,0:T(8,128)(2,1)S(1)}, bf16[28,512]{1,0:T(8,128)(2,1)}, u32[]{:S(2)}) copy-start(bf16[28,512]{1,0:T(8,128)(2,1)} %w_ref.1) | copy-start | bytes 86020
  (8 other events, 32.6 us)

commit v9 on v7

--- a/solution.py
+++ b/solution.py
@@ -14,7 +14,6 @@
 GROUPS = ((7, 6), (5, 4), (3, 2, 1, 0))
 LATER = {6: (1, 0), 4: (2, 0), 3: (2, 2)}
 DUE = {(6, 0): 1, (4, 0): 2}
-CHAINS = ((0, 224), (224, 448))
 VMEM = 56 * 1024 * 1024
 f32 = jnp.float32
 f16 = jnp.float16
@@ -103,6 +102,7 @@
 
 
 def first_kernel(a_ref, b_ref, c_ref, d_ref, out_ref, right_ref):
+    own = lax.axis_index("core")
     refs = (a_ref, b_ref, c_ref, d_ref)
     seg2 = a_ref.shape[1]
     height = out_ref.shape[0]
@@ -112,9 +112,11 @@
         rows = [ref[at + b * seg2:at + (b + 1) * seg2] for b in range(n_lane)]
         feats = jnp.concatenate(rows, axis=1)
         half = seg2 // 2
-        none = jnp.zeros((half, feats.shape[1]), feats.dtype)
-        right_ref[k * seg2:k * seg2 + half] = jnp.concatenate([feats[:half], none], axis=1)
-        right_ref[k * seg2 + half:(k + 1) * seg2] = jnp.concatenate([none, feats[half:]], axis=1)
+        for e in range(2):
+            mine = feats[e * half:(e + 1) * half].astype(f32)
+            at = k * seg2 + e * half
+            columns = [jnp.where(own == e, mine, 0.0), jnp.where(own == e, 0.0, mine)]
+            right_ref[at:at + half] = jnp.concatenate(columns, axis=1).astype(feats.dtype)
     left = jnp.concatenate([ref[:height] for ref in refs], axis=1)
     out_ref[...] = jnp.dot(left, right_ref[...], preferred_element_type=f32)
 
@@ -271,21 +273,21 @@
     got = got.astype(f32)
     none = jnp.zeros_like(got)
     got = jnp.where(core == 0, jnp.concatenate([got, none], axis=0), jnp.concatenate([none, got], axis=0))
-    sums = [(parts[FAR - 1][a:b] + got[a:b]).astype(f16) for a, b in CHAINS]
+    chains = ((0, rows), (rows, 2 * rows))
+    sums = [(parts[FAR - 1][:, a:b] + got[:, a:b]).astype(f16) for a, b in chains]
     last = sums[-1]
     for dist in range(FAR - 2, 0, -1):
-        for k, (a, b) in enumerate(CHAINS):
+        for k, (a, b) in enumerate(chains):
             got = ring(sums[k])
             due = [arrived[DUE[dist, k]]] if (dist, k) in DUE else []
             got = after(got, last, *due)
-            sums[k] = last = (got.astype(f32) + parts[dist][a:b]).astype(f16)
+            sums[k] = last = (got.astype(f32) + parts[dist][:, a:b]).astype(f16)
             if k == 0 and dist in LATER:
                 multiply(*LATER[dist], last)
-    pick = lambda x, i: lax.dynamic_slice_in_dim(x, i * rows, rows, 1)
-    same = [ring(pick(x, core)).astype(f32) for x in sums]
-    cross = ring(jnp.concatenate([pick(x, 1 - core) for x in sums], axis=0), 1).astype(f32)
+    total = after(ring(sums[0]), last).astype(f32) + parts[0][:, :rows]
+    total = total + after(ring(sums[1], 1), total).astype(f32)
     length = lax.dynamic_index_in_dim(lengths, core, 0, keepdims=False).astype(f32)
-    total = (jnp.concatenate(same, axis=0) + cross + pick(parts[0], core)) * (4096.0 / length)
+    total = total * (4096.0 / length)
     pieces = total.astype(f16).reshape(2 * n_groups, -1, rows)
     owned = lax.all_to_all(pieces, ("ylo", "x", "core"), 0, 0, tiled=True)
     own_units = owned.shape[1]

time: 161 us -> 154 us (0.957)
  other arithmetic: 9.18 us -> 5.34 us
  waiting for transfers between devices: 14.8 us -> 12.1 us
    convert_element_type x13, other arithmetic: 6.34 us -> 2.32 us  [the longest x12 1.83 us: body(): sums[k] = last = (got.astype(f32) + parts[dist][:, a:b]).astype(f16)]
    ppermute x16 -> x15, waiting for transfers between devices: 10.6 us -> 7.86 us  [body(): ring = lambda x, cross=0: lax.ppermute(x, ('z', 'core'), ring_pairs(cross))]
    ppermute x16 -> x15, starting transfers between devices: 72.7 us -> 72.6 us  [body(): ring = lambda x, cross=0: lax.ppermute(x, ('z', 'core'), ring_pairs(cross))]
  transfers between devices with their start and end apart: 23 -> 22, of which waited for: 8 -> 9; matrix products, arithmetic and copies ran while one was open for 5% -> 4% of each run, Pallas kernels for 4% -> 5%
where the time goes in v9:
time: 154 us; the launch traced here: 153 us
  starting transfers between devices  101 us (66%)
  Pallas kernels  16 us (10%)
  blocking collectives  14.2 us (9%)
  waiting for transfers between devices  12.1 us (8%)
  other arithmetic  5.34 us (3%)
  local copies, waits for them, and re-layouts  2.7 us (2%)
  between operations  1.93 us (1%)
    ppermute x15, starting transfers between devices, body(): ring = lambda x, cross=0: lax.ppermute(x, ('z', 'core'), ring_pairs(cross))  72.6 us
    ppermute x7, starting transfers between devices, body(): lax.ppermute(x, ('yhi', 'core'), [(j, j ^ i) for j in range(4)])  28.2 us
    all_to_all x1, blocking collectives, body(): owned = lax.all_to_all(pieces, ('ylo', 'x', 'core'), 0, 0, tiled=True)  14.2 us
    ppermute x15, waiting for transfers between devices, body(): ring = lambda x, cross=0: lax.ppermute(x, ('z', 'core'), ring_pairs(cross))  7.86 us
    pallas_call x4, Pallas kernels, product(): pl.pallas_call(product_kernel, grid=(2 * count,), in_specs=[pl.BlockSpec(...  6.69 us
    pallas_call x1, Pallas kernels, turn(): pl.pallas_call(turn_kernel, grid_spec=pltpu.PrefetchScalarGridSpec(num_sc...  6.45 us
    ppermute x7, waiting for transfers between devices, body(): lax.ppermute(x, ('yhi', 'core'), [(j, j ^ i) for j in range(4)])  4.25 us
  transfers between devices with their start and end apart: 22, of which 9 were waited for; matrix products, arithmetic and copies ran while one was open for 4% of the time, Pallas kernels for 5%

profile of v9, /device:TPU:1, one launch (start us, length us, event | category | flops | bytes accessed | tf_op | source)
XLA Modules:
  0.0 153.0 jit_solution(5886956107713510221)
XLA Ops:
  0.6 6.5 %shard_map.67 = (bf16[736,128]{1,0:T(8,128)(2,1)}, bf16[896,128]{1,0:T(8,128)(2,1)}, bf16[896,128]{1,0:T(8,128)(2,1)}, bf16[1792,128]{1,0:T(8,128)(2,1)}, bf16[7...) custom-call(s32[2]{0:T(128)} %len_ref.1, ...), custom_call_target="tpu_custom_call" | custom-call | tf_op jit(solution)/shard_map/pallas_call | solution.py:90
  7.1 8.8 %collective-permute-start = (bf16[2752,128]{1,0:T(8,128)(2,1)}, bf16[2752,128]{1,0:T(8,128)(2,1)S(1)}, u32[]{:S(2)}, u32[]{:S(2)}) collective-permute-start(bf16[2752,128]{1,0:T(8,128)(2,1)} %get-tuple-element.37), channel_id=1, source_target_pairs={{0,1},{1,0},{32,33},{33,32},{2,3},{3,2},{34,35},{35,34},{4,5},{5,4... | collective-permute-start | bytes 2113544 | tf_op jit(solution)/shard_map/ppermute | solution.py:237
  15.9 1.9 %collective-permute-start.2 = (bf16[736,128]{1,0:T(8,128)(2,1)}, bf16[736,128]{1,0:T(8,128)(2,1)S(1)}, u32[]{:S(2)}, u32[]{:S(2)}) collective-permute-start(bf16[736,128]{1,0:T(8,128)(2,1)} %get-tuple-element.40), channel_id=1, source_target_pairs={{0,32},{1,33},{32,0},{33,1},{2,34},{3,35},{34,2},{35,3},{4,36},{5,... | collective-permute-start | bytes 565256 | tf_op jit(solution)/shard_map/ppermute | solution.py:237
  17.9 4.8 %collective-permute-start.3 = (bf16[736,128]{1,0:T(8,128)(2,1)S(1)}, bf16[736,128]{1,0:T(8,128)(2,1)S(1)}, u32[]{:S(2)}, u32[]{:S(2)}) collective-permute-start(bf16[736,128]{1,0:T(8,128)(2,1)S(1)} %slice.108), channel_id=1, source_target_pairs={{0,32},{1,33},{32,0},{33,1},{2,34},{3,35},{34,2},{35,3},{4,36},{5,... | collective-permute-start | bytes 565256 | tf_op jit(solution)/shard_map/ppermute | solution.py:237
  23.7 2.0 %collective-permute-start.1 = (bf16[1792,128]{1,0:T(8,128)(2,1)S(1)}, bf16[1792,128]{1,0:T(8,128)(2,1)S(1)}, u32[]{:S(2)}, u32[]{:S(2)}) collective-permute-start(bf16[1792,128]{1,0:T(8,128)(2,1)S(1)} %pad_maximum_fusion.1), channel_id=1, source_target_pairs={{0,32},{1,33},{32,0},{33,1},{2,34},{3,35},{34,2},{35,3},{4,36},{5,... | collective-permute-start | bytes 1376264 | tf_op jit(solution)/shard_map/ppermute | solution.py:237
  25.8 4.0 %collective-permute-done.3.d_ref = bf16[736,128]{1,0:T(8,128)(2,1)S(1)} collective-permute-done((bf16[736,128]{1,0:T(8,128)(2,1)S(1)}, bf16[736,128]{1,0:T(8,128)(2,1)S(1)}, u32[]{:S(2)}, u32[]{:S(2)}) %collective-permute-start.3) | collective-permute-done | bytes 188448 | tf_op jit(solution)/shard_map/ppermute | solution.py:237
  32.1 3.1 %collective-permute-start.5 = (bf16[5376,128]{1,0:T(8,128)(2,1)S(1)}, bf16[5376,128]{1,0:T(8,128)(2,1)S(1)}, u32[]{:S(2)}, u32[]{:S(2)}) collective-permute-start(bf16[5376,128]{1,0:T(8,128)(2,1)S(1)} %copy-done.9), channel_id=1, source_target_pairs={{0,1},{1,0},{32,33},{33,32},{2,3},{3,2},{34,35},{35,34},{4,5},{5,4... | collective-permute-start | bytes 4128776 | tf_op jit(solution)/shard_map/ppermute | solution.py:237
  35.2 6.7 %collective-permute-start.4 = (f16[224,1024]{1,0:T(8,128)(2,1)S(1)}, f16[224,1024]{1,0:T(8,128)(2,1)S(1)}, u32[]{:S(2)}, u32[]{:S(2)}) collective-permute-start(f16[224,1024]{1,0:T(8,128)(2,1)S(1)} %convert_element_type.102), channel_id=1, source_target_pairs={{0,2},{1,31},{2,4},{3,1},{4,6},{5,3},{6,8},{7,5},{8,10},{9,7},{10,... | collective-permute-start | bytes 1376264 | tf_op jit(solution)/shard_map/ppermute | solution.py:266
  41.9 1.7 %shard_map.69 = f32[896,1024]{1,0:T(8,128)S(1)} custom-call(bf16[896,128]{1,0:T(8,128)(2,1)S(1)} %copy-done.4, bf16[2752,128]{1,0:T(8,128)(2,1)S(1)} %collective-permute-done.b_ref, bf16[1792,128]{1,0:T(8,128)(2,1)S(1)} %collective-permute-done.1.c_ref.d_ref, bf16[1792,128]{1,0:T(8,128)(2,1)S(1)} %collective-permute-done.1.c_ref.d_ref, ...), custom_call_target="tpu_custom_call" | custom-call | flops 37580963840 | bytes 5505024 | tf_op jit(solution)/shard_map/pallas_call | solution.py:147
  43.7 3.9 %collective-permute-start.7 = (bf16[1792,128]{1,0:T(8,128)(2,1)S(1)}, bf16[1792,128]{1,0:T(8,128)(2,1)S(1)}, u32[]{:S(2)}, u32[]{:S(2)}) collective-permute-start(bf16[1792,128]{1,0:T(8,128)(2,1)S(1)} %pad_maximum_fusion.2), channel_id=1, source_target_pairs={{0,32},{1,33},{32,0},{33,1},{2,34},{3,35},{34,2},{35,3},{4,36},{5,... | collective-permute-start | bytes 1376264 | tf_op jit(solution)/shard_map/ppermute | solution.py:237
  48.4 4.9 %collective-permute-start.6 = (f16[448,512]{1,0:T(8,128)(2,1)S(1)}, f16[448,512]{1,0:T(8,128)(2,1)S(1)}, u32[]{:S(2)}, u32[]{:S(2)}) collective-permute-start(f16[448,512]{1,0:T(8,128)(2,1)S(1)} %get-tuple-element.70), channel_id=1, source_target_pairs={{0,2},{1,31},{2,4},{3,1},{4,6},{5,3},{6,8},{7,5},{8,10},{9,7},{10,... | collective-permute-start | bytes 1376264 | tf_op jit(solution)/shard_map/ppermute | solution.py:266
  53.3 2.1 %collective-permute-start.9 = (f16[448,512]{1,0:T(8,128)(2,1)S(1)}, f16[448,512]{1,0:T(8,128)(2,1)S(1)}, u32[]{:S(2)}, u32[]{:S(2)}) collective-permute-start(f16[448,512]{1,0:T(8,128)(2,1)S(1)} %get-tuple-element.69), channel_id=1, source_target_pairs={{0,2},{1,31},{2,4},{3,1},{4,6},{5,3},{6,8},{7,5},{8,10},{9,7},{10,... | collective-permute-start | bytes 1376264 | tf_op jit(solution)/shard_map/ppermute | solution.py:266
  55.5 3.7 %collective-permute-start.12 = (bf16[3584,128]{1,0:T(8,128)(2,1)S(1)}, bf16[3584,128]{1,0:T(8,128)(2,1)S(1)}, u32[]{:S(2)}, u32[]{:S(2)}) collective-permute-start(bf16[3584,128]{1,0:T(8,128)(2,1)S(1)} %pad_maximum_fusion), channel_id=1, source_target_pairs={{0,32},{1,33},{32,0},{33,1},{2,34},{3,35},{34,2},{35,3},{4,36},{5,... | collective-permute-start | bytes 2752520 | tf_op jit(solution)/shard_map/ppermute | solution.py:237
  59.4 4.5 %collective-permute-start.8 = (f16[448,512]{1,0:T(8,128)(2,1)S(1)}, f16[448,512]{1,0:T(8,128)(2,1)S(1)}, u32[]{:S(2)}, u32[]{:S(2)}) collective-permute-start(f16[448,512]{1,0:T(8,128)(2,1)S(1)} %fusion.11), channel_id=1, source_target_pairs={{0,2},{1,31},{2,4},{3,1},{4,6},{5,3},{6,8},{7,5},{8,10},{9,7},{10,... | collective-permute-start | bytes 1376264 | tf_op jit(solution)/shard_map/ppermute | solution.py:266
  64.1 5.0 %collective-permute-start.11 = (f16[448,512]{1,0:T(8,128)(2,1)S(1)}, f16[448,512]{1,0:T(8,128)(2,1)S(1)}, u32[]{:S(2)}, u32[]{:S(2)}) collective-permute-start(f16[448,512]{1,0:T(8,128)(2,1)S(1)} %fusion.10), channel_id=1, source_target_pairs={{0,2},{1,31},{2,4},{3,1},{4,6},{5,3},{6,8},{7,5},{8,10},{9,7},{10,... | collective-permute-start | bytes 1376264 | tf_op jit(solution)/shard_map/ppermute | solution.py:266
  69.1 1.7 %shard_map.70 = f32[896,1024]{1,0:T(8,128)S(1)} custom-call(bf16[896,128]{1,0:T(8,128)(2,1)S(1)} %copy-done.3, bf16[5376,128]{1,0:T(8,128)(2,1)S(1)} %collective-permute-done.5.b_ref, bf16[1792,128]{1,0:T(8,128)(2,1)S(1)} %collective-permute-done.7.c_ref.d_ref, bf16[1792,128]{1,0:T(8,128)(2,1)S(1)} %collective-permute-done.7.c_ref.d_ref, ...), custom_call_target="tpu_custom_call" | custom-call | flops 37580963840 | bytes 5505024 | tf_op jit(solution)/shard_map/pallas_call | solution.py:147
  71.0 3.8 %collective-permute-start.10 = (f16[448,512]{1,0:T(8,128)(2,1)S(1)}, f16[448,512]{1,0:T(8,128)(2,1)S(1)}, u32[]{:S(2)}, u32[]{:S(2)}) collective-permute-start(f16[448,512]{1,0:T(8,128)(2,1)S(1)} %fusion.9), channel_id=1, source_target_pairs={{0,2},{1,31},{2,4},{3,1},{4,6},{5,3},{6,8},{7,5},{8,10},{9,7},{10,... | collective-permute-start | bytes 1376264 | tf_op jit(solution)/shard_map/ppermute | solution.py:266
  74.9 5.0 %collective-permute-start.14 = (f16[448,512]{1,0:T(8,128)(2,1)S(1)}, f16[448,512]{1,0:T(8,128)(2,1)S(1)}, u32[]{:S(2)}, u32[]{:S(2)}) collective-permute-start(f16[448,512]{1,0:T(8,128)(2,1)S(1)} %fusion.8), channel_id=1, source_target_pairs={{0,2},{1,31},{2,4},{3,1},{4,6},{5,3},{6,8},{7,5},{8,10},{9,7},{10,... | collective-permute-start | bytes 1376264 | tf_op jit(solution)/shard_map/ppermute | solution.py:266
  80.7 4.7 %collective-permute-start.13 = (f16[448,512]{1,0:T(8,128)(2,1)S(1)}, f16[448,512]{1,0:T(8,128)(2,1)S(1)}, u32[]{:S(2)}, u32[]{:S(2)}) collective-permute-start(f16[448,512]{1,0:T(8,128)(2,1)S(1)} %fusion.7), channel_id=1, source_target_pairs={{0,2},{1,31},{2,4},{3,1},{4,6},{5,3},{6,8},{7,5},{8,10},{9,7},{10,... | collective-permute-start | bytes 1376264 | tf_op jit(solution)/shard_map/ppermute | solution.py:266
  85.6 5.0 %collective-permute-start.16 = (f16[448,512]{1,0:T(8,128)(2,1)S(1)}, f16[448,512]{1,0:T(8,128)(2,1)S(1)}, u32[]{:S(2)}, u32[]{:S(2)}) collective-permute-start(f16[448,512]{1,0:T(8,128)(2,1)S(1)} %fusion.6), channel_id=1, source_target_pairs={{0,2},{1,31},{2,4},{3,1},{4,6},{5,3},{6,8},{7,5},{8,10},{9,7},{10,... | collective-permute-start | bytes 1376264 | tf_op jit(solution)/shard_map/ppermute | solution.py:266
  90.6 1.7 %shard_map.71 = f32[896,1024]{1,0:T(8,128)S(1)} custom-call(bf16[1792,128]{1,0:T(8,128)(2,1)S(1)} %copy-done.2, bf16[5376,128]{1,0:T(8,128)(2,1)S(1)} %collective-permute-done.5.b_ref, bf16[3584,128]{1,0:T(8,128)(2,1)S(1)} %collective-permute-done.12.c_ref.d_ref, bf16[3584,128]{1,0:T(8,128)(2,1)S(1)} %collective-permute-done.12.c_ref.d_ref, ...), custom_call_target="tpu_custom_call" | custom-call | flops 37580963840 | bytes 5505024 | tf_op jit(solution)/shard_map/pallas_call | solution.py:147
  92.5 3.5 %collective-permute-start.15 = (f16[448,512]{1,0:T(8,128)(2,1)S(1)}, f16[448,512]{1,0:T(8,128)(2,1)S(1)}, u32[]{:S(2)}, u32[]{:S(2)}) collective-permute-start(f16[448,512]{1,0:T(8,128)(2,1)S(1)} %fusion.5), channel_id=1, source_target_pairs={{0,2},{1,31},{2,4},{3,1},{4,6},{5,3},{6,8},{7,5},{8,10},{9,7},{10,... | collective-permute-start | bytes 1376264 | tf_op jit(solution)/shard_map/ppermute | solution.py:266
  96.2 5.0 %collective-permute-start.18 = (f16[448,512]{1,0:T(8,128)(2,1)S(1)}, f16[448,512]{1,0:T(8,128)(2,1)S(1)}, u32[]{:S(2)}, u32[]{:S(2)}) collective-permute-start(f16[448,512]{1,0:T(8,128)(2,1)S(1)} %fusion.4), channel_id=1, source_target_pairs={{0,2},{1,31},{2,4},{3,1},{4,6},{5,3},{6,8},{7,5},{8,10},{9,7},{10,... | collective-permute-start | bytes 1376264 | tf_op jit(solution)/shard_map/ppermute | solution.py:266
  101.8 4.7 %collective-permute-start.17 = (f16[448,512]{1,0:T(8,128)(2,1)S(1)}, f16[448,512]{1,0:T(8,128)(2,1)S(1)}, u32[]{:S(2)}, u32[]{:S(2)}) collective-permute-start(f16[448,512]{1,0:T(8,128)(2,1)S(1)} %fusion.3), channel_id=1, source_target_pairs={{0,2},{1,31},{2,4},{3,1},{4,6},{5,3},{6,8},{7,5},{8,10},{9,7},{10,... | collective-permute-start | bytes 1376264 | tf_op jit(solution)/shard_map/ppermute | solution.py:266
  107.0 4.7 %collective-permute-start.20 = (f16[448,512]{1,0:T(8,128)(2,1)S(1)}, f16[448,512]{1,0:T(8,128)(2,1)S(1)}, u32[]{:S(2)}, u32[]{:S(2)}) collective-permute-start(f16[448,512]{1,0:T(8,128)(2,1)S(1)} %fusion.2), channel_id=1, source_target_pairs={{0,2},{1,31},{2,4},{3,1},{4,6},{5,3},{6,8},{7,5},{8,10},{9,7},{10,... | collective-permute-start | bytes 1376264 | tf_op jit(solution)/shard_map/ppermute | solution.py:266
  111.8 1.7 %shard_map.72 = f32[896,1024]{1,0:T(8,128)S(1)} custom-call(bf16[1792,128]{1,0:T(8,128)(2,1)S(1)} %copy-done.2, bf16[5376,128]{1,0:T(8,128)(2,1)S(1)} %collective-permute-done.5.b_ref, bf16[3584,128]{1,0:T(8,128)(2,1)S(1)} %collective-permute-done.12.c_ref.d_ref, bf16[3584,128]{1,0:T(8,128)(2,1)S(1)} %collective-permute-done.12.c_ref.d_ref, ...), custom_call_target="tpu_custom_call" | custom-call | flops 37580963840 | bytes 5505024 | tf_op jit(solution)/shard_map/pallas_call | solution.py:147
  113.6 3.5 %collective-permute-start.19 = (f16[448,512]{1,0:T(8,128)(2,1)S(1)}, f16[448,512]{1,0:T(8,128)(2,1)S(1)}, u32[]{:S(2)}, u32[]{:S(2)}) collective-permute-start(f16[448,512]{1,0:T(8,128)(2,1)S(1)} %fusion.1), channel_id=1, source_target_pairs={{0,2},{1,31},{2,4},{3,1},{4,6},{5,3},{6,8},{7,5},{8,10},{9,7},{10,... | collective-permute-start | bytes 1376264 | tf_op jit(solution)/shard_map/ppermute | solution.py:266
  117.3 9.5 %collective-permute-start.21 = (f16[448,512]{1,0:T(8,128)(2,1)S(1)}, f16[448,512]{1,0:T(8,128)(2,1)S(1)}, u32[]{:S(2)}, u32[]{:S(2)}) collective-permute-start(f16[448,512]{1,0:T(8,128)(2,1)S(1)} %fusion), channel_id=1, source_target_pairs={{0,3},{1,30},{2,5},{3,0},{4,7},{5,2},{6,9},{7,4},{8,11},{9,6},{10,... | collective-permute-start | bytes 1376264 | tf_op jit(solution)/shard_map/ppermute | solution.py:266
  128.2 1.3 slice_add_fusion
  129.5 6.3 %collective-permute-done.21 = f16[448,512]{1,0:T(8,128)(2,1)S(1)} collective-permute-done((f16[448,512]{1,0:T(8,128)(2,1)S(1)}, f16[448,512]{1,0:T(8,128)(2,1)S(1)}, u32[]{:S(2)}, u32[]{:S(2)}) %collective-permute-start.21) | collective-permute-done | bytes 458784 | tf_op jit(solution)/shard_map/ppermute | solution.py:266
  136.1 14.2 %all_to_all.5 = f16[16,28,512]{2,1,0:T(8,128)(2,1)S(1)} all-to-all(f16[16,28,512]{2,1,0:T(8,128)(2,1)S(1)} %reshape.12), channel_id=1, replica_groups=mesh['ylo'=2,'x'=4,'yhi'=2,'z'=16,'core'=2] {'ylo','x','core'}, dimensions={0} | all-to-all | bytes 917504 | tf_op jit(solution)/shard_map/all_to_all | solution.py:292
  150.6 2.4 %shard_map.73 = (f32[28,512]{1,0:T(8,128)}, f32[28,512]{1,0:T(8,128)}, f32[28,512]{1,0:T(8,128)}) custom-call(f32[16,32,512]{2,1,0:T(8,128)S(1)} %pad.6.g_ref, bf16[28,512]{1,0:T(8,128)(2,1)S(1)} %copy-done.1), custom_call_target="tpu_custom_call" | custom-call | tf_op jit(solution)/shard_map/pallas_call | solution.py:213
  (69 shorter events, 8.9 us)
Async XLA Ops:
  7.1 10.8 %collective-permute-start = (bf16[2752,128]{1,0:T(8,128)(2,1)}, bf16[2752,128]{1,0:T(8,128)(2,1)S(1)}, u32[]{:S(2)}, u32[]{:S(2)}) collective-permute-start(bf16[2752,128]{1,0:T(8,128)(2,1)} %get-tuple-element.37), channel_id=1, source_target_pairs={{0,1},{1,0},{32,33},{33,32},{2,3},{3,2},{34,35},{35,34},{4,5},{5,4... | collective-permute-start | bytes 2113544 | tf_op jit(solution)/shard_map/ppermute | solution.py:237
  15.9 10.0 %collective-permute-start.2 = (bf16[736,128]{1,0:T(8,128)(2,1)}, bf16[736,128]{1,0:T(8,128)(2,1)S(1)}, u32[]{:S(2)}, u32[]{:S(2)}) collective-permute-start(bf16[736,128]{1,0:T(8,128)(2,1)} %get-tuple-element.40), channel_id=1, source_target_pairs={{0,32},{1,33},{32,0},{33,1},{2,34},{3,35},{34,2},{35,3},{4,36},{5,... | collective-permute-start | bytes 565256 | tf_op jit(solution)/shard_map/ppermute | solution.py:237
  17.9 12.0 %collective-permute-start.3 = (bf16[736,128]{1,0:T(8,128)(2,1)S(1)}, bf16[736,128]{1,0:T(8,128)(2,1)S(1)}, u32[]{:S(2)}, u32[]{:S(2)}) collective-permute-start(bf16[736,128]{1,0:T(8,128)(2,1)S(1)} %slice.108), channel_id=1, source_target_pairs={{0,32},{1,33},{32,0},{33,1},{2,34},{3,35},{34,2},{35,3},{4,36},{5,... | collective-permute-start | bytes 565256 | tf_op jit(solution)/shard_map/ppermute | solution.py:237
  23.7 18.2 %collective-permute-start.1 = (bf16[1792,128]{1,0:T(8,128)(2,1)S(1)}, bf16[1792,128]{1,0:T(8,128)(2,1)S(1)}, u32[]{:S(2)}, u32[]{:S(2)}) collective-permute-start(bf16[1792,128]{1,0:T(8,128)(2,1)S(1)} %pad_maximum_fusion.1), channel_id=1, source_target_pairs={{0,32},{1,33},{32,0},{33,1},{2,34},{3,35},{34,2},{35,3},{4,36},{5,... | collective-permute-start | bytes 1376264 | tf_op jit(solution)/shard_map/ppermute | solution.py:237
  29.9 0.9 copy-start.5
  30.8 1.3 copy-start.9
  30.8 11.1 %copy-start.4 = (bf16[896,128]{1,0:T(8,128)(2,1)S(1)}, bf16[896,128]{1,0:T(8,128)(2,1)}, u32[]{:S(2)}) copy-start(bf16[896,128]{1,0:T(8,128)(2,1)} %get-tuple-element.36.a_ref) | copy-start | bytes 688132
  32.1 11.5 %collective-permute-start.5 = (bf16[5376,128]{1,0:T(8,128)(2,1)S(1)}, bf16[5376,128]{1,0:T(8,128)(2,1)S(1)}, u32[]{:S(2)}, u32[]{:S(2)}) collective-permute-start(bf16[5376,128]{1,0:T(8,128)(2,1)S(1)} %copy-done.9), channel_id=1, source_target_pairs={{0,1},{1,0},{32,33},{33,32},{2,3},{3,2},{34,35},{35,34},{4,5},{5,4... | collective-permute-start | bytes 4128776 | tf_op jit(solution)/shard_map/ppermute | solution.py:237
  35.2 12.4 %collective-permute-start.4 = (f16[224,1024]{1,0:T(8,128)(2,1)S(1)}, f16[224,1024]{1,0:T(8,128)(2,1)S(1)}, u32[]{:S(2)}, u32[]{:S(2)}) collective-permute-start(f16[224,1024]{1,0:T(8,128)(2,1)S(1)} %convert_element_type.102), channel_id=1, source_target_pairs={{0,2},{1,31},{2,4},{3,1},{4,6},{5,3},{6,8},{7,5},{8,10},{9,7},{10,... | collective-permute-start | bytes 1376264 | tf_op jit(solution)/shard_map/ppermute | solution.py:266
  41.9 1.7 %copy-start.7 = (bf16[896,128]{1,0:T(8,128)(2,1)S(1)}, bf16[896,128]{1,0:T(8,128)(2,1)}, u32[]{:S(2)}) copy-start(bf16[896,128]{1,0:T(8,128)(2,1)} %get-tuple-element.44) | copy-start | bytes 688132
  43.7 15.5 %collective-permute-start.7 = (bf16[1792,128]{1,0:T(8,128)(2,1)S(1)}, bf16[1792,128]{1,0:T(8,128)(2,1)S(1)}, u32[]{:S(2)}, u32[]{:S(2)}) collective-permute-start(bf16[1792,128]{1,0:T(8,128)(2,1)S(1)} %pad_maximum_fusion.2), channel_id=1, source_target_pairs={{0,32},{1,33},{32,0},{33,1},{2,34},{3,35},{34,2},{35,3},{4,36},{5,... | collective-permute-start | bytes 1376264 | tf_op jit(solution)/shard_map/ppermute | solution.py:237
  47.7 7.7 %copy-start.6 = (bf16[1792,128]{1,0:T(8,128)(2,1)S(1)}, bf16[1792,128]{1,0:T(8,128)(2,1)}, u32[]{:S(2)}) copy-start(bf16[1792,128]{1,0:T(8,128)(2,1)} %get-tuple-element.54) | copy-start | bytes 1376260
  48.4 20.7 %copy-start.3 = (bf16[896,128]{1,0:T(8,128)(2,1)S(1)}, bf16[896,128]{1,0:T(8,128)(2,1)}, u32[]{:S(2)}) copy-start(bf16[896,128]{1,0:T(8,128)(2,1)} %get-tuple-element.51.a_ref) | copy-start | bytes 688132
  48.4 10.8 %collective-permute-start.6 = (f16[448,512]{1,0:T(8,128)(2,1)S(1)}, f16[448,512]{1,0:T(8,128)(2,1)S(1)}, u32[]{:S(2)}, u32[]{:S(2)}) collective-permute-start(f16[448,512]{1,0:T(8,128)(2,1)S(1)} %get-tuple-element.70), channel_id=1, source_target_pairs={{0,2},{1,31},{2,4},{3,1},{4,6},{5,3},{6,8},{7,5},{8,10},{9,7},{10,... | collective-permute-start | bytes 1376264 | tf_op jit(solution)/shard_map/ppermute | solution.py:266
  53.3 10.6 %collective-permute-start.9 = (f16[448,512]{1,0:T(8,128)(2,1)S(1)}, f16[448,512]{1,0:T(8,128)(2,1)S(1)}, u32[]{:S(2)}, u32[]{:S(2)}) collective-permute-start(f16[448,512]{1,0:T(8,128)(2,1)S(1)} %get-tuple-element.69), channel_id=1, source_target_pairs={{0,2},{1,31},{2,4},{3,1},{4,6},{5,3},{6,8},{7,5},{8,10},{9,7},{10,... | collective-permute-start | bytes 1376264 | tf_op jit(solution)/shard_map/ppermute | solution.py:266
  55.5 24.5 %collective-permute-start.12 = (bf16[3584,128]{1,0:T(8,128)(2,1)S(1)}, bf16[3584,128]{1,0:T(8,128)(2,1)S(1)}, u32[]{:S(2)}, u32[]{:S(2)}) collective-permute-start(bf16[3584,128]{1,0:T(8,128)(2,1)S(1)} %pad_maximum_fusion), channel_id=1, source_target_pairs={{0,32},{1,33},{32,0},{33,1},{2,34},{3,35},{34,2},{35,3},{4,36},{5,... | collective-permute-start | bytes 2752520 | tf_op jit(solution)/shard_map/ppermute | solution.py:237
  59.4 11.4 %collective-permute-start.8 = (f16[448,512]{1,0:T(8,128)(2,1)S(1)}, f16[448,512]{1,0:T(8,128)(2,1)S(1)}, u32[]{:S(2)}, u32[]{:S(2)}) collective-permute-start(f16[448,512]{1,0:T(8,128)(2,1)S(1)} %fusion.11), channel_id=1, source_target_pairs={{0,2},{1,31},{2,4},{3,1},{4,6},{5,3},{6,8},{7,5},{8,10},{9,7},{10,... | collective-permute-start | bytes 1376264 | tf_op jit(solution)/shard_map/ppermute | solution.py:266
  64.1 10.7 %collective-permute-start.11 = (f16[448,512]{1,0:T(8,128)(2,1)S(1)}, f16[448,512]{1,0:T(8,128)(2,1)S(1)}, u32[]{:S(2)}, u32[]{:S(2)}) collective-permute-start(f16[448,512]{1,0:T(8,128)(2,1)S(1)} %fusion.10), channel_id=1, source_target_pairs={{0,2},{1,31},{2,4},{3,1},{4,6},{5,3},{6,8},{7,5},{8,10},{9,7},{10,... | collective-permute-start | bytes 1376264 | tf_op jit(solution)/shard_map/ppermute | solution.py:266
  70.8 19.8 %copy-start.2 = (bf16[1792,128]{1,0:T(8,128)(2,1)S(1)}, bf16[1792,128]{1,0:T(8,128)(2,1)}, u32[]{:S(2)}) copy-start(bf16[1792,128]{1,0:T(8,128)(2,1)} %get-tuple-element.59.a_ref) | copy-start | bytes 1376260
  71.0 9.5 %collective-permute-start.10 = (f16[448,512]{1,0:T(8,128)(2,1)S(1)}, f16[448,512]{1,0:T(8,128)(2,1)S(1)}, u32[]{:S(2)}, u32[]{:S(2)}) collective-permute-start(f16[448,512]{1,0:T(8,128)(2,1)S(1)} %fusion.9), channel_id=1, source_target_pairs={{0,2},{1,31},{2,4},{3,1},{4,6},{5,3},{6,8},{7,5},{8,10},{9,7},{10,... | collective-permute-start | bytes 1376264 | tf_op jit(solution)/shard_map/ppermute | solution.py:266
  74.9 10.5 %collective-permute-start.14 = (f16[448,512]{1,0:T(8,128)(2,1)S(1)}, f16[448,512]{1,0:T(8,128)(2,1)S(1)}, u32[]{:S(2)}, u32[]{:S(2)}) collective-permute-start(f16[448,512]{1,0:T(8,128)(2,1)S(1)} %fusion.8), channel_id=1, source_target_pairs={{0,2},{1,31},{2,4},{3,1},{4,6},{5,3},{6,8},{7,5},{8,10},{9,7},{10,... | collective-permute-start | bytes 1376264 | tf_op jit(solution)/shard_map/ppermute | solution.py:266
  80.7 11.6 %collective-permute-start.13 = (f16[448,512]{1,0:T(8,128)(2,1)S(1)}, f16[448,512]{1,0:T(8,128)(2,1)S(1)}, u32[]{:S(2)}, u32[]{:S(2)}) collective-permute-start(f16[448,512]{1,0:T(8,128)(2,1)S(1)} %fusion.7), channel_id=1, source_target_pairs={{0,2},{1,31},{2,4},{3,1},{4,6},{5,3},{6,8},{7,5},{8,10},{9,7},{10,... | collective-permute-start | bytes 1376264 | tf_op jit(solution)/shard_map/ppermute | solution.py:266
  85.6 10.4 %collective-permute-start.16 = (f16[448,512]{1,0:T(8,128)(2,1)S(1)}, f16[448,512]{1,0:T(8,128)(2,1)S(1)}, u32[]{:S(2)}, u32[]{:S(2)}) collective-permute-start(f16[448,512]{1,0:T(8,128)(2,1)S(1)} %fusion.6), channel_id=1, source_target_pairs={{0,2},{1,31},{2,4},{3,1},{4,6},{5,3},{6,8},{7,5},{8,10},{9,7},{10,... | collective-permute-start | bytes 1376264 | tf_op jit(solution)/shard_map/ppermute | solution.py:266
  92.5 9.2 %collective-permute-start.15 = (f16[448,512]{1,0:T(8,128)(2,1)S(1)}, f16[448,512]{1,0:T(8,128)(2,1)S(1)}, u32[]{:S(2)}, u32[]{:S(2)}) collective-permute-start(f16[448,512]{1,0:T(8,128)(2,1)S(1)} %fusion.5), channel_id=1, source_target_pairs={{0,2},{1,31},{2,4},{3,1},{4,6},{5,3},{6,8},{7,5},{8,10},{9,7},{10,... | collective-permute-start | bytes 1376264 | tf_op jit(solution)/shard_map/ppermute | solution.py:266
  96.2 10.7 %collective-permute-start.18 = (f16[448,512]{1,0:T(8,128)(2,1)S(1)}, f16[448,512]{1,0:T(8,128)(2,1)S(1)}, u32[]{:S(2)}, u32[]{:S(2)}) collective-permute-start(f16[448,512]{1,0:T(8,128)(2,1)S(1)} %fusion.4), channel_id=1, source_target_pairs={{0,2},{1,31},{2,4},{3,1},{4,6},{5,3},{6,8},{7,5},{8,10},{9,7},{10,... | collective-permute-start | bytes 1376264 | tf_op jit(solution)/shard_map/ppermute | solution.py:266
  101.8 11.6 %collective-permute-start.17 = (f16[448,512]{1,0:T(8,128)(2,1)S(1)}, f16[448,512]{1,0:T(8,128)(2,1)S(1)}, u32[]{:S(2)}, u32[]{:S(2)}) collective-permute-start(f16[448,512]{1,0:T(8,128)(2,1)S(1)} %fusion.3), channel_id=1, source_target_pairs={{0,2},{1,31},{2,4},{3,1},{4,6},{5,3},{6,8},{7,5},{8,10},{9,7},{10,... | collective-permute-start | bytes 1376264 | tf_op jit(solution)/shard_map/ppermute | solution.py:266
  107.0 10.1 %collective-permute-start.20 = (f16[448,512]{1,0:T(8,128)(2,1)S(1)}, f16[448,512]{1,0:T(8,128)(2,1)S(1)}, u32[]{:S(2)}, u32[]{:S(2)}) collective-permute-start(f16[448,512]{1,0:T(8,128)(2,1)S(1)} %fusion.2), channel_id=1, source_target_pairs={{0,2},{1,31},{2,4},{3,1},{4,6},{5,3},{6,8},{7,5},{8,10},{9,7},{10,... | collective-permute-start | bytes 1376264 | tf_op jit(solution)/shard_map/ppermute | solution.py:266
  113.4 3.7 %copy-start = (f32[896,1024]{1,0:T(8,128)}, f32[896,1024]{1,0:T(8,128)S(1)}, u32[]{:S(2)}) copy-start(f32[896,1024]{1,0:T(8,128)S(1)} %shard_map.72) | copy-start | bytes 11010052
  113.5 13.4 %copy-start.8 = (s32[2]{0:T(128)S(1)}, s32[2]{0:T(128)}, u32[]{:S(2)}) copy-start(s32[2]{0:T(128)} %len_ref.1) | copy-start | bytes 28
  113.6 14.5 %collective-permute-start.19 = (f16[448,512]{1,0:T(8,128)(2,1)S(1)}, f16[448,512]{1,0:T(8,128)(2,1)S(1)}, u32[]{:S(2)}, u32[]{:S(2)}) collective-permute-start(f16[448,512]{1,0:T(8,128)(2,1)S(1)} %fusion.1), channel_id=1, source_target_pairs={{0,2},{1,31},{2,4},{3,1},{4,6},{5,3},{6,8},{7,5},{8,10},{9,7},{10,... | collective-permute-start | bytes 1376264 | tf_op jit(solution)/shard_map/ppermute | solution.py:266
  117.3 18.5 %collective-permute-start.21 = (f16[448,512]{1,0:T(8,128)(2,1)S(1)}, f16[448,512]{1,0:T(8,128)(2,1)S(1)}, u32[]{:S(2)}, u32[]{:S(2)}) collective-permute-start(f16[448,512]{1,0:T(8,128)(2,1)S(1)} %fusion), channel_id=1, source_target_pairs={{0,3},{1,30},{2,5},{3,0},{4,7},{5,2},{6,9},{7,4},{8,11},{9,6},{10,... | collective-permute-start | bytes 1376264 | tf_op jit(solution)/shard_map/ppermute | solution.py:266
  135.8 14.8 %copy-start.1 = (bf16[28,512]{1,0:T(8,128)(2,1)S(1)}, bf16[28,512]{1,0:T(8,128)(2,1)}, u32[]{:S(2)}) copy-start(bf16[28,512]{1,0:T(8,128)(2,1)} %w_ref.1) | copy-start | bytes 86020

commit v10 on v9

--- a/solution.py
+++ b/solution.py
@@ -12,7 +12,7 @@
 NZ = 16
 FAR = NZ // 2
 GROUPS = ((7, 6), (5, 4), (3, 2, 1, 0))
-LATER = {6: (1, 0), 4: (2, 0), 3: (2, 2)}
+LATER = {6: (1, 0), 4: (2, 0), 2: (2, 2)}
 DUE = {(6, 0): 1, (4, 0): 2}
 VMEM = 56 * 1024 * 1024
 f32 = jnp.float32
@@ -265,11 +265,12 @@
 
     ring = lambda x, cross=0: lax.ppermute(x, ("z", "core"), ring_pairs(cross))
     arrived = [send(0)]
-    sib_rest = quad(after(made[2 * n_out + 1], far), 1)
+    far16 = far.astype(f16)
+    sib_rest = quad(after(made[2 * n_out + 1], far16), 1)
     arrived.append(send(1))
     nearest = multiply(0, 0, far)
     arrived.append(send(2, far))
-    got = after(ring(far.astype(f16)), nearest, sent[1])
+    got = after(ring(far16), nearest, sent[1])
     got = got.astype(f32)
     none = jnp.zeros_like(got)
     got = jnp.where(core == 0, jnp.concatenate([got, none], axis=0), jnp.concatenate([none, got], axis=0))

time: 154 us -> 154 us (level)
    ppermute x7, starting transfers between devices: 28.2 us -> 26.4 us  [body(): lax.ppermute(x, ('yhi', 'core'), [(j, j ^ i) for j in range(4)])]
where the time goes in v10:
time: 154 us; the launch traced here: 153 us
  starting transfers between devices  100 us (65%)
  Pallas kernels  16 us (10%)
  blocking collectives  14.2 us (9%)
  waiting for transfers between devices  13.2 us (9%)
  other arithmetic  5.34 us (3%)
  between operations  1.92 us (1%)
  local copies, waits for them, and re-layouts  1.88 us (1%)
    ppermute x15, starting transfers between devices, body(): ring = lambda x, cross=0: lax.ppermute(x, ('z', 'core'), ring_pairs(cross))  73.7 us
    ppermute x7, starting transfers between devices, body(): lax.ppermute(x, ('yhi', 'core'), [(j, j ^ i) for j in range(4)])  26.4 us
    all_to_all x1, blocking collectives, body(): owned = lax.all_to_all(pieces, ('ylo', 'x', 'core'), 0, 0, tiled=True)  14.2 us
    ppermute x15, waiting for transfers between devices, body(): ring = lambda x, cross=0: lax.ppermute(x, ('z', 'core'), ring_pairs(cross))  7.54 us
    pallas_call x4, Pallas kernels, product(): pl.pallas_call(product_kernel, grid=(2 * count,), in_specs=[pl.BlockSpec(...  6.66 us
    pallas_call x1, Pallas kernels, turn(): pl.pallas_call(turn_kernel, grid_spec=pltpu.PrefetchScalarGridSpec(num_sc...  6.45 us
    ppermute x7, waiting for transfers between devices, body(): lax.ppermute(x, ('yhi', 'core'), [(j, j ^ i) for j in range(4)])  5.67 us
  transfers between devices with their start and end apart: 22, of which 9 were waited for; matrix products, arithmetic and copies ran while one was open for 4% of the time, Pallas kernels for 5%

profile of v10, /device:TPU:1, one launch (start us, length us, event | category | flops | bytes accessed | tf_op | source)
XLA Modules:
  0.0 152.6 jit_solution(11377982385827652694)
XLA Ops:
  0.6 6.5 %shard_map.67 = (bf16[736,128]{1,0:T(8,128)(2,1)}, bf16[896,128]{1,0:T(8,128)(2,1)}, bf16[896,128]{1,0:T(8,128)(2,1)}, bf16[1792,128]{1,0:T(8,128)(2,1)}, bf16[7...) custom-call(s32[2]{0:T(128)} %len_ref.1, ...), custom_call_target="tpu_custom_call" | custom-call | tf_op jit(solution)/shard_map/pallas_call | solution.py:90
  7.1 8.8 %collective-permute-start = (bf16[2752,128]{1,0:T(8,128)(2,1)}, bf16[2752,128]{1,0:T(8,128)(2,1)S(1)}, u32[]{:S(2)}, u32[]{:S(2)}) collective-permute-start(bf16[2752,128]{1,0:T(8,128)(2,1)} %get-tuple-element.37), channel_id=1, source_target_pairs={{0,1},{1,0},{32,33},{33,32},{2,3},{3,2},{34,35},{35,34},{4,5},{5,4... | collective-permute-start | bytes 2113544 | tf_op jit(solution)/shard_map/ppermute | solution.py:237
  15.9 1.9 %collective-permute-start.2 = (bf16[736,128]{1,0:T(8,128)(2,1)}, bf16[736,128]{1,0:T(8,128)(2,1)S(1)}, u32[]{:S(2)}, u32[]{:S(2)}) collective-permute-start(bf16[736,128]{1,0:T(8,128)(2,1)} %get-tuple-element.40), channel_id=1, source_target_pairs={{0,32},{1,33},{32,0},{33,1},{2,34},{3,35},{34,2},{35,3},{4,36},{5,... | collective-permute-start | bytes 565256 | tf_op jit(solution)/shard_map/ppermute | solution.py:237
  17.9 4.8 %collective-permute-start.3 = (bf16[736,128]{1,0:T(8,128)(2,1)S(1)}, bf16[736,128]{1,0:T(8,128)(2,1)S(1)}, u32[]{:S(2)}, u32[]{:S(2)}) collective-permute-start(bf16[736,128]{1,0:T(8,128)(2,1)S(1)} %slice.108), channel_id=1, source_target_pairs={{0,32},{1,33},{32,0},{33,1},{2,34},{3,35},{34,2},{35,3},{4,36},{5,... | collective-permute-start | bytes 565256 | tf_op jit(solution)/shard_map/ppermute | solution.py:237
  23.7 2.0 %collective-permute-start.1 = (bf16[1792,128]{1,0:T(8,128)(2,1)S(1)}, bf16[1792,128]{1,0:T(8,128)(2,1)S(1)}, u32[]{:S(2)}, u32[]{:S(2)}) collective-permute-start(bf16[1792,128]{1,0:T(8,128)(2,1)S(1)} %pad_maximum_fusion.1), channel_id=1, source_target_pairs={{0,32},{1,33},{32,0},{33,1},{2,34},{3,35},{34,2},{35,3},{4,36},{5,... | collective-permute-start | bytes 1376264 | tf_op jit(solution)/shard_map/ppermute | solution.py:237
  25.8 4.0 %collective-permute-done.3.d_ref = bf16[736,128]{1,0:T(8,128)(2,1)S(1)} collective-permute-done((bf16[736,128]{1,0:T(8,128)(2,1)S(1)}, bf16[736,128]{1,0:T(8,128)(2,1)S(1)}, u32[]{:S(2)}, u32[]{:S(2)}) %collective-permute-start.3) | collective-permute-done | bytes 188448 | tf_op jit(solution)/shard_map/ppermute | solution.py:237
  31.3 6.1 %collective-permute-start.4 = (f16[224,1024]{1,0:T(8,128)(2,1)S(1)}, f16[224,1024]{1,0:T(8,128)(2,1)S(1)}, u32[]{:S(2)}, u32[]{:S(2)}) collective-permute-start(f16[224,1024]{1,0:T(8,128)(2,1)S(1)} %convert_element_type.102), channel_id=1, source_target_pairs={{0,2},{1,31},{2,4},{3,1},{4,6},{5,3},{6,8},{7,5},{8,10},{9,7},{10,... | collective-permute-start | bytes 1376264 | tf_op jit(solution)/shard_map/ppermute | solution.py:266
  37.4 1.9 %collective-permute-start.5 = (bf16[5376,128]{1,0:T(8,128)(2,1)S(1)}, bf16[5376,128]{1,0:T(8,128)(2,1)S(1)}, u32[]{:S(2)}, u32[]{:S(2)}) collective-permute-start(bf16[5376,128]{1,0:T(8,128)(2,1)S(1)} %copy-done.9), channel_id=1, source_target_pairs={{0,1},{1,0},{32,33},{33,32},{2,3},{3,2},{34,35},{35,34},{4,5},{5,4... | collective-permute-start | bytes 4128776 | tf_op jit(solution)/shard_map/ppermute | solution.py:237
  39.4 1.7 %shard_map.69 = f32[896,1024]{1,0:T(8,128)S(1)} custom-call(bf16[896,128]{1,0:T(8,128)(2,1)S(1)} %copy-done.4, bf16[2752,128]{1,0:T(8,128)(2,1)S(1)} %collective-permute-done.b_ref, bf16[1792,128]{1,0:T(8,128)(2,1)S(1)} %collective-permute-done.1.c_ref.d_ref, bf16[1792,128]{1,0:T(8,128)(2,1)S(1)} %collective-permute-done.1.c_ref.d_ref, ...), custom_call_target="tpu_custom_call" | custom-call | flops 37580963840 | bytes 5505024 | tf_op jit(solution)/shard_map/pallas_call | solution.py:147
  42.5 4.5 %collective-permute-start.7 = (bf16[1792,128]{1,0:T(8,128)(2,1)S(1)}, bf16[1792,128]{1,0:T(8,128)(2,1)S(1)}, u32[]{:S(2)}, u32[]{:S(2)}) collective-permute-start(bf16[1792,128]{1,0:T(8,128)(2,1)S(1)} %pad_maximum_fusion.2), channel_id=1, source_target_pairs={{0,32},{1,33},{32,0},{33,1},{2,34},{3,35},{34,2},{35,3},{4,36},{5,... | collective-permute-start | bytes 1376264 | tf_op jit(solution)/shard_map/ppermute | solution.py:237
  47.8 4.9 %collective-permute-start.6 = (f16[448,512]{1,0:T(8,128)(2,1)S(1)}, f16[448,512]{1,0:T(8,128)(2,1)S(1)}, u32[]{:S(2)}, u32[]{:S(2)}) collective-permute-start(f16[448,512]{1,0:T(8,128)(2,1)S(1)} %get-tuple-element.70), channel_id=1, source_target_pairs={{0,2},{1,31},{2,4},{3,1},{4,6},{5,3},{6,8},{7,5},{8,10},{9,7},{10,... | collective-permute-start | bytes 1376264 | tf_op jit(solution)/shard_map/ppermute | solution.py:266
  52.7 2.6 %collective-permute-start.9 = (f16[448,512]{1,0:T(8,128)(2,1)S(1)}, f16[448,512]{1,0:T(8,128)(2,1)S(1)}, u32[]{:S(2)}, u32[]{:S(2)}) collective-permute-start(f16[448,512]{1,0:T(8,128)(2,1)S(1)} %get-tuple-element.69), channel_id=1, source_target_pairs={{0,2},{1,31},{2,4},{3,1},{4,6},{5,3},{6,8},{7,5},{8,10},{9,7},{10,... | collective-permute-start | bytes 1376264 | tf_op jit(solution)/shard_map/ppermute | solution.py:266
  55.5 2.5 %collective-permute-start.12 = (bf16[3584,128]{1,0:T(8,128)(2,1)S(1)}, bf16[3584,128]{1,0:T(8,128)(2,1)S(1)}, u32[]{:S(2)}, u32[]{:S(2)}) collective-permute-start(bf16[3584,128]{1,0:T(8,128)(2,1)S(1)} %pad_maximum_fusion), channel_id=1, source_target_pairs={{0,32},{1,33},{32,0},{33,1},{2,34},{3,35},{34,2},{35,3},{4,36},{5,... | collective-permute-start | bytes 2752520 | tf_op jit(solution)/shard_map/ppermute | solution.py:237
  58.3 5.3 %collective-permute-start.8 = (f16[448,512]{1,0:T(8,128)(2,1)S(1)}, f16[448,512]{1,0:T(8,128)(2,1)S(1)}, u32[]{:S(2)}, u32[]{:S(2)}) collective-permute-start(f16[448,512]{1,0:T(8,128)(2,1)S(1)} %fusion.11), channel_id=1, source_target_pairs={{0,2},{1,31},{2,4},{3,1},{4,6},{5,3},{6,8},{7,5},{8,10},{9,7},{10,... | collective-permute-start | bytes 1376264 | tf_op jit(solution)/shard_map/ppermute | solution.py:266
  63.8 4.7 %collective-permute-start.11 = (f16[448,512]{1,0:T(8,128)(2,1)S(1)}, f16[448,512]{1,0:T(8,128)(2,1)S(1)}, u32[]{:S(2)}, u32[]{:S(2)}) collective-permute-start(f16[448,512]{1,0:T(8,128)(2,1)S(1)} %fusion.10), channel_id=1, source_target_pairs={{0,2},{1,31},{2,4},{3,1},{4,6},{5,3},{6,8},{7,5},{8,10},{9,7},{10,... | collective-permute-start | bytes 1376264 | tf_op jit(solution)/shard_map/ppermute | solution.py:266
  68.6 1.7 %shard_map.70 = f32[896,1024]{1,0:T(8,128)S(1)} custom-call(bf16[896,128]{1,0:T(8,128)(2,1)S(1)} %copy-done.3, bf16[5376,128]{1,0:T(8,128)(2,1)S(1)} %collective-permute-done.5.b_ref, bf16[1792,128]{1,0:T(8,128)(2,1)S(1)} %collective-permute-done.7.c_ref.d_ref, bf16[1792,128]{1,0:T(8,128)(2,1)S(1)} %collective-permute-done.7.c_ref.d_ref, ...), custom_call_target="tpu_custom_call" | custom-call | flops 37580963840 | bytes 5505024 | tf_op jit(solution)/shard_map/pallas_call | solution.py:147
  70.4 4.1 %collective-permute-start.10 = (f16[448,512]{1,0:T(8,128)(2,1)S(1)}, f16[448,512]{1,0:T(8,128)(2,1)S(1)}, u32[]{:S(2)}, u32[]{:S(2)}) collective-permute-start(f16[448,512]{1,0:T(8,128)(2,1)S(1)} %fusion.9), channel_id=1, source_target_pairs={{0,2},{1,31},{2,4},{3,1},{4,6},{5,3},{6,8},{7,5},{8,10},{9,7},{10,... | collective-permute-start | bytes 1376264 | tf_op jit(solution)/shard_map/ppermute | solution.py:266
  74.7 4.8 %collective-permute-start.14 = (f16[448,512]{1,0:T(8,128)(2,1)S(1)}, f16[448,512]{1,0:T(8,128)(2,1)S(1)}, u32[]{:S(2)}, u32[]{:S(2)}) collective-permute-start(f16[448,512]{1,0:T(8,128)(2,1)S(1)} %fusion.8), channel_id=1, source_target_pairs={{0,2},{1,31},{2,4},{3,1},{4,6},{5,3},{6,8},{7,5},{8,10},{9,7},{10,... | collective-permute-start | bytes 1376264 | tf_op jit(solution)/shard_map/ppermute | solution.py:266
  80.1 5.0 %collective-permute-start.13 = (f16[448,512]{1,0:T(8,128)(2,1)S(1)}, f16[448,512]{1,0:T(8,128)(2,1)S(1)}, u32[]{:S(2)}, u32[]{:S(2)}) collective-permute-start(f16[448,512]{1,0:T(8,128)(2,1)S(1)} %fusion.7), channel_id=1, source_target_pairs={{0,2},{1,31},{2,4},{3,1},{4,6},{5,3},{6,8},{7,5},{8,10},{9,7},{10,... | collective-permute-start | bytes 1376264 | tf_op jit(solution)/shard_map/ppermute | solution.py:266
  85.3 4.8 %collective-permute-start.16 = (f16[448,512]{1,0:T(8,128)(2,1)S(1)}, f16[448,512]{1,0:T(8,128)(2,1)S(1)}, u32[]{:S(2)}, u32[]{:S(2)}) collective-permute-start(f16[448,512]{1,0:T(8,128)(2,1)S(1)} %fusion.6), channel_id=1, source_target_pairs={{0,2},{1,31},{2,4},{3,1},{4,6},{5,3},{6,8},{7,5},{8,10},{9,7},{10,... | collective-permute-start | bytes 1376264 | tf_op jit(solution)/shard_map/ppermute | solution.py:266
  90.0 1.7 %shard_map.71 = f32[896,1024]{1,0:T(8,128)S(1)} custom-call(bf16[1792,128]{1,0:T(8,128)(2,1)S(1)} %copy-done.2, bf16[5376,128]{1,0:T(8,128)(2,1)S(1)} %collective-permute-done.5.b_ref, bf16[3584,128]{1,0:T(8,128)(2,1)S(1)} %collective-permute-done.12.c_ref.d_ref, bf16[3584,128]{1,0:T(8,128)(2,1)S(1)} %collective-permute-done.12.c_ref.d_ref, ...), custom_call_target="tpu_custom_call" | custom-call | flops 37580963840 | bytes 5505024 | tf_op jit(solution)/shard_map/pallas_call | solution.py:147
  91.9 3.8 %collective-permute-start.15 = (f16[448,512]{1,0:T(8,128)(2,1)S(1)}, f16[448,512]{1,0:T(8,128)(2,1)S(1)}, u32[]{:S(2)}, u32[]{:S(2)}) collective-permute-start(f16[448,512]{1,0:T(8,128)(2,1)S(1)} %fusion.5), channel_id=1, source_target_pairs={{0,2},{1,31},{2,4},{3,1},{4,6},{5,3},{6,8},{7,5},{8,10},{9,7},{10,... | collective-permute-start | bytes 1376264 | tf_op jit(solution)/shard_map/ppermute | solution.py:266
  95.8 4.8 %collective-permute-start.18 = (f16[448,512]{1,0:T(8,128)(2,1)S(1)}, f16[448,512]{1,0:T(8,128)(2,1)S(1)}, u32[]{:S(2)}, u32[]{:S(2)}) collective-permute-start(f16[448,512]{1,0:T(8,128)(2,1)S(1)} %fusion.4), channel_id=1, source_target_pairs={{0,2},{1,31},{2,4},{3,1},{4,6},{5,3},{6,8},{7,5},{8,10},{9,7},{10,... | collective-permute-start | bytes 1376264 | tf_op jit(solution)/shard_map/ppermute | solution.py:266
  101.3 5.0 %collective-permute-start.17 = (f16[448,512]{1,0:T(8,128)(2,1)S(1)}, f16[448,512]{1,0:T(8,128)(2,1)S(1)}, u32[]{:S(2)}, u32[]{:S(2)}) collective-permute-start(f16[448,512]{1,0:T(8,128)(2,1)S(1)} %fusion.3), channel_id=1, source_target_pairs={{0,2},{1,31},{2,4},{3,1},{4,6},{5,3},{6,8},{7,5},{8,10},{9,7},{10,... | collective-permute-start | bytes 1376264 | tf_op jit(solution)/shard_map/ppermute | solution.py:266
  106.5 4.7 %collective-permute-start.20 = (f16[448,512]{1,0:T(8,128)(2,1)S(1)}, f16[448,512]{1,0:T(8,128)(2,1)S(1)}, u32[]{:S(2)}, u32[]{:S(2)}) collective-permute-start(f16[448,512]{1,0:T(8,128)(2,1)S(1)} %fusion.2), channel_id=1, source_target_pairs={{0,2},{1,31},{2,4},{3,1},{4,6},{5,3},{6,8},{7,5},{8,10},{9,7},{10,... | collective-permute-start | bytes 1376264 | tf_op jit(solution)/shard_map/ppermute | solution.py:266
  111.2 1.7 %shard_map.72 = f32[896,1024]{1,0:T(8,128)S(1)} custom-call(bf16[1792,128]{1,0:T(8,128)(2,1)S(1)} %copy-done.2, bf16[5376,128]{1,0:T(8,128)(2,1)S(1)} %collective-permute-done.5.b_ref, bf16[3584,128]{1,0:T(8,128)(2,1)S(1)} %collective-permute-done.12.c_ref.d_ref, bf16[3584,128]{1,0:T(8,128)(2,1)S(1)} %collective-permute-done.12.c_ref.d_ref, ...), custom_call_target="tpu_custom_call" | custom-call | flops 37580963840 | bytes 5505024 | tf_op jit(solution)/shard_map/pallas_call | solution.py:147
  113.1 3.7 %collective-permute-start.19 = (f16[448,512]{1,0:T(8,128)(2,1)S(1)}, f16[448,512]{1,0:T(8,128)(2,1)S(1)}, u32[]{:S(2)}, u32[]{:S(2)}) collective-permute-start(f16[448,512]{1,0:T(8,128)(2,1)S(1)} %fusion.1), channel_id=1, source_target_pairs={{0,2},{1,31},{2,4},{3,1},{4,6},{5,3},{6,8},{7,5},{8,10},{9,7},{10,... | collective-permute-start | bytes 1376264 | tf_op jit(solution)/shard_map/ppermute | solution.py:266
  117.0 9.5 %collective-permute-start.21 = (f16[448,512]{1,0:T(8,128)(2,1)S(1)}, f16[448,512]{1,0:T(8,128)(2,1)S(1)}, u32[]{:S(2)}, u32[]{:S(2)}) collective-permute-start(f16[448,512]{1,0:T(8,128)(2,1)S(1)} %fusion), channel_id=1, source_target_pairs={{0,3},{1,30},{2,5},{3,0},{4,7},{5,2},{6,9},{7,4},{8,11},{9,6},{10,... | collective-permute-start | bytes 1376264 | tf_op jit(solution)/shard_map/ppermute | solution.py:266
  127.8 1.3 slice_add_fusion
  129.1 6.3 %collective-permute-done.21 = f16[448,512]{1,0:T(8,128)(2,1)S(1)} collective-permute-done((f16[448,512]{1,0:T(8,128)(2,1)S(1)}, f16[448,512]{1,0:T(8,128)(2,1)S(1)}, u32[]{:S(2)}, u32[]{:S(2)}) %collective-permute-start.21) | collective-permute-done | bytes 458784 | tf_op jit(solution)/shard_map/ppermute | solution.py:266
  135.7 14.2 %all_to_all.5 = f16[16,28,512]{2,1,0:T(8,128)(2,1)S(1)} all-to-all(f16[16,28,512]{2,1,0:T(8,128)(2,1)S(1)} %reshape.12), channel_id=1, replica_groups=mesh['ylo'=2,'x'=4,'yhi'=2,'z'=16,'core'=2] {'ylo','x','core'}, dimensions={0} | all-to-all | bytes 917504 | tf_op jit(solution)/shard_map/all_to_all | solution.py:293
  150.2 2.4 %shard_map.73 = (f32[28,512]{1,0:T(8,128)}, f32[28,512]{1,0:T(8,128)}, f32[28,512]{1,0:T(8,128)}) custom-call(f32[16,32,512]{2,1,0:T(8,128)S(1)} %pad.6.g_ref, bf16[28,512]{1,0:T(8,128)(2,1)S(1)} %copy-done.1), custom_call_target="tpu_custom_call" | custom-call | tf_op jit(solution)/shard_map/pallas_call | solution.py:213
  (69 shorter events, 9.2 us)
Async XLA Ops:
  7.1 10.8 %collective-permute-start = (bf16[2752,128]{1,0:T(8,128)(2,1)}, bf16[2752,128]{1,0:T(8,128)(2,1)S(1)}, u32[]{:S(2)}, u32[]{:S(2)}) collective-permute-start(bf16[2752,128]{1,0:T(8,128)(2,1)} %get-tuple-element.37), channel_id=1, source_target_pairs={{0,1},{1,0},{32,33},{33,32},{2,3},{3,2},{34,35},{35,34},{4,5},{5,4... | collective-permute-start | bytes 2113544 | tf_op jit(solution)/shard_map/ppermute | solution.py:237
  15.9 10.0 %collective-permute-start.2 = (bf16[736,128]{1,0:T(8,128)(2,1)}, bf16[736,128]{1,0:T(8,128)(2,1)S(1)}, u32[]{:S(2)}, u32[]{:S(2)}) collective-permute-start(bf16[736,128]{1,0:T(8,128)(2,1)} %get-tuple-element.40), channel_id=1, source_target_pairs={{0,32},{1,33},{32,0},{33,1},{2,34},{3,35},{34,2},{35,3},{4,36},{5,... | collective-permute-start | bytes 565256 | tf_op jit(solution)/shard_map/ppermute | solution.py:237
  17.9 12.0 %collective-permute-start.3 = (bf16[736,128]{1,0:T(8,128)(2,1)S(1)}, bf16[736,128]{1,0:T(8,128)(2,1)S(1)}, u32[]{:S(2)}, u32[]{:S(2)}) collective-permute-start(bf16[736,128]{1,0:T(8,128)(2,1)S(1)} %slice.108), channel_id=1, source_target_pairs={{0,32},{1,33},{32,0},{33,1},{2,34},{3,35},{34,2},{35,3},{4,36},{5,... | collective-permute-start | bytes 565256 | tf_op jit(solution)/shard_map/ppermute | solution.py:237
  23.7 15.7 %collective-permute-start.1 = (bf16[1792,128]{1,0:T(8,128)(2,1)S(1)}, bf16[1792,128]{1,0:T(8,128)(2,1)S(1)}, u32[]{:S(2)}, u32[]{:S(2)}) collective-permute-start(bf16[1792,128]{1,0:T(8,128)(2,1)S(1)} %pad_maximum_fusion.1), channel_id=1, source_target_pairs={{0,32},{1,33},{32,0},{33,1},{2,34},{3,35},{34,2},{35,3},{4,36},{5,... | collective-permute-start | bytes 1376264 | tf_op jit(solution)/shard_map/ppermute | solution.py:237
  29.9 0.9 copy-start.5
  30.8 6.6 %copy-start.9 = (bf16[5376,128]{1,0:T(8,128)(2,1)S(1)}, bf16[5376,128]{1,0:T(8,128)(2,1)}, u32[]{:S(2)}) copy-start(bf16[5376,128]{1,0:T(8,128)(2,1)} %get-tuple-element.46) | copy-start | bytes 4128772
  30.8 8.7 %copy-start.4 = (bf16[896,128]{1,0:T(8,128)(2,1)S(1)}, bf16[896,128]{1,0:T(8,128)(2,1)}, u32[]{:S(2)}) copy-start(bf16[896,128]{1,0:T(8,128)(2,1)} %get-tuple-element.36.a_ref) | copy-start | bytes 688132
  31.3 15.7 %collective-permute-start.4 = (f16[224,1024]{1,0:T(8,128)(2,1)S(1)}, f16[224,1024]{1,0:T(8,128)(2,1)S(1)}, u32[]{:S(2)}, u32[]{:S(2)}) collective-permute-start(f16[224,1024]{1,0:T(8,128)(2,1)S(1)} %convert_element_type.102), channel_id=1, source_target_pairs={{0,2},{1,31},{2,4},{3,1},{4,6},{5,3},{6,8},{7,5},{8,10},{9,7},{10,... | collective-permute-start | bytes 1376264 | tf_op jit(solution)/shard_map/ppermute | solution.py:266
  37.4 5.0 %collective-permute-start.5 = (bf16[5376,128]{1,0:T(8,128)(2,1)S(1)}, bf16[5376,128]{1,0:T(8,128)(2,1)S(1)}, u32[]{:S(2)}, u32[]{:S(2)}) collective-permute-start(bf16[5376,128]{1,0:T(8,128)(2,1)S(1)} %copy-done.9), channel_id=1, source_target_pairs={{0,1},{1,0},{32,33},{33,32},{2,3},{3,2},{34,35},{35,34},{4,5},{5,4... | collective-permute-start | bytes 4128776 | tf_op jit(solution)/shard_map/ppermute | solution.py:237
  39.4 3.0 %copy-start.7 = (bf16[896,128]{1,0:T(8,128)(2,1)S(1)}, bf16[896,128]{1,0:T(8,128)(2,1)}, u32[]{:S(2)}) copy-start(bf16[896,128]{1,0:T(8,128)(2,1)} %get-tuple-element.44) | copy-start | bytes 688132
  42.5 15.7 %collective-permute-start.7 = (bf16[1792,128]{1,0:T(8,128)(2,1)S(1)}, bf16[1792,128]{1,0:T(8,128)(2,1)S(1)}, u32[]{:S(2)}, u32[]{:S(2)}) collective-permute-start(bf16[1792,128]{1,0:T(8,128)(2,1)S(1)} %pad_maximum_fusion.2), channel_id=1, source_target_pairs={{0,32},{1,33},{32,0},{33,1},{2,34},{3,35},{34,2},{35,3},{4,36},{5,... | collective-permute-start | bytes 1376264 | tf_op jit(solution)/shard_map/ppermute | solution.py:237
  47.1 8.3 %copy-start.6 = (bf16[1792,128]{1,0:T(8,128)(2,1)S(1)}, bf16[1792,128]{1,0:T(8,128)(2,1)}, u32[]{:S(2)}) copy-start(bf16[1792,128]{1,0:T(8,128)(2,1)} %get-tuple-element.54) | copy-start | bytes 1376260
  47.8 20.8 %copy-start.3 = (bf16[896,128]{1,0:T(8,128)(2,1)S(1)}, bf16[896,128]{1,0:T(8,128)(2,1)}, u32[]{:S(2)}) copy-start(bf16[896,128]{1,0:T(8,128)(2,1)} %get-tuple-element.51.a_ref) | copy-start | bytes 688132
  47.8 10.3 %collective-permute-start.6 = (f16[448,512]{1,0:T(8,128)(2,1)S(1)}, f16[448,512]{1,0:T(8,128)(2,1)S(1)}, u32[]{:S(2)}, u32[]{:S(2)}) collective-permute-start(f16[448,512]{1,0:T(8,128)(2,1)S(1)} %get-tuple-element.70), channel_id=1, source_target_pairs={{0,2},{1,31},{2,4},{3,1},{4,6},{5,3},{6,8},{7,5},{8,10},{9,7},{10,... | collective-permute-start | bytes 1376264 | tf_op jit(solution)/shard_map/ppermute | solution.py:266
  52.7 10.9 %collective-permute-start.9 = (f16[448,512]{1,0:T(8,128)(2,1)S(1)}, f16[448,512]{1,0:T(8,128)(2,1)S(1)}, u32[]{:S(2)}, u32[]{:S(2)}) collective-permute-start(f16[448,512]{1,0:T(8,128)(2,1)S(1)} %get-tuple-element.69), channel_id=1, source_target_pairs={{0,2},{1,31},{2,4},{3,1},{4,6},{5,3},{6,8},{7,5},{8,10},{9,7},{10,... | collective-permute-start | bytes 1376264 | tf_op jit(solution)/shard_map/ppermute | solution.py:266
  55.5 23.9 %collective-permute-start.12 = (bf16[3584,128]{1,0:T(8,128)(2,1)S(1)}, bf16[3584,128]{1,0:T(8,128)(2,1)S(1)}, u32[]{:S(2)}, u32[]{:S(2)}) collective-permute-start(bf16[3584,128]{1,0:T(8,128)(2,1)S(1)} %pad_maximum_fusion), channel_id=1, source_target_pairs={{0,32},{1,33},{32,0},{33,1},{2,34},{3,35},{34,2},{35,3},{4,36},{5,... | collective-permute-start | bytes 2752520 | tf_op jit(solution)/shard_map/ppermute | solution.py:237
  58.3 11.9 %collective-permute-start.8 = (f16[448,512]{1,0:T(8,128)(2,1)S(1)}, f16[448,512]{1,0:T(8,128)(2,1)S(1)}, u32[]{:S(2)}, u32[]{:S(2)}) collective-permute-start(f16[448,512]{1,0:T(8,128)(2,1)S(1)} %fusion.11), channel_id=1, source_target_pairs={{0,2},{1,31},{2,4},{3,1},{4,6},{5,3},{6,8},{7,5},{8,10},{9,7},{10,... | collective-permute-start | bytes 1376264 | tf_op jit(solution)/shard_map/ppermute | solution.py:266
  63.8 10.7 %collective-permute-start.11 = (f16[448,512]{1,0:T(8,128)(2,1)S(1)}, f16[448,512]{1,0:T(8,128)(2,1)S(1)}, u32[]{:S(2)}, u32[]{:S(2)}) collective-permute-start(f16[448,512]{1,0:T(8,128)(2,1)S(1)} %fusion.10), channel_id=1, source_target_pairs={{0,2},{1,31},{2,4},{3,1},{4,6},{5,3},{6,8},{7,5},{8,10},{9,7},{10,... | collective-permute-start | bytes 1376264 | tf_op jit(solution)/shard_map/ppermute | solution.py:266
  70.2 19.8 %copy-start.2 = (bf16[1792,128]{1,0:T(8,128)(2,1)S(1)}, bf16[1792,128]{1,0:T(8,128)(2,1)}, u32[]{:S(2)}) copy-start(bf16[1792,128]{1,0:T(8,128)(2,1)} %get-tuple-element.59.a_ref) | copy-start | bytes 1376260
  70.4 9.5 %collective-permute-start.10 = (f16[448,512]{1,0:T(8,128)(2,1)S(1)}, f16[448,512]{1,0:T(8,128)(2,1)S(1)}, u32[]{:S(2)}, u32[]{:S(2)}) collective-permute-start(f16[448,512]{1,0:T(8,128)(2,1)S(1)} %fusion.9), channel_id=1, source_target_pairs={{0,2},{1,31},{2,4},{3,1},{4,6},{5,3},{6,8},{7,5},{8,10},{9,7},{10,... | collective-permute-start | bytes 1376264 | tf_op jit(solution)/shard_map/ppermute | solution.py:266
  74.7 10.4 %collective-permute-start.14 = (f16[448,512]{1,0:T(8,128)(2,1)S(1)}, f16[448,512]{1,0:T(8,128)(2,1)S(1)}, u32[]{:S(2)}, u32[]{:S(2)}) collective-permute-start(f16[448,512]{1,0:T(8,128)(2,1)S(1)} %fusion.8), channel_id=1, source_target_pairs={{0,2},{1,31},{2,4},{3,1},{4,6},{5,3},{6,8},{7,5},{8,10},{9,7},{10,... | collective-permute-start | bytes 1376264 | tf_op jit(solution)/shard_map/ppermute | solution.py:266
  80.1 11.7 %collective-permute-start.13 = (f16[448,512]{1,0:T(8,128)(2,1)S(1)}, f16[448,512]{1,0:T(8,128)(2,1)S(1)}, u32[]{:S(2)}, u32[]{:S(2)}) collective-permute-start(f16[448,512]{1,0:T(8,128)(2,1)S(1)} %fusion.7), channel_id=1, source_target_pairs={{0,2},{1,31},{2,4},{3,1},{4,6},{5,3},{6,8},{7,5},{8,10},{9,7},{10,... | collective-permute-start | bytes 1376264 | tf_op jit(solution)/shard_map/ppermute | solution.py:266
  85.3 10.4 %collective-permute-start.16 = (f16[448,512]{1,0:T(8,128)(2,1)S(1)}, f16[448,512]{1,0:T(8,128)(2,1)S(1)}, u32[]{:S(2)}, u32[]{:S(2)}) collective-permute-start(f16[448,512]{1,0:T(8,128)(2,1)S(1)} %fusion.6), channel_id=1, source_target_pairs={{0,2},{1,31},{2,4},{3,1},{4,6},{5,3},{6,8},{7,5},{8,10},{9,7},{10,... | collective-permute-start | bytes 1376264 | tf_op jit(solution)/shard_map/ppermute | solution.py:266
  91.9 9.2 %collective-permute-start.15 = (f16[448,512]{1,0:T(8,128)(2,1)S(1)}, f16[448,512]{1,0:T(8,128)(2,1)S(1)}, u32[]{:S(2)}, u32[]{:S(2)}) collective-permute-start(f16[448,512]{1,0:T(8,128)(2,1)S(1)} %fusion.5), channel_id=1, source_target_pairs={{0,2},{1,31},{2,4},{3,1},{4,6},{5,3},{6,8},{7,5},{8,10},{9,7},{10,... | collective-permute-start | bytes 1376264 | tf_op jit(solution)/shard_map/ppermute | solution.py:266
  95.8 10.5 %collective-permute-start.18 = (f16[448,512]{1,0:T(8,128)(2,1)S(1)}, f16[448,512]{1,0:T(8,128)(2,1)S(1)}, u32[]{:S(2)}, u32[]{:S(2)}) collective-permute-start(f16[448,512]{1,0:T(8,128)(2,1)S(1)} %fusion.4), channel_id=1, source_target_pairs={{0,2},{1,31},{2,4},{3,1},{4,6},{5,3},{6,8},{7,5},{8,10},{9,7},{10,... | collective-permute-start | bytes 1376264 | tf_op jit(solution)/shard_map/ppermute | solution.py:266
  101.3 11.6 %collective-permute-start.17 = (f16[448,512]{1,0:T(8,128)(2,1)S(1)}, f16[448,512]{1,0:T(8,128)(2,1)S(1)}, u32[]{:S(2)}, u32[]{:S(2)}) collective-permute-start(f16[448,512]{1,0:T(8,128)(2,1)S(1)} %fusion.3), channel_id=1, source_target_pairs={{0,2},{1,31},{2,4},{3,1},{4,6},{5,3},{6,8},{7,5},{8,10},{9,7},{10,... | collective-permute-start | bytes 1376264 | tf_op jit(solution)/shard_map/ppermute | solution.py:266
  106.5 10.4 %collective-permute-start.20 = (f16[448,512]{1,0:T(8,128)(2,1)S(1)}, f16[448,512]{1,0:T(8,128)(2,1)S(1)}, u32[]{:S(2)}, u32[]{:S(2)}) collective-permute-start(f16[448,512]{1,0:T(8,128)(2,1)S(1)} %fusion.2), channel_id=1, source_target_pairs={{0,2},{1,31},{2,4},{3,1},{4,6},{5,3},{6,8},{7,5},{8,10},{9,7},{10,... | collective-permute-start | bytes 1376264 | tf_op jit(solution)/shard_map/ppermute | solution.py:266
  112.9 4.0 %copy-start = (f32[896,1024]{1,0:T(8,128)}, f32[896,1024]{1,0:T(8,128)S(1)}, u32[]{:S(2)}) copy-start(f32[896,1024]{1,0:T(8,128)S(1)} %shard_map.72) | copy-start | bytes 11010052
  112.9 13.6 %copy-start.8 = (s32[2]{0:T(128)S(1)}, s32[2]{0:T(128)}, u32[]{:S(2)}) copy-start(s32[2]{0:T(128)} %len_ref.1) | copy-start | bytes 28
  113.1 14.7 %collective-permute-start.19 = (f16[448,512]{1,0:T(8,128)(2,1)S(1)}, f16[448,512]{1,0:T(8,128)(2,1)S(1)}, u32[]{:S(2)}, u32[]{:S(2)}) collective-permute-start(f16[448,512]{1,0:T(8,128)(2,1)S(1)} %fusion.1), channel_id=1, source_target_pairs={{0,2},{1,31},{2,4},{3,1},{4,6},{5,3},{6,8},{7,5},{8,10},{9,7},{10,... | collective-permute-start | bytes 1376264 | tf_op jit(solution)/shard_map/ppermute | solution.py:266
  117.0 18.4 %collective-permute-start.21 = (f16[448,512]{1,0:T(8,128)(2,1)S(1)}, f16[448,512]{1,0:T(8,128)(2,1)S(1)}, u32[]{:S(2)}, u32[]{:S(2)}) collective-permute-start(f16[448,512]{1,0:T(8,128)(2,1)S(1)} %fusion), channel_id=1, source_target_pairs={{0,3},{1,30},{2,5},{3,0},{4,7},{5,2},{6,9},{7,4},{8,11},{9,6},{10,... | collective-permute-start | bytes 1376264 | tf_op jit(solution)/shard_map/ppermute | solution.py:266
  135.4 14.8 %copy-start.1 = (bf16[28,512]{1,0:T(8,128)(2,1)S(1)}, bf16[28,512]{1,0:T(8,128)(2,1)}, u32[]{:S(2)}) copy-start(bf16[28,512]{1,0:T(8,128)(2,1)} %w_ref.1) | copy-start | bytes 86020

commit v11 on v10

--- a/solution.py
+++ b/solution.py
@@ -264,8 +264,8 @@
         return part
 
     ring = lambda x, cross=0: lax.ppermute(x, ("z", "core"), ring_pairs(cross))
-    arrived = [send(0)]
     far16 = far.astype(f16)
+    arrived = [send(0, far16)]
     sib_rest = quad(after(made[2 * n_out + 1], far16), 1)
     arrived.append(send(1))
     nearest = multiply(0, 0, far)

time: 154 us -> 161 us (1.045)
  starting transfers between devices: 100 us -> 104 us
  waiting for transfers between devices: 13.2 us -> 16.9 us
    ppermute x15, starting transfers between devices: 73.7 us -> 80.1 us  [body(): ring = lambda x, cross=0: lax.ppermute(x, ('z', 'core'), ring_pairs(cross))]
    ppermute x7, starting transfers between devices: 26.4 us -> 23.6 us  [body(): lax.ppermute(x, ('yhi', 'core'), [(j, j ^ i) for j in range(4)])]
    ppermute x7, waiting for transfers between devices: 5.67 us -> 8.34 us  [body(): lax.ppermute(x, ('yhi', 'core'), [(j, j ^ i) for j in range(4)])]
  transfers between devices with their start and end apart: 22 -> 22, of which waited for: 9 -> 9; matrix products, arithmetic and copies ran while one was open for 4% -> 4% of each run, Pallas kernels for 5% -> 4%
where the time goes in v11:
time: 161 us; the launch traced here: 160 us
  starting transfers between devices  104 us (65%)
  waiting for transfers between devices  16.9 us (10%)
  Pallas kernels  16 us (10%)
  blocking collectives  14.2 us (9%)
  other arithmetic  5.32 us (3%)
  between operations  1.89 us (1%)
  local copies, waits for them, and re-layouts  1.88 us (1%)
    ppermute x15, starting transfers between devices, body(): ring = lambda x, cross=0: lax.ppermute(x, ('z', 'core'), ring_pairs(cross))  80.1 us
    ppermute x7, starting transfers between devices, body(): lax.ppermute(x, ('yhi', 'core'), [(j, j ^ i) for j in range(4)])  23.6 us
    all_to_all x1, blocking collectives, body(): owned = lax.all_to_all(pieces, ('ylo', 'x', 'core'), 0, 0, tiled=True)  14.2 us
    ppermute x15, waiting for transfers between devices, body(): ring = lambda x, cross=0: lax.ppermute(x, ('z', 'core'), ring_pairs(cross))  8.56 us
    ppermute x7, waiting for transfers between devices, body(): lax.ppermute(x, ('yhi', 'core'), [(j, j ^ i) for j in range(4)])  8.34 us
    pallas_call x4, Pallas kernels, product(): pl.pallas_call(product_kernel, grid=(2 * count,), in_specs=[pl.BlockSpec(...  6.67 us
    pallas_call x1, Pallas kernels, turn(): pl.pallas_call(turn_kernel, grid_spec=pltpu.PrefetchScalarGridSpec(num_sc...  6.47 us
  transfers between devices with their start and end apart: 22, of which 9 were waited for; matrix products, arithmetic and copies ran while one was open for 4% of the time, Pallas kernels for 4%

profile of v11, /device:TPU:1, one launch (start us, length us, event | category | flops | bytes accessed | tf_op | source)
XLA Modules:
  0.0 159.8 jit_solution(3984997219341150991)
XLA Ops:
  0.6 6.5 %shard_map.67 = (bf16[736,128]{1,0:T(8,128)(2,1)}, bf16[896,128]{1,0:T(8,128)(2,1)}, bf16[896,128]{1,0:T(8,128)(2,1)}, bf16[1792,128]{1,0:T(8,128)(2,1)}, bf16[7...) custom-call(s32[2]{0:T(128)} %len_ref.1, ...), custom_call_target="tpu_custom_call" | custom-call | tf_op jit(solution)/shard_map/pallas_call | solution.py:90
  7.1 8.8 %collective-permute-start = (bf16[2752,128]{1,0:T(8,128)(2,1)}, bf16[2752,128]{1,0:T(8,128)(2,1)S(1)}, u32[]{:S(2)}, u32[]{:S(2)}) collective-permute-start(bf16[2752,128]{1,0:T(8,128)(2,1)} %get-tuple-element.38), channel_id=1, source_target_pairs={{0,1},{1,0},{32,33},{33,32},{2,3},{3,2},{34,35},{35,34},{4,5},{5,4... | collective-permute-start | bytes 2113544 | tf_op jit(solution)/shard_map/ppermute | solution.py:237
  15.9 1.9 %collective-permute-start.1 = (bf16[736,128]{1,0:T(8,128)(2,1)}, bf16[736,128]{1,0:T(8,128)(2,1)S(1)}, u32[]{:S(2)}, u32[]{:S(2)}) collective-permute-start(bf16[736,128]{1,0:T(8,128)(2,1)} %get-tuple-element.41), channel_id=1, source_target_pairs={{0,32},{1,33},{32,0},{33,1},{2,34},{3,35},{34,2},{35,3},{4,36},{5,... | collective-permute-start | bytes 565256 | tf_op jit(solution)/shard_map/ppermute | solution.py:237
  17.9 4.8 %collective-permute-start.2 = (bf16[736,128]{1,0:T(8,128)(2,1)S(1)}, bf16[736,128]{1,0:T(8,128)(2,1)S(1)}, u32[]{:S(2)}, u32[]{:S(2)}) collective-permute-start(bf16[736,128]{1,0:T(8,128)(2,1)S(1)} %slice.108), channel_id=1, source_target_pairs={{0,32},{1,33},{32,0},{33,1},{2,34},{3,35},{34,2},{35,3},{4,36},{5,... | collective-permute-start | bytes 565256 | tf_op jit(solution)/shard_map/ppermute | solution.py:237
  23.7 2.1 %collective-permute-done.1.c_ref = bf16[736,128]{1,0:T(8,128)(2,1)S(1)} collective-permute-done((bf16[736,128]{1,0:T(8,128)(2,1)}, bf16[736,128]{1,0:T(8,128)(2,1)S(1)}, u32[]{:S(2)}, u32[]{:S(2)}) %collective-permute-start.1) | collective-permute-done | bytes 188448 | tf_op jit(solution)/shard_map/ppermute | solution.py:237
  25.8 4.0 %collective-permute-done.2.d_ref = bf16[736,128]{1,0:T(8,128)(2,1)S(1)} collective-permute-done((bf16[736,128]{1,0:T(8,128)(2,1)S(1)}, bf16[736,128]{1,0:T(8,128)(2,1)S(1)}, u32[]{:S(2)}, u32[]{:S(2)}) %collective-permute-start.2) | collective-permute-done | bytes 188448 | tf_op jit(solution)/shard_map/ppermute | solution.py:237
  31.3 2.3 %collective-permute-start.3 = (bf16[1792,128]{1,0:T(8,128)(2,1)S(1)}, bf16[1792,128]{1,0:T(8,128)(2,1)S(1)}, u32[]{:S(2)}, u32[]{:S(2)}) collective-permute-start(bf16[1792,128]{1,0:T(8,128)(2,1)S(1)} %pad_maximum_fusion.1), channel_id=1, source_target_pairs={{0,32},{1,33},{32,0},{33,1},{2,34},{3,35},{34,2},{35,3},{4,36},{5,... | collective-permute-start | bytes 1376264 | tf_op jit(solution)/shard_map/ppermute | solution.py:237
  33.6 8.3 %collective-permute-start.4 = (f16[224,1024]{1,0:T(8,128)(2,1)S(1)}, f16[224,1024]{1,0:T(8,128)(2,1)S(1)}, u32[]{:S(2)}, u32[]{:S(2)}) collective-permute-start(f16[224,1024]{1,0:T(8,128)(2,1)S(1)} %convert_element_type.102), channel_id=1, source_target_pairs={{0,2},{1,31},{2,4},{3,1},{4,6},{5,3},{6,8},{7,5},{8,10},{9,7},{10,... | collective-permute-start | bytes 1376264 | tf_op jit(solution)/shard_map/ppermute | solution.py:266
  41.9 1.9 %collective-permute-start.5 = (bf16[5376,128]{1,0:T(8,128)(2,1)}, bf16[5376,128]{1,0:T(8,128)(2,1)S(1)}, u32[]{:S(2)}, u32[]{:S(2)}) collective-permute-start(bf16[5376,128]{1,0:T(8,128)(2,1)} %get-tuple-element.48), channel_id=1, source_target_pairs={{0,1},{1,0},{32,33},{33,32},{2,3},{3,2},{34,35},{35,34},{4,5},{5,4... | collective-permute-start | bytes 4128776 | tf_op jit(solution)/shard_map/ppermute | solution.py:237
  43.8 2.1 %collective-permute-done.3.c_ref.d_ref = bf16[1792,128]{1,0:T(8,128)(2,1)S(1)} collective-permute-done((bf16[1792,128]{1,0:T(8,128)(2,1)S(1)}, bf16[1792,128]{1,0:T(8,128)(2,1)S(1)}, u32[]{:S(2)}, u32[]{:S(2)}) %collective-permute-start.3) | collective-permute-done | bytes 458784 | tf_op jit(solution)/shard_map/ppermute | solution.py:237
  47.7 1.9 %collective-permute-start.7 = (bf16[1792,128]{1,0:T(8,128)(2,1)S(1)}, bf16[1792,128]{1,0:T(8,128)(2,1)S(1)}, u32[]{:S(2)}, u32[]{:S(2)}) collective-permute-start(bf16[1792,128]{1,0:T(8,128)(2,1)S(1)} %pad_maximum_fusion.2), channel_id=1, source_target_pairs={{0,32},{1,33},{32,0},{33,1},{2,34},{3,35},{34,2},{35,3},{4,36},{5,... | collective-permute-start | bytes 1376264 | tf_op jit(solution)/shard_map/ppermute | solution.py:237
  50.5 8.8 %collective-permute-start.6 = (f16[448,512]{1,0:T(8,128)(2,1)S(1)}, f16[448,512]{1,0:T(8,128)(2,1)S(1)}, u32[]{:S(2)}, u32[]{:S(2)}) collective-permute-start(f16[448,512]{1,0:T(8,128)(2,1)S(1)} %get-tuple-element.72), channel_id=1, source_target_pairs={{0,2},{1,31},{2,4},{3,1},{4,6},{5,3},{6,8},{7,5},{8,10},{9,7},{10,... | collective-permute-start | bytes 1376264 | tf_op jit(solution)/shard_map/ppermute | solution.py:266
  59.2 2.6 %collective-permute-start.9 = (f16[448,512]{1,0:T(8,128)(2,1)S(1)}, f16[448,512]{1,0:T(8,128)(2,1)S(1)}, u32[]{:S(2)}, u32[]{:S(2)}) collective-permute-start(f16[448,512]{1,0:T(8,128)(2,1)S(1)} %get-tuple-element.71), channel_id=1, source_target_pairs={{0,2},{1,31},{2,4},{3,1},{4,6},{5,3},{6,8},{7,5},{8,10},{9,7},{10,... | collective-permute-start | bytes 1376264 | tf_op jit(solution)/shard_map/ppermute | solution.py:266
  62.0 1.9 %collective-permute-start.12 = (bf16[3584,128]{1,0:T(8,128)(2,1)S(1)}, bf16[3584,128]{1,0:T(8,128)(2,1)S(1)}, u32[]{:S(2)}, u32[]{:S(2)}) collective-permute-start(bf16[3584,128]{1,0:T(8,128)(2,1)S(1)} %pad_maximum_fusion), channel_id=1, source_target_pairs={{0,32},{1,33},{32,0},{33,1},{2,34},{3,35},{34,2},{35,3},{4,36},{5,... | collective-permute-start | bytes 2752520 | tf_op jit(solution)/shard_map/ppermute | solution.py:237
  64.8 5.0 %collective-permute-start.8 = (f16[448,512]{1,0:T(8,128)(2,1)S(1)}, f16[448,512]{1,0:T(8,128)(2,1)S(1)}, u32[]{:S(2)}, u32[]{:S(2)}) collective-permute-start(f16[448,512]{1,0:T(8,128)(2,1)S(1)} %fusion.11), channel_id=1, source_target_pairs={{0,2},{1,31},{2,4},{3,1},{4,6},{5,3},{6,8},{7,5},{8,10},{9,7},{10,... | collective-permute-start | bytes 1376264 | tf_op jit(solution)/shard_map/ppermute | solution.py:266
  70.0 5.0 %collective-permute-start.11 = (f16[448,512]{1,0:T(8,128)(2,1)S(1)}, f16[448,512]{1,0:T(8,128)(2,1)S(1)}, u32[]{:S(2)}, u32[]{:S(2)}) collective-permute-start(f16[448,512]{1,0:T(8,128)(2,1)S(1)} %fusion.10), channel_id=1, source_target_pairs={{0,2},{1,31},{2,4},{3,1},{4,6},{5,3},{6,8},{7,5},{8,10},{9,7},{10,... | collective-permute-start | bytes 1376264 | tf_op jit(solution)/shard_map/ppermute | solution.py:266
  75.1 1.7 %shard_map.70 = f32[896,1024]{1,0:T(8,128)S(1)} custom-call(bf16[896,128]{1,0:T(8,128)(2,1)S(1)} %copy-done.3, bf16[5376,128]{1,0:T(8,128)(2,1)S(1)} %collective-permute-done.5.b_ref, bf16[1792,128]{1,0:T(8,128)(2,1)S(1)} %collective-permute-done.7.c_ref.d_ref, bf16[1792,128]{1,0:T(8,128)(2,1)S(1)} %collective-permute-done.7.c_ref.d_ref, ...), custom_call_target="tpu_custom_call" | custom-call | flops 37580963840 | bytes 5505024 | tf_op jit(solution)/shard_map/pallas_call | solution.py:147
  76.9 3.8 %collective-permute-start.10 = (f16[448,512]{1,0:T(8,128)(2,1)S(1)}, f16[448,512]{1,0:T(8,128)(2,1)S(1)}, u32[]{:S(2)}, u32[]{:S(2)}) collective-permute-start(f16[448,512]{1,0:T(8,128)(2,1)S(1)} %fusion.9), channel_id=1, source_target_pairs={{0,2},{1,31},{2,4},{3,1},{4,6},{5,3},{6,8},{7,5},{8,10},{9,7},{10,... | collective-permute-start | bytes 1376264 | tf_op jit(solution)/shard_map/ppermute | solution.py:266
  80.9 5.0 %collective-permute-start.14 = (f16[448,512]{1,0:T(8,128)(2,1)S(1)}, f16[448,512]{1,0:T(8,128)(2,1)S(1)}, u32[]{:S(2)}, u32[]{:S(2)}) collective-permute-start(f16[448,512]{1,0:T(8,128)(2,1)S(1)} %fusion.8), channel_id=1, source_target_pairs={{0,2},{1,31},{2,4},{3,1},{4,6},{5,3},{6,8},{7,5},{8,10},{9,7},{10,... | collective-permute-start | bytes 1376264 | tf_op jit(solution)/shard_map/ppermute | solution.py:266
  86.6 4.7 %collective-permute-start.13 = (f16[448,512]{1,0:T(8,128)(2,1)S(1)}, f16[448,512]{1,0:T(8,128)(2,1)S(1)}, u32[]{:S(2)}, u32[]{:S(2)}) collective-permute-start(f16[448,512]{1,0:T(8,128)(2,1)S(1)} %fusion.7), channel_id=1, source_target_pairs={{0,2},{1,31},{2,4},{3,1},{4,6},{5,3},{6,8},{7,5},{8,10},{9,7},{10,... | collective-permute-start | bytes 1376264 | tf_op jit(solution)/shard_map/ppermute | solution.py:266
  91.5 5.0 %collective-permute-start.16 = (f16[448,512]{1,0:T(8,128)(2,1)S(1)}, f16[448,512]{1,0:T(8,128)(2,1)S(1)}, u32[]{:S(2)}, u32[]{:S(2)}) collective-permute-start(f16[448,512]{1,0:T(8,128)(2,1)S(1)} %fusion.6), channel_id=1, source_target_pairs={{0,2},{1,31},{2,4},{3,1},{4,6},{5,3},{6,8},{7,5},{8,10},{9,7},{10,... | collective-permute-start | bytes 1376264 | tf_op jit(solution)/shard_map/ppermute | solution.py:266
  96.5 1.7 %shard_map.71 = f32[896,1024]{1,0:T(8,128)S(1)} custom-call(bf16[1792,128]{1,0:T(8,128)(2,1)S(1)} %copy-done.2, bf16[5376,128]{1,0:T(8,128)(2,1)S(1)} %collective-permute-done.5.b_ref, bf16[3584,128]{1,0:T(8,128)(2,1)S(1)} %collective-permute-done.12.c_ref.d_ref, bf16[3584,128]{1,0:T(8,128)(2,1)S(1)} %collective-permute-done.12.c_ref.d_ref, ...), custom_call_target="tpu_custom_call" | custom-call | flops 37580963840 | bytes 5505024 | tf_op jit(solution)/shard_map/pallas_call | solution.py:147
  98.4 3.5 %collective-permute-start.15 = (f16[448,512]{1,0:T(8,128)(2,1)S(1)}, f16[448,512]{1,0:T(8,128)(2,1)S(1)}, u32[]{:S(2)}, u32[]{:S(2)}) collective-permute-start(f16[448,512]{1,0:T(8,128)(2,1)S(1)} %fusion.5), channel_id=1, source_target_pairs={{0,2},{1,31},{2,4},{3,1},{4,6},{5,3},{6,8},{7,5},{8,10},{9,7},{10,... | collective-permute-start | bytes 1376264 | tf_op jit(solution)/shard_map/ppermute | solution.py:266
  102.1 5.0 %collective-permute-start.18 = (f16[448,512]{1,0:T(8,128)(2,1)S(1)}, f16[448,512]{1,0:T(8,128)(2,1)S(1)}, u32[]{:S(2)}, u32[]{:S(2)}) collective-permute-start(f16[448,512]{1,0:T(8,128)(2,1)S(1)} %fusion.4), channel_id=1, source_target_pairs={{0,2},{1,31},{2,4},{3,1},{4,6},{5,3},{6,8},{7,5},{8,10},{9,7},{10,... | collective-permute-start | bytes 1376264 | tf_op jit(solution)/shard_map/ppermute | solution.py:266
  107.8 4.6 %collective-permute-start.17 = (f16[448,512]{1,0:T(8,128)(2,1)S(1)}, f16[448,512]{1,0:T(8,128)(2,1)S(1)}, u32[]{:S(2)}, u32[]{:S(2)}) collective-permute-start(f16[448,512]{1,0:T(8,128)(2,1)S(1)} %fusion.3), channel_id=1, source_target_pairs={{0,2},{1,31},{2,4},{3,1},{4,6},{5,3},{6,8},{7,5},{8,10},{9,7},{10,... | collective-permute-start | bytes 1376264 | tf_op jit(solution)/shard_map/ppermute | solution.py:266
  113.0 4.7 %collective-permute-start.20 = (f16[448,512]{1,0:T(8,128)(2,1)S(1)}, f16[448,512]{1,0:T(8,128)(2,1)S(1)}, u32[]{:S(2)}, u32[]{:S(2)}) collective-permute-start(f16[448,512]{1,0:T(8,128)(2,1)S(1)} %fusion.2), channel_id=1, source_target_pairs={{0,2},{1,31},{2,4},{3,1},{4,6},{5,3},{6,8},{7,5},{8,10},{9,7},{10,... | collective-permute-start | bytes 1376264 | tf_op jit(solution)/shard_map/ppermute | solution.py:266
  117.7 1.7 %shard_map.72 = f32[896,1024]{1,0:T(8,128)S(1)} custom-call(bf16[1792,128]{1,0:T(8,128)(2,1)S(1)} %copy-done.2, bf16[5376,128]{1,0:T(8,128)(2,1)S(1)} %collective-permute-done.5.b_ref, bf16[3584,128]{1,0:T(8,128)(2,1)S(1)} %collective-permute-done.12.c_ref.d_ref, bf16[3584,128]{1,0:T(8,128)(2,1)S(1)} %collective-permute-done.12.c_ref.d_ref, ...), custom_call_target="tpu_custom_call" | custom-call | flops 37580963840 | bytes 5505024 | tf_op jit(solution)/shard_map/pallas_call | solution.py:147
  119.6 3.5 %collective-permute-start.19 = (f16[448,512]{1,0:T(8,128)(2,1)S(1)}, f16[448,512]{1,0:T(8,128)(2,1)S(1)}, u32[]{:S(2)}, u32[]{:S(2)}) collective-permute-start(f16[448,512]{1,0:T(8,128)(2,1)S(1)} %fusion.1), channel_id=1, source_target_pairs={{0,2},{1,31},{2,4},{3,1},{4,6},{5,3},{6,8},{7,5},{8,10},{9,7},{10,... | collective-permute-start | bytes 1376264 | tf_op jit(solution)/shard_map/ppermute | solution.py:266
  123.3 10.4 %collective-permute-start.21 = (f16[448,512]{1,0:T(8,128)(2,1)S(1)}, f16[448,512]{1,0:T(8,128)(2,1)S(1)}, u32[]{:S(2)}, u32[]{:S(2)}) collective-permute-start(f16[448,512]{1,0:T(8,128)(2,1)S(1)} %fusion), channel_id=1, source_target_pairs={{0,3},{1,30},{2,5},{3,0},{4,7},{5,2},{6,9},{7,4},{8,11},{9,6},{10,... | collective-permute-start | bytes 1376264 | tf_op jit(solution)/shard_map/ppermute | solution.py:266
  136.3 6.3 %collective-permute-done.21 = f16[448,512]{1,0:T(8,128)(2,1)S(1)} collective-permute-done((f16[448,512]{1,0:T(8,128)(2,1)S(1)}, f16[448,512]{1,0:T(8,128)(2,1)S(1)}, u32[]{:S(2)}, u32[]{:S(2)}) %collective-permute-start.21) | collective-permute-done | bytes 458784 | tf_op jit(solution)/shard_map/ppermute | solution.py:266
  142.9 14.2 %all_to_all.5 = f16[16,28,512]{2,1,0:T(8,128)(2,1)S(1)} all-to-all(f16[16,28,512]{2,1,0:T(8,128)(2,1)S(1)} %reshape.12), channel_id=1, replica_groups=mesh['ylo'=2,'x'=4,'yhi'=2,'z'=16,'core'=2] {'ylo','x','core'}, dimensions={0} | all-to-all | bytes 917504 | tf_op jit(solution)/shard_map/all_to_all | solution.py:293
  157.4 2.4 %shard_map.73 = (f32[28,512]{1,0:T(8,128)}, f32[28,512]{1,0:T(8,128)}, f32[28,512]{1,0:T(8,128)}) custom-call(f32[16,32,512]{2,1,0:T(8,128)S(1)} %pad.6.g_ref, bf16[28,512]{1,0:T(8,128)(2,1)S(1)} %copy-done.1), custom_call_target="tpu_custom_call" | custom-call | tf_op jit(solution)/shard_map/pallas_call | solution.py:213
  (67 shorter events, 11.6 us)
Async XLA Ops:
  7.1 10.8 %collective-permute-start = (bf16[2752,128]{1,0:T(8,128)(2,1)}, bf16[2752,128]{1,0:T(8,128)(2,1)S(1)}, u32[]{:S(2)}, u32[]{:S(2)}) collective-permute-start(bf16[2752,128]{1,0:T(8,128)(2,1)} %get-tuple-element.38), channel_id=1, source_target_pairs={{0,1},{1,0},{32,33},{33,32},{2,3},{3,2},{34,35},{35,34},{4,5},{5,4... | collective-permute-start | bytes 2113544 | tf_op jit(solution)/shard_map/ppermute | solution.py:237
  15.9 10.0 %collective-permute-start.1 = (bf16[736,128]{1,0:T(8,128)(2,1)}, bf16[736,128]{1,0:T(8,128)(2,1)S(1)}, u32[]{:S(2)}, u32[]{:S(2)}) collective-permute-start(bf16[736,128]{1,0:T(8,128)(2,1)} %get-tuple-element.41), channel_id=1, source_target_pairs={{0,32},{1,33},{32,0},{33,1},{2,34},{3,35},{34,2},{35,3},{4,36},{5,... | collective-permute-start | bytes 565256 | tf_op jit(solution)/shard_map/ppermute | solution.py:237
  17.9 12.0 %collective-permute-start.2 = (bf16[736,128]{1,0:T(8,128)(2,1)S(1)}, bf16[736,128]{1,0:T(8,128)(2,1)S(1)}, u32[]{:S(2)}, u32[]{:S(2)}) collective-permute-start(bf16[736,128]{1,0:T(8,128)(2,1)S(1)} %slice.108), channel_id=1, source_target_pairs={{0,32},{1,33},{32,0},{33,1},{2,34},{3,35},{34,2},{35,3},{4,36},{5,... | collective-permute-start | bytes 565256 | tf_op jit(solution)/shard_map/ppermute | solution.py:237
  29.9 0.9 copy-start.5
  30.8 15.2 %copy-start.4 = (bf16[896,128]{1,0:T(8,128)(2,1)S(1)}, bf16[896,128]{1,0:T(8,128)(2,1)}, u32[]{:S(2)}) copy-start(bf16[896,128]{1,0:T(8,128)(2,1)} %get-tuple-element.37.a_ref) | copy-start | bytes 688132
  31.3 14.6 %collective-permute-start.3 = (bf16[1792,128]{1,0:T(8,128)(2,1)S(1)}, bf16[1792,128]{1,0:T(8,128)(2,1)S(1)}, u32[]{:S(2)}, u32[]{:S(2)}) collective-permute-start(bf16[1792,128]{1,0:T(8,128)(2,1)S(1)} %pad_maximum_fusion.1), channel_id=1, source_target_pairs={{0,32},{1,33},{32,0},{33,1},{2,34},{3,35},{34,2},{35,3},{4,36},{5,... | collective-permute-start | bytes 1376264 | tf_op jit(solution)/shard_map/ppermute | solution.py:237
  33.6 16.1 %collective-permute-start.4 = (f16[224,1024]{1,0:T(8,128)(2,1)S(1)}, f16[224,1024]{1,0:T(8,128)(2,1)S(1)}, u32[]{:S(2)}, u32[]{:S(2)}) collective-permute-start(f16[224,1024]{1,0:T(8,128)(2,1)S(1)} %convert_element_type.102), channel_id=1, source_target_pairs={{0,2},{1,31},{2,4},{3,1},{4,6},{5,3},{6,8},{7,5},{8,10},{9,7},{10,... | collective-permute-start | bytes 1376264 | tf_op jit(solution)/shard_map/ppermute | solution.py:266
  41.9 5.7 %collective-permute-start.5 = (bf16[5376,128]{1,0:T(8,128)(2,1)}, bf16[5376,128]{1,0:T(8,128)(2,1)S(1)}, u32[]{:S(2)}, u32[]{:S(2)}) collective-permute-start(bf16[5376,128]{1,0:T(8,128)(2,1)} %get-tuple-element.48), channel_id=1, source_target_pairs={{0,1},{1,0},{32,33},{33,32},{2,3},{3,2},{34,35},{35,34},{4,5},{5,4... | collective-permute-start | bytes 4128776 | tf_op jit(solution)/shard_map/ppermute | solution.py:237
  46.0 1.7 %copy-start.7 = (bf16[896,128]{1,0:T(8,128)(2,1)S(1)}, bf16[896,128]{1,0:T(8,128)(2,1)}, u32[]{:S(2)}) copy-start(bf16[896,128]{1,0:T(8,128)(2,1)} %get-tuple-element.46) | copy-start | bytes 688132
  47.7 16.9 %collective-permute-start.7 = (bf16[1792,128]{1,0:T(8,128)(2,1)S(1)}, bf16[1792,128]{1,0:T(8,128)(2,1)S(1)}, u32[]{:S(2)}, u32[]{:S(2)}) collective-permute-start(bf16[1792,128]{1,0:T(8,128)(2,1)S(1)} %pad_maximum_fusion.2), channel_id=1, source_target_pairs={{0,32},{1,33},{32,0},{33,1},{2,34},{3,35},{34,2},{35,3},{4,36},{5,... | collective-permute-start | bytes 1376264 | tf_op jit(solution)/shard_map/ppermute | solution.py:237
  49.7 12.2 %copy-start.6 = (bf16[1792,128]{1,0:T(8,128)(2,1)S(1)}, bf16[1792,128]{1,0:T(8,128)(2,1)}, u32[]{:S(2)}) copy-start(bf16[1792,128]{1,0:T(8,128)(2,1)} %get-tuple-element.56) | copy-start | bytes 1376260
  50.5 24.6 %copy-start.3 = (bf16[896,128]{1,0:T(8,128)(2,1)S(1)}, bf16[896,128]{1,0:T(8,128)(2,1)}, u32[]{:S(2)}) copy-start(bf16[896,128]{1,0:T(8,128)(2,1)} %get-tuple-element.53.a_ref) | copy-start | bytes 688132
  50.5 14.2 %collective-permute-start.6 = (f16[448,512]{1,0:T(8,128)(2,1)S(1)}, f16[448,512]{1,0:T(8,128)(2,1)S(1)}, u32[]{:S(2)}, u32[]{:S(2)}) collective-permute-start(f16[448,512]{1,0:T(8,128)(2,1)S(1)} %get-tuple-element.72), channel_id=1, source_target_pairs={{0,2},{1,31},{2,4},{3,1},{4,6},{5,3},{6,8},{7,5},{8,10},{9,7},{10,... | collective-permute-start | bytes 1376264 | tf_op jit(solution)/shard_map/ppermute | solution.py:266
  59.2 10.6 %collective-permute-start.9 = (f16[448,512]{1,0:T(8,128)(2,1)S(1)}, f16[448,512]{1,0:T(8,128)(2,1)S(1)}, u32[]{:S(2)}, u32[]{:S(2)}) collective-permute-start(f16[448,512]{1,0:T(8,128)(2,1)S(1)} %get-tuple-element.71), channel_id=1, source_target_pairs={{0,2},{1,31},{2,4},{3,1},{4,6},{5,3},{6,8},{7,5},{8,10},{9,7},{10,... | collective-permute-start | bytes 1376264 | tf_op jit(solution)/shard_map/ppermute | solution.py:266
  62.0 23.9 %collective-permute-start.12 = (bf16[3584,128]{1,0:T(8,128)(2,1)S(1)}, bf16[3584,128]{1,0:T(8,128)(2,1)S(1)}, u32[]{:S(2)}, u32[]{:S(2)}) collective-permute-start(bf16[3584,128]{1,0:T(8,128)(2,1)S(1)} %pad_maximum_fusion), channel_id=1, source_target_pairs={{0,32},{1,33},{32,0},{33,1},{2,34},{3,35},{34,2},{35,3},{4,36},{5,... | collective-permute-start | bytes 2752520 | tf_op jit(solution)/shard_map/ppermute | solution.py:237
  64.8 11.9 %collective-permute-start.8 = (f16[448,512]{1,0:T(8,128)(2,1)S(1)}, f16[448,512]{1,0:T(8,128)(2,1)S(1)}, u32[]{:S(2)}, u32[]{:S(2)}) collective-permute-start(f16[448,512]{1,0:T(8,128)(2,1)S(1)} %fusion.11), channel_id=1, source_target_pairs={{0,2},{1,31},{2,4},{3,1},{4,6},{5,3},{6,8},{7,5},{8,10},{9,7},{10,... | collective-permute-start | bytes 1376264 | tf_op jit(solution)/shard_map/ppermute | solution.py:266
  70.0 10.7 %collective-permute-start.11 = (f16[448,512]{1,0:T(8,128)(2,1)S(1)}, f16[448,512]{1,0:T(8,128)(2,1)S(1)}, u32[]{:S(2)}, u32[]{:S(2)}) collective-permute-start(f16[448,512]{1,0:T(8,128)(2,1)S(1)} %fusion.10), channel_id=1, source_target_pairs={{0,2},{1,31},{2,4},{3,1},{4,6},{5,3},{6,8},{7,5},{8,10},{9,7},{10,... | collective-permute-start | bytes 1376264 | tf_op jit(solution)/shard_map/ppermute | solution.py:266
  76.8 19.8 %copy-start.2 = (bf16[1792,128]{1,0:T(8,128)(2,1)S(1)}, bf16[1792,128]{1,0:T(8,128)(2,1)}, u32[]{:S(2)}) copy-start(bf16[1792,128]{1,0:T(8,128)(2,1)} %get-tuple-element.61.a_ref) | copy-start | bytes 1376260
  76.9 9.5 %collective-permute-start.10 = (f16[448,512]{1,0:T(8,128)(2,1)S(1)}, f16[448,512]{1,0:T(8,128)(2,1)S(1)}, u32[]{:S(2)}, u32[]{:S(2)}) collective-permute-start(f16[448,512]{1,0:T(8,128)(2,1)S(1)} %fusion.9), channel_id=1, source_target_pairs={{0,2},{1,31},{2,4},{3,1},{4,6},{5,3},{6,8},{7,5},{8,10},{9,7},{10,... | collective-permute-start | bytes 1376264 | tf_op jit(solution)/shard_map/ppermute | solution.py:266
  80.9 10.5 %collective-permute-start.14 = (f16[448,512]{1,0:T(8,128)(2,1)S(1)}, f16[448,512]{1,0:T(8,128)(2,1)S(1)}, u32[]{:S(2)}, u32[]{:S(2)}) collective-permute-start(f16[448,512]{1,0:T(8,128)(2,1)S(1)} %fusion.8), channel_id=1, source_target_pairs={{0,2},{1,31},{2,4},{3,1},{4,6},{5,3},{6,8},{7,5},{8,10},{9,7},{10,... | collective-permute-start | bytes 1376264 | tf_op jit(solution)/shard_map/ppermute | solution.py:266
  86.6 11.6 %collective-permute-start.13 = (f16[448,512]{1,0:T(8,128)(2,1)S(1)}, f16[448,512]{1,0:T(8,128)(2,1)S(1)}, u32[]{:S(2)}, u32[]{:S(2)}) collective-permute-start(f16[448,512]{1,0:T(8,128)(2,1)S(1)} %fusion.7), channel_id=1, source_target_pairs={{0,2},{1,31},{2,4},{3,1},{4,6},{5,3},{6,8},{7,5},{8,10},{9,7},{10,... | collective-permute-start | bytes 1376264 | tf_op jit(solution)/shard_map/ppermute | solution.py:266
  91.5 10.4 %collective-permute-start.16 = (f16[448,512]{1,0:T(8,128)(2,1)S(1)}, f16[448,512]{1,0:T(8,128)(2,1)S(1)}, u32[]{:S(2)}, u32[]{:S(2)}) collective-permute-start(f16[448,512]{1,0:T(8,128)(2,1)S(1)} %fusion.6), channel_id=1, source_target_pairs={{0,2},{1,31},{2,4},{3,1},{4,6},{5,3},{6,8},{7,5},{8,10},{9,7},{10,... | collective-permute-start | bytes 1376264 | tf_op jit(solution)/shard_map/ppermute | solution.py:266
  98.4 9.3 %collective-permute-start.15 = (f16[448,512]{1,0:T(8,128)(2,1)S(1)}, f16[448,512]{1,0:T(8,128)(2,1)S(1)}, u32[]{:S(2)}, u32[]{:S(2)}) collective-permute-start(f16[448,512]{1,0:T(8,128)(2,1)S(1)} %fusion.5), channel_id=1, source_target_pairs={{0,2},{1,31},{2,4},{3,1},{4,6},{5,3},{6,8},{7,5},{8,10},{9,7},{10,... | collective-permute-start | bytes 1376264 | tf_op jit(solution)/shard_map/ppermute | solution.py:266
  102.1 10.7 %collective-permute-start.18 = (f16[448,512]{1,0:T(8,128)(2,1)S(1)}, f16[448,512]{1,0:T(8,128)(2,1)S(1)}, u32[]{:S(2)}, u32[]{:S(2)}) collective-permute-start(f16[448,512]{1,0:T(8,128)(2,1)S(1)} %fusion.4), channel_id=1, source_target_pairs={{0,2},{1,31},{2,4},{3,1},{4,6},{5,3},{6,8},{7,5},{8,10},{9,7},{10,... | collective-permute-start | bytes 1376264 | tf_op jit(solution)/shard_map/ppermute | solution.py:266
  107.8 11.6 %collective-permute-start.17 = (f16[448,512]{1,0:T(8,128)(2,1)S(1)}, f16[448,512]{1,0:T(8,128)(2,1)S(1)}, u32[]{:S(2)}, u32[]{:S(2)}) collective-permute-start(f16[448,512]{1,0:T(8,128)(2,1)S(1)} %fusion.3), channel_id=1, source_target_pairs={{0,2},{1,31},{2,4},{3,1},{4,6},{5,3},{6,8},{7,5},{8,10},{9,7},{10,... | collective-permute-start | bytes 1376264 | tf_op jit(solution)/shard_map/ppermute | solution.py:266
  113.0 10.1 %collective-permute-start.20 = (f16[448,512]{1,0:T(8,128)(2,1)S(1)}, f16[448,512]{1,0:T(8,128)(2,1)S(1)}, u32[]{:S(2)}, u32[]{:S(2)}) collective-permute-start(f16[448,512]{1,0:T(8,128)(2,1)S(1)} %fusion.2), channel_id=1, source_target_pairs={{0,2},{1,31},{2,4},{3,1},{4,6},{5,3},{6,8},{7,5},{8,10},{9,7},{10,... | collective-permute-start | bytes 1376264 | tf_op jit(solution)/shard_map/ppermute | solution.py:266
  119.4 3.7 %copy-start = (f32[896,1024]{1,0:T(8,128)}, f32[896,1024]{1,0:T(8,128)S(1)}, u32[]{:S(2)}) copy-start(f32[896,1024]{1,0:T(8,128)S(1)} %shard_map.72) | copy-start | bytes 11010052
  119.4 14.2 %copy-start.8 = (s32[2]{0:T(128)S(1)}, s32[2]{0:T(128)}, u32[]{:S(2)}) copy-start(s32[2]{0:T(128)} %len_ref.1) | copy-start | bytes 28
  119.6 15.4 %collective-permute-start.19 = (f16[448,512]{1,0:T(8,128)(2,1)S(1)}, f16[448,512]{1,0:T(8,128)(2,1)S(1)}, u32[]{:S(2)}, u32[]{:S(2)}) collective-permute-start(f16[448,512]{1,0:T(8,128)(2,1)S(1)} %fusion.1), channel_id=1, source_target_pairs={{0,2},{1,31},{2,4},{3,1},{4,6},{5,3},{6,8},{7,5},{8,10},{9,7},{10,... | collective-permute-start | bytes 1376264 | tf_op jit(solution)/shard_map/ppermute | solution.py:266
  123.3 19.3 %collective-permute-start.21 = (f16[448,512]{1,0:T(8,128)(2,1)S(1)}, f16[448,512]{1,0:T(8,128)(2,1)S(1)}, u32[]{:S(2)}, u32[]{:S(2)}) collective-permute-start(f16[448,512]{1,0:T(8,128)(2,1)S(1)} %fusion), channel_id=1, source_target_pairs={{0,3},{1,30},{2,5},{3,0},{4,7},{5,2},{6,9},{7,4},{8,11},{9,6},{10,... | collective-permute-start | bytes 1376264 | tf_op jit(solution)/shard_map/ppermute | solution.py:266
  142.6 14.8 %copy-start.1 = (bf16[28,512]{1,0:T(8,128)(2,1)S(1)}, bf16[28,512]{1,0:T(8,128)(2,1)}, u32[]{:S(2)}) copy-start(bf16[28,512]{1,0:T(8,128)(2,1)} %w_ref.1) | copy-start | bytes 86020
